TPU v7x, 32 devices: a whole 2x2x4 slice. The times are simulated.
32 devices in a mesh: ctx: 16 (over z, y, core), fsdp: 2 (over x).
Axes of the slice: x: 2, y: 2, z: 4, core: 2. Of those that a mesh axis runs over, the one named last changes fastest.
Arguments:
- hidden: bfloat16 [2, 4096, 5376], P('fsdp', 'ctx'), may hold values from -6 to 6
- queries: bfloat16 [2, 4096, 2048], P('fsdp', 'ctx'), may hold values from -23 to 23
- key_heads: bfloat16 [2, 4096, 1024], P('fsdp', 'ctx'), may hold values from -6 to 6
- w_value: bfloat16 [5376, 1024], P('fsdp'), may hold values from -0.078125 to 0.078125
- d_out: bfloat16 [2, 4096, 2048], P('fsdp', 'ctx'), may hold values from -6 to 6
- segments: int32 [2, 4096], P('fsdp', 'ctx'), may hold values from 0 to 3, never falling along the last dimension, each value on 1 to 2048 neighbouring positions
Outputs:
- attn_out: bfloat16 [2, 4096, 2048], P('fsdp', 'ctx')
- d_queries: bfloat16 [2, 4096, 2048], P('fsdp', 'ctx')
- d_keys: bfloat16 [2, 4096, 1024], P('fsdp', 'ctx')
- d_hidden: bfloat16 [2, 4096, 5376], P('fsdp', 'ctx')
- d_w_value: float32 [5376, 1024], P(('ctx', 'fsdp'))
Inputs may be any that keep to these rules, and one draw needn't show every extreme that they name: `segments`: document ids never fall along a sequence; a document holds at most half of the 4096 tokens.
All inputs are finite; a program needn't handle non-finite values.
Results may differ from a plain program's by a relative error of at most 0.024.
Values may be sent and summed in bfloat16 or wider, within the bound.
No kernel may reach another device: no remote copies, remote signals or barrier semaphores. Data moves between devices by JAX's collectives and lax.ppermute only.
A program may use at most 256 MiB of HBM per device.

v0:
```python
import functools
import math

import jax
import jax.numpy as jnp
from jax import lax
from jax.experimental import pallas as pl
from jax.experimental.pallas import tpu as pltpu
from jax.sharding import PartitionSpec as P

HQ = 16
HK = 8
HD = 128
WINDOW = 1024
GROUP = 2
NEG = -1e30

score_scale = 1.0 / math.sqrt(168.0)
exp2_scale = score_scale / math.log(2.0)

BF16 = jnp.bfloat16
F32 = jnp.float32
NT = (((1,), (1,)), ((), ()))
TN = (((0,), (0,)), ((), ()))


def dot(a, b, dims=(((1,), (0,)), ((), ()))):
    return lax.dot_general(a, b, dims, preferred_element_type=F32)


def probs_kernel(blk, n_back, core_ref, low_ref, q_own, q_other, do_own, do_other, *refs):
    n_arr = n_back + 1
    k_refs = refs[:n_arr]
    e_ref, inv_ref, dot_ref = refs[n_arr : n_arr + 3]
    dv_refs = refs[n_arr + 3 : 2 * n_arr + 3]
    bias, s_scr, dv_acc, q_buf, do_buf = refs[2 * n_arr + 3 :]
    span_blocks = WINDOW // blk + 1
    core = core_ref[0]

    @pl.when(pl.program_id(0) == 0)
    def _():
        for qb in range(2):
            kpos = lax.broadcasted_iota(jnp.int32, (span_blocks * blk, blk), 0) + qb * blk
            qpos = lax.broadcasted_iota(jnp.int32, (span_blocks * blk, blk), 1) + (qb * blk + WINDOW)
            low = low_ref[:, qb * blk : (qb + 1) * blk]
            ok = (kpos >= low) & (kpos <= qpos)
            bias[qb] = jnp.where(ok, 0.0, NEG)

    q_buf[core] = q_own[...]
    q_buf[1 - core] = q_other[...]
    do_buf[core] = do_own[...]
    do_buf[1 - core] = do_other[...]

    def key_block(j):
        return k_refs[j // 2][(j % 2) * blk : (j % 2 + 1) * blk, :]

    def stacked(buf, qb):
        return jnp.concatenate([buf[qb, :, r * HD : (r + 1) * HD] for r in range(GROUP)], 0)

    for qb in range(2):
        qs = stacked(q_buf, qb)
        top = None
        for j in range(span_blocks):
            s = dot(key_block(qb + j), qs, NT)
            b = bias[qb, j * blk : (j + 1) * blk, :]
            s = s * exp2_scale + jnp.concatenate([b] * GROUP, 1)
            s_scr[j] = s
            part = jnp.max(s.reshape(blk // 8, 8, GROUP * blk), axis=0)
            top = part if top is None else jnp.maximum(top, part)
        top = jnp.max(top, axis=0, keepdims=True)
        total = None
        for j in range(span_blocks):
            e = jnp.exp2(s_scr[j] - top)
            part = jnp.sum(e.reshape(blk // 8, 8, GROUP * blk), axis=0)
            total = part if total is None else total + part
            e_ref[0, qb, j * blk : (j + 1) * blk, :] = e.astype(BF16)
        inv = 1.0 / jnp.sum(total, axis=0, keepdims=True)
        inv_ref[0, qb] = inv
        do_t = (stacked(do_buf, qb).astype(F32).T * inv).astype(BF16)
        dot_ref[0, qb] = do_t
        for j in range(span_blocks):
            term = dot(e_ref[0, qb, j * blk : (j + 1) * blk, :], do_t, NT)
            at = slice((qb + j) * blk, (qb + j + 1) * blk)
            if qb == 0 or j == span_blocks - 1:
                dv_acc[at, :] = term
            else:
                dv_acc[at, :] += term
    for a in range(n_arr):
        dv_refs[a][...] = dv_acc[a * 2 * blk : (a + 1) * 2 * blk, :].astype(BF16)


def grads_kernel(blk, n_back, core_ref, e_ref, inv_ref, dot_ref, q_own, q_other, *refs):
    n_arr = n_back + 1
    k_refs = refs[:n_arr]
    v_refs = refs[n_arr : 2 * n_arr]
    out_ref, dq_ref, other_ref = refs[2 * n_arr : 2 * n_arr + 3]
    dk_refs = refs[2 * n_arr + 3 : 3 * n_arr + 3]
    dk_acc, q_buf, out_buf, dq_buf = refs[3 * n_arr + 3 :]
    span_blocks = WINDOW // blk + 1
    core = core_ref[0]

    q_buf[core] = q_own[...]
    q_buf[1 - core] = q_other[...]

    def block_of(arrays, j):
        return arrays[j // 2][(j % 2) * blk : (j % 2 + 1) * blk, :]

    for qb in range(2):
        qs = jnp.concatenate([q_buf[qb, :, r * HD : (r + 1) * HD] for r in range(GROUP)], 0)
        do_t = dot_ref[0, qb]
        out_t = None
        for j in range(span_blocks):
            e = e_ref[0, qb, j * blk : (j + 1) * blk, :]
            part = dot(block_of(v_refs, qb + j), e, TN)
            out_t = part if out_t is None else out_t + part
        out_t = (out_t * inv_ref[0, qb]).astype(BF16).astype(F32)
        delta = jnp.sum(out_t * do_t.astype(F32), axis=0, keepdims=True)
        out = out_t.T.astype(BF16)
        dq_t = None
        for j in range(span_blocks):
            e = e_ref[0, qb, j * blk : (j + 1) * blk, :].astype(F32)
            dp = dot(block_of(v_refs, qb + j), do_t)
            ds = (e * (dp - delta)).astype(BF16)
            term = dot(ds, qs)
            at = slice((qb + j) * blk, (qb + j + 1) * blk)
            if qb == 0 or j == span_blocks - 1:
                dk_acc[at, :] = term
            else:
                dk_acc[at, :] += term
            part = dot(block_of(k_refs, qb + j), ds, TN)
            dq_t = part if dq_t is None else dq_t + part
        dq = (dq_t * score_scale).T.astype(BF16)
        for r in range(GROUP):
            out_buf[qb, :, r * HD : (r + 1) * HD] = out[r * blk : (r + 1) * blk, :]
            dq_buf[qb, :, r * HD : (r + 1) * HD] = dq[r * blk : (r + 1) * blk, :]
    out_ref[...] = out_buf[core]
    dq_ref[...] = dq_buf[core]
    other_ref[0] = out_buf[1 - core]
    other_ref[1] = dq_buf[1 - core]
    for a in range(n_arr):
        dk_refs[a][...] = (dk_acc[a * 2 * blk : (a + 1) * 2 * blk, :] * score_scale).astype(BF16)


def specs_of(rows, width):
    blk = rows // 2
    heads = width // HD
    span = WINDOW + blk
    lanes = GROUP * blk
    head = pl.BlockSpec((rows, HD), lambda g, c: (0, g))
    own = pl.BlockSpec((blk, GROUP * HD), lambda g, c: (0, c[0] * heads + g))
    return blk, heads, span, lanes, head, own


def run_probs(core, low, q, q_other, do, keys, rows, width):
    blk, heads, span, lanes, head, own = specs_of(rows, width)
    n_arr = len(keys)
    return pl.pallas_call(
        functools.partial(probs_kernel, blk, n_arr - 1),
        grid_spec=pltpu.PrefetchScalarGridSpec(
            num_scalar_prefetch=1,
            grid=(heads,),
            in_specs=[
                pl.BlockSpec((1, rows), lambda g, c: (0, 0)),
                own,
                pl.BlockSpec((blk, GROUP * HD), lambda g, c: (0, g)),
                own,
                pl.BlockSpec((blk, GROUP * HD), lambda g, c: (0, heads + g)),
            ]
            + [head] * n_arr,
            out_specs=[
                pl.BlockSpec((1, 2, span, lanes), lambda g, c: (g, 0, 0, 0)),
                pl.BlockSpec((1, 2, 1, lanes), lambda g, c: (g, 0, 0, 0)),
                pl.BlockSpec((1, 2, HD, lanes), lambda g, c: (g, 0, 0, 0)),
            ]
            + [head] * n_arr,
            scratch_shapes=[
                pltpu.VMEM((2, span, blk), F32),
                pltpu.VMEM((span // blk, blk, lanes), F32),
                pltpu.VMEM((WINDOW + rows, HD), F32),
                pltpu.VMEM((2, blk, GROUP * HD), BF16),
                pltpu.VMEM((2, blk, GROUP * HD), BF16),
            ],
        ),
        out_shape=[
            jax.ShapeDtypeStruct((heads, 2, span, lanes), BF16),
            jax.ShapeDtypeStruct((heads, 2, 1, lanes), F32),
            jax.ShapeDtypeStruct((heads, 2, HD, lanes), BF16),
        ]
        + [jax.ShapeDtypeStruct((rows, width), BF16)] * n_arr,
        compiler_params=pltpu.CompilerParams(vmem_limit_bytes=40 * 1024 * 1024),
        cost_estimate=small_cost(),
        name="probs",
    )(core, low, q, q_other, do, q_other, *keys)


def run_grads(core, e, inv, do_t, q, q_other, keys, values, rows, width, head_range, earlier):
    blk, heads, span, lanes, _, _ = specs_of(rows, width)
    n_arr = len(keys)
    low, high = head_range
    full = jax.ShapeDtypeStruct(q.shape, BF16)
    head = pl.BlockSpec((rows, HD), lambda g, c: (0, low + g))
    own = pl.BlockSpec((blk, GROUP * HD), lambda g, c: (0, c[0] * heads + low + g))
    n_in = 5 + 2 * n_arr

    def kernel(*refs):
        grads_kernel(blk, n_arr - 1, *refs[: 1 + n_in], *refs[1 + n_in + len(earlier) :])

    return pl.pallas_call(
        kernel,
        grid_spec=pltpu.PrefetchScalarGridSpec(
            num_scalar_prefetch=1,
            grid=(high - low,),
            in_specs=[
                pl.BlockSpec((1, 2, span, lanes), lambda g, c: (low + g, 0, 0, 0)),
                pl.BlockSpec((1, 2, 1, lanes), lambda g, c: (low + g, 0, 0, 0)),
                pl.BlockSpec((1, 2, HD, lanes), lambda g, c: (low + g, 0, 0, 0)),
                own,
                pl.BlockSpec((blk, GROUP * HD), lambda g, c: (0, low + g)),
            ]
            + [head] * (2 * n_arr)
            + [pl.BlockSpec(memory_space=pl.ANY)] * len(earlier),
            out_specs=[own, own, pl.BlockSpec((2, blk, GROUP * HD), lambda g, c: (0, 0, low + g))] + [head] * n_arr,
            scratch_shapes=[
                pltpu.VMEM((WINDOW + rows, HD), F32),
                pltpu.VMEM((2, blk, GROUP * HD), BF16),
                pltpu.VMEM((2, blk, GROUP * HD), BF16),
                pltpu.VMEM((2, blk, GROUP * HD), BF16),
            ],
        ),
        out_shape=[full, full, jax.ShapeDtypeStruct((2, blk, GROUP * width), BF16)]
        + [jax.ShapeDtypeStruct((rows, width), BF16)] * n_arr,
        input_output_aliases={1 + n_in + i: i for i in range(len(earlier))},
        compiler_params=pltpu.CompilerParams(vmem_limit_bytes=40 * 1024 * 1024),
        cost_estimate=small_cost(),
        name="grads",
    )(core, e, inv, do_t, q, q_other, *keys, *values, *earlier)


def small_cost():
    return pl.CostEstimate(flops=1 << 20, bytes_accessed=1 << 12, transcendentals=0)


def whole():
    return pl.BlockSpec(memory_space=pltpu.VMEM)


def pieces_kernel(dims, at_ref, x_ref, *refs):
    n_z, n_fsdp, out_rows = dims
    outs = refs[: 2 * n_fsdp]
    turned = refs[2 * n_fsdp]
    my_y, my_fsdp = at_ref[0], at_ref[1]
    for c in range(x_ref.shape[1] // HD):
        turned[c * HD : (c + 1) * HD, :] = x_ref[:, c * HD : (c + 1) * HD].astype(F32).T
    for p, out in enumerate(outs):
        flip, s = p // n_fsdp, p % n_fsdp
        y = lax.rem(my_y + flip, 2)
        f = lax.rem(my_fsdp + s, n_fsdp)
        for z in range(n_z):
            parts = []
            for core in range(2):
                block = ((z * 2 + y) * 2 + core) * n_fsdp + f
                parts.append(turned[pl.ds(pl.multiple_of(block * out_rows, 8), out_rows), :])
            out[z * 2 * out_rows : (z + 1) * 2 * out_rows, :] = jnp.concatenate(parts, 0).astype(BF16)


def run_pieces(at, tokens, n_z, n_fsdp, out_rows):
    rows, model = tokens.shape
    shape = jax.ShapeDtypeStruct((n_z * 2 * out_rows, rows), BF16)
    return pl.pallas_call(
        functools.partial(pieces_kernel, (n_z, n_fsdp, out_rows)),
        in_specs=[pl.BlockSpec(memory_space=pltpu.SMEM), whole()],
        out_specs=[whole()] * (2 * n_fsdp),
        out_shape=[shape] * (2 * n_fsdp),
        scratch_shapes=[pltpu.VMEM((model, rows), F32)],
        compiler_params=pltpu.CompilerParams(vmem_limit_bytes=32 * 1024 * 1024),
        cost_estimate=small_cost(),
        name="pieces",
    )(at, tokens)


def product_kernel(at_ref, x_ref, w_ref, o_ref):
    o_ref[...] = dot(x_ref[...], w_ref[...]).astype(o_ref.dtype)


def run_product(at, x, w, kind):
    rows = x.shape[0]
    depth, width = w.shape
    tile = 512
    return pl.pallas_call(
        product_kernel,
        grid_spec=pltpu.PrefetchScalarGridSpec(
            num_scalar_prefetch=1,
            grid=(width // tile,),
            in_specs=[
                pl.BlockSpec((rows, depth), lambda j, at: (0, at[0])),
                pl.BlockSpec((depth, tile), lambda j, at: (0, j)),
            ],
            out_specs=pl.BlockSpec((rows, tile), lambda j, at: (0, j)),
        ),
        out_shape=jax.ShapeDtypeStruct((rows, width), kind),
        compiler_params=pltpu.CompilerParams(vmem_limit_bytes=32 * 1024 * 1024),
        cost_estimate=small_cost(),
        name="product",
    )(at, x, w)


def weight_kernel(n_z, at_ref, *refs):
    n = (len(refs) - 1 - n_z) // 2
    mine, theirs = refs[:n], refs[n]
    dv_refs = refs[n + 1 : 2 * n + 1]
    outs = refs[2 * n + 1 :]
    core, my_z = at_ref[0], at_ref[1]
    count = mine[0].shape[0] // n_z
    rows = mine[0].shape[1]
    for d, out in enumerate(outs):
        z = lax.rem(my_z + d, n_z)
        at = pl.ds(pl.multiple_of(z * count, 16), count)
        total = None
        for p in range(n):
            own = pl.ds(pl.multiple_of(core * rows, rows), rows)
            other = pl.ds(pl.multiple_of((1 - core) * rows, rows), rows)
            term = dot(mine[p][at, :], dv_refs[p][own, :])
            term = term + dot(theirs[at, p * rows : (p + 1) * rows], dv_refs[p][other, :])
            total = term if total is None else total + term
        out[...] = total.astype(out.dtype)


def run_weight(at, mine, theirs, dv_places, n_z):
    count = theirs.shape[0] // n_z
    width = dv_places[0].shape[1]
    shapes = [jax.ShapeDtypeStruct((count, width), F32 if d == 0 else BF16) for d in range(n_z)]
    return pl.pallas_call(
        functools.partial(weight_kernel, n_z),
        in_specs=[pl.BlockSpec(memory_space=pltpu.SMEM)] + [whole()] * (2 * len(mine) + 1),
        out_specs=[whole()] * n_z,
        out_shape=shapes,
        compiler_params=pltpu.CompilerParams(vmem_limit_bytes=40 * 1024 * 1024),
        cost_estimate=small_cost(),
        name="weight",
    )(at, *mine, theirs, *dv_places)


def tokens_kernel(n_fsdp, at_ref, dv_ref, w_ref, own_ref, *others):
    made = dot(dv_ref[...], w_ref[...], NT).astype(BF16)
    rows = own_ref.shape[0]
    own_ref[...] = made[:rows]
    for s, ref in enumerate(others):
        ref[...] = made[(s + 1) * rows : (s + 2) * rows]


def run_tokens(at, dv_rows, w, n_fsdp):
    slab, width = w.shape
    rows = dv_rows.shape[0] // n_fsdp
    tile = slab // 3 if slab % (3 * HD) == 0 else slab
    n_tiles = slab // tile
    return pl.pallas_call(
        functools.partial(tokens_kernel, n_fsdp),
        grid_spec=pltpu.PrefetchScalarGridSpec(
            num_scalar_prefetch=1,
            grid=(n_tiles,),
            in_specs=[
                pl.BlockSpec(dv_rows.shape, lambda j, at: (0, 0)),
                pl.BlockSpec((tile, width), lambda j, at: (j, 0)),
            ],
            out_specs=[pl.BlockSpec((rows, tile), lambda j, at: (0, at[0] * n_tiles + j))]
            + [pl.BlockSpec((rows, tile), lambda j, at: (0, j))] * (n_fsdp - 1),
        ),
        out_shape=[jax.ShapeDtypeStruct((rows, slab * n_fsdp), BF16)]
        + [jax.ShapeDtypeStruct((rows, slab), BF16)] * (n_fsdp - 1),
        compiler_params=pltpu.CompilerParams(vmem_limit_bytes=40 * 1024 * 1024),
        cost_estimate=small_cost(),
        name="tokens",
    )(at, dv_rows, w)


def shifted(x, by):
    length = lax.axis_size("ctx")
    return lax.ppermute(x, "ctx", [(i, i + by) for i in range(length) if 0 <= i + by < length])


def swapped(x):
    return lax.ppermute(x, "ctx", [(i, i ^ 1) for i in range(lax.axis_size("ctx"))])


def rotated(x, by):
    length = lax.axis_size("fsdp")
    return lax.ppermute(x, "fsdp", [(i, (i + by) % length) for i in range(length)])


def moved(x, flip, by):
    n_ctx, n_fsdp = lax.axis_size("ctx"), lax.axis_size("fsdp")
    pairs = [
        (c * n_fsdp + f, (c ^ (2 * flip)) * n_fsdp + (f + by) % n_fsdp)
        for c in range(n_ctx)
        for f in range(n_fsdp)
    ]
    return lax.ppermute(x, ("ctx", "fsdp"), pairs)


def cols(x, at, width):
    return lax.dynamic_slice_in_dim(x, at * width, width, x.ndim - 1)


def rows_of(x, at, count):
    return lax.dynamic_slice_in_dim(x, at * count, count, 0)


def placed(core, own, other, axis):
    both = jnp.concatenate([own, own], axis)
    return lax.dynamic_update_slice_in_dim(both, other, (1 - core) * own.shape[axis], axis)


def after(x, *earlier):
    return lax.optimization_barrier((x, *earlier))[0]


def shards(hidden, queries, key_heads, w_value, d_out, segments):
    shard_rows = hidden.shape[1]
    model = hidden.shape[2]
    kv_width = w_value.shape[1]
    n_ctx = lax.axis_size("ctx")
    n_fsdp = lax.axis_size("fsdp")
    chip_rows = 2 * shard_rows
    n_back = WINDOW // chip_rows
    n_z = n_ctx // 4
    my_ctx = lax.axis_index("ctx")
    my_fsdp = lax.axis_index("fsdp")
    core = my_ctx % 2
    core_arg = core.astype(jnp.int32).reshape(1)
    chip = my_ctx // 2
    my_y = chip % 2
    my_z = chip // 2
    half_kv = kv_width // 2
    slab = model // n_fsdp
    tokens = hidden[0]
    first = chip * chip_rows

    own_tags = segments[0].astype(BF16)
    tag_row = lax.dynamic_update_slice_in_dim(jnp.zeros((half_kv,), BF16), own_tags, core * shard_rows, 0)
    tag_rows = jnp.concatenate([tag_row[None], jnp.zeros((15, half_kv), BF16)], 0)
    k_sent = jnp.concatenate([cols(key_heads[0], 1 - core, half_kv), tag_rows], 0)
    got = swapped(k_sent)

    slabs = [after(cols(tokens, (my_fsdp + s) % n_fsdp, slab), k_sent) for s in range(1, n_fsdp)]
    sent = [rotated(x, s + 1) for s, x in enumerate(slabs)]
    half_q = queries.shape[2] // 2
    q_sent = jnp.concatenate([cols(queries[0], 1 - core, half_q), cols(d_out[0], 1 - core, half_q)], 1)
    q_other = swapped(after(q_sent, *slabs))

    k_own = jnp.concatenate(
        [
            placed(core, cols(key_heads[0], core, half_kv), got[:shard_rows], 0),
            tag_rows + got[shard_rows:],
        ],
        0,
    )
    keys = [shifted(k_own, 2 * d) for d in range(n_back, 0, -1)] + [k_own]
    aligned = slab % HD == 0
    fsdp_arg = my_fsdp.astype(jnp.int32).reshape(1)
    zero_arg = jnp.zeros((1,), jnp.int32)
    if aligned:
        value_own = run_product(after(fsdp_arg, k_own), tokens, w_value, F32)
    else:
        value_own = dot(cols(tokens, my_fsdp, slab), w_value)

    out_rows = model // (n_ctx * n_fsdp)
    places = [(flip, s) for flip in range(2) for s in range(n_fsdp)]
    if out_rows % 8 == 0:
        at = jnp.stack([my_y, my_fsdp]).astype(jnp.int32)
        pieces = run_pieces(after(at, k_own), tokens, n_z, n_fsdp, out_rows)
    else:
        by_place = tokens.T.reshape(n_z, 2, 2, n_fsdp, out_rows, shard_rows)
        pieces = []
        for flip, s in places:
            piece = lax.dynamic_index_in_dim(by_place, my_y ^ flip, 1, keepdims=False)
            piece = lax.dynamic_index_in_dim(piece, (my_fsdp + s) % n_fsdp, 2, keepdims=False)
            pieces.append(piece.reshape(n_z * 2 * out_rows, shard_rows))

    span_tags = jnp.concatenate([k[chip_rows, :chip_rows] for k in keys], 0)
    key_at = jnp.arange(WINDOW + chip_rows, dtype=jnp.int32)
    chip_tags = keys[n_back][chip_rows, :chip_rows]
    before = (span_tags[None, :] < chip_tags[:, None]) | (key_at + first < WINDOW)[None, :]
    low = jnp.sum(before.astype(jnp.int32), axis=1)
    low = jnp.maximum(low, jnp.arange(1, chip_rows + 1, dtype=jnp.int32))[None, :]

    if aligned:
        partial = [run_product(zero_arg, x, w_value, BF16) for x in sent]
    else:
        partial = [dot(x, w_value).astype(BF16) for x in sent]
    low = after(low, value_own, *pieces, *partial)
    e, inv, do_t, *dv_terms = run_probs(
        core_arg, low, queries[0], q_other, d_out[0], keys, chip_rows, half_kv
    )
    dv_back = [shifted(dv_terms[n_back - d], -2 * d) for d in range(1, n_back + 1)]

    value_back = [rotated(x, -s - 1) for s, x in enumerate(partial)]
    *value_back, _ = lax.optimization_barrier((*value_back, dv_terms[n_back]))
    value_sum = value_own
    for x in value_back:
        value_sum = value_sum + x.astype(F32)
    own_values = value_sum.astype(BF16)
    v_own = placed(core, cols(own_values, core, half_kv), swapped(cols(own_values, 1 - core, half_kv)), 0)
    vals = [shifted(v_own, 2 * d) for d in range(n_back, 0, -1)] + [v_own]

    *pieces, _ = lax.optimization_barrier((*pieces, partial))
    pieces = [moved(x, flip, s) if flip or s else x for x, (flip, s) in zip(pieces, places)]
    *pieces, _ = lax.optimization_barrier((*pieces, v_own))
    mine = jnp.concatenate(pieces, 1)
    theirs = swapped(mine)

    *dv_back, _ = lax.optimization_barrier((*dv_back, (vals[n_back - 1], pieces)))
    dv_total = dv_terms[n_back].astype(F32)
    for term in dv_back:
        dv_total = dv_total + term.astype(F32)
    dv_chip = dv_total.astype(BF16)

    dv_places = [moved(dv_chip, flip, s) if flip or s else dv_chip for flip, s in places]
    if out_rows % 8 == 0:
        by_z = run_weight(jnp.stack([core, my_z]).astype(jnp.int32), pieces, theirs, dv_places, n_z)
    else:
        weight_term = None
        for at, dv_of in enumerate(dv_places):
            window = slice(at * shard_rows, (at + 1) * shard_rows)
            term = dot(mine[:, window], rows_of(dv_of, core, shard_rows))
            term = term + dot(theirs[:, window], rows_of(dv_of, 1 - core, shard_rows))
            weight_term = term if weight_term is None else weight_term + term
        weight_term = weight_term.reshape(n_z, 2 * out_rows, half_kv)
        by_z = [
            lax.dynamic_index_in_dim(weight_term, (my_z + d) % n_z, 0, keepdims=False).astype(BF16 if d else F32)
            for d in range(n_z)
        ]
    row_sum = by_z[0]
    for d in range(1, n_z):
        piece = lax.ppermute(by_z[d], "ctx", [(i, (i + 4 * d) % n_ctx) for i in range(n_ctx)])
        row_sum = row_sum + piece.astype(F32)
    d_weight = placed(core, rows_of(row_sum, core, out_rows), swapped(rows_of(row_sum, 1 - core, out_rows)), 1)

    dv_fsdp = [dv_places[s] for s in range(n_fsdp)]
    dv_other = swapped(jnp.concatenate([rows_of(x, 1 - core, shard_rows) for x in dv_fsdp], 0))
    dv_rows = placed(
        core, jnp.concatenate([rows_of(x, core, shard_rows) for x in dv_fsdp], 0), dv_other, 1
    )
    if aligned:
        d_tokens, *made = run_tokens(fsdp_arg, dv_rows, w_value, n_fsdp)
    else:
        made = dot(dv_rows, w_value, NT).astype(BF16)
        made = [made[s * shard_rows : (s + 1) * shard_rows] for s in range(n_fsdp)]
        d_tokens = jnp.concatenate([made[0]] * n_fsdp, 1)
        made = made[1:]
    for s in range(1, n_fsdp):
        back = rotated(made[s - 1], -s)
        d_tokens = lax.dynamic_update_slice_in_dim(d_tokens, back, ((my_fsdp + s) % n_fsdp) * slab, 1)

    n_heads = half_kv // HD
    grad_args = (e, inv, do_t, queries[0], q_other, keys, vals, chip_rows, half_kv)
    early = run_grads(core_arg, *grad_args, (0, n_heads // 2), ())
    core_late = after(core_arg, *dv_places, *made)
    out, dq, other, *dk_terms = run_grads(core_late, *grad_args, (n_heads // 2, n_heads), early)
    dk_back = [shifted(dk_terms[n_back - d], -2 * d) for d in range(1, n_back + 1)]
    *dk_back, _ = lax.optimization_barrier((*dk_back, by_z[0]))
    dk_total = dk_terms[n_back].astype(F32)
    for term in dk_back:
        dk_total = dk_total + term.astype(F32)
    dk_chip = dk_total.astype(BF16)
    d_keys = placed(core, rows_of(dk_chip, core, shard_rows), swapped(rows_of(dk_chip, 1 - core, shard_rows)), 1)
    other = swapped(other)
    out = lax.dynamic_update_slice_in_dim(out, other[0], (1 - core) * half_q, 1)
    dq = lax.dynamic_update_slice_in_dim(dq, other[1], (1 - core) * half_q, 1)
    return (out[None], dq[None], d_keys[None], d_tokens[None], d_weight)


def solution(mesh):
    in_specs = (
        P("fsdp", "ctx", None),
        P("fsdp", "ctx", None),
        P("fsdp", "ctx", None),
        P("fsdp", None),
        P("fsdp", "ctx", None),
        P("fsdp", "ctx"),
    )
    out_specs = (
        P("fsdp", "ctx", None),
        P("fsdp", "ctx", None),
        P("fsdp", "ctx", None),
        P("fsdp", "ctx", None),
        P(("ctx", "fsdp"), None),
    )
    return jax.shard_map(shards, mesh=mesh, in_specs=in_specs, out_specs=out_specs, check_vma=False)
```

profile of v0, /device:TPU:9, one launch (start us, length us, event | category | flops | bytes accessed | tf_op | source)
XLA Modules:
  0.0 218.7 jit_solution(2123653242182402599)
XLA Ops:
  1.6 1.1 dynamic-slice_bitcast_fusion.4
  4.2 2.5 %dynamic-slice_bitcast_fusion = bf16[256,2688]{1,0:T(8,128)(2,1)} fusion(bf16[1,256,5376]{2,1,0:T(8,128)(2,1)} %param.6, s32[]{:T(128)S(6)} %select_n.72), kind=kLoop, calls=%fused_computation.3 | loop fusion | bytes 2752516 | tf_op jit(solution)/shard_map/dynamic_slice | solution.py:401
  6.7 1.2 collective-permute-start.3
  10.6 3.1 %collective-permute-start.2 = (bf16[528,512]{1,0:T(8,128)(2,1)}, bf16[528,512]{1,0:T(8,128)(2,1)}, u32[]{:S(2)}, u32[]{:S(2)}) collective-permute-start(bf16[528,512]{1,0:T(8,128)(2,1)} %pad_maximum_fusion.3.refs_2_.refs_8_), channel_id=1, source_target_pairs={{0,4},{2,6},{4,8},{6,10},{8,12},{10,14},{12,16},{14,18},{16,20},{1... | collective-permute-start | bytes 1622024 | tf_op jit(solution)/shard_map/ppermute | solution.py:378
  13.7 3.2 %collective-permute-start.1 = (bf16[528,512]{1,0:T(8,128)(2,1)}, bf16[528,512]{1,0:T(8,128)(2,1)}, u32[]{:S(2)}, u32[]{:S(2)}) collective-permute-start(bf16[528,512]{1,0:T(8,128)(2,1)} %pad_maximum_fusion.3.refs_2_.refs_8_), channel_id=1, source_target_pairs={{0,8},{2,10},{4,12},{6,14},{8,16},{10,18},{12,20},{14,22},{16,24},... | collective-permute-start | bytes 1622024 | tf_op jit(solution)/shard_map/ppermute | solution.py:378
  18.9 1.8 copy-done.1
  20.7 1.6 pieces.1
  22.5 2.6 %copy-done = bf16[2688,1024]{1,0:T(8,128)(2,1)S(1)} copy-done((bf16[2688,1024]{1,0:T(8,128)(2,1)S(1)}, bf16[2688,1024]{1,0:T(8,128)(2,1)}, u32[]{:S(2)}) %copy-start) | copy-done | bytes 5505048
  25.1 2.4 %product.2 = f32[256,1024]{1,0:T(8,128)S(1)} custom-call(s32[1]{0:T(128)} %bitcast.4.at_ref, bf16[256,5376]{1,0:T(8,128)(2,1)S(1)} %bitcast.30, bf16[2688,1024]{1,0:T(8,128)(2,1)S(1)} %copy-done), custom_call_target="tpu_custom_call" | custom-call | flops 1048576 | bytes 4096 | tf_op jit(solution)/shard_map/product/pallas_call | solution.py:289
  28.2 10.6 %collective-permute-done.3.x_ref = bf16[256,2688]{1,0:T(8,128)(2,1)} collective-permute-done((bf16[256,2688]{1,0:T(8,128)(2,1)}, bf16[256,2688]{1,0:T(8,128)(2,1)}, u32[]{:S(2)}, u32[]{:S(2)}) %collective-permute-start.3) | collective-permute-done | bytes 1376288 | tf_op jit(solution)/shard_map/ppermute | solution.py:387
  38.8 3.4 %product.3 = bf16[256,1024]{1,0:T(8,128)(2,1)S(1)} custom-call(s32[1]{0:T(128)} %constant.78.clone.1.at_ref, bf16[256,2688]{1,0:T(8,128)(2,1)} %collective-permute-done.3.x_ref, bf16[2688,1024]{1,0:T(8,128)(2,1)S(1)} %bitcast.28), custom_call_target="tpu_custom_call" | custom-call | flops 1048576 | bytes 4096 | tf_op jit(solution)/shard_map/product/pallas_call | solution.py:289
  42.2 1.3 collective-permute-start.7
  45.2 1.2 collective-permute-start.11
  46.4 1.2 collective-permute-start.12
  47.6 14.1 %probs.1 = (bf16[4,2,1280,512]{3,2,1,0:T(8,128)(2,1)}, f32[4,2,1,512]{3,2,1,0:T(1,128)S(1)}, bf16[4,2,128,512]{3,2,1,0:T(8,128)(2,1)S(1)}, bf16[512,512]{1,0:T(8...) custom-call(s32[1]{0:T(128)} %bitcast.core_ref.refs_0_, ...), custom_call_target="tpu_custom_call" | custom-call | flops 1048576 | bytes 4096 | tf_op jit(solution)/shard_map/probs/pallas_call | solution.py:157
  61.9 2.0 collective-permute-start.8
  63.9 3.0 %collective-permute-start.5 = (bf16[512,512]{1,0:T(8,128)(2,1)S(1)}, bf16[512,512]{1,0:T(8,128)(2,1)S(1)}, u32[]{:S(2)}, u32[]{:S(2)}) collective-permute-start(bf16[512,512]{1,0:T(8,128)(2,1)S(1)} %get-tuple-element.62), channel_id=1, source_target_pairs={{4,0},{6,2},{8,4},{10,6},{12,8},{14,10},{16,12},{18,14},{20,16},{2... | collective-permute-start | bytes 1572872 | tf_op jit(solution)/shard_map/ppermute | solution.py:378
  67.0 1.9 collective-permute-start.6
  69.7 3.1 %collective-permute-start.9 = (bf16[512,512]{1,0:T(8,128)(2,1)S(1)}, bf16[512,512]{1,0:T(8,128)(2,1)S(1)}, u32[]{:S(2)}, u32[]{:S(2)}) collective-permute-start(bf16[512,512]{1,0:T(8,128)(2,1)S(1)} %constant_dynamic-update-slice_fusion.2.refs_11_), channel_id=1, source_target_pairs={{0,4},{2,6},{4,8},{6,10},{8,12},{10,14},{12,16},{14,18},{16,20},{1... | collective-permute-start | bytes 1572872 | tf_op jit(solution)/shard_map/ppermute | solution.py:378
  72.8 22.6 %collective-permute-done.12.refs_3_ = bf16[1344,256]{1,0:T(8,128)(2,1)S(1)} collective-permute-done((bf16[1344,256]{1,0:T(8,128)(2,1)S(1)}, bf16[1344,256]{1,0:T(8,128)(2,1)S(1)}, u32[]{:S(2)}, u32[]{:S(2)}) %collective-permute-start.12) | collective-permute-done | bytes 688160 | tf_op jit(solution)/shard_map/ppermute | solution.py:397
  95.4 1.7 pad_maximum_fusion
  97.2 3.0 %collective-permute-start.21 = (bf16[1344,1024]{1,0:T(8,128)(2,1)}, bf16[1344,1024]{1,0:T(8,128)(2,1)}, u32[]{:S(2)}, u32[]{:S(2)}) collective-permute-start(bf16[1344,1024]{1,0:T(8,128)(2,1)} %pad_maximum_fusion), channel_id=1, source_target_pairs={{0,2},{2,0},{4,6},{6,4},{8,10},{10,8},{12,14},{14,12},{16,18},{18,... | collective-permute-start | bytes 8257544 | tf_op jit(solution)/shard_map/ppermute | solution.py:382
  100.2 5.1 %collective-permute-done.5 = bf16[512,512]{1,0:T(8,128)(2,1)S(1)} collective-permute-done((bf16[512,512]{1,0:T(8,128)(2,1)S(1)}, bf16[512,512]{1,0:T(8,128)(2,1)S(1)}, u32[]{:S(2)}, u32[]{:S(2)}) %collective-permute-start.5) | collective-permute-done | bytes 524320 | tf_op jit(solution)/shard_map/ppermute | solution.py:378
  106.1 3.4 %collective-permute-start.17 = (bf16[512,512]{1,0:T(8,128)(2,1)S(1)}, bf16[512,512]{1,0:T(8,128)(2,1)S(1)}, u32[]{:S(2)}, u32[]{:S(2)}) collective-permute-start(bf16[512,512]{1,0:T(8,128)(2,1)S(1)} %constant_dynamic-update-slice_fusion.2.refs_11_), channel_id=1, source_target_pairs={{0,8},{2,10},{4,12},{6,14},{8,16},{10,18},{12,20},{14,22},{16,24},... | collective-permute-start | bytes 1572872 | tf_op jit(solution)/shard_map/ppermute | solution.py:378
  109.5 9.2 %collective-permute-done.13.refs_6_ = bf16[512,512]{1,0:T(8,128)(2,1)S(1)} collective-permute-done((bf16[512,512]{1,0:T(8,128)(2,1)S(1)}, bf16[512,512]{1,0:T(8,128)(2,1)S(1)}, u32[]{:S(2)}, u32[]{:S(2)}) %collective-permute-start.13) | collective-permute-done | bytes 524320 | tf_op jit(solution)/shard_map/ppermute | solution.py:397
  118.8 1.5 collective-permute-start.16
  120.3 2.2 collective-permute-start.15
  122.5 9.0 %grads.2 = (bf16[256,2048]{1,0:T(8,128)(2,1)}, bf16[256,2048]{1,0:T(8,128)(2,1)}, bf16[2,256,1024]{2,1,0:T(8,128)(2,1)}, bf16[512,512]{1,0:T(8,128)(2,1)}, bf16[...) custom-call(s32[1]{0:T(128)} %bitcast.core_ref.refs_0_, bf16[4,2,1280,512]{3,2,1,0:T(8,128)(2,1)} %get-tuple-element.77.refs_1_, ...), custom_call_target="tpu_custom_call" | custom-call | flops 1048576 | bytes 4096 | tf_op jit(solution)/shard_map/grads/pallas_call | solution.py:208
  131.7 4.9 %tokens.1 = (bf16[256,5376]{1,0:T(8,128)(2,1)}, bf16[256,2688]{1,0:T(8,128)(2,1)}) custom-call(s32[1]{0:T(128)} %bitcast.4.at_ref, bf16[512,1024]{1,0:T(8,128)(2,1)S(1)} %constant_dynamic-update-slice_fusion.1.dv_ref, bf16[2688,1024]{1,0:T(8,128)(2,1)S(1)} %bitcast.28), custom_call_target="tpu_custom_call" | custom-call | flops 1048576 | bytes 4096 | tf_op jit(solution)/shard_map/tokens/pallas_call | solution.py:356
  136.6 9.8 %collective-permute-done.14.refs_7_ = bf16[512,512]{1,0:T(8,128)(2,1)S(1)} collective-permute-done((bf16[512,512]{1,0:T(8,128)(2,1)S(1)}, bf16[512,512]{1,0:T(8,128)(2,1)S(1)}, u32[]{:S(2)}, u32[]{:S(2)}) %collective-permute-start.14) | collective-permute-done | bytes 524320 | tf_op jit(solution)/shard_map/ppermute | solution.py:397
  146.3 9.2 %grads.3 = (bf16[256,2048]{1,0:T(8,128)(2,1)}, bf16[256,2048]{1,0:T(8,128)(2,1)}, bf16[2,256,1024]{2,1,0:T(8,128)(2,1)}, bf16[512,512]{1,0:T(8,128)(2,1)}, bf16[...) custom-call(s32[1]{0:T(128)} %bitcast.core_ref.refs_0_, ...), custom_call_target="tpu_custom_call", output_to_operand_aliasing={{0}: (12, {}), {1}: (13, {}), {2}: (14, {}), {3}: (15, {}),... | custom-call | flops 1048576 | bytes 4096 | tf_op jit(solution)/shard_map/grads/pallas_call | solution.py:208
  157.9 3.2 %collective-permute-start.19 = (bf16[512,512]{1,0:T(8,128)(2,1)}, bf16[512,512]{1,0:T(8,128)(2,1)S(1)}, u32[]{:S(2)}, u32[]{:S(2)}) collective-permute-start(bf16[512,512]{1,0:T(8,128)(2,1)} %get-tuple-element.90), channel_id=1, source_target_pairs={{4,0},{6,2},{8,4},{10,6},{12,8},{14,10},{16,12},{18,14},{20,16},{2... | collective-permute-start | bytes 1572872 | tf_op jit(solution)/shard_map/ppermute | solution.py:378
  161.1 1.9 collective-permute-start.20
  163.2 2.2 %slice_dynamic-update-slice_fusion = (bf16[1,256,2048]{2,1,0:T(8,128)(2,1)}, bf16[1,256,2048]{2,1,0:T(8,128)(2,1)}) fusion(bf16[1,256,2048]{2,1,0:T(8,128)(2,1)} %bitcast.36, s32[]{:T(128)S(6)} %select_n.73, bf16[2,256,1024]{2,1,0:T(8,128)(2,1)} %collective-permute-done.18, bf16[1,256,2048]{2,1,0:T(8,128)(2,1)} %bitcast.35), kind=kLoop, calls=%fused_computation.12 | loop fusion | bytes 2097156 | tf_op jit(solution)/shard_map/dynamic_update_slice | solution.py:568
  165.4 1.1 copy-done.9
  166.5 1.1 copy-done.11
  167.6 1.1 copy-done.13
  171.8 4.9 %weight.1 = (f32[336,512]{1,0:T(8,128)S(1)}, bf16[336,512]{1,0:T(8,128)(2,1)S(1)}, bf16[336,512]{1,0:T(8,128)(2,1)S(1)}, bf16[336,512]{1,0:T(8,128)(2,1)S(1)}) custom-call(s32[2]{0:T(128)S(1)} %pad_add_fusion.1.at_ref, bf16[1344,256]{1,0:T(8,128)(2,1)S(1)} %copy-done.7, bf16[1344,256]{1,0:T(8,128)(2,1)S(1)} %copy-done.9, bf16[1344,256]{1,0:T(8,128)(2,1)S(1)} %copy-done.11, ...), custom_call_target="tpu_custom_call" | custom-call | flops 1048576 | bytes 4096 | tf_op jit(solution)/shard_map/weight/pallas_call | solution.py:332
  176.8 1.5 collective-permute-start.24
  178.3 1.8 collective-permute-start.25
  180.1 1.4 collective-permute-start.26
  181.5 4.1 %collective-permute-done.20 = bf16[512,512]{1,0:T(8,128)(2,1)} collective-permute-done((bf16[512,512]{1,0:T(8,128)(2,1)}, bf16[512,512]{1,0:T(8,128)(2,1)}, u32[]{:S(2)}, u32[]{:S(2)}) %collective-permute-start.20) | collective-permute-done | bytes 524320 | tf_op jit(solution)/shard_map/ppermute | solution.py:378
  185.6 1.2 add_convert_fusion
  186.9 2.6 %collective-permute-start.22 = (bf16[256,512]{1,0:T(8,128)(2,1)S(1)}, bf16[256,512]{1,0:T(8,128)(2,1)S(1)}, u32[]{:S(2)}, u32[]{:S(2)}) collective-permute-start(bf16[256,512]{1,0:T(8,128)(2,1)S(1)} %get-tuple-element.103), channel_id=1, source_target_pairs={{0,2},{2,0},{4,6},{6,4},{8,10},{10,8},{12,14},{14,12},{16,18},{18,... | collective-permute-start | bytes 786440 | tf_op jit(solution)/shard_map/ppermute | solution.py:382
  189.8 17.1 %collective-permute-done.25 = bf16[336,512]{1,0:T(8,128)(2,1)S(1)} collective-permute-done((bf16[336,512]{1,0:T(8,128)(2,1)S(1)}, bf16[336,512]{1,0:T(8,128)(2,1)S(1)}, u32[]{:S(2)}, u32[]{:S(2)}) %collective-permute-start.25) | collective-permute-done | bytes 344096 | tf_op jit(solution)/shard_map/ppermute | solution.py:534
  206.8 8.2 %collective-permute-done.26 = bf16[336,512]{1,0:T(8,128)(2,1)S(1)} collective-permute-done((bf16[336,512]{1,0:T(8,128)(2,1)S(1)}, bf16[336,512]{1,0:T(8,128)(2,1)S(1)}, u32[]{:S(2)}, u32[]{:S(2)}) %collective-permute-start.26) | collective-permute-done | bytes 344096 | tf_op jit(solution)/shard_map/ppermute | solution.py:534
  215.3 1.2 collective-permute-start.27
  216.6 1.2 collective-permute-done.27
  (120 shorter events, 18.8 us)
Async XLA Ops:
  0.6 7.3 %copy-start.14 = (bf16[1,256,2048]{2,1,0:T(8,128)(2,1)S(1)}, bf16[1,256,2048]{2,1,0:T(8,128)(2,1)}, u32[]{:S(2)}) copy-start(bf16[1,256,2048]{2,1,0:T(8,128)(2,1)} %param.10) | copy-start | bytes 3145732
  0.6 7.2 %copy-start.3 = (bf16[1,256,2048]{2,1,0:T(8,128)(2,1)S(1)}, bf16[1,256,2048]{2,1,0:T(8,128)(2,1)}, u32[]{:S(2)}) copy-start(bf16[1,256,2048]{2,1,0:T(8,128)(2,1)} %param.7) | copy-start | bytes 3145732
  3.5 4.5 %collective-permute-start = (bf16[272,512]{1,0:T(8,128)(2,1)}, bf16[272,512]{1,0:T(8,128)(2,1)}, u32[]{:S(2)}, u32[]{:S(2)}) collective-permute-start(bf16[272,512]{1,0:T(8,128)(2,1)} %maximum_maximum_fusion.1), channel_id=1, source_target_pairs={{0,2},{2,0},{4,6},{6,4},{8,10},{10,8},{12,14},{14,12},{16,18},{18,... | collective-permute-start | bytes 835592 | tf_op jit(solution)/shard_map/ppermute | solution.py:382
  6.7 32.1 %collective-permute-start.3 = (bf16[256,2688]{1,0:T(8,128)(2,1)}, bf16[256,2688]{1,0:T(8,128)(2,1)}, u32[]{:S(2)}, u32[]{:S(2)}) collective-permute-start(bf16[256,2688]{1,0:T(8,128)(2,1)} %dynamic-slice_bitcast_fusion), channel_id=1, source_target_pairs={{0,1},{1,0},{2,3},{3,2},{4,5},{5,4},{6,7},{7,6},{8,9},{9,8},{10,11... | collective-permute-start | bytes 4128776 | tf_op jit(solution)/shard_map/ppermute | solution.py:387
  10.6 16.9 %collective-permute-start.2 = (bf16[528,512]{1,0:T(8,128)(2,1)}, bf16[528,512]{1,0:T(8,128)(2,1)}, u32[]{:S(2)}, u32[]{:S(2)}) collective-permute-start(bf16[528,512]{1,0:T(8,128)(2,1)} %pad_maximum_fusion.3.refs_2_.refs_8_), channel_id=1, source_target_pairs={{0,4},{2,6},{4,8},{6,10},{8,12},{10,14},{12,16},{14,18},{16,20},{1... | collective-permute-start | bytes 1622024 | tf_op jit(solution)/shard_map/ppermute | solution.py:378
  13.7 29.8 %collective-permute-start.1 = (bf16[528,512]{1,0:T(8,128)(2,1)}, bf16[528,512]{1,0:T(8,128)(2,1)}, u32[]{:S(2)}, u32[]{:S(2)}) collective-permute-start(bf16[528,512]{1,0:T(8,128)(2,1)} %pad_maximum_fusion.3.refs_2_.refs_8_), channel_id=1, source_target_pairs={{0,8},{2,10},{4,12},{6,14},{8,16},{10,18},{12,20},{14,22},{16,24},... | collective-permute-start | bytes 1622024 | tf_op jit(solution)/shard_map/ppermute | solution.py:378
  16.9 21.9 %slice-start = ((s8[5505024]{0:T(1024)(128)(4,1)}), s8[1310720]{0:T(1024)(128)(4,1)S(1)}, s32[]{:S(2)}) async-start(s8[5505024]{0:T(1024)(128)(4,1)} %bitcast.27), calls=%async_computation | async-start | bytes 2621440
  18.0 29.5 %collective-permute-start.4 = (bf16[256,2048]{1,0:T(8,128)(2,1)}, bf16[256,2048]{1,0:T(8,128)(2,1)S(1)}, u32[]{:S(2)}, u32[]{:S(2)}) collective-permute-start(bf16[256,2048]{1,0:T(8,128)(2,1)} %pad_maximum_fusion.1), channel_id=1, source_target_pairs={{0,2},{2,0},{4,6},{6,4},{8,10},{10,8},{12,14},{14,12},{16,18},{18,... | collective-permute-start | bytes 3145736 | tf_op jit(solution)/shard_map/ppermute | solution.py:382
  18.9 1.8 copy-start.1
  20.7 1.8 copy-start.2
  22.5 2.6 %copy-start = (bf16[2688,1024]{1,0:T(8,128)(2,1)S(1)}, bf16[2688,1024]{1,0:T(8,128)(2,1)}, u32[]{:S(2)}) copy-start(bf16[2688,1024]{1,0:T(8,128)(2,1)} %w_ref.5) | copy-start | bytes 16515076
  25.1 70.4 %copy-start.6 = (bf16[1344,256]{1,0:T(8,128)(2,1)}, bf16[1344,256]{1,0:T(8,128)(2,1)S(1)}, u32[]{:S(2)}) copy-start(bf16[1344,256]{1,0:T(8,128)(2,1)S(1)} %get-tuple-element.69.refs_0_) | copy-start | bytes 2064388
  25.1 13.7 %slice-start.1 = ((s8[5505024]{0:T(1024)(128)(4,1)}), s8[4194304]{0:T(1024)(128)(4,1)S(1)}, s32[]{:S(2)}) async-start(s8[5505024]{0:T(1024)(128)(4,1)} %bitcast.27), calls=%async_computation.1 | async-start | bytes 8388608
  28.2 19.3 %copy-start.15 = (bf16[1,256,2048]{2,1,0:T(8,128)(2,1)S(1)}, bf16[1,256,2048]{2,1,0:T(8,128)(2,1)}, u32[]{:S(2)}) copy-start(bf16[1,256,2048]{2,1,0:T(8,128)(2,1)} %param.10) | copy-start | bytes 3145732
  42.2 19.5 %collective-permute-start.7 = (bf16[256,1024]{1,0:T(8,128)(2,1)S(1)}, bf16[256,1024]{1,0:T(8,128)(2,1)S(1)}, u32[]{:S(2)}, u32[]{:S(2)}) collective-permute-start(bf16[256,1024]{1,0:T(8,128)(2,1)S(1)} %product.3), channel_id=1, source_target_pairs={{0,1},{1,0},{2,3},{3,2},{4,5},{5,4},{6,7},{7,6},{8,9},{9,8},{10,11... | collective-permute-start | bytes 1572872 | tf_op jit(solution)/shard_map/ppermute | solution.py:387
  44.8 24.8 %collective-permute-start.10 = (bf16[1344,256]{1,0:T(8,128)(2,1)S(1)}, bf16[1344,256]{1,0:T(8,128)(2,1)S(1)}, u32[]{:S(2)}, u32[]{:S(2)}) collective-permute-start(bf16[1344,256]{1,0:T(8,128)(2,1)S(1)} %get-tuple-element.66), channel_id=1, source_target_pairs={{0,1},{1,0},{2,3},{3,2},{4,5},{5,4},{6,7},{7,6},{8,9},{9,8},{10,11... | collective-permute-start | bytes 2064392 | tf_op jit(solution)/shard_map/ppermute | solution.py:397
  45.2 27.7 %collective-permute-start.11 = (bf16[1344,256]{1,0:T(8,128)(2,1)S(1)}, bf16[1344,256]{1,0:T(8,128)(2,1)S(1)}, u32[]{:S(2)}, u32[]{:S(2)}) collective-permute-start(bf16[1344,256]{1,0:T(8,128)(2,1)S(1)} %get-tuple-element.67), channel_id=1, source_target_pairs={{0,4},{1,5},{2,6},{3,7},{4,0},{5,1},{6,2},{7,3},{8,12},{9,13},{10,... | collective-permute-start | bytes 2064392 | tf_op jit(solution)/shard_map/ppermute | solution.py:397
  46.4 49.0 %collective-permute-start.12 = (bf16[1344,256]{1,0:T(8,128)(2,1)S(1)}, bf16[1344,256]{1,0:T(8,128)(2,1)S(1)}, u32[]{:S(2)}, u32[]{:S(2)}) collective-permute-start(bf16[1344,256]{1,0:T(8,128)(2,1)S(1)} %get-tuple-element.68), channel_id=1, source_target_pairs={{0,5},{1,4},{2,7},{3,6},{4,1},{5,0},{6,3},{7,2},{8,13},{9,12},{10,... | collective-permute-start | bytes 2064392 | tf_op jit(solution)/shard_map/ppermute | solution.py:397
  61.9 5.1 %collective-permute-start.8 = (bf16[256,512]{1,0:T(8,128)(2,1)S(1)}, bf16[256,512]{1,0:T(8,128)(2,1)S(1)}, u32[]{:S(2)}, u32[]{:S(2)}) collective-permute-start(bf16[256,512]{1,0:T(8,128)(2,1)S(1)} %get-tuple-element.109), channel_id=1, source_target_pairs={{0,2},{2,0},{4,6},{6,4},{8,10},{10,8},{12,14},{14,12},{16,18},{18,... | collective-permute-start | bytes 786440 | tf_op jit(solution)/shard_map/ppermute | solution.py:382
  63.9 41.4 %collective-permute-start.5 = (bf16[512,512]{1,0:T(8,128)(2,1)S(1)}, bf16[512,512]{1,0:T(8,128)(2,1)S(1)}, u32[]{:S(2)}, u32[]{:S(2)}) collective-permute-start(bf16[512,512]{1,0:T(8,128)(2,1)S(1)} %get-tuple-element.62), channel_id=1, source_target_pairs={{4,0},{6,2},{8,4},{10,6},{12,8},{14,10},{16,12},{18,14},{20,16},{2... | collective-permute-start | bytes 1572872 | tf_op jit(solution)/shard_map/ppermute | solution.py:378
  67.0 38.3 %collective-permute-start.6 = (bf16[512,512]{1,0:T(8,128)(2,1)S(1)}, bf16[512,512]{1,0:T(8,128)(2,1)S(1)}, u32[]{:S(2)}, u32[]{:S(2)}) collective-permute-start(bf16[512,512]{1,0:T(8,128)(2,1)S(1)} %get-tuple-element.63), channel_id=1, source_target_pairs={{8,0},{10,2},{12,4},{14,6},{16,8},{18,10},{20,12},{22,14},{24,16},... | collective-permute-start | bytes 1572872 | tf_op jit(solution)/shard_map/ppermute | solution.py:378
  69.7 27.5 %copy-start.8 = (bf16[1344,256]{1,0:T(8,128)(2,1)}, bf16[1344,256]{1,0:T(8,128)(2,1)S(1)}, u32[]{:S(2)}) copy-start(bf16[1344,256]{1,0:T(8,128)(2,1)S(1)} %collective-permute-done.10.refs_1_) | copy-start | bytes 2064388
  69.7 35.8 %collective-permute-start.9 = (bf16[512,512]{1,0:T(8,128)(2,1)S(1)}, bf16[512,512]{1,0:T(8,128)(2,1)S(1)}, u32[]{:S(2)}, u32[]{:S(2)}) collective-permute-start(bf16[512,512]{1,0:T(8,128)(2,1)S(1)} %constant_dynamic-update-slice_fusion.2.refs_11_), channel_id=1, source_target_pairs={{0,4},{2,6},{4,8},{6,10},{8,12},{10,14},{12,16},{14,18},{16,20},{1... | collective-permute-start | bytes 1572872 | tf_op jit(solution)/shard_map/ppermute | solution.py:378
  72.8 24.3 %copy-start.10 = (bf16[1344,256]{1,0:T(8,128)(2,1)}, bf16[1344,256]{1,0:T(8,128)(2,1)S(1)}, u32[]{:S(2)}) copy-start(bf16[1344,256]{1,0:T(8,128)(2,1)S(1)} %collective-permute-done.11.refs_2_) | copy-start | bytes 2064388
  97.2 68.3 %collective-permute-start.21 = (bf16[1344,1024]{1,0:T(8,128)(2,1)}, bf16[1344,1024]{1,0:T(8,128)(2,1)}, u32[]{:S(2)}, u32[]{:S(2)}) collective-permute-start(bf16[1344,1024]{1,0:T(8,128)(2,1)} %pad_maximum_fusion), channel_id=1, source_target_pairs={{0,2},{2,0},{4,6},{6,4},{8,10},{10,8},{12,14},{14,12},{16,18},{18,... | collective-permute-start | bytes 8257544 | tf_op jit(solution)/shard_map/ppermute | solution.py:382
  105.7 25.8 %copy-start.4 = (bf16[512,512]{1,0:T(8,128)(2,1)}, bf16[512,512]{1,0:T(8,128)(2,1)S(1)}, u32[]{:S(2)}) copy-start(bf16[512,512]{1,0:T(8,128)(2,1)S(1)} %add_convert_fusion.1.refs_5_) | copy-start | bytes 1572868
  105.7 13.0 %collective-permute-start.13 = (bf16[512,512]{1,0:T(8,128)(2,1)S(1)}, bf16[512,512]{1,0:T(8,128)(2,1)S(1)}, u32[]{:S(2)}, u32[]{:S(2)}) collective-permute-start(bf16[512,512]{1,0:T(8,128)(2,1)S(1)} %add_convert_fusion.1.refs_5_), channel_id=1, source_target_pairs={{0,1},{1,0},{2,3},{3,2},{4,5},{5,4},{6,7},{7,6},{8,9},{9,8},{10,11... | collective-permute-start | bytes 1572872 | tf_op jit(solution)/shard_map/ppermute | solution.py:397
  106.1 16.4 %collective-permute-start.17 = (bf16[512,512]{1,0:T(8,128)(2,1)S(1)}, bf16[512,512]{1,0:T(8,128)(2,1)S(1)}, u32[]{:S(2)}, u32[]{:S(2)}) collective-permute-start(bf16[512,512]{1,0:T(8,128)(2,1)S(1)} %constant_dynamic-update-slice_fusion.2.refs_11_), channel_id=1, source_target_pairs={{0,8},{2,10},{4,12},{6,14},{8,16},{10,18},{12,20},{14,22},{16,24},... | collective-permute-start | bytes 1572872 | tf_op jit(solution)/shard_map/ppermute | solution.py:378
  118.7 3.8 %copy-start.18 = (bf16[512,512]{1,0:T(8,128)(2,1)}, bf16[512,512]{1,0:T(8,128)(2,1)S(1)}, u32[]{:S(2)}) copy-start(bf16[512,512]{1,0:T(8,128)(2,1)S(1)} %collective-permute-done.13.refs_6_) | copy-start | bytes 1572868
  118.8 12.8 %collective-permute-start.16 = (bf16[512,512]{1,0:T(8,128)(2,1)S(1)}, bf16[512,512]{1,0:T(8,128)(2,1)S(1)}, u32[]{:S(2)}, u32[]{:S(2)}) collective-permute-start(bf16[512,512]{1,0:T(8,128)(2,1)S(1)} %pad_maximum_fusion.6), channel_id=1, source_target_pairs={{0,2},{2,0},{4,6},{6,4},{8,10},{10,8},{12,14},{14,12},{16,18},{18,... | collective-permute-start | bytes 1572872 | tf_op jit(solution)/shard_map/ppermute | solution.py:382
  120.3 16.3 %collective-permute-start.15 = (bf16[512,512]{1,0:T(8,128)(2,1)S(1)}, bf16[512,512]{1,0:T(8,128)(2,1)S(1)}, u32[]{:S(2)}, u32[]{:S(2)}) collective-permute-start(bf16[512,512]{1,0:T(8,128)(2,1)S(1)} %add_convert_fusion.1.refs_5_), channel_id=1, source_target_pairs={{0,5},{1,4},{2,7},{3,6},{4,1},{5,0},{6,3},{7,2},{8,13},{9,12},{10,... | collective-permute-start | bytes 1572872 | tf_op jit(solution)/shard_map/ppermute | solution.py:397
  122.5 23.8 %collective-permute-start.14 = (bf16[512,512]{1,0:T(8,128)(2,1)S(1)}, bf16[512,512]{1,0:T(8,128)(2,1)S(1)}, u32[]{:S(2)}, u32[]{:S(2)}) collective-permute-start(bf16[512,512]{1,0:T(8,128)(2,1)S(1)} %add_convert_fusion.1.refs_5_), channel_id=1, source_target_pairs={{0,4},{1,5},{2,6},{3,7},{4,0},{5,1},{6,2},{7,3},{8,12},{9,13},{10,... | collective-permute-start | bytes 1572872 | tf_op jit(solution)/shard_map/ppermute | solution.py:397
  136.6 19.0 %copy-start.20 = (bf16[512,512]{1,0:T(8,128)(2,1)}, bf16[512,512]{1,0:T(8,128)(2,1)S(1)}, u32[]{:S(2)}) copy-start(bf16[512,512]{1,0:T(8,128)(2,1)S(1)} %collective-permute-done.15.refs_8_) | copy-start | bytes 1572868
  146.3 9.3 %copy-start.22 = (bf16[512,512]{1,0:T(8,128)(2,1)}, bf16[512,512]{1,0:T(8,128)(2,1)S(1)}, u32[]{:S(2)}) copy-start(bf16[512,512]{1,0:T(8,128)(2,1)S(1)} %collective-permute-done.14.refs_7_) | copy-start | bytes 1572868
  146.3 19.1 %copy-start.5 = (bf16[512,512]{1,0:T(8,128)(2,1)S(1)}, bf16[512,512]{1,0:T(8,128)(2,1)}, u32[]{:S(2)}) copy-start(bf16[512,512]{1,0:T(8,128)(2,1)} %copy-done.4) | copy-start | bytes 1572868
  146.3 19.1 %copy-start.7 = (bf16[1344,256]{1,0:T(8,128)(2,1)S(1)}, bf16[1344,256]{1,0:T(8,128)(2,1)}, u32[]{:S(2)}) copy-start(bf16[1344,256]{1,0:T(8,128)(2,1)} %copy-done.6) | copy-start | bytes 2064388
  156.4 6.8 %collective-permute-start.18 = (bf16[2,256,1024]{2,1,0:T(8,128)(2,1)}, bf16[2,256,1024]{2,1,0:T(8,128)(2,1)}, u32[]{:S(2)}, u32[]{:S(2)}) collective-permute-start(bf16[2,256,1024]{2,1,0:T(8,128)(2,1)} %get-tuple-element.87), channel_id=1, source_target_pairs={{0,2},{2,0},{4,6},{6,4},{8,10},{10,8},{12,14},{14,12},{16,18},{18,... | collective-permute-start | bytes 3145736 | tf_op jit(solution)/shard_map/ppermute | solution.py:382
  156.9 32.7 %collective-permute-start.23 = (bf16[256,2688]{1,0:T(8,128)(2,1)}, bf16[256,2688]{1,0:T(8,128)(2,1)S(1)}, u32[]{:S(2)}, u32[]{:S(2)}) collective-permute-start(bf16[256,2688]{1,0:T(8,128)(2,1)} %get-tuple-element.75), channel_id=1, source_target_pairs={{0,1},{1,0},{2,3},{3,2},{4,5},{5,4},{6,7},{7,6},{8,9},{9,8},{10,11... | collective-permute-start | bytes 4128776 | tf_op jit(solution)/shard_map/ppermute | solution.py:387
  157.9 22.2 %collective-permute-start.19 = (bf16[512,512]{1,0:T(8,128)(2,1)}, bf16[512,512]{1,0:T(8,128)(2,1)S(1)}, u32[]{:S(2)}, u32[]{:S(2)}) collective-permute-start(bf16[512,512]{1,0:T(8,128)(2,1)} %get-tuple-element.90), channel_id=1, source_target_pairs={{4,0},{6,2},{8,4},{10,6},{12,8},{14,10},{16,12},{18,14},{20,16},{2... | collective-permute-start | bytes 1572872 | tf_op jit(solution)/shard_map/ppermute | solution.py:378
  161.1 24.5 %collective-permute-start.20 = (bf16[512,512]{1,0:T(8,128)(2,1)}, bf16[512,512]{1,0:T(8,128)(2,1)}, u32[]{:S(2)}, u32[]{:S(2)}) collective-permute-start(bf16[512,512]{1,0:T(8,128)(2,1)} %get-tuple-element.91), channel_id=1, source_target_pairs={{8,0},{10,2},{12,4},{14,6},{16,8},{18,10},{20,12},{22,14},{24,16},... | collective-permute-start | bytes 1572872 | tf_op jit(solution)/shard_map/ppermute | solution.py:378
  171.8 13.8 %copy-start.17 = (bf16[512,512]{1,0:T(8,128)(2,1)S(1)}, bf16[512,512]{1,0:T(8,128)(2,1)}, u32[]{:S(2)}) copy-start(bf16[512,512]{1,0:T(8,128)(2,1)} %copy-done.16) | copy-start | bytes 1572868
  176.7 12.8 %copy-start.26 = (bf16[256,5376]{1,0:T(8,128)(2,1)S(1)}, bf16[256,5376]{1,0:T(8,128)(2,1)}, u32[]{:S(2)}) copy-start(bf16[256,5376]{1,0:T(8,128)(2,1)} %get-tuple-element.95) | copy-start | bytes 8257540
  176.8 13.0 %collective-permute-start.24 = (bf16[336,512]{1,0:T(8,128)(2,1)S(1)}, bf16[336,512]{1,0:T(8,128)(2,1)S(1)}, u32[]{:S(2)}, u32[]{:S(2)}) collective-permute-start(bf16[336,512]{1,0:T(8,128)(2,1)S(1)} %get-tuple-element.96), channel_id=1, source_target_pairs={{0,8},{2,10},{4,12},{6,14},{8,16},{10,18},{12,20},{14,22},{16,24},... | collective-permute-start | bytes 1032200 | tf_op jit(solution)/shard_map/ppermute | solution.py:534
  178.3 28.6 %collective-permute-start.25 = (bf16[336,512]{1,0:T(8,128)(2,1)S(1)}, bf16[336,512]{1,0:T(8,128)(2,1)S(1)}, u32[]{:S(2)}, u32[]{:S(2)}) collective-permute-start(bf16[336,512]{1,0:T(8,128)(2,1)S(1)} %get-tuple-element.97), channel_id=1, source_target_pairs={{0,16},{2,18},{4,20},{6,22},{8,24},{10,26},{12,28},{14,30},{16,0},... | collective-permute-start | bytes 1032200 | tf_op jit(solution)/shard_map/ppermute | solution.py:534
  180.1 34.9 %collective-permute-start.26 = (bf16[336,512]{1,0:T(8,128)(2,1)S(1)}, bf16[336,512]{1,0:T(8,128)(2,1)S(1)}, u32[]{:S(2)}, u32[]{:S(2)}) collective-permute-start(bf16[336,512]{1,0:T(8,128)(2,1)S(1)} %get-tuple-element.98), channel_id=1, source_target_pairs={{0,24},{2,26},{4,28},{6,30},{8,0},{10,2},{12,4},{14,6},{16,8},{18,... | collective-permute-start | bytes 1032200 | tf_op jit(solution)/shard_map/ppermute | solution.py:534
  186.9 29.6 %collective-permute-start.22 = (bf16[256,512]{1,0:T(8,128)(2,1)S(1)}, bf16[256,512]{1,0:T(8,128)(2,1)S(1)}, u32[]{:S(2)}, u32[]{:S(2)}) collective-permute-start(bf16[256,512]{1,0:T(8,128)(2,1)S(1)} %get-tuple-element.103), channel_id=1, source_target_pairs={{0,2},{2,0},{4,6},{6,4},{8,10},{10,8},{12,14},{14,12},{16,18},{18,... | collective-permute-start | bytes 786440 | tf_op jit(solution)/shard_map/ppermute | solution.py:382
  189.8 28.1 %copy-start.27 = (bf16[1,256,5376]{2,1,0:T(8,128)(2,1)}, bf16[1,256,5376]{2,1,0:T(8,128)(2,1)S(1)}, u32[]{:S(2)}) copy-start(bf16[1,256,5376]{2,1,0:T(8,128)(2,1)S(1)} %bitcast_dynamic-update-slice_fusion) | copy-start | bytes 8257540
  215.3 2.5 %collective-permute-start.27 = (f32[168,512]{1,0:T(8,128)S(1)}, f32[168,512]{1,0:T(8,128)S(1)}, u32[]{:S(2)}, u32[]{:S(2)}) collective-permute-start(f32[168,512]{1,0:T(8,128)S(1)} %get-tuple-element.101), channel_id=1, source_target_pairs={{0,2},{2,0},{4,6},{6,4},{8,10},{10,8},{12,14},{14,12},{16,18},{18,... | collective-permute-start | bytes 1032200 | tf_op jit(solution)/shard_map/ppermute | solution.py:382
  (10 other events, 11.1 us)
where the time goes:
time: 220 us; the launch traced here: 219 us
  waiting for transfers between devices  88.8 us (40%)
  Pallas kernels  49.5 us (22%)
  starting transfers between devices  48.7 us (22%)
  local copies, waits for them, and re-layouts  21.6 us (10%)
  other arithmetic  8.84 us (4%)
    ppermute x6, waiting for transfers between devices, moved(): return lax.ppermute(x, ('ctx', 'fsdp'), pairs)  42.3 us
    ppermute x3, waiting for transfers between devices, shards(): lax.ppermute(by_z[d], 'ctx', [(i, (i + 4 * d) % n_ctx) for i in range(n_c...  25.2 us
    ppermute x8, starting transfers between devices, shifted(): lax.ppermute(x, 'ctx', [(i, i + by) for i in range(length) if 0 <= i + by...  23 us
    pallas_call x2, Pallas kernels, run_grads(): pl.pallas_call(kernel, grid_spec=pltpu.PrefetchScalarGridSpec(num_scalar_...  18.2 us
    pallas_call x1, Pallas kernels, run_probs(): pl.pallas_call(functools.partial(probs_kernel, blk, n_arr - 1), grid_spec...  14.1 us
    unnamed x60, local copies, waits for them, and re-layouts  12.7 us
    ppermute x8, starting transfers between devices, swapped(): lax.ppermute(x, 'ctx', [(i, i ^ 1) for i in range(lax.axis_size('ctx'))])  12.3 us
    ppermute x3, waiting for transfers between devices, rotated(): lax.ppermute(x, 'fsdp', [(i, (i + by) % length) for i in range(length)])  10.6 us
  transfers between devices with their start and end apart: 28, of which 11 were waited for; matrix products, arithmetic and copies ran while one was open for 7% of the time, Pallas kernels for 23%

commit v1 on v0

--- a/solution.py
+++ b/solution.py
@@ -397,6 +397,14 @@
     return lax.ppermute(x, ("ctx", "fsdp"), pairs)
 
 
+def relayed(my_y, far, got):
+    return (far.astype(F32) + jnp.where(my_y == 1, got.astype(F32), 0.0)).astype(BF16)
+
+
+def gathered_terms(my_y, mine, got, back):
+    return (mine.astype(F32) + back.astype(F32) + jnp.where(my_y == 0, got.astype(F32), 0.0)).astype(BF16)
+
+
 def cols(x, at, width):
     return lax.dynamic_slice_in_dim(x, at * width, width, x.ndim - 1)
 
@@ -408,6 +416,10 @@
 def placed(core, own, other, axis):
     both = jnp.concatenate([own, own], axis)
     return lax.dynamic_update_slice_in_dim(both, other, (1 - core) * own.shape[axis], axis)
+
+
+def flipped(x):
+    return lax.ppermute(x, "ctx", [(i, i ^ 2) for i in range(lax.axis_size("ctx"))])
 
 
 def after(x, *earlier):
@@ -421,8 +433,8 @@
     n_ctx = lax.axis_size("ctx")
     n_fsdp = lax.axis_size("fsdp")
     chip_rows = 2 * shard_rows
-    n_back = WINDOW // chip_rows
     n_z = n_ctx // 4
+    assert WINDOW == 2 * chip_rows
     my_ctx = lax.axis_index("ctx")
     my_fsdp = lax.axis_index("fsdp")
     core = my_ctx % 2
@@ -435,6 +447,13 @@
     tokens = hidden[0]
     first = chip * chip_rows
 
+    aligned = slab % HD == 0
+    fsdp_arg = my_fsdp.astype(jnp.int32).reshape(1)
+    zero_arg = jnp.zeros((1,), jnp.int32)
+    half_q = queries.shape[2] // 2
+    out_rows = model // (n_ctx * n_fsdp)
+    places = [(flip, s) for flip in range(2) for s in range(n_fsdp)]
+
     own_tags = segments[0].astype(BF16)
     tag_row = lax.dynamic_update_slice_in_dim(jnp.zeros((half_kv,), BF16), own_tags, core * shard_rows, 0)
     tag_rows = jnp.concatenate([tag_row[None], jnp.zeros((15, half_kv), BF16)], 0)
@@ -443,9 +462,18 @@
 
     slabs = [after(cols(tokens, (my_fsdp + s) % n_fsdp, slab), k_sent) for s in range(1, n_fsdp)]
     sent = [rotated(x, s + 1) for s, x in enumerate(slabs)]
-    half_q = queries.shape[2] // 2
-    q_sent = jnp.concatenate([cols(queries[0], 1 - core, half_q), cols(d_out[0], 1 - core, half_q)], 1)
-    q_other = swapped(after(q_sent, *slabs))
+
+    if out_rows % 8 == 0:
+        at = jnp.stack([my_y, my_fsdp]).astype(jnp.int32)
+        pieces = run_pieces(after(at, *slabs), tokens, n_z, n_fsdp, out_rows)
+    else:
+        turned = tokens.T.reshape(n_z, 2, 2, n_fsdp, out_rows, shard_rows)
+        pieces = []
+        for flip, s in places:
+            piece = lax.dynamic_index_in_dim(turned, my_y ^ flip, 1, keepdims=False)
+            piece = lax.dynamic_index_in_dim(piece, (my_fsdp + s) % n_fsdp, 2, keepdims=False)
+            pieces.append(piece.reshape(n_z * 2 * out_rows, shard_rows))
+    by_place = dict(zip(places, pieces))
 
     k_own = jnp.concatenate(
         [
@@ -454,31 +482,22 @@
         ],
         0,
     )
-    keys = [shifted(k_own, 2 * d) for d in range(n_back, 0, -1)] + [k_own]
-    aligned = slab % HD == 0
-    fsdp_arg = my_fsdp.astype(jnp.int32).reshape(1)
-    zero_arg = jnp.zeros((1,), jnp.int32)
+    k_own = after(k_own, *pieces)
+    k_far = shifted(k_own, 4)
+    over_y = {s: flipped(after(by_place[1, s], k_own)) for s in range(1, n_fsdp)}
+    q_sent = jnp.concatenate([cols(queries[0], 1 - core, half_q), cols(d_out[0], 1 - core, half_q)], 1)
+    q_other = swapped(after(q_sent, k_own))
     if aligned:
-        value_own = run_product(after(fsdp_arg, k_own), tokens, w_value, F32)
+        value_own = run_product(after(fsdp_arg, q_sent), tokens, w_value, F32)
     else:
         value_own = dot(cols(tokens, my_fsdp, slab), w_value)
-
-    out_rows = model // (n_ctx * n_fsdp)
-    places = [(flip, s) for flip in range(2) for s in range(n_fsdp)]
-    if out_rows % 8 == 0:
-        at = jnp.stack([my_y, my_fsdp]).astype(jnp.int32)
-        pieces = run_pieces(after(at, k_own), tokens, n_z, n_fsdp, out_rows)
-    else:
-        by_place = tokens.T.reshape(n_z, 2, 2, n_fsdp, out_rows, shard_rows)
-        pieces = []
-        for flip, s in places:
-            piece = lax.dynamic_index_in_dim(by_place, my_y ^ flip, 1, keepdims=False)
-            piece = lax.dynamic_index_in_dim(piece, (my_fsdp + s) % n_fsdp, 2, keepdims=False)
-            pieces.append(piece.reshape(n_z * 2 * out_rows, shard_rows))
+    k_far, over_y, _ = lax.optimization_barrier((k_far, over_y, value_own))
+    k_near = flipped(jnp.where(my_y == 0, k_own, k_far))
+    keys = [k_far, k_near, k_own]
 
     span_tags = jnp.concatenate([k[chip_rows, :chip_rows] for k in keys], 0)
     key_at = jnp.arange(WINDOW + chip_rows, dtype=jnp.int32)
-    chip_tags = keys[n_back][chip_rows, :chip_rows]
+    chip_tags = k_own[chip_rows, :chip_rows]
     before = (span_tags[None, :] < chip_tags[:, None]) | (key_at + first < WINDOW)[None, :]
     low = jnp.sum(before.astype(jnp.int32), axis=1)
     low = jnp.maximum(low, jnp.arange(1, chip_rows + 1, dtype=jnp.int32))[None, :]
@@ -487,55 +506,49 @@
         partial = [run_product(zero_arg, x, w_value, BF16) for x in sent]
     else:
         partial = [dot(x, w_value).astype(BF16) for x in sent]
-    low = after(low, value_own, *pieces, *partial)
-    e, inv, do_t, *dv_terms = run_probs(
+    low = after(low, *partial)
+    e, inv, do_t, dv_far, dv_near, dv_mine = run_probs(
         core_arg, low, queries[0], q_other, d_out[0], keys, chip_rows, half_kv
     )
-    dv_back = [shifted(dv_terms[n_back - d], -2 * d) for d in range(1, n_back + 1)]
+    dv_got = flipped(dv_near)
 
     value_back = [rotated(x, -s - 1) for s, x in enumerate(partial)]
-    *value_back, _ = lax.optimization_barrier((*value_back, dv_terms[n_back]))
+    *value_back, _ = lax.optimization_barrier((*value_back, dv_near))
     value_sum = value_own
     for x in value_back:
         value_sum = value_sum + x.astype(F32)
     own_values = value_sum.astype(BF16)
     v_own = placed(core, cols(own_values, core, half_kv), swapped(cols(own_values, 1 - core, half_kv)), 0)
-    vals = [shifted(v_own, 2 * d) for d in range(n_back, 0, -1)] + [v_own]
-
-    *pieces, _ = lax.optimization_barrier((*pieces, partial))
-    pieces = [moved(x, flip, s) if flip or s else x for x, (flip, s) in zip(pieces, places)]
-    *pieces, _ = lax.optimization_barrier((*pieces, v_own))
-    mine = jnp.concatenate(pieces, 1)
-    theirs = swapped(mine)
-
-    *dv_back, _ = lax.optimization_barrier((*dv_back, (vals[n_back - 1], pieces)))
-    dv_total = dv_terms[n_back].astype(F32)
-    for term in dv_back:
-        dv_total = dv_total + term.astype(F32)
-    dv_chip = dv_total.astype(BF16)
-
+
+    over_y[0] = flipped(after(by_place[1, 0], k_near))
+    v_own, over_y[0] = lax.optimization_barrier((v_own, over_y[0]))
+    v_far = shifted(v_own, 4)
+    over_fsdp = {}
+    for s in range(1, n_fsdp):
+        both = jnp.concatenate([by_place[0, s], over_y[s]], 1)
+        over_fsdp[s] = rotated(after(both, own_values), s)
+
+    dv_got = after(dv_got, v_own)
+    dv_back = shifted(relayed(my_y, dv_far, dv_got), -4)
+    v_sent = jnp.where(my_y == 0, v_own, v_far)
+    v_near = flipped(v_sent)
+    vals = [v_far, v_near, v_own]
+    dv_chip = gathered_terms(my_y, dv_mine, dv_got, after(dv_back, v_sent))
     dv_places = [moved(dv_chip, flip, s) if flip or s else dv_chip for flip, s in places]
-    if out_rows % 8 == 0:
-        by_z = run_weight(jnp.stack([core, my_z]).astype(jnp.int32), pieces, theirs, dv_places, n_z)
-    else:
-        weight_term = None
-        for at, dv_of in enumerate(dv_places):
-            window = slice(at * shard_rows, (at + 1) * shard_rows)
-            term = dot(mine[:, window], rows_of(dv_of, core, shard_rows))
-            term = term + dot(theirs[:, window], rows_of(dv_of, 1 - core, shard_rows))
-            weight_term = term if weight_term is None else weight_term + term
-        weight_term = weight_term.reshape(n_z, 2 * out_rows, half_kv)
-        by_z = [
-            lax.dynamic_index_in_dim(weight_term, (my_z + d) % n_z, 0, keepdims=False).astype(BF16 if d else F32)
-            for d in range(n_z)
-        ]
-    row_sum = by_z[0]
-    for d in range(1, n_z):
-        piece = lax.ppermute(by_z[d], "ctx", [(i, (i + 4 * d) % n_ctx) for i in range(n_ctx)])
-        row_sum = row_sum + piece.astype(F32)
-    d_weight = placed(core, rows_of(row_sum, core, out_rows), swapped(rows_of(row_sum, 1 - core, out_rows)), 1)
-
-    dv_fsdp = [dv_places[s] for s in range(n_fsdp)]
+
+    n_heads = half_kv // HD
+    grad_args = (e, inv, do_t, queries[0], q_other, keys, vals, chip_rows, half_kv)
+    early = run_grads(core_arg, *grad_args, (0, n_heads // 2), ())
+
+    over_fsdp, dv_places, _ = lax.optimization_barrier((over_fsdp, dv_places, early[0]))
+    arrived = {(0, 0): by_place[0, 0], (1, 0): over_y[0]}
+    for s in range(1, n_fsdp):
+        arrived[0, s] = over_fsdp[s][:, :shard_rows]
+        arrived[1, s] = over_fsdp[s][:, shard_rows:]
+    pieces = [arrived[place] for place in places]
+    theirs = swapped(jnp.concatenate(pieces, 1))
+
+    dv_fsdp = dv_places[:n_fsdp]
     dv_other = swapped(jnp.concatenate([rows_of(x, 1 - core, shard_rows) for x in dv_fsdp], 0))
     dv_rows = placed(
         core, jnp.concatenate([rows_of(x, core, shard_rows) for x in dv_fsdp], 0), dv_other, 1
@@ -551,17 +564,38 @@
         back = rotated(made[s - 1], -s)
         d_tokens = lax.dynamic_update_slice_in_dim(d_tokens, back, ((my_fsdp + s) % n_fsdp) * slab, 1)
 
-    n_heads = half_kv // HD
-    grad_args = (e, inv, do_t, queries[0], q_other, keys, vals, chip_rows, half_kv)
-    early = run_grads(core_arg, *grad_args, (0, n_heads // 2), ())
-    core_late = after(core_arg, *dv_places, *made)
-    out, dq, other, *dk_terms = run_grads(core_late, *grad_args, (n_heads // 2, n_heads), early)
-    dk_back = [shifted(dk_terms[n_back - d], -2 * d) for d in range(1, n_back + 1)]
-    *dk_back, _ = lax.optimization_barrier((*dk_back, by_z[0]))
-    dk_total = dk_terms[n_back].astype(F32)
-    for term in dk_back:
-        dk_total = dk_total + term.astype(F32)
-    dk_chip = dk_total.astype(BF16)
+    if out_rows % 8 == 0:
+        at = after(jnp.stack([core, my_z]).astype(jnp.int32), *made)
+        by_z = run_weight(at, pieces, theirs, dv_places, n_z)
+    else:
+        weight_term = None
+        for at, dv_of in enumerate(dv_places):
+            window = slice(at * shard_rows, (at + 1) * shard_rows)
+            term = dot(pieces[at], rows_of(dv_of, core, shard_rows))
+            term = term + dot(theirs[:, window], rows_of(dv_of, 1 - core, shard_rows))
+            weight_term = term if weight_term is None else weight_term + term
+        weight_term = weight_term.reshape(n_z, 2 * out_rows, half_kv)
+        by_z = [
+            lax.dynamic_index_in_dim(weight_term, (my_z + d) % n_z, 0, keepdims=False).astype(BF16 if d else F32)
+            for d in range(n_z)
+        ]
+    over_z = [
+        lax.ppermute(by_z[d], "ctx", [(i, (i + 4 * d) % n_ctx) for i in range(n_ctx)]) for d in range(1, n_z)
+    ]
+
+    core_late = after(core_arg, by_z[0])
+    out, dq, other, dk_far, dk_near, dk_mine = run_grads(core_late, *grad_args, (n_heads // 2, n_heads), early)
+    dk_got = flipped(dk_near)
+    dk_sent = relayed(my_y, dk_far, dk_got)
+    dk_back = shifted(dk_sent, -4)
+
+    over_z, _ = lax.optimization_barrier((over_z, dk_sent))
+    row_sum = by_z[0]
+    for x in over_z:
+        row_sum = row_sum + x.astype(F32)
+    d_weight = placed(core, rows_of(row_sum, core, out_rows), swapped(rows_of(row_sum, 1 - core, out_rows)), 1)
+
+    dk_chip = gathered_terms(my_y, dk_mine, dk_got, dk_back)
     d_keys = placed(core, rows_of(dk_chip, core, shard_rows), swapped(rows_of(dk_chip, 1 - core, shard_rows)), 1)
     other = swapped(other)
     out = lax.dynamic_update_slice_in_dim(out, other[0], (1 - core) * half_q, 1)

time: 220 us -> 215 us (0.977)
  starting transfers between devices: 48.7 us -> 34.2 us
  local copies, waits for them, and re-layouts: 21.6 us -> 31.5 us
  waiting for transfers between devices: 88.8 us -> 84.6 us
  other arithmetic: 8.84 us -> 11.8 us
    ppermute x6 -> x3, waiting for transfers between devices: 42.3 us -> 12.9 us  [moved(): return lax.ppermute(x, ('ctx', 'fsdp'), pairs)]
    ppermute x0 -> x6, waiting for transfers between devices: none -> 16.5 us  [flipped(): lax.ppermute(x, 'ctx', [(i, i ^ 2) for i in range(lax.axis_size('ctx'))])]
    ppermute x8 -> x4, starting transfers between devices: 23 us -> 10.7 us  [shifted(): lax.ppermute(x, 'ctx', [(i, i + by) for i in range(length) if 0 <= i + by...]
    ppermute x8 -> x4, waiting for transfers between devices: 9.5 us -> 21.7 us  [shifted(): lax.ppermute(x, 'ctx', [(i, i + by) for i in range(length) if 0 <= i + by...]
    unnamed x60 -> x116, local copies, waits for them, and re-layouts: 12.7 us -> 21.7 us
    ppermute x3, waiting for transfers between devices: 25.2 us -> 16.9 us  [shards(): lax.ppermute(by_z[d], 'ctx', [(i, (i + 4 * d) % n_ctx) for i in range(n_c...]
    ppermute x0 -> x6, starting transfers between devices: none -> 6.18 us  [flipped(): lax.ppermute(x, 'ctx', [(i, i ^ 2) for i in range(lax.axis_size('ctx'))])]
    ppermute x8, waiting for transfers between devices: 1.17 us -> 5.99 us  [swapped(): lax.ppermute(x, 'ctx', [(i, i ^ 1) for i in range(lax.axis_size('ctx'))])]
  transfers between devices with their start and end apart: 28 -> 28, of which waited for: 11 -> 14; matrix products, arithmetic and copies ran while one was open for 7% -> 7% of each run, Pallas kernels for 23% -> 24%
where the time goes in v1:
time: 215 us; the launch traced here: 214 us
  waiting for transfers between devices  84.6 us (39%)
  Pallas kernels  50.6 us (24%)
  starting transfers between devices  34.2 us (16%)
  local copies, waits for them, and re-layouts  31.5 us (15%)
  other arithmetic  11.8 us (5%)
    unnamed x116, local copies, waits for them, and re-layouts  21.7 us
    ppermute x4, waiting for transfers between devices, shifted(): lax.ppermute(x, 'ctx', [(i, i + by) for i in range(length) if 0 <= i + by...  21.7 us
    pallas_call x2, Pallas kernels, run_grads(): pl.pallas_call(kernel, grid_spec=pltpu.PrefetchScalarGridSpec(num_scalar_...  18.3 us
    ppermute x3, waiting for transfers between devices, shards(): lax.ppermute(by_z[d], 'ctx', [(i, (i + 4 * d) % n_ctx) for i in range(n_c...  16.9 us
    ppermute x6, waiting for transfers between devices, flipped(): lax.ppermute(x, 'ctx', [(i, i ^ 2) for i in range(lax.axis_size('ctx'))])  16.5 us
    pallas_call x1, Pallas kernels, run_probs(): pl.pallas_call(functools.partial(probs_kernel, blk, n_arr - 1), grid_spec...  14.1 us
    ppermute x3, waiting for transfers between devices, moved(): return lax.ppermute(x, ('ctx', 'fsdp'), pairs)  12.9 us
    ppermute x4, waiting for transfers between devices, rotated(): lax.ppermute(x, 'fsdp', [(i, (i + by) % length) for i in range(length)])  10.7 us
  transfers between devices with their start and end apart: 28, of which 14 were waited for; matrix products, arithmetic and copies ran while one was open for 7% of the time, Pallas kernels for 24%

profile of v1, /device:TPU:9, one launch (start us, length us, event | category | flops | bytes accessed | tf_op | source)
XLA Modules:
  0.0 214.0 jit_solution(10098412917120511024)
XLA Ops:
  0.8 1.2 dynamic-slice_bitcast_fusion.3
  4.2 2.5 %dynamic-slice_bitcast_fusion = bf16[256,2688]{1,0:T(8,128)(2,1)} fusion(bf16[1,256,5376]{2,1,0:T(8,128)(2,1)} %param.6, s32[]{:T(128)S(6)} %select_n.105), kind=kLoop, calls=%fused_computation.4 | loop fusion | bytes 2752516 | tf_op jit(solution)/shard_map/dynamic_slice | solution.py:409
  6.8 2.4 %pieces.1 = (bf16[1344,256]{1,0:T(8,128)(2,1)S(1)}, bf16[1344,256]{1,0:T(8,128)(2,1)S(1)}, bf16[1344,256]{1,0:T(8,128)(2,1)S(1)}, bf16[1344,256]{1,0:T(8,128)(2,1)}) custom-call(s32[2]{0:T(128)S(1)} %pad_add_fusion.1.at_ref, bf16[256,5376]{1,0:T(8,128)(2,1)S(1)} %bitcast.29), custom_call_target="tpu_custom_call" | custom-call | flops 1048576 | bytes 4096 | tf_op jit(solution)/shard_map/pieces/pallas_call | solution.py:269
  11.0 1.3 collective-permute-start.2
  12.3 1.2 collective-permute-start.3
  13.6 3.2 %collective-permute-start.1 = (bf16[528,512]{1,0:T(8,128)(2,1)S(1)}, bf16[528,512]{1,0:T(8,128)(2,1)}, u32[]{:S(2)}, u32[]{:S(2)}) collective-permute-start(bf16[528,512]{1,0:T(8,128)(2,1)S(1)} %pad_maximum_fusion.4.refs_2_.refs_8_), channel_id=1, source_target_pairs={{0,8},{2,10},{4,12},{6,14},{8,16},{10,18},{12,20},{14,22},{16,24},... | collective-permute-start | bytes 1622024 | tf_op jit(solution)/shard_map/ppermute | solution.py:378
  20.0 2.6 %copy-done = bf16[2688,1024]{1,0:T(8,128)(2,1)S(1)} copy-done((bf16[2688,1024]{1,0:T(8,128)(2,1)S(1)}, bf16[2688,1024]{1,0:T(8,128)(2,1)}, u32[]{:S(2)}) %copy-start) | copy-done | bytes 5505048
  22.6 2.4 %product.2 = f32[256,1024]{1,0:T(8,128)S(1)} custom-call(s32[1]{0:T(128)} %bitcast.2.at_ref, bf16[256,5376]{1,0:T(8,128)(2,1)S(1)} %bitcast.30, bf16[2688,1024]{1,0:T(8,128)(2,1)S(1)} %copy-done), custom_call_target="tpu_custom_call" | custom-call | flops 1048576 | bytes 4096 | tf_op jit(solution)/shard_map/product/pallas_call | solution.py:289
  25.0 3.8 %collective-permute-done.1.refs_0_.refs_6_ = bf16[528,512]{1,0:T(8,128)(2,1)} collective-permute-done((bf16[528,512]{1,0:T(8,128)(2,1)S(1)}, bf16[528,512]{1,0:T(8,128)(2,1)}, u32[]{:S(2)}, u32[]{:S(2)}) %collective-permute-start.1) | collective-permute-done | bytes 540704 | tf_op jit(solution)/shard_map/ppermute | solution.py:378
  29.7 1.9 collective-permute-start.5
  33.4 10.7 %collective-permute-done.3.x_ref = bf16[256,2688]{1,0:T(8,128)(2,1)} collective-permute-done((bf16[256,2688]{1,0:T(8,128)(2,1)}, bf16[256,2688]{1,0:T(8,128)(2,1)}, u32[]{:S(2)}, u32[]{:S(2)}) %collective-permute-start.3) | collective-permute-done | bytes 1376288 | tf_op jit(solution)/shard_map/ppermute | solution.py:387
  44.2 2.6 %copy-done.1 = bf16[2688,1024]{1,0:T(8,128)(2,1)S(1)} copy-done((bf16[2688,1024]{1,0:T(8,128)(2,1)S(1)}, bf16[2688,1024]{1,0:T(8,128)(2,1)}, u32[]{:S(2)}) %copy-start.1) | copy-done | bytes 5505048
  46.7 3.5 %product.3 = bf16[256,1024]{1,0:T(8,128)(2,1)S(1)} custom-call(s32[1]{0:T(128)} %constant.82.clone.1.at_ref, bf16[256,2688]{1,0:T(8,128)(2,1)} %collective-permute-done.3.x_ref, bf16[2688,1024]{1,0:T(8,128)(2,1)S(1)} %copy-done.1), custom_call_target="tpu_custom_call" | custom-call | flops 1048576 | bytes 4096 | tf_op jit(solution)/shard_map/product/pallas_call | solution.py:289
  50.3 1.3 collective-permute-start.4
  52.5 14.1 %probs.1 = (bf16[4,2,1280,512]{3,2,1,0:T(8,128)(2,1)}, f32[4,2,1,512]{3,2,1,0:T(1,128)S(1)}, bf16[4,2,128,512]{3,2,1,0:T(8,128)(2,1)S(1)}, bf16[512,512]{1,0:T(8...) custom-call(s32[1]{0:T(128)} %bitcast.core_ref.refs_0_, ...), custom_call_target="tpu_custom_call" | custom-call | flops 1048576 | bytes 4096 | tf_op jit(solution)/shard_map/probs/pallas_call | solution.py:157
  66.7 1.3 collective-permute-start.8
  68.2 2.0 collective-permute-start.9
  70.2 1.2 pad_maximum_fusion.1
  71.9 3.3 %collective-permute-start.12 = (bf16[512,512]{1,0:T(8,128)(2,1)S(1)}, bf16[512,512]{1,0:T(8,128)(2,1)S(1)}, u32[]{:S(2)}, u32[]{:S(2)}) collective-permute-start(bf16[512,512]{1,0:T(8,128)(2,1)S(1)} %constant_dynamic-update-slice_fusion.2.refs_11_), channel_id=1, source_target_pairs={{0,8},{2,10},{4,12},{6,14},{8,16},{10,18},{12,20},{14,22},{16,24},... | collective-permute-start | bytes 1572872 | tf_op jit(solution)/shard_map/ppermute | solution.py:378
  75.2 3.9 %collective-permute-done.8 = bf16[512,512]{1,0:T(8,128)(2,1)S(1)} collective-permute-done((bf16[512,512]{1,0:T(8,128)(2,1)S(1)}, bf16[512,512]{1,0:T(8,128)(2,1)S(1)}, u32[]{:S(2)}, u32[]{:S(2)}) %collective-permute-start.8) | collective-permute-done | bytes 524320 | tf_op jit(solution)/shard_map/ppermute | solution.py:422
  79.3 2.3 %collective-permute-start.11 = (bf16[512,512]{1,0:T(8,128)(2,1)S(1)}, bf16[512,512]{1,0:T(8,128)(2,1)S(1)}, u32[]{:S(2)}, u32[]{:S(2)}) collective-permute-start(bf16[512,512]{1,0:T(8,128)(2,1)S(1)} %fusion.1), channel_id=1, source_target_pairs={{8,0},{10,2},{12,4},{14,6},{16,8},{18,10},{20,12},{22,14},{24,16},... | collective-permute-start | bytes 1572872 | tf_op jit(solution)/shard_map/ppermute | solution.py:378
  81.5 5.5 %collective-permute-done.12.refs_9_ = bf16[512,512]{1,0:T(8,128)(2,1)S(1)} collective-permute-done((bf16[512,512]{1,0:T(8,128)(2,1)S(1)}, bf16[512,512]{1,0:T(8,128)(2,1)S(1)}, u32[]{:S(2)}, u32[]{:S(2)}) %collective-permute-start.12) | collective-permute-done | bytes 524320 | tf_op jit(solution)/shard_map/ppermute | solution.py:378
  87.2 5.1 %collective-permute-done.11 = bf16[512,512]{1,0:T(8,128)(2,1)S(1)} collective-permute-done((bf16[512,512]{1,0:T(8,128)(2,1)S(1)}, bf16[512,512]{1,0:T(8,128)(2,1)S(1)}, u32[]{:S(2)}, u32[]{:S(2)}) %collective-permute-start.11) | collective-permute-done | bytes 524320 | tf_op jit(solution)/shard_map/ppermute | solution.py:378
  93.2 2.1 collective-permute-start.15
  95.3 4.2 %collective-permute-done.16.refs_10_ = bf16[512,512]{1,0:T(8,128)(2,1)S(1)} collective-permute-done((bf16[512,512]{1,0:T(8,128)(2,1)S(1)}, bf16[512,512]{1,0:T(8,128)(2,1)S(1)}, u32[]{:S(2)}, u32[]{:S(2)}) %collective-permute-start.16) | collective-permute-done | bytes 524320 | tf_op jit(solution)/shard_map/ppermute | solution.py:422
  99.5 9.1 %grads.2 = (bf16[256,2048]{1,0:T(8,128)(2,1)}, bf16[256,2048]{1,0:T(8,128)(2,1)}, bf16[2,256,1024]{2,1,0:T(8,128)(2,1)S(1)}, bf16[512,512]{1,0:T(8,128)(2,1)S(1)...) custom-call(s32[1]{0:T(128)} %bitcast.core_ref.refs_0_, bf16[4,2,1280,512]{3,2,1,0:T(8,128)(2,1)} %get-tuple-element.81.refs_1_, ...), custom_call_target="tpu_custom_call" | custom-call | flops 1048576 | bytes 4096 | tf_op jit(solution)/shard_map/grads/pallas_call | solution.py:208
  111.3 3.2 %collective-permute-done.13.refs_6_ = bf16[512,512]{1,0:T(8,128)(2,1)S(1)} collective-permute-done((bf16[512,512]{1,0:T(8,128)(2,1)S(1)}, bf16[512,512]{1,0:T(8,128)(2,1)S(1)}, u32[]{:S(2)}, u32[]{:S(2)}) %collective-permute-start.13) | collective-permute-done | bytes 524320 | tf_op jit(solution)/shard_map/ppermute | solution.py:397
  115.3 9.7 %collective-permute-done.15.refs_8_ = bf16[512,512]{1,0:T(8,128)(2,1)S(1)} collective-permute-done((bf16[512,512]{1,0:T(8,128)(2,1)S(1)}, bf16[512,512]{1,0:T(8,128)(2,1)S(1)}, u32[]{:S(2)}, u32[]{:S(2)}) %collective-permute-start.15) | collective-permute-done | bytes 524320 | tf_op jit(solution)/shard_map/ppermute | solution.py:397
  126.0 1.8 pad_maximum_fusion
  128.0 1.5 collective-permute-start.18
  129.8 5.0 %collective-permute-done.17 = bf16[512,512]{1,0:T(8,128)(2,1)S(1)} collective-permute-done((bf16[512,512]{1,0:T(8,128)(2,1)S(1)}, bf16[512,512]{1,0:T(8,128)(2,1)S(1)}, u32[]{:S(2)}, u32[]{:S(2)}) %collective-permute-start.17) | collective-permute-done | bytes 524320 | tf_op jit(solution)/shard_map/ppermute | solution.py:382
  134.9 4.8 %tokens.1 = (bf16[256,5376]{1,0:T(8,128)(2,1)}, bf16[256,2688]{1,0:T(8,128)(2,1)}) custom-call(s32[1]{0:T(128)} %bitcast.2.at_ref, bf16[512,1024]{1,0:T(8,128)(2,1)S(1)} %constant_dynamic-update-slice_fusion.1.dv_ref, bf16[2688,1024]{1,0:T(8,128)(2,1)S(1)} %bitcast.28), custom_call_target="tpu_custom_call" | custom-call | flops 1048576 | bytes 4096 | tf_op jit(solution)/shard_map/tokens/pallas_call | solution.py:356
  140.1 1.1 copy-done.5
  144.4 1.1 copy-done.23
  148.7 5.0 %weight.1 = (f32[336,512]{1,0:T(8,128)S(1)}, bf16[336,512]{1,0:T(8,128)(2,1)}, bf16[336,512]{1,0:T(8,128)(2,1)}, bf16[336,512]{1,0:T(8,128)(2,1)S(1)}) custom-call(s32[2]{0:T(128)S(1)} %pad_add_fusion.at_ref, bf16[1344,256]{1,0:T(8,128)(2,1)S(1)} %copy-done.21, bf16[1344,256]{1,0:T(8,128)(2,1)S(1)} %copy-done.7, bf16[1344,256]{1,0:T(8,128)(2,1)S(1)} %copy-done.23, ...), custom_call_target="tpu_custom_call" | custom-call | flops 1048576 | bytes 4096 | tf_op jit(solution)/shard_map/weight/pallas_call | solution.py:332
  153.7 9.2 %grads.3 = (bf16[256,2048]{1,0:T(8,128)(2,1)}, bf16[256,2048]{1,0:T(8,128)(2,1)}, bf16[2,256,1024]{2,1,0:T(8,128)(2,1)S(1)}, bf16[512,512]{1,0:T(8,128)(2,1)S(1)...) custom-call(s32[1]{0:T(128)} %bitcast.core_ref.refs_0_, ...), custom_call_target="tpu_custom_call", output_to_operand_aliasing={{0}: (12, {}), {1}: (13, {}), {2}: (14, {}), {3}: (15, {}),... | custom-call | flops 1048576 | bytes 4096 | tf_op jit(solution)/shard_map/grads/pallas_call | solution.py:208
  165.5 1.2 collective-permute-start.20
  166.7 1.3 collective-permute-start.24
  169.0 1.5 collective-permute-start.26
  170.5 8.3 %collective-permute-done.20 = bf16[512,512]{1,0:T(8,128)(2,1)S(1)} collective-permute-done((bf16[512,512]{1,0:T(8,128)(2,1)}, bf16[512,512]{1,0:T(8,128)(2,1)S(1)}, u32[]{:S(2)}, u32[]{:S(2)}) %collective-permute-start.20) | collective-permute-done | bytes 524320 | tf_op jit(solution)/shard_map/ppermute | solution.py:422
  178.7 1.3 collective-permute-start.19
  180.0 1.2 fusion.5
  181.2 1.9 collective-permute-start.21
  183.2 14.0 %collective-permute-done.25 = bf16[336,512]{1,0:T(8,128)(2,1)} collective-permute-done((bf16[336,512]{1,0:T(8,128)(2,1)}, bf16[336,512]{1,0:T(8,128)(2,1)}, u32[]{:S(2)}, u32[]{:S(2)}) %collective-permute-start.25) | collective-permute-done | bytes 344096 | tf_op jit(solution)/shard_map/ppermute | solution.py:583
  197.1 2.9 %collective-permute-done.26 = bf16[336,512]{1,0:T(8,128)(2,1)} collective-permute-done((bf16[336,512]{1,0:T(8,128)(2,1)S(1)}, bf16[336,512]{1,0:T(8,128)(2,1)}, u32[]{:S(2)}, u32[]{:S(2)}) %collective-permute-start.26) | collective-permute-done | bytes 344096 | tf_op jit(solution)/shard_map/ppermute | solution.py:583
  200.0 1.5 convert_add_fusion
  202.3 1.5 bitcast_dynamic-update-slice_fusion
  204.0 7.2 %collective-permute-done.21 = bf16[512,512]{1,0:T(8,128)(2,1)S(1)} collective-permute-done((bf16[512,512]{1,0:T(8,128)(2,1)S(1)}, bf16[512,512]{1,0:T(8,128)(2,1)S(1)}, u32[]{:S(2)}, u32[]{:S(2)}) %collective-permute-start.21) | collective-permute-done | bytes 524320 | tf_op jit(solution)/shard_map/ppermute | solution.py:378
  (182 shorter events, 31.7 us)
Async XLA Ops:
  0.6 6.1 %copy-start.2 = (bf16[1,256,5376]{2,1,0:T(8,128)(2,1)S(1)}, bf16[1,256,5376]{2,1,0:T(8,128)(2,1)}, u32[]{:S(2)}) copy-start(bf16[1,256,5376]{2,1,0:T(8,128)(2,1)} %param.6) | copy-start | bytes 8257540
  3.5 5.8 %collective-permute-start = (bf16[272,512]{1,0:T(8,128)(2,1)}, bf16[272,512]{1,0:T(8,128)(2,1)}, u32[]{:S(2)}, u32[]{:S(2)}) collective-permute-start(bf16[272,512]{1,0:T(8,128)(2,1)} %maximum_maximum_fusion.1), channel_id=1, source_target_pairs={{0,2},{2,0},{4,6},{6,4},{8,10},{10,8},{12,14},{14,12},{16,18},{18,... | collective-permute-start | bytes 835592 | tf_op jit(solution)/shard_map/ppermute | solution.py:382
  11.0 17.8 %collective-permute-start.2 = (bf16[1344,256]{1,0:T(8,128)(2,1)}, bf16[1344,256]{1,0:T(8,128)(2,1)}, u32[]{:S(2)}, u32[]{:S(2)}) collective-permute-start(bf16[1344,256]{1,0:T(8,128)(2,1)} %get-tuple-element.66), channel_id=1, source_target_pairs={{0,4},{2,6},{4,0},{6,2},{8,12},{10,14},{12,8},{14,10},{16,20},{18,... | collective-permute-start | bytes 2064392 | tf_op jit(solution)/shard_map/ppermute | solution.py:422
  12.3 31.8 %collective-permute-start.3 = (bf16[256,2688]{1,0:T(8,128)(2,1)}, bf16[256,2688]{1,0:T(8,128)(2,1)}, u32[]{:S(2)}, u32[]{:S(2)}) collective-permute-start(bf16[256,2688]{1,0:T(8,128)(2,1)} %dynamic-slice_bitcast_fusion), channel_id=1, source_target_pairs={{0,1},{1,0},{2,3},{3,2},{4,5},{5,4},{6,7},{7,6},{8,9},{9,8},{10,11... | collective-permute-start | bytes 4128776 | tf_op jit(solution)/shard_map/ppermute | solution.py:387
  13.6 15.3 %collective-permute-start.1 = (bf16[528,512]{1,0:T(8,128)(2,1)S(1)}, bf16[528,512]{1,0:T(8,128)(2,1)}, u32[]{:S(2)}, u32[]{:S(2)}) collective-permute-start(bf16[528,512]{1,0:T(8,128)(2,1)S(1)} %pad_maximum_fusion.4.refs_2_.refs_8_), channel_id=1, source_target_pairs={{0,8},{2,10},{4,12},{6,14},{8,16},{10,18},{12,20},{14,22},{16,24},... | collective-permute-start | bytes 1622024 | tf_op jit(solution)/shard_map/ppermute | solution.py:378
  29.7 21.9 %collective-permute-start.5 = (bf16[528,512]{1,0:T(8,128)(2,1)}, bf16[528,512]{1,0:T(8,128)(2,1)S(1)}, u32[]{:S(2)}, u32[]{:S(2)}) collective-permute-start(bf16[528,512]{1,0:T(8,128)(2,1)} %broadcast_select_fusion), channel_id=1, source_target_pairs={{0,4},{2,6},{4,0},{6,2},{8,12},{10,14},{12,8},{14,10},{16,20},{18,... | collective-permute-start | bytes 1622024 | tf_op jit(solution)/shard_map/ppermute | solution.py:422
  31.6 20.9 %collective-permute-start.6 = (bf16[256,2048]{1,0:T(8,128)(2,1)}, bf16[256,2048]{1,0:T(8,128)(2,1)S(1)}, u32[]{:S(2)}, u32[]{:S(2)}) collective-permute-start(bf16[256,2048]{1,0:T(8,128)(2,1)} %pad_maximum_fusion.2), channel_id=1, source_target_pairs={{0,2},{2,0},{4,6},{6,4},{8,10},{10,8},{12,14},{14,12},{16,18},{18,... | collective-permute-start | bytes 3145736 | tf_op jit(solution)/shard_map/ppermute | solution.py:382
  50.3 17.7 %collective-permute-start.4 = (bf16[256,1024]{1,0:T(8,128)(2,1)S(1)}, bf16[256,1024]{1,0:T(8,128)(2,1)S(1)}, u32[]{:S(2)}, u32[]{:S(2)}) collective-permute-start(bf16[256,1024]{1,0:T(8,128)(2,1)S(1)} %product.3), channel_id=1, source_target_pairs={{0,1},{1,0},{2,3},{3,2},{4,5},{5,4},{6,7},{7,6},{8,9},{9,8},{10,11... | collective-permute-start | bytes 1572872 | tf_op jit(solution)/shard_map/ppermute | solution.py:387
  51.6 15.1 %copy-start.8 = (bf16[528,512]{1,0:T(8,128)(2,1)}, bf16[528,512]{1,0:T(8,128)(2,1)S(1)}, u32[]{:S(2)}) copy-start(bf16[528,512]{1,0:T(8,128)(2,1)S(1)} %collective-permute-done.5.refs_1_.refs_7_) | copy-start | bytes 1622020
  52.2 19.6 %collective-permute-start.10 = (bf16[1344,256]{1,0:T(8,128)(2,1)S(1)}, bf16[1344,256]{1,0:T(8,128)(2,1)S(1)}, u32[]{:S(2)}, u32[]{:S(2)}) collective-permute-start(bf16[1344,256]{1,0:T(8,128)(2,1)S(1)} %copy-done.47), channel_id=1, source_target_pairs={{0,4},{2,6},{4,0},{6,2},{8,12},{10,14},{12,8},{14,10},{16,20},{18,... | collective-permute-start | bytes 2064392 | tf_op jit(solution)/shard_map/ppermute | solution.py:422
  52.5 15.5 %copy-start.18 = (f32[256,1024]{1,0:T(8,128)S(1)}, f32[256,1024]{1,0:T(8,128)}, u32[]{:S(2)}) copy-start(f32[256,1024]{1,0:T(8,128)} %copy-done.17) | copy-start | bytes 3145732
  66.6 32.9 %copy-start.15 = (bf16[4,2,128,512]{3,2,1,0:T(8,128)(2,1)}, bf16[4,2,128,512]{3,2,1,0:T(8,128)(2,1)S(1)}, u32[]{:S(2)}) copy-start(bf16[4,2,128,512]{3,2,1,0:T(8,128)(2,1)S(1)} %get-tuple-element.83.refs_3_) | copy-start | bytes 3145732
  66.7 12.5 %collective-permute-start.8 = (bf16[512,512]{1,0:T(8,128)(2,1)S(1)}, bf16[512,512]{1,0:T(8,128)(2,1)S(1)}, u32[]{:S(2)}, u32[]{:S(2)}) collective-permute-start(bf16[512,512]{1,0:T(8,128)(2,1)S(1)} %get-tuple-element.72), channel_id=1, source_target_pairs={{0,4},{2,6},{4,0},{6,2},{8,12},{10,14},{12,8},{14,10},{16,20},{18,... | collective-permute-start | bytes 1572872 | tf_op jit(solution)/shard_map/ppermute | solution.py:422
  68.2 3.6 %collective-permute-start.9 = (bf16[256,512]{1,0:T(8,128)(2,1)S(1)}, bf16[256,512]{1,0:T(8,128)(2,1)S(1)}, u32[]{:S(2)}, u32[]{:S(2)}) collective-permute-start(bf16[256,512]{1,0:T(8,128)(2,1)S(1)} %get-tuple-element.125), channel_id=1, source_target_pairs={{0,2},{2,0},{4,6},{6,4},{8,10},{10,8},{12,14},{14,12},{16,18},{18,... | collective-permute-start | bytes 786440 | tf_op jit(solution)/shard_map/ppermute | solution.py:382
  71.4 54.4 %collective-permute-start.7 = (bf16[1344,512]{1,0:T(8,128)(2,1)S(1)}, bf16[1344,512]{1,0:T(8,128)(2,1)S(1)}, u32[]{:S(2)}, u32[]{:S(2)}) collective-permute-start(bf16[1344,512]{1,0:T(8,128)(2,1)S(1)} %pad_maximum_fusion.1), channel_id=1, source_target_pairs={{0,1},{1,0},{2,3},{3,2},{4,5},{5,4},{6,7},{7,6},{8,9},{9,8},{10,11... | collective-permute-start | bytes 4128776 | tf_op jit(solution)/shard_map/ppermute | solution.py:387
  71.8 27.7 %copy-start.9 = (bf16[528,512]{1,0:T(8,128)(2,1)S(1)}, bf16[528,512]{1,0:T(8,128)(2,1)}, u32[]{:S(2)}) copy-start(bf16[528,512]{1,0:T(8,128)(2,1)} %copy-done.8) | copy-start | bytes 1622020
  71.8 54.1 %copy-start.22 = (bf16[1344,256]{1,0:T(8,128)(2,1)}, bf16[1344,256]{1,0:T(8,128)(2,1)S(1)}, u32[]{:S(2)}) copy-start(bf16[1344,256]{1,0:T(8,128)(2,1)S(1)} %collective-permute-done.10.refs_2_) | copy-start | bytes 2064388
  71.9 15.2 %collective-permute-start.12 = (bf16[512,512]{1,0:T(8,128)(2,1)S(1)}, bf16[512,512]{1,0:T(8,128)(2,1)S(1)}, u32[]{:S(2)}, u32[]{:S(2)}) collective-permute-start(bf16[512,512]{1,0:T(8,128)(2,1)S(1)} %constant_dynamic-update-slice_fusion.2.refs_11_), channel_id=1, source_target_pairs={{0,8},{2,10},{4,12},{6,14},{8,16},{10,18},{12,20},{14,22},{16,24},... | collective-permute-start | bytes 1572872 | tf_op jit(solution)/shard_map/ppermute | solution.py:378
  79.3 13.0 %collective-permute-start.11 = (bf16[512,512]{1,0:T(8,128)(2,1)S(1)}, bf16[512,512]{1,0:T(8,128)(2,1)S(1)}, u32[]{:S(2)}, u32[]{:S(2)}) collective-permute-start(bf16[512,512]{1,0:T(8,128)(2,1)S(1)} %fusion.1), channel_id=1, source_target_pairs={{8,0},{10,2},{12,4},{14,6},{16,8},{18,10},{20,12},{22,14},{24,16},... | collective-permute-start | bytes 1572872 | tf_op jit(solution)/shard_map/ppermute | solution.py:378
  87.1 21.6 %copy-start.11 = (bf16[512,512]{1,0:T(8,128)(2,1)}, bf16[512,512]{1,0:T(8,128)(2,1)S(1)}, u32[]{:S(2)}) copy-start(bf16[512,512]{1,0:T(8,128)(2,1)S(1)} %collective-permute-done.12.refs_9_) | copy-start | bytes 1572868
  87.1 12.4 %collective-permute-start.16 = (bf16[512,512]{1,0:T(8,128)(2,1)S(1)}, bf16[512,512]{1,0:T(8,128)(2,1)S(1)}, u32[]{:S(2)}, u32[]{:S(2)}) collective-permute-start(bf16[512,512]{1,0:T(8,128)(2,1)S(1)} %broadcast_select_fusion.1), channel_id=1, source_target_pairs={{0,4},{2,6},{4,0},{6,2},{8,12},{10,14},{12,8},{14,10},{16,20},{18,... | collective-permute-start | bytes 1572872 | tf_op jit(solution)/shard_map/ppermute | solution.py:422
  92.5 36.9 %copy-start.13 = (bf16[512,512]{1,0:T(8,128)(2,1)}, bf16[512,512]{1,0:T(8,128)(2,1)S(1)}, u32[]{:S(2)}) copy-start(bf16[512,512]{1,0:T(8,128)(2,1)S(1)} %fusion.3.refs_5_) | copy-start | bytes 1572868
  92.6 21.9 %collective-permute-start.13 = (bf16[512,512]{1,0:T(8,128)(2,1)S(1)}, bf16[512,512]{1,0:T(8,128)(2,1)S(1)}, u32[]{:S(2)}, u32[]{:S(2)}) collective-permute-start(bf16[512,512]{1,0:T(8,128)(2,1)S(1)} %fusion.3.refs_5_), channel_id=1, source_target_pairs={{0,1},{1,0},{2,3},{3,2},{4,5},{5,4},{6,7},{7,6},{8,9},{9,8},{10,11... | collective-permute-start | bytes 1572872 | tf_op jit(solution)/shard_map/ppermute | solution.py:397
  92.9 21.6 %collective-permute-start.14 = (bf16[512,512]{1,0:T(8,128)(2,1)S(1)}, bf16[512,512]{1,0:T(8,128)(2,1)S(1)}, u32[]{:S(2)}, u32[]{:S(2)}) collective-permute-start(bf16[512,512]{1,0:T(8,128)(2,1)S(1)} %fusion.3.refs_5_), channel_id=1, source_target_pairs={{0,4},{1,5},{2,6},{3,7},{4,0},{5,1},{6,2},{7,3},{8,12},{9,13},{10,... | collective-permute-start | bytes 1572872 | tf_op jit(solution)/shard_map/ppermute | solution.py:397
  93.2 31.8 %collective-permute-start.15 = (bf16[512,512]{1,0:T(8,128)(2,1)S(1)}, bf16[512,512]{1,0:T(8,128)(2,1)S(1)}, u32[]{:S(2)}, u32[]{:S(2)}) collective-permute-start(bf16[512,512]{1,0:T(8,128)(2,1)S(1)} %fusion.3.refs_5_), channel_id=1, source_target_pairs={{0,5},{1,4},{2,7},{3,6},{4,1},{5,0},{6,3},{7,2},{8,13},{9,12},{10,... | collective-permute-start | bytes 1572872 | tf_op jit(solution)/shard_map/ppermute | solution.py:397
  99.5 9.1 %copy-start.25 = (bf16[512,512]{1,0:T(8,128)(2,1)}, bf16[512,512]{1,0:T(8,128)(2,1)S(1)}, u32[]{:S(2)}) copy-start(bf16[512,512]{1,0:T(8,128)(2,1)S(1)} %collective-permute-done.16.refs_10_) | copy-start | bytes 1572868
  111.3 14.7 %copy-start.20 = (bf16[1344,256]{1,0:T(8,128)(2,1)S(1)}, bf16[1344,256]{1,0:T(8,128)(2,1)}, u32[]{:S(2)}) copy-start(bf16[1344,256]{1,0:T(8,128)(2,1)} %copy-done.19) | copy-start | bytes 2064388
  114.5 15.0 %copy-start.34 = (bf16[512,512]{1,0:T(8,128)(2,1)}, bf16[512,512]{1,0:T(8,128)(2,1)S(1)}, u32[]{:S(2)}) copy-start(bf16[512,512]{1,0:T(8,128)(2,1)S(1)} %collective-permute-done.13.refs_6_) | copy-start | bytes 1572868
  125.8 9.1 %slice-start = ((s8[5505024]{0:T(1024)(128)(4,1)}), s8[4194304]{0:T(1024)(128)(4,1)S(1)}, s32[]{:S(2)}) async-start(s8[5505024]{0:T(1024)(128)(4,1)} %bitcast.27), calls=%async_computation | async-start | bytes 8388608
  125.9 8.9 %slice-start.1 = ((s8[5505024]{0:T(1024)(128)(4,1)}), s8[1310720]{0:T(1024)(128)(4,1)S(1)}, s32[]{:S(2)}) async-start(s8[5505024]{0:T(1024)(128)(4,1)} %bitcast.27), calls=%async_computation.1 | async-start | bytes 2621440
  128.0 12.1 %collective-permute-start.18 = (bf16[1344,1024]{1,0:T(8,128)(2,1)}, bf16[1344,1024]{1,0:T(8,128)(2,1)}, u32[]{:S(2)}, u32[]{:S(2)}) collective-permute-start(bf16[1344,1024]{1,0:T(8,128)(2,1)} %pad_maximum_fusion), channel_id=1, source_target_pairs={{0,2},{2,0},{4,6},{6,4},{8,10},{10,8},{12,14},{14,12},{16,18},{18,... | collective-permute-start | bytes 8257544 | tf_op jit(solution)/shard_map/ppermute | solution.py:382
  129.6 5.2 %collective-permute-start.17 = (bf16[512,512]{1,0:T(8,128)(2,1)S(1)}, bf16[512,512]{1,0:T(8,128)(2,1)S(1)}, u32[]{:S(2)}, u32[]{:S(2)}) collective-permute-start(bf16[512,512]{1,0:T(8,128)(2,1)S(1)} %pad_maximum_fusion.7), channel_id=1, source_target_pairs={{0,2},{2,0},{4,6},{6,4},{8,10},{10,8},{12,14},{14,12},{16,18},{18,... | collective-permute-start | bytes 1572872 | tf_op jit(solution)/shard_map/ppermute | solution.py:382
  139.7 62.5 %collective-permute-start.23 = (bf16[256,2688]{1,0:T(8,128)(2,1)}, bf16[256,2688]{1,0:T(8,128)(2,1)}, u32[]{:S(2)}, u32[]{:S(2)}) collective-permute-start(bf16[256,2688]{1,0:T(8,128)(2,1)} %get-tuple-element.87), channel_id=1, source_target_pairs={{0,1},{1,0},{2,3},{3,2},{4,5},{5,4},{6,7},{7,6},{8,9},{9,8},{10,11... | collective-permute-start | bytes 4128776 | tf_op jit(solution)/shard_map/ppermute | solution.py:387
  153.7 9.2 %copy-start.41 = (f32[336,512]{1,0:T(8,128)}, f32[336,512]{1,0:T(8,128)S(1)}, u32[]{:S(2)}) copy-start(f32[336,512]{1,0:T(8,128)S(1)} %get-tuple-element.93) | copy-start | bytes 2064388
  165.5 13.3 %collective-permute-start.20 = (bf16[512,512]{1,0:T(8,128)(2,1)}, bf16[512,512]{1,0:T(8,128)(2,1)S(1)}, u32[]{:S(2)}, u32[]{:S(2)}) collective-permute-start(bf16[512,512]{1,0:T(8,128)(2,1)} %get-tuple-element.105), channel_id=1, source_target_pairs={{0,4},{2,6},{4,0},{6,2},{8,12},{10,14},{12,8},{14,10},{16,20},{18,... | collective-permute-start | bytes 1572872 | tf_op jit(solution)/shard_map/ppermute | solution.py:422
  166.7 14.5 %collective-permute-start.24 = (bf16[336,512]{1,0:T(8,128)(2,1)}, bf16[336,512]{1,0:T(8,128)(2,1)S(1)}, u32[]{:S(2)}, u32[]{:S(2)}) collective-permute-start(bf16[336,512]{1,0:T(8,128)(2,1)} %get-tuple-element.107), channel_id=1, source_target_pairs={{0,8},{2,10},{4,12},{6,14},{8,16},{10,18},{12,20},{14,22},{16,24},... | collective-permute-start | bytes 1032200 | tf_op jit(solution)/shard_map/ppermute | solution.py:583
  168.0 29.2 %collective-permute-start.25 = (bf16[336,512]{1,0:T(8,128)(2,1)}, bf16[336,512]{1,0:T(8,128)(2,1)}, u32[]{:S(2)}, u32[]{:S(2)}) collective-permute-start(bf16[336,512]{1,0:T(8,128)(2,1)} %get-tuple-element.108), channel_id=1, source_target_pairs={{0,16},{2,18},{4,20},{6,22},{8,24},{10,26},{12,28},{14,30},{16,0},... | collective-permute-start | bytes 1032200 | tf_op jit(solution)/shard_map/ppermute | solution.py:583
  169.0 31.0 %collective-permute-start.26 = (bf16[336,512]{1,0:T(8,128)(2,1)S(1)}, bf16[336,512]{1,0:T(8,128)(2,1)}, u32[]{:S(2)}, u32[]{:S(2)}) collective-permute-start(bf16[336,512]{1,0:T(8,128)(2,1)S(1)} %get-tuple-element.109), channel_id=1, source_target_pairs={{0,24},{2,26},{4,28},{6,30},{8,0},{10,2},{12,4},{14,6},{16,8},{18,... | collective-permute-start | bytes 1032200 | tf_op jit(solution)/shard_map/ppermute | solution.py:583
  170.5 31.8 %copy-start.54 = (bf16[256,5376]{1,0:T(8,128)(2,1)S(1)}, bf16[256,5376]{1,0:T(8,128)(2,1)}, u32[]{:S(2)}) copy-start(bf16[256,5376]{1,0:T(8,128)(2,1)} %get-tuple-element.106) | copy-start | bytes 8257540
  178.7 33.3 %collective-permute-start.19 = (bf16[2,256,1024]{2,1,0:T(8,128)(2,1)}, bf16[2,256,1024]{2,1,0:T(8,128)(2,1)S(1)}, u32[]{:S(2)}, u32[]{:S(2)}) collective-permute-start(bf16[2,256,1024]{2,1,0:T(8,128)(2,1)} %copy-done.38), channel_id=1, source_target_pairs={{0,2},{2,0},{4,6},{6,4},{8,10},{10,8},{12,14},{14,12},{16,18},{18,... | collective-permute-start | bytes 3145736 | tf_op jit(solution)/shard_map/ppermute | solution.py:382
  181.2 29.9 %collective-permute-start.21 = (bf16[512,512]{1,0:T(8,128)(2,1)S(1)}, bf16[512,512]{1,0:T(8,128)(2,1)S(1)}, u32[]{:S(2)}, u32[]{:S(2)}) collective-permute-start(bf16[512,512]{1,0:T(8,128)(2,1)S(1)} %fusion.5), channel_id=1, source_target_pairs={{8,0},{10,2},{12,4},{14,6},{16,8},{18,10},{20,12},{22,14},{24,16},... | collective-permute-start | bytes 1572872 | tf_op jit(solution)/shard_map/ppermute | solution.py:378
  201.5 9.6 %copy-start.30 = (bf16[512,512]{1,0:T(8,128)(2,1)S(1)}, bf16[512,512]{1,0:T(8,128)(2,1)}, u32[]{:S(2)}) copy-start(bf16[512,512]{1,0:T(8,128)(2,1)} %copy-done.29) | copy-start | bytes 1572868
  201.6 2.3 %collective-permute-start.27 = (f32[168,512]{1,0:T(8,128)S(1)}, f32[168,512]{1,0:T(8,128)S(1)}, u32[]{:S(2)}, u32[]{:S(2)}) collective-permute-start(f32[168,512]{1,0:T(8,128)S(1)} %get-tuple-element.117), channel_id=1, source_target_pairs={{0,2},{2,0},{4,6},{6,4},{8,10},{10,8},{12,14},{14,12},{16,18},{18,... | collective-permute-start | bytes 1032200 | tf_op jit(solution)/shard_map/ppermute | solution.py:382
  203.8 8.3 %copy-start.55 = (bf16[1,256,5376]{2,1,0:T(8,128)(2,1)}, bf16[1,256,5376]{2,1,0:T(8,128)(2,1)S(1)}, u32[]{:S(2)}) copy-start(bf16[1,256,5376]{2,1,0:T(8,128)(2,1)S(1)} %bitcast_dynamic-update-slice_fusion) | copy-start | bytes 8257540
  203.8 8.3 %copy-start.48 = (bf16[256,2048]{1,0:T(8,128)(2,1)S(1)}, bf16[256,2048]{1,0:T(8,128)(2,1)}, u32[]{:S(2)}) copy-start(bf16[256,2048]{1,0:T(8,128)(2,1)} %get-tuple-element.100) | copy-start | bytes 3145732
  203.8 8.3 %copy-start.50 = (bf16[256,2048]{1,0:T(8,128)(2,1)S(1)}, bf16[256,2048]{1,0:T(8,128)(2,1)}, u32[]{:S(2)}) copy-start(bf16[256,2048]{1,0:T(8,128)(2,1)} %get-tuple-element.102) | copy-start | bytes 3145732
  203.9 8.3 %copy-start.52 = (f32[168,1024]{1,0:T(8,128)}, f32[168,1024]{1,0:T(8,128)S(1)}, u32[]{:S(2)}) copy-start(f32[168,1024]{1,0:T(8,128)S(1)} %constant_dynamic-update-slice_fusion) | copy-start | bytes 2064388
  211.4 1.7 collective-permute-start.22
  (38 other events, 100.0 us)

commit v2 on v1

--- a/solution.py
+++ b/solution.py
@@ -193,33 +193,28 @@
     )(core, low, q, q_other, do, q_other, *keys)
 
 
-def run_grads(core, e, inv, do_t, q, q_other, keys, values, rows, width, head_range, earlier):
+def run_grads(core, e, inv, do_t, q, q_other, keys, values, rows, width, low, high):
     blk, heads, span, lanes, _, _ = specs_of(rows, width)
     n_arr = len(keys)
-    low, high = head_range
-    full = jax.ShapeDtypeStruct(q.shape, BF16)
+    count = high - low
     head = pl.BlockSpec((rows, HD), lambda g, c: (0, low + g))
-    own = pl.BlockSpec((blk, GROUP * HD), lambda g, c: (0, c[0] * heads + low + g))
-    n_in = 5 + 2 * n_arr
-
-    def kernel(*refs):
-        grads_kernel(blk, n_arr - 1, *refs[: 1 + n_in], *refs[1 + n_in + len(earlier) :])
-
+    head_out = pl.BlockSpec((rows, HD), lambda g, c: (0, g))
+    group_out = pl.BlockSpec((blk, GROUP * HD), lambda g, c: (0, g))
     return pl.pallas_call(
-        kernel,
+        functools.partial(grads_kernel, blk, n_arr - 1),
         grid_spec=pltpu.PrefetchScalarGridSpec(
             num_scalar_prefetch=1,
-            grid=(high - low,),
+            grid=(count,),
             in_specs=[
                 pl.BlockSpec((1, 2, span, lanes), lambda g, c: (low + g, 0, 0, 0)),
                 pl.BlockSpec((1, 2, 1, lanes), lambda g, c: (low + g, 0, 0, 0)),
                 pl.BlockSpec((1, 2, HD, lanes), lambda g, c: (low + g, 0, 0, 0)),
-                own,
+                pl.BlockSpec((blk, GROUP * HD), lambda g, c: (0, c[0] * heads + low + g)),
                 pl.BlockSpec((blk, GROUP * HD), lambda g, c: (0, low + g)),
             ]
-            + [head] * (2 * n_arr)
-            + [pl.BlockSpec(memory_space=pl.ANY)] * len(earlier),
-            out_specs=[own, own, pl.BlockSpec((2, blk, GROUP * HD), lambda g, c: (0, 0, low + g))] + [head] * n_arr,
+            + [head] * (2 * n_arr),
+            out_specs=[group_out, group_out, pl.BlockSpec((2, blk, GROUP * HD), lambda g, c: (0, 0, g))]
+            + [head_out] * n_arr,
             scratch_shapes=[
                 pltpu.VMEM((WINDOW + rows, HD), F32),
                 pltpu.VMEM((2, blk, GROUP * HD), BF16),
@@ -227,13 +222,13 @@
                 pltpu.VMEM((2, blk, GROUP * HD), BF16),
             ],
         ),
-        out_shape=[full, full, jax.ShapeDtypeStruct((2, blk, GROUP * width), BF16)]
-        + [jax.ShapeDtypeStruct((rows, width), BF16)] * n_arr,
-        input_output_aliases={1 + n_in + i: i for i in range(len(earlier))},
+        out_shape=[jax.ShapeDtypeStruct((blk, GROUP * HD * count), BF16)] * 2
+        + [jax.ShapeDtypeStruct((2, blk, GROUP * HD * count), BF16)]
+        + [jax.ShapeDtypeStruct((rows, HD * count), BF16)] * n_arr,
         compiler_params=pltpu.CompilerParams(vmem_limit_bytes=40 * 1024 * 1024),
         cost_estimate=small_cost(),
         name="grads",
-    )(core, e, inv, do_t, q, q_other, *keys, *values, *earlier)
+    )(core, e, inv, do_t, q, q_other, *keys, *values)
 
 
 def small_cost():
@@ -304,40 +299,50 @@
     )(at, x, w)
 
 
-def weight_kernel(n_z, at_ref, *refs):
-    n = (len(refs) - 1 - n_z) // 2
-    mine, theirs = refs[:n], refs[n]
-    dv_refs = refs[n + 1 : 2 * n + 1]
-    outs = refs[2 * n + 1 :]
-    core, my_z = at_ref[0], at_ref[1]
-    count = mine[0].shape[0] // n_z
-    rows = mine[0].shape[1]
+def weight_kernel(n_z, n, at_ref, *refs):
+    own_pairs, other_pairs = refs[:n], refs[n : 2 * n]
+    dv_refs = refs[2 * n : 4 * n]
+    outs = refs[4 * n :]
+    core = at_ref[0]
+    step = pl.program_id(0)
+    rows = own_pairs[0].shape[1] // 2
+    own = pl.ds(pl.multiple_of(core * rows, rows), rows)
+    other = pl.ds(pl.multiple_of((1 - core) * rows, rows), rows)
+    total = None
+    for p in range(n):
+        for flip in range(2):
+            window = slice(flip * rows, (flip + 1) * rows)
+            term = dot(own_pairs[p][:, window], dv_refs[2 * p + flip][own, :])
+            term = term + dot(other_pairs[p][:, window], dv_refs[2 * p + flip][other, :])
+            total = term if total is None else total + term
     for d, out in enumerate(outs):
-        z = lax.rem(my_z + d, n_z)
-        at = pl.ds(pl.multiple_of(z * count, 16), count)
-        total = None
-        for p in range(n):
-            own = pl.ds(pl.multiple_of(core * rows, rows), rows)
-            other = pl.ds(pl.multiple_of((1 - core) * rows, rows), rows)
-            term = dot(mine[p][at, :], dv_refs[p][own, :])
-            term = term + dot(theirs[at, p * rows : (p + 1) * rows], dv_refs[p][other, :])
-            total = term if total is None else total + term
-        out[...] = total.astype(out.dtype)
-
-
-def run_weight(at, mine, theirs, dv_places, n_z):
-    count = theirs.shape[0] // n_z
-    width = dv_places[0].shape[1]
+
+        @pl.when(step == (n_z - 1 if d == 0 else d - 1))
+        def _():
+            out[...] = total.astype(out.dtype)
+
+
+def run_weight(at, own_pairs, other_pairs, dv_pairs, n_z):
+    n = len(own_pairs)
+    count = own_pairs[0].shape[0] // n_z
+    rows2 = own_pairs[0].shape[1]
+    dvs = [x for pair_of in dv_pairs for x in pair_of]
+    width = dvs[0].shape[1]
     shapes = [jax.ShapeDtypeStruct((count, width), F32 if d == 0 else BF16) for d in range(n_z)]
+    pair_block = pl.BlockSpec((count, rows2), lambda d, at: (lax.rem(at[1] + d + 1, n_z), 0))
     return pl.pallas_call(
-        functools.partial(weight_kernel, n_z),
-        in_specs=[pl.BlockSpec(memory_space=pltpu.SMEM)] + [whole()] * (2 * len(mine) + 1),
-        out_specs=[whole()] * n_z,
+        functools.partial(weight_kernel, n_z, n),
+        grid_spec=pltpu.PrefetchScalarGridSpec(
+            num_scalar_prefetch=1,
+            grid=(n_z,),
+            in_specs=[pair_block] * (2 * n) + [pl.BlockSpec(dvs[0].shape, lambda d, at: (0, 0))] * (2 * n),
+            out_specs=[pl.BlockSpec((count, width), lambda d, at: (0, 0))] * n_z,
+        ),
         out_shape=shapes,
         compiler_params=pltpu.CompilerParams(vmem_limit_bytes=40 * 1024 * 1024),
         cost_estimate=small_cost(),
         name="weight",
-    )(at, *mine, theirs, *dv_places)
+    )(at, *own_pairs, *other_pairs, *dvs)
 
 
 def tokens_kernel(n_fsdp, at_ref, dv_ref, w_ref, own_ref, *others):
@@ -454,18 +459,18 @@
     out_rows = model // (n_ctx * n_fsdp)
     places = [(flip, s) for flip in range(2) for s in range(n_fsdp)]
 
+    slabs = [cols(tokens, (my_fsdp + s) % n_fsdp, slab) for s in range(1, n_fsdp)]
+    sent = [rotated(x, s + 1) for s, x in enumerate(slabs)]
+
     own_tags = segments[0].astype(BF16)
     tag_row = lax.dynamic_update_slice_in_dim(jnp.zeros((half_kv,), BF16), own_tags, core * shard_rows, 0)
     tag_rows = jnp.concatenate([tag_row[None], jnp.zeros((15, half_kv), BF16)], 0)
     k_sent = jnp.concatenate([cols(key_heads[0], 1 - core, half_kv), tag_rows], 0)
-    got = swapped(k_sent)
-
-    slabs = [after(cols(tokens, (my_fsdp + s) % n_fsdp, slab), k_sent) for s in range(1, n_fsdp)]
-    sent = [rotated(x, s + 1) for s, x in enumerate(slabs)]
+    got = swapped(after(k_sent, *slabs))
 
     if out_rows % 8 == 0:
         at = jnp.stack([my_y, my_fsdp]).astype(jnp.int32)
-        pieces = run_pieces(after(at, *slabs), tokens, n_z, n_fsdp, out_rows)
+        pieces = run_pieces(after(at, k_sent), tokens, n_z, n_fsdp, out_rows)
     else:
         turned = tokens.T.reshape(n_z, 2, 2, n_fsdp, out_rows, shard_rows)
         pieces = []
@@ -523,10 +528,11 @@
     over_y[0] = flipped(after(by_place[1, 0], k_near))
     v_own, over_y[0] = lax.optimization_barrier((v_own, over_y[0]))
     v_far = shifted(v_own, 4)
-    over_fsdp = {}
+    own_pairs = [jnp.concatenate([by_place[0, 0], over_y[0]], 1)]
+    other_pairs = [swapped(after(own_pairs[0], v_own))]
     for s in range(1, n_fsdp):
         both = jnp.concatenate([by_place[0, s], over_y[s]], 1)
-        over_fsdp[s] = rotated(after(both, own_values), s)
+        own_pairs.append(rotated(after(both, own_values), s))
 
     dv_got = after(dv_got, v_own)
     dv_back = shifted(relayed(my_y, dv_far, dv_got), -4)
@@ -534,25 +540,23 @@
     v_near = flipped(v_sent)
     vals = [v_far, v_near, v_own]
     dv_chip = gathered_terms(my_y, dv_mine, dv_got, after(dv_back, v_sent))
-    dv_places = [moved(dv_chip, flip, s) if flip or s else dv_chip for flip, s in places]
-
+    dv_fsdp = [dv_chip] + [rotated(dv_chip, s) for s in range(1, n_fsdp)]
+    dv_over_y = [flipped(dv_chip)]
     n_heads = half_kv // HD
     grad_args = (e, inv, do_t, queries[0], q_other, keys, vals, chip_rows, half_kv)
-    early = run_grads(core_arg, *grad_args, (0, n_heads // 2), ())
-
-    over_fsdp, dv_places, _ = lax.optimization_barrier((over_fsdp, dv_places, early[0]))
-    arrived = {(0, 0): by_place[0, 0], (1, 0): over_y[0]}
-    for s in range(1, n_fsdp):
-        arrived[0, s] = over_fsdp[s][:, :shard_rows]
-        arrived[1, s] = over_fsdp[s][:, shard_rows:]
-    pieces = [arrived[place] for place in places]
-    theirs = swapped(jnp.concatenate(pieces, 1))
-
-    dv_fsdp = dv_places[:n_fsdp]
+    early = run_grads(after(core_arg, *own_pairs), *grad_args, 0, n_heads // 2)
+    dv_fsdp[1:], dv_over_y[0], _ = lax.optimization_barrier((dv_fsdp[1:], dv_over_y[0], early[0]))
+    dv_over_y += [flipped(x) for x in dv_fsdp[1:]]
+    core_late = after(core_arg, dv_over_y[0], *dv_fsdp)
+    late = run_grads(core_late, *grad_args, n_heads // 2, n_heads)
+    dk_got = [flipped(early[4]), flipped(late[4])]
+
     dv_other = swapped(jnp.concatenate([rows_of(x, 1 - core, shard_rows) for x in dv_fsdp], 0))
     dv_rows = placed(
         core, jnp.concatenate([rows_of(x, core, shard_rows) for x in dv_fsdp], 0), dv_other, 1
     )
+    other_pairs += [swapped(after(x, early[0])) for x in own_pairs[1:]]
+    dv_rows, dv_over_y, _ = lax.optimization_barrier((dv_rows, dv_over_y, late[0]))
     if aligned:
         d_tokens, *made = run_tokens(fsdp_arg, dv_rows, w_value, n_fsdp)
     else:
@@ -564,16 +568,17 @@
         back = rotated(made[s - 1], -s)
         d_tokens = lax.dynamic_update_slice_in_dim(d_tokens, back, ((my_fsdp + s) % n_fsdp) * slab, 1)
 
+    dv_pairs = list(zip(dv_fsdp, dv_over_y))
     if out_rows % 8 == 0:
         at = after(jnp.stack([core, my_z]).astype(jnp.int32), *made)
-        by_z = run_weight(at, pieces, theirs, dv_places, n_z)
+        by_z = run_weight(at, own_pairs, other_pairs, dv_pairs, n_z)
     else:
-        weight_term = None
-        for at, dv_of in enumerate(dv_places):
-            window = slice(at * shard_rows, (at + 1) * shard_rows)
-            term = dot(pieces[at], rows_of(dv_of, core, shard_rows))
-            term = term + dot(theirs[:, window], rows_of(dv_of, 1 - core, shard_rows))
-            weight_term = term if weight_term is None else weight_term + term
+        weight_term = 0.0
+        for p in range(n_fsdp):
+            for flip in range(2):
+                window = slice(flip * shard_rows, (flip + 1) * shard_rows)
+                weight_term += dot(own_pairs[p][:, window], rows_of(dv_pairs[p][flip], core, shard_rows))
+                weight_term += dot(other_pairs[p][:, window], rows_of(dv_pairs[p][flip], 1 - core, shard_rows))
         weight_term = weight_term.reshape(n_z, 2 * out_rows, half_kv)
         by_z = [
             lax.dynamic_index_in_dim(weight_term, (my_z + d) % n_z, 0, keepdims=False).astype(BF16 if d else F32)
@@ -583,9 +588,8 @@
         lax.ppermute(by_z[d], "ctx", [(i, (i + 4 * d) % n_ctx) for i in range(n_ctx)]) for d in range(1, n_z)
     ]
 
-    core_late = after(core_arg, by_z[0])
-    out, dq, other, dk_far, dk_near, dk_mine = run_grads(core_late, *grad_args, (n_heads // 2, n_heads), early)
-    dk_got = flipped(dk_near)
+    *dk_got, _ = lax.optimization_barrier((*dk_got, by_z[0]))
+    dk_got, dk_far, dk_mine = [jnp.concatenate(x, 1) for x in (dk_got, (early[3], late[3]), (early[5], late[5]))]
     dk_sent = relayed(my_y, dk_far, dk_got)
     dk_back = shifted(dk_sent, -4)
 
@@ -597,9 +601,11 @@
 
     dk_chip = gathered_terms(my_y, dk_mine, dk_got, dk_back)
     d_keys = placed(core, rows_of(dk_chip, core, shard_rows), swapped(rows_of(dk_chip, 1 - core, shard_rows)), 1)
+    early, late, _ = lax.optimization_barrier((early, late, made))
+    out, dq, other = [jnp.concatenate((early[i], late[i]), early[i].ndim - 1) for i in range(3)]
     other = swapped(other)
-    out = lax.dynamic_update_slice_in_dim(out, other[0], (1 - core) * half_q, 1)
-    dq = lax.dynamic_update_slice_in_dim(dq, other[1], (1 - core) * half_q, 1)
+    out = placed(core, out, other[0], 1)
+    dq = placed(core, dq, other[1], 1)
     return (out[None], dq[None], d_keys[None], d_tokens[None], d_weight)
 
 

time: 215 us -> 215 us (level)
  starting transfers between devices: 34.2 us -> 42.3 us
  local copies, waits for them, and re-layouts: 31.5 us -> 24.3 us
    ppermute x4 -> x5, waiting for transfers between devices: 10.7 us -> 24.5 us  [rotated(): lax.ppermute(x, 'fsdp', [(i, (i + by) % length) for i in range(length)])]
    ppermute x3 -> x0, waiting for transfers between devices: 12.9 us -> none  [moved(): return lax.ppermute(x, ('ctx', 'fsdp'), pairs)]
    unnamed x116 -> x101, local copies, waits for them, and re-layouts: 21.7 us -> 12 us
    ppermute x3, waiting for transfers between devices: 16.9 us -> 24.8 us  [shards(): lax.ppermute(by_z[d], 'ctx', [(i, (i + 4 * d) % n_ctx) for i in range(n_c...]
    ppermute x8 -> x9, starting transfers between devices: 7.74 us -> 13.5 us  [swapped(): lax.ppermute(x, 'ctx', [(i, i ^ 1) for i in range(lax.axis_size('ctx'))])]
    ppermute x6 -> x9, waiting for transfers between devices: 16.5 us -> 10.7 us  [flipped(): lax.ppermute(x, 'ctx', [(i, i ^ 2) for i in range(lax.axis_size('ctx'))])]
    ppermute x8 -> x9, waiting for transfers between devices: 5.99 us -> 2.31 us  [swapped(): lax.ppermute(x, 'ctx', [(i, i ^ 1) for i in range(lax.axis_size('ctx'))])]
    ppermute x6 -> x9, starting transfers between devices: 6.18 us -> 9.16 us  [flipped(): lax.ppermute(x, 'ctx', [(i, i ^ 2) for i in range(lax.axis_size('ctx'))])]
  transfers between devices with their start and end apart: 28 -> 30, of which waited for: 14 -> 14; matrix products, arithmetic and copies ran while one was open for 7% -> 8% of each run, Pallas kernels for 24% -> 23%
where the time goes in v2:
time: 215 us; the launch traced here: 214 us
  waiting for transfers between devices  85.3 us (40%)
  Pallas kernels  50.1 us (23%)
  starting transfers between devices  42.3 us (20%)
  local copies, waits for them, and re-layouts  24.3 us (11%)
  other arithmetic  10.6 us (5%)
    ppermute x3, waiting for transfers between devices, shards(): lax.ppermute(by_z[d], 'ctx', [(i, (i + 4 * d) % n_ctx) for i in range(n_c...  24.8 us
    ppermute x5, waiting for transfers between devices, rotated(): lax.ppermute(x, 'fsdp', [(i, (i + by) % length) for i in range(length)])  24.5 us
    ppermute x4, waiting for transfers between devices, shifted(): lax.ppermute(x, 'ctx', [(i, i + by) for i in range(length) if 0 <= i + by...  23 us
    pallas_call x2, Pallas kernels, run_grads(): pl.pallas_call(functools.partial(grads_kernel, blk, n_arr - 1), grid_spec...  16.8 us
    pallas_call x1, Pallas kernels, run_probs(): pl.pallas_call(functools.partial(probs_kernel, blk, n_arr - 1), grid_spec...  14.1 us
    ppermute x9, starting transfers between devices, swapped(): lax.ppermute(x, 'ctx', [(i, i ^ 1) for i in range(lax.axis_size('ctx'))])  13.5 us
    unnamed x101, local copies, waits for them, and re-layouts  12 us
    ppermute x4, starting transfers between devices, shifted(): lax.ppermute(x, 'ctx', [(i, i + by) for i in range(length) if 0 <= i + by...  11.8 us
  transfers between devices with their start and end apart: 30, of which 14 were waited for; matrix products, arithmetic and copies ran while one was open for 8% of the time, Pallas kernels for 23%

profile of v2, /device:TPU:9, one launch (start us, length us, event | category | flops | bytes accessed | tf_op | source)
XLA Modules:
  0.0 214.1 jit_solution(2913866537891774462)
XLA Ops:
  0.8 2.7 %dynamic-slice_bitcast_fusion = bf16[256,2688]{1,0:T(8,128)(2,1)} fusion(bf16[1,256,5376]{2,1,0:T(8,128)(2,1)} %param.6, s32[]{:T(128)S(6)} %select_n.107), kind=kLoop, calls=%fused_computation.3 | loop fusion | bytes 2752516 | tf_op jit(solution)/shard_map/dynamic_slice | solution.py:414
  3.5 1.1 dynamic-slice_bitcast_fusion.3
  6.1 2.6 %pieces.1 = (bf16[1344,256]{1,0:T(8,128)(2,1)S(1)}, bf16[1344,256]{1,0:T(8,128)(2,1)S(1)}, bf16[1344,256]{1,0:T(8,128)(2,1)}, bf16[1344,256]{1,0:T(8,128)(2,1)}) custom-call(s32[2]{0:T(128)S(1)} %pad_add_fusion.at_ref, bf16[256,5376]{1,0:T(8,128)(2,1)S(1)} %bitcast.31), custom_call_target="tpu_custom_call" | custom-call | flops 1048576 | bytes 4096 | tf_op jit(solution)/shard_map/pieces/pallas_call | solution.py:264
  10.5 1.3 collective-permute-start.4
  11.8 1.2 collective-permute-start
  13.1 3.2 %collective-permute-start.3 = (bf16[528,512]{1,0:T(8,128)(2,1)S(1)}, bf16[528,512]{1,0:T(8,128)(2,1)}, u32[]{:S(2)}, u32[]{:S(2)}) collective-permute-start(bf16[528,512]{1,0:T(8,128)(2,1)S(1)} %pad_maximum_fusion.4.refs_2_), channel_id=1, source_target_pairs={{0,8},{2,10},{4,12},{6,14},{8,16},{10,18},{12,20},{14,22},{16,24},... | collective-permute-start | bytes 1622024 | tf_op jit(solution)/shard_map/ppermute | solution.py:383
  16.3 1.3 dynamic-slice_bitcast_fusion.1
  18.6 2.6 %copy-done = bf16[2688,1024]{1,0:T(8,128)(2,1)S(1)} copy-done((bf16[2688,1024]{1,0:T(8,128)(2,1)S(1)}, bf16[2688,1024]{1,0:T(8,128)(2,1)}, u32[]{:S(2)}) %copy-start) | copy-done | bytes 5505048
  21.2 2.4 %product.2 = f32[256,1024]{1,0:T(8,128)S(1)} custom-call(s32[1]{0:T(128)} %bitcast.2.at_ref, bf16[256,5376]{1,0:T(8,128)(2,1)S(1)} %bitcast.32, bf16[2688,1024]{1,0:T(8,128)(2,1)S(1)} %copy-done), custom_call_target="tpu_custom_call" | custom-call | flops 1048576 | bytes 4096 | tf_op jit(solution)/shard_map/product/pallas_call | solution.py:284
  23.6 4.7 %collective-permute-done.3.refs_0_ = bf16[528,512]{1,0:T(8,128)(2,1)} collective-permute-done((bf16[528,512]{1,0:T(8,128)(2,1)S(1)}, bf16[528,512]{1,0:T(8,128)(2,1)}, u32[]{:S(2)}, u32[]{:S(2)}) %collective-permute-start.3) | collective-permute-done | bytes 540704 | tf_op jit(solution)/shard_map/ppermute | solution.py:383
  29.2 1.9 collective-permute-start.5
  31.1 1.1 collective-permute-start.6
  33.0 10.7 %collective-permute-done.x_ref = bf16[256,2688]{1,0:T(8,128)(2,1)} collective-permute-done((bf16[256,2688]{1,0:T(8,128)(2,1)}, bf16[256,2688]{1,0:T(8,128)(2,1)}, u32[]{:S(2)}, u32[]{:S(2)}) %collective-permute-start) | collective-permute-done | bytes 1376288 | tf_op jit(solution)/shard_map/ppermute | solution.py:392
  43.6 2.6 %copy-done.1 = bf16[2688,1024]{1,0:T(8,128)(2,1)S(1)} copy-done((bf16[2688,1024]{1,0:T(8,128)(2,1)S(1)}, bf16[2688,1024]{1,0:T(8,128)(2,1)}, u32[]{:S(2)}) %copy-start.1) | copy-done | bytes 5505048
  46.2 3.5 %product.3 = bf16[256,1024]{1,0:T(8,128)(2,1)S(1)} custom-call(s32[1]{0:T(128)} %constant.80.clone.1.at_ref, bf16[256,2688]{1,0:T(8,128)(2,1)} %collective-permute-done.x_ref, bf16[2688,1024]{1,0:T(8,128)(2,1)S(1)} %copy-done.1), custom_call_target="tpu_custom_call" | custom-call | flops 1048576 | bytes 4096 | tf_op jit(solution)/shard_map/product/pallas_call | solution.py:284
  49.7 1.3 collective-permute-start.1
  52.0 14.1 %probs.1 = (bf16[4,2,1280,512]{3,2,1,0:T(8,128)(2,1)}, f32[4,2,1,512]{3,2,1,0:T(1,128)S(1)}, bf16[4,2,128,512]{3,2,1,0:T(8,128)(2,1)S(1)}, bf16[512,512]{1,0:T(8...) custom-call(s32[1]{0:T(128)} %bitcast.core_ref, s32[1,512]{1,0:T(1,128)S(1)} %add_maximum_fusion.low_ref, ...), custom_call_target="tpu_custom_call" | custom-call | flops 1048576 | bytes 4096 | tf_op jit(solution)/shard_map/probs/pallas_call | solution.py:157
  67.1 1.2 collective-permute-start.12
  69.2 1.9 collective-permute-start.7
  71.2 1.5 collective-permute-done.7
  73.6 3.2 %collective-permute-start.10 = (bf16[512,512]{1,0:T(8,128)(2,1)S(1)}, bf16[512,512]{1,0:T(8,128)(2,1)S(1)}, u32[]{:S(2)}, u32[]{:S(2)}) collective-permute-start(bf16[512,512]{1,0:T(8,128)(2,1)S(1)} %constant_dynamic-update-slice_fusion.4.refs_5_), channel_id=1, source_target_pairs={{0,8},{2,10},{4,12},{6,14},{8,16},{10,18},{12,20},{14,22},{16,24},... | collective-permute-start | bytes 1572872 | tf_op jit(solution)/shard_map/ppermute | solution.py:383
  76.8 2.3 %collective-permute-done.12 = bf16[512,512]{1,0:T(8,128)(2,1)} collective-permute-done((bf16[512,512]{1,0:T(8,128)(2,1)}, bf16[512,512]{1,0:T(8,128)(2,1)}, u32[]{:S(2)}, u32[]{:S(2)}) %collective-permute-start.12) | collective-permute-done | bytes 524320 | tf_op jit(solution)/shard_map/ppermute | solution.py:427
  79.1 1.4 fusion.1
  80.5 2.4 %collective-permute-start.13 = (bf16[512,512]{1,0:T(8,128)(2,1)S(1)}, bf16[512,512]{1,0:T(8,128)(2,1)S(1)}, u32[]{:S(2)}, u32[]{:S(2)}) collective-permute-start(bf16[512,512]{1,0:T(8,128)(2,1)S(1)} %fusion.1), channel_id=1, source_target_pairs={{8,0},{10,2},{12,4},{14,6},{16,8},{18,10},{20,12},{22,14},{24,16},... | collective-permute-start | bytes 1572872 | tf_op jit(solution)/shard_map/ppermute | solution.py:383
  82.9 1.2 pad_maximum_fusion
  84.9 3.7 %collective-permute-done.10.refs_3_ = bf16[512,512]{1,0:T(8,128)(2,1)S(1)} collective-permute-done((bf16[512,512]{1,0:T(8,128)(2,1)S(1)}, bf16[512,512]{1,0:T(8,128)(2,1)S(1)}, u32[]{:S(2)}, u32[]{:S(2)}) %collective-permute-start.10) | collective-permute-done | bytes 524320 | tf_op jit(solution)/shard_map/ppermute | solution.py:383
  89.1 4.3 %collective-permute-done.13 = bf16[512,512]{1,0:T(8,128)(2,1)S(1)} collective-permute-done((bf16[512,512]{1,0:T(8,128)(2,1)S(1)}, bf16[512,512]{1,0:T(8,128)(2,1)S(1)}, u32[]{:S(2)}, u32[]{:S(2)}) %collective-permute-start.13) | collective-permute-done | bytes 524320 | tf_op jit(solution)/shard_map/ppermute | solution.py:383
  93.5 1.3 fusion.3.refs_4_
  95.1 1.2 collective-permute-start.15
  97.2 2.0 constant_dynamic-update-slice_fusion.refs_0_
  99.3 13.8 %collective-permute-done.9.refs_1_ = bf16[1344,512]{1,0:T(8,128)(2,1)} collective-permute-done((bf16[1344,512]{1,0:T(8,128)(2,1)S(1)}, bf16[1344,512]{1,0:T(8,128)(2,1)}, u32[]{:S(2)}, u32[]{:S(2)}) %collective-permute-start.9) | collective-permute-done | bytes 1376288 | tf_op jit(solution)/shard_map/ppermute | solution.py:392
  113.1 8.4 %grads.2 = (bf16[256,512]{1,0:T(8,128)(2,1)S(1)}, bf16[256,512]{1,0:T(8,128)(2,1)S(1)}, bf16[2,256,512]{2,1,0:T(8,128)(2,1)S(1)}, bf16[512,256]{1,0:T(8,128)(2,1...) custom-call(s32[1]{0:T(128)} %bitcast.core_ref, bf16[4,2,1280,512]{3,2,1,0:T(8,128)(2,1)} %get-tuple-element.89.e_ref, ...), custom_call_target="tpu_custom_call" | custom-call | flops 1048576 | bytes 4096 | tf_op jit(solution)/shard_map/grads/pallas_call | solution.py:203
  125.2 7.2 %collective-permute-start.16 = (bf16[512,512]{1,0:T(8,128)(2,1)S(1)}, bf16[512,512]{1,0:T(8,128)(2,1)S(1)}, u32[]{:S(2)}, u32[]{:S(2)}) collective-permute-start(bf16[512,512]{1,0:T(8,128)(2,1)S(1)} %pad_maximum_fusion.7), channel_id=1, source_target_pairs={{0,2},{2,0},{4,6},{6,4},{8,10},{10,8},{12,14},{14,12},{16,18},{18,... | collective-permute-start | bytes 1572872 | tf_op jit(solution)/shard_map/ppermute | solution.py:387
  132.4 1.3 collective-permute-start.17
  134.2 8.4 %grads.3 = (bf16[256,512]{1,0:T(8,128)(2,1)S(1)}, bf16[256,512]{1,0:T(8,128)(2,1)S(1)}, bf16[2,256,512]{2,1,0:T(8,128)(2,1)S(1)}, bf16[512,256]{1,0:T(8,128)(2,1...) custom-call(s32[1]{0:T(128)} %bitcast.core_ref, bf16[4,2,1280,512]{3,2,1,0:T(8,128)(2,1)} %get-tuple-element.89.e_ref, ...), custom_call_target="tpu_custom_call" | custom-call | flops 1048576 | bytes 4096 | tf_op jit(solution)/shard_map/grads/pallas_call | solution.py:203
  142.8 3.1 %collective-permute-done.17.refs_7_ = bf16[512,512]{1,0:T(8,128)(2,1)S(1)} collective-permute-done((bf16[512,512]{1,0:T(8,128)(2,1)S(1)}, bf16[512,512]{1,0:T(8,128)(2,1)S(1)}, u32[]{:S(2)}, u32[]{:S(2)}) %collective-permute-start.17) | collective-permute-done | bytes 524320 | tf_op jit(solution)/shard_map/ppermute | solution.py:427
  145.9 4.7 %tokens.1 = (bf16[256,5376]{1,0:T(8,128)(2,1)}, bf16[256,2688]{1,0:T(8,128)(2,1)S(1)}) custom-call(s32[1]{0:T(128)} %bitcast.2.at_ref, bf16[512,1024]{1,0:T(8,128)(2,1)S(1)} %constant_dynamic-update-slice_fusion.3.dv_ref, bf16[2688,1024]{1,0:T(8,128)(2,1)S(1)} %bitcast.30), custom_call_target="tpu_custom_call" | custom-call | flops 1048576 | bytes 4096 | tf_op jit(solution)/shard_map/tokens/pallas_call | solution.py:361
  150.7 1.1 pad_maximum_fusion.2
  153.0 1.3 collective-permute-start.19
  155.4 6.1 %weight.1 = (f32[336,512]{1,0:T(8,128)S(1)}, bf16[336,512]{1,0:T(8,128)(2,1)S(1)}, bf16[336,512]{1,0:T(8,128)(2,1)S(1)}, bf16[336,512]{1,0:T(8,128)(2,1)S(1)}) custom-call(s32[2]{0:T(128)S(1)} %pad_add_fusion.1.at_ref, bf16[1344,512]{1,0:T(8,128)(2,1)} %constant_dynamic-update-slice_fusion.refs_0_, bf16[1344,512]{1,0:T(8,128)(2,1)} %collective-permute-done.9.refs_1_, ...), custom_call_target="tpu_custom_call" | custom-call | flops 1048576 | bytes 4096 | tf_op jit(solution)/shard_map/weight/pallas_call | solution.py:333
  161.4 5.3 %collective-permute-done.20 = bf16[512,256]{1,0:T(8,128)(2,1)S(1)} collective-permute-done((bf16[512,256]{1,0:T(8,128)(2,1)}, bf16[512,256]{1,0:T(8,128)(2,1)S(1)}, u32[]{:S(2)}, u32[]{:S(2)}) %collective-permute-start.20) | collective-permute-done | bytes 262176 | tf_op jit(solution)/shard_map/ppermute | solution.py:427
  166.7 1.3 collective-permute-start.26
  169.1 1.5 collective-permute-start.28
  170.7 3.0 %collective-permute-start.23 = (bf16[512,512]{1,0:T(8,128)(2,1)S(1)}, bf16[512,512]{1,0:T(8,128)(2,1)S(1)}, u32[]{:S(2)}, u32[]{:S(2)}) collective-permute-start(bf16[512,512]{1,0:T(8,128)(2,1)S(1)} %fusion.5), channel_id=1, source_target_pairs={{8,0},{10,2},{12,4},{14,6},{16,8},{18,10},{20,12},{22,14},{24,16},... | collective-permute-start | bytes 1572872 | tf_op jit(solution)/shard_map/ppermute | solution.py:383
  173.7 1.3 slice_dynamic-update-slice_fusion
  175.5 21.2 %collective-permute-done.27 = bf16[336,512]{1,0:T(8,128)(2,1)S(1)} collective-permute-done((bf16[336,512]{1,0:T(8,128)(2,1)S(1)}, bf16[336,512]{1,0:T(8,128)(2,1)S(1)}, u32[]{:S(2)}, u32[]{:S(2)}) %collective-permute-start.27) | collective-permute-done | bytes 344096 | tf_op jit(solution)/shard_map/ppermute | solution.py:588
  196.7 3.1 %collective-permute-done.28 = bf16[336,512]{1,0:T(8,128)(2,1)S(1)} collective-permute-done((bf16[336,512]{1,0:T(8,128)(2,1)S(1)}, bf16[336,512]{1,0:T(8,128)(2,1)S(1)}, u32[]{:S(2)}, u32[]{:S(2)}) %collective-permute-start.28) | collective-permute-done | bytes 344096 | tf_op jit(solution)/shard_map/ppermute | solution.py:588
  200.8 10.2 %collective-permute-done.23 = bf16[512,512]{1,0:T(8,128)(2,1)S(1)} collective-permute-done((bf16[512,512]{1,0:T(8,128)(2,1)S(1)}, bf16[512,512]{1,0:T(8,128)(2,1)S(1)}, u32[]{:S(2)}, u32[]{:S(2)}) %collective-permute-start.23) | collective-permute-done | bytes 524320 | tf_op jit(solution)/shard_map/ppermute | solution.py:383
  (173 shorter events, 24.7 us)
Async XLA Ops:
  5.4 3.4 %collective-permute-start.2 = (bf16[272,512]{1,0:T(8,128)(2,1)}, bf16[272,512]{1,0:T(8,128)(2,1)}, u32[]{:S(2)}, u32[]{:S(2)}) collective-permute-start(bf16[272,512]{1,0:T(8,128)(2,1)} %maximum_maximum_fusion.1), channel_id=1, source_target_pairs={{0,2},{2,0},{4,6},{6,4},{8,10},{10,8},{12,14},{14,12},{16,18},{18,... | collective-permute-start | bytes 835592 | tf_op jit(solution)/shard_map/ppermute | solution.py:387
  10.5 17.8 %collective-permute-start.4 = (bf16[1344,256]{1,0:T(8,128)(2,1)}, bf16[1344,256]{1,0:T(8,128)(2,1)}, u32[]{:S(2)}, u32[]{:S(2)}) collective-permute-start(bf16[1344,256]{1,0:T(8,128)(2,1)} %get-tuple-element.78), channel_id=1, source_target_pairs={{0,4},{2,6},{4,0},{6,2},{8,12},{10,14},{12,8},{14,10},{16,20},{18,... | collective-permute-start | bytes 2064392 | tf_op jit(solution)/shard_map/ppermute | solution.py:427
  11.8 31.8 %collective-permute-start = (bf16[256,2688]{1,0:T(8,128)(2,1)}, bf16[256,2688]{1,0:T(8,128)(2,1)}, u32[]{:S(2)}, u32[]{:S(2)}) collective-permute-start(bf16[256,2688]{1,0:T(8,128)(2,1)} %dynamic-slice_bitcast_fusion), channel_id=1, source_target_pairs={{0,1},{1,0},{2,3},{3,2},{4,5},{5,4},{6,7},{7,6},{8,9},{9,8},{10,11... | collective-permute-start | bytes 4128776 | tf_op jit(solution)/shard_map/ppermute | solution.py:392
  13.1 15.3 %collective-permute-start.3 = (bf16[528,512]{1,0:T(8,128)(2,1)S(1)}, bf16[528,512]{1,0:T(8,128)(2,1)}, u32[]{:S(2)}, u32[]{:S(2)}) collective-permute-start(bf16[528,512]{1,0:T(8,128)(2,1)S(1)} %pad_maximum_fusion.4.refs_2_), channel_id=1, source_target_pairs={{0,8},{2,10},{4,12},{6,14},{8,16},{10,18},{12,20},{14,22},{16,24},... | collective-permute-start | bytes 1622024 | tf_op jit(solution)/shard_map/ppermute | solution.py:383
  29.2 21.8 %collective-permute-start.5 = (bf16[528,512]{1,0:T(8,128)(2,1)}, bf16[528,512]{1,0:T(8,128)(2,1)S(1)}, u32[]{:S(2)}, u32[]{:S(2)}) collective-permute-start(bf16[528,512]{1,0:T(8,128)(2,1)} %broadcast_select_fusion), channel_id=1, source_target_pairs={{0,4},{2,6},{4,0},{6,2},{8,12},{10,14},{12,8},{14,10},{16,20},{18,... | collective-permute-start | bytes 1622024 | tf_op jit(solution)/shard_map/ppermute | solution.py:427
  31.1 20.8 %collective-permute-start.6 = (bf16[256,2048]{1,0:T(8,128)(2,1)}, bf16[256,2048]{1,0:T(8,128)(2,1)S(1)}, u32[]{:S(2)}, u32[]{:S(2)}) collective-permute-start(bf16[256,2048]{1,0:T(8,128)(2,1)} %pad_maximum_fusion.1), channel_id=1, source_target_pairs={{0,2},{2,0},{4,6},{6,4},{8,10},{10,8},{12,14},{14,12},{16,18},{18,... | collective-permute-start | bytes 3145736 | tf_op jit(solution)/shard_map/ppermute | solution.py:387
  49.7 18.6 %collective-permute-start.1 = (bf16[256,1024]{1,0:T(8,128)(2,1)S(1)}, bf16[256,1024]{1,0:T(8,128)(2,1)S(1)}, u32[]{:S(2)}, u32[]{:S(2)}) collective-permute-start(bf16[256,1024]{1,0:T(8,128)(2,1)S(1)} %product.3), channel_id=1, source_target_pairs={{0,1},{1,0},{2,3},{3,2},{4,5},{5,4},{6,7},{7,6},{8,9},{9,8},{10,11... | collective-permute-start | bytes 1572872 | tf_op jit(solution)/shard_map/ppermute | solution.py:392
  51.7 21.9 %collective-permute-start.8 = (bf16[1344,256]{1,0:T(8,128)(2,1)}, bf16[1344,256]{1,0:T(8,128)(2,1)}, u32[]{:S(2)}, u32[]{:S(2)}) collective-permute-start(bf16[1344,256]{1,0:T(8,128)(2,1)} %get-tuple-element.84), channel_id=1, source_target_pairs={{0,4},{2,6},{4,0},{6,2},{8,12},{10,14},{12,8},{14,10},{16,20},{18,... | collective-permute-start | bytes 2064392 | tf_op jit(solution)/shard_map/ppermute | solution.py:427
  52.0 16.3 %copy-start.9 = (f32[256,1024]{1,0:T(8,128)S(1)}, f32[256,1024]{1,0:T(8,128)}, u32[]{:S(2)}) copy-start(f32[256,1024]{1,0:T(8,128)} %copy-done.8) | copy-start | bytes 3145732
  67.1 12.1 %collective-permute-start.12 = (bf16[512,512]{1,0:T(8,128)(2,1)}, bf16[512,512]{1,0:T(8,128)(2,1)}, u32[]{:S(2)}, u32[]{:S(2)}) collective-permute-start(bf16[512,512]{1,0:T(8,128)(2,1)} %get-tuple-element.82), channel_id=1, source_target_pairs={{0,4},{2,6},{4,0},{6,2},{8,12},{10,14},{12,8},{14,10},{16,20},{18,... | collective-permute-start | bytes 1572872 | tf_op jit(solution)/shard_map/ppermute | solution.py:427
  69.2 3.4 %collective-permute-start.7 = (bf16[256,512]{1,0:T(8,128)(2,1)}, bf16[256,512]{1,0:T(8,128)(2,1)}, u32[]{:S(2)}, u32[]{:S(2)}) collective-permute-start(bf16[256,512]{1,0:T(8,128)(2,1)} %get-tuple-element.145), channel_id=1, source_target_pairs={{0,2},{2,0},{4,6},{6,4},{8,10},{10,8},{12,14},{14,12},{16,18},{18,... | collective-permute-start | bytes 786440 | tf_op jit(solution)/shard_map/ppermute | solution.py:387
  71.1 11.8 %copy-start.16 = (bf16[1344,256]{1,0:T(8,128)(2,1)S(1)}, bf16[1344,256]{1,0:T(8,128)(2,1)}, u32[]{:S(2)}) copy-start(bf16[1344,256]{1,0:T(8,128)(2,1)} %copy-done.15) | copy-start | bytes 2064388
  73.6 15.0 %collective-permute-start.10 = (bf16[512,512]{1,0:T(8,128)(2,1)S(1)}, bf16[512,512]{1,0:T(8,128)(2,1)S(1)}, u32[]{:S(2)}, u32[]{:S(2)}) collective-permute-start(bf16[512,512]{1,0:T(8,128)(2,1)S(1)} %constant_dynamic-update-slice_fusion.4.refs_5_), channel_id=1, source_target_pairs={{0,8},{2,10},{4,12},{6,14},{8,16},{10,18},{12,20},{14,22},{16,24},... | collective-permute-start | bytes 1572872 | tf_op jit(solution)/shard_map/ppermute | solution.py:383
  80.5 13.0 %copy-start.18 = (bf16[512,512]{1,0:T(8,128)(2,1)S(1)}, bf16[512,512]{1,0:T(8,128)(2,1)}, u32[]{:S(2)}) copy-start(bf16[512,512]{1,0:T(8,128)(2,1)} %copy-done.17) | copy-start | bytes 1572868
  80.5 13.0 %collective-permute-start.13 = (bf16[512,512]{1,0:T(8,128)(2,1)S(1)}, bf16[512,512]{1,0:T(8,128)(2,1)S(1)}, u32[]{:S(2)}, u32[]{:S(2)}) collective-permute-start(bf16[512,512]{1,0:T(8,128)(2,1)S(1)} %fusion.1), channel_id=1, source_target_pairs={{8,0},{10,2},{12,4},{14,6},{16,8},{18,10},{20,12},{22,14},{24,16},... | collective-permute-start | bytes 1572872 | tf_op jit(solution)/shard_map/ppermute | solution.py:383
  84.1 12.2 %copy-start.14 = (bf16[1344,256]{1,0:T(8,128)(2,1)S(1)}, bf16[1344,256]{1,0:T(8,128)(2,1)}, u32[]{:S(2)}) copy-start(bf16[1344,256]{1,0:T(8,128)(2,1)} %copy-done.13) | copy-start | bytes 2064388
  84.1 29.0 %collective-permute-start.9 = (bf16[1344,512]{1,0:T(8,128)(2,1)S(1)}, bf16[1344,512]{1,0:T(8,128)(2,1)}, u32[]{:S(2)}, u32[]{:S(2)}) collective-permute-start(bf16[1344,512]{1,0:T(8,128)(2,1)S(1)} %pad_maximum_fusion), channel_id=1, source_target_pairs={{0,1},{1,0},{2,3},{3,2},{4,5},{5,4},{6,7},{7,6},{8,9},{9,8},{10,11... | collective-permute-start | bytes 4128776 | tf_op jit(solution)/shard_map/ppermute | solution.py:392
  88.7 24.4 %collective-permute-start.11 = (bf16[512,512]{1,0:T(8,128)(2,1)S(1)}, bf16[512,512]{1,0:T(8,128)(2,1)S(1)}, u32[]{:S(2)}, u32[]{:S(2)}) collective-permute-start(bf16[512,512]{1,0:T(8,128)(2,1)S(1)} %broadcast_select_fusion.1), channel_id=1, source_target_pairs={{0,4},{2,6},{4,0},{6,2},{8,12},{10,14},{12,8},{14,10},{16,20},{18,... | collective-permute-start | bytes 1572872 | tf_op jit(solution)/shard_map/ppermute | solution.py:427
  94.7 26.8 %copy-start.4 = (bf16[512,512]{1,0:T(8,128)(2,1)}, bf16[512,512]{1,0:T(8,128)(2,1)S(1)}, u32[]{:S(2)}) copy-start(bf16[512,512]{1,0:T(8,128)(2,1)S(1)} %fusion.3.refs_4_) | copy-start | bytes 1572868
  94.8 18.4 %copy-start.7 = (bf16[4,2,128,512]{3,2,1,0:T(8,128)(2,1)S(1)}, bf16[4,2,128,512]{3,2,1,0:T(8,128)(2,1)}, u32[]{:S(2)}) copy-start(bf16[4,2,128,512]{3,2,1,0:T(8,128)(2,1)} %copy-done.6) | copy-start | bytes 3145732
  94.8 29.5 %collective-permute-start.14 = (bf16[512,512]{1,0:T(8,128)(2,1)S(1)}, bf16[512,512]{1,0:T(8,128)(2,1)S(1)}, u32[]{:S(2)}, u32[]{:S(2)}) collective-permute-start(bf16[512,512]{1,0:T(8,128)(2,1)S(1)} %fusion.3.refs_4_), channel_id=1, source_target_pairs={{0,1},{1,0},{2,3},{3,2},{4,5},{5,4},{6,7},{7,6},{8,9},{9,8},{10,11... | collective-permute-start | bytes 1572872 | tf_op jit(solution)/shard_map/ppermute | solution.py:392
  95.1 29.2 %collective-permute-start.15 = (bf16[512,512]{1,0:T(8,128)(2,1)S(1)}, bf16[512,512]{1,0:T(8,128)(2,1)S(1)}, u32[]{:S(2)}, u32[]{:S(2)}) collective-permute-start(bf16[512,512]{1,0:T(8,128)(2,1)S(1)} %fusion.3.refs_4_), channel_id=1, source_target_pairs={{0,4},{2,6},{4,0},{6,2},{8,12},{10,14},{12,8},{14,10},{16,20},{18,... | collective-permute-start | bytes 1572872 | tf_op jit(solution)/shard_map/ppermute | solution.py:427
  124.3 18.3 %copy-start.11 = (bf16[512,512]{1,0:T(8,128)(2,1)}, bf16[512,512]{1,0:T(8,128)(2,1)S(1)}, u32[]{:S(2)}) copy-start(bf16[512,512]{1,0:T(8,128)(2,1)S(1)} %collective-permute-done.14.refs_6_) | copy-start | bytes 1572868
  125.2 20.7 %slice-start = ((s8[5505024]{0:T(1024)(128)(4,1)}), s8[4194304]{0:T(1024)(128)(4,1)S(1)}, s32[]{:S(2)}) async-start(s8[5505024]{0:T(1024)(128)(4,1)} %bitcast.29), calls=%async_computation | async-start | bytes 8388608
  125.2 20.7 %slice-start.1 = ((s8[5505024]{0:T(1024)(128)(4,1)}), s8[1310720]{0:T(1024)(128)(4,1)S(1)}, s32[]{:S(2)}) async-start(s8[5505024]{0:T(1024)(128)(4,1)} %bitcast.29), calls=%async_computation.1 | async-start | bytes 2621440
  125.2 17.5 %collective-permute-start.16 = (bf16[512,512]{1,0:T(8,128)(2,1)S(1)}, bf16[512,512]{1,0:T(8,128)(2,1)S(1)}, u32[]{:S(2)}, u32[]{:S(2)}) collective-permute-start(bf16[512,512]{1,0:T(8,128)(2,1)S(1)} %pad_maximum_fusion.7), channel_id=1, source_target_pairs={{0,2},{2,0},{4,6},{6,4},{8,10},{10,8},{12,14},{14,12},{16,18},{18,... | collective-permute-start | bytes 1572872 | tf_op jit(solution)/shard_map/ppermute | solution.py:387
  132.4 13.5 %collective-permute-start.17 = (bf16[512,512]{1,0:T(8,128)(2,1)S(1)}, bf16[512,512]{1,0:T(8,128)(2,1)S(1)}, u32[]{:S(2)}, u32[]{:S(2)}) collective-permute-start(bf16[512,512]{1,0:T(8,128)(2,1)S(1)} %collective-permute-done.14.refs_6_), channel_id=1, source_target_pairs={{0,4},{2,6},{4,0},{6,2},{8,12},{10,14},{12,8},{14,10},{16,20},{18,... | collective-permute-start | bytes 1572872 | tf_op jit(solution)/shard_map/ppermute | solution.py:427
  133.7 21.2 %collective-permute-start.21 = (bf16[1344,512]{1,0:T(8,128)(2,1)}, bf16[1344,512]{1,0:T(8,128)(2,1)}, u32[]{:S(2)}, u32[]{:S(2)}) collective-permute-start(bf16[1344,512]{1,0:T(8,128)(2,1)} %constant_dynamic-update-slice_fusion.refs_0_), channel_id=1, source_target_pairs={{0,2},{2,0},{4,6},{6,4},{8,10},{10,8},{12,14},{14,12},{16,18},{18,... | collective-permute-start | bytes 4128776 | tf_op jit(solution)/shard_map/ppermute | solution.py:387
  134.0 21.3 %collective-permute-start.22 = (bf16[1344,512]{1,0:T(8,128)(2,1)}, bf16[1344,512]{1,0:T(8,128)(2,1)}, u32[]{:S(2)}, u32[]{:S(2)}) collective-permute-start(bf16[1344,512]{1,0:T(8,128)(2,1)} %collective-permute-done.9.refs_1_), channel_id=1, source_target_pairs={{0,2},{2,0},{4,6},{6,4},{8,10},{10,8},{12,14},{14,12},{16,18},{18,... | collective-permute-start | bytes 4128776 | tf_op jit(solution)/shard_map/ppermute | solution.py:387
  142.6 8.0 %copy-start.24 = (bf16[512,256]{1,0:T(8,128)(2,1)}, bf16[512,256]{1,0:T(8,128)(2,1)S(1)}, u32[]{:S(2)}) copy-start(bf16[512,256]{1,0:T(8,128)(2,1)S(1)} %get-tuple-element.111) | copy-start | bytes 786436
  142.6 8.0 %copy-start.28 = (bf16[512,256]{1,0:T(8,128)(2,1)}, bf16[512,256]{1,0:T(8,128)(2,1)S(1)}, u32[]{:S(2)}) copy-start(bf16[512,256]{1,0:T(8,128)(2,1)S(1)} %get-tuple-element.109) | copy-start | bytes 786436
  142.6 8.0 %copy-start.34 = (bf16[256,512]{1,0:T(8,128)(2,1)}, bf16[256,512]{1,0:T(8,128)(2,1)S(1)}, u32[]{:S(2)}) copy-start(bf16[256,512]{1,0:T(8,128)(2,1)S(1)} %get-tuple-element.115) | copy-start | bytes 786436
  152.1 18.7 %collective-permute-start.18 = (bf16[2,256,1024]{2,1,0:T(8,128)(2,1)}, bf16[2,256,1024]{2,1,0:T(8,128)(2,1)}, u32[]{:S(2)}, u32[]{:S(2)}) collective-permute-start(bf16[2,256,1024]{2,1,0:T(8,128)(2,1)} %pad_maximum_fusion.2), channel_id=1, source_target_pairs={{0,2},{2,0},{4,6},{6,4},{8,10},{10,8},{12,14},{14,12},{16,18},{18,... | collective-permute-start | bytes 3145736 | tf_op jit(solution)/shard_map/ppermute | solution.py:387
  153.0 8.4 %collective-permute-start.19 = (bf16[512,256]{1,0:T(8,128)(2,1)}, bf16[512,256]{1,0:T(8,128)(2,1)S(1)}, u32[]{:S(2)}, u32[]{:S(2)}) collective-permute-start(bf16[512,256]{1,0:T(8,128)(2,1)} %copy-done.39), channel_id=1, source_target_pairs={{0,4},{2,6},{4,0},{6,2},{8,12},{10,14},{12,8},{14,10},{16,20},{18,... | collective-permute-start | bytes 786440 | tf_op jit(solution)/shard_map/ppermute | solution.py:427
  154.3 12.4 %collective-permute-start.20 = (bf16[512,256]{1,0:T(8,128)(2,1)}, bf16[512,256]{1,0:T(8,128)(2,1)S(1)}, u32[]{:S(2)}, u32[]{:S(2)}) collective-permute-start(bf16[512,256]{1,0:T(8,128)(2,1)} %copy-done.40), channel_id=1, source_target_pairs={{0,4},{2,6},{4,0},{6,2},{8,12},{10,14},{12,8},{14,10},{16,20},{18,... | collective-permute-start | bytes 786440 | tf_op jit(solution)/shard_map/ppermute | solution.py:427
  154.8 15.7 %copy-start.27 = (bf16[512,256]{1,0:T(8,128)(2,1)S(1)}, bf16[512,256]{1,0:T(8,128)(2,1)}, u32[]{:S(2)}) copy-start(bf16[512,256]{1,0:T(8,128)(2,1)} %copy-done.26) | copy-start | bytes 786436
  154.8 15.7 %copy-start.29 = (bf16[512,256]{1,0:T(8,128)(2,1)S(1)}, bf16[512,256]{1,0:T(8,128)(2,1)}, u32[]{:S(2)}) copy-start(bf16[512,256]{1,0:T(8,128)(2,1)} %copy-done.28) | copy-start | bytes 786436
  154.8 57.1 %collective-permute-start.25 = (bf16[256,2688]{1,0:T(8,128)(2,1)}, bf16[256,2688]{1,0:T(8,128)(2,1)S(1)}, u32[]{:S(2)}, u32[]{:S(2)}) collective-permute-start(bf16[256,2688]{1,0:T(8,128)(2,1)} %copy-done.38), channel_id=1, source_target_pairs={{0,1},{1,0},{2,3},{3,2},{4,5},{5,4},{6,7},{7,6},{8,9},{9,8},{10,11... | collective-permute-start | bytes 4128776 | tf_op jit(solution)/shard_map/ppermute | solution.py:392
  166.7 8.7 %collective-permute-start.26 = (bf16[336,512]{1,0:T(8,128)(2,1)S(1)}, bf16[336,512]{1,0:T(8,128)(2,1)S(1)}, u32[]{:S(2)}, u32[]{:S(2)}) collective-permute-start(bf16[336,512]{1,0:T(8,128)(2,1)S(1)} %get-tuple-element.129), channel_id=1, source_target_pairs={{0,8},{2,10},{4,12},{6,14},{8,16},{10,18},{12,20},{14,22},{16,24},... | collective-permute-start | bytes 1032200 | tf_op jit(solution)/shard_map/ppermute | solution.py:588
  168.0 28.7 %collective-permute-start.27 = (bf16[336,512]{1,0:T(8,128)(2,1)S(1)}, bf16[336,512]{1,0:T(8,128)(2,1)S(1)}, u32[]{:S(2)}, u32[]{:S(2)}) collective-permute-start(bf16[336,512]{1,0:T(8,128)(2,1)S(1)} %get-tuple-element.130), channel_id=1, source_target_pairs={{0,16},{2,18},{4,20},{6,22},{8,24},{10,26},{12,28},{14,30},{16,0},... | collective-permute-start | bytes 1032200 | tf_op jit(solution)/shard_map/ppermute | solution.py:588
  169.1 30.7 %collective-permute-start.28 = (bf16[336,512]{1,0:T(8,128)(2,1)S(1)}, bf16[336,512]{1,0:T(8,128)(2,1)S(1)}, u32[]{:S(2)}, u32[]{:S(2)}) collective-permute-start(bf16[336,512]{1,0:T(8,128)(2,1)S(1)} %get-tuple-element.131), channel_id=1, source_target_pairs={{0,24},{2,26},{4,28},{6,30},{8,0},{10,2},{12,4},{14,6},{16,8},{18,... | collective-permute-start | bytes 1032200 | tf_op jit(solution)/shard_map/ppermute | solution.py:588
  170.7 40.3 %collective-permute-start.23 = (bf16[512,512]{1,0:T(8,128)(2,1)S(1)}, bf16[512,512]{1,0:T(8,128)(2,1)S(1)}, u32[]{:S(2)}, u32[]{:S(2)}) collective-permute-start(bf16[512,512]{1,0:T(8,128)(2,1)S(1)} %fusion.5), channel_id=1, source_target_pairs={{8,0},{10,2},{12,4},{14,6},{16,8},{18,10},{20,12},{22,14},{24,16},... | collective-permute-start | bytes 1572872 | tf_op jit(solution)/shard_map/ppermute | solution.py:383
  175.0 25.8 %copy-start.41 = (bf16[1,256,2048]{2,1,0:T(8,128)(2,1)}, bf16[1,256,2048]{2,1,0:T(8,128)(2,1)S(1)}, u32[]{:S(2)}) copy-start(bf16[1,256,2048]{2,1,0:T(8,128)(2,1)S(1)} %get-tuple-element.135) | copy-start | bytes 3145732
  175.0 25.8 %copy-start.42 = (bf16[1,256,2048]{2,1,0:T(8,128)(2,1)}, bf16[1,256,2048]{2,1,0:T(8,128)(2,1)S(1)}, u32[]{:S(2)}) copy-start(bf16[1,256,2048]{2,1,0:T(8,128)(2,1)S(1)} %get-tuple-element.136) | copy-start | bytes 3145732
  175.0 36.0 %copy-start.25 = (bf16[512,256]{1,0:T(8,128)(2,1)S(1)}, bf16[512,256]{1,0:T(8,128)(2,1)}, u32[]{:S(2)}) copy-start(bf16[512,256]{1,0:T(8,128)(2,1)} %copy-done.24) | copy-start | bytes 786436
  200.0 12.1 %collective-permute-start.29 = (f32[168,512]{1,0:T(8,128)S(1)}, f32[168,512]{1,0:T(8,128)S(1)}, u32[]{:S(2)}, u32[]{:S(2)}) collective-permute-start(f32[168,512]{1,0:T(8,128)S(1)} %get-tuple-element.137), channel_id=1, source_target_pairs={{0,2},{2,0},{4,6},{6,4},{8,10},{10,8},{12,14},{14,12},{16,18},{18,... | collective-permute-start | bytes 1032200 | tf_op jit(solution)/shard_map/ppermute | solution.py:387
  200.8 11.1 %copy-start.46 = (bf16[256,5376]{1,0:T(8,128)(2,1)S(1)}, bf16[256,5376]{1,0:T(8,128)(2,1)}, u32[]{:S(2)}) copy-start(bf16[256,5376]{1,0:T(8,128)(2,1)} %get-tuple-element.128) | copy-start | bytes 8257540
  211.3 1.7 collective-permute-start.24
  (32 other events, 101.3 us)

commit v3 on v2

--- a/solution.py
+++ b/solution.py
@@ -193,28 +193,24 @@
     )(core, low, q, q_other, do, q_other, *keys)
 
 
-def run_grads(core, e, inv, do_t, q, q_other, keys, values, rows, width, low, high):
-    blk, heads, span, lanes, _, _ = specs_of(rows, width)
+def run_grads(core, e, inv, do_t, q, q_other, keys, values, rows, width):
+    blk, heads, span, lanes, head, own = specs_of(rows, width)
     n_arr = len(keys)
-    count = high - low
-    head = pl.BlockSpec((rows, HD), lambda g, c: (0, low + g))
-    head_out = pl.BlockSpec((rows, HD), lambda g, c: (0, g))
-    group_out = pl.BlockSpec((blk, GROUP * HD), lambda g, c: (0, g))
+    full = jax.ShapeDtypeStruct(q.shape, BF16)
     return pl.pallas_call(
         functools.partial(grads_kernel, blk, n_arr - 1),
         grid_spec=pltpu.PrefetchScalarGridSpec(
             num_scalar_prefetch=1,
-            grid=(count,),
+            grid=(heads,),
             in_specs=[
-                pl.BlockSpec((1, 2, span, lanes), lambda g, c: (low + g, 0, 0, 0)),
-                pl.BlockSpec((1, 2, 1, lanes), lambda g, c: (low + g, 0, 0, 0)),
-                pl.BlockSpec((1, 2, HD, lanes), lambda g, c: (low + g, 0, 0, 0)),
-                pl.BlockSpec((blk, GROUP * HD), lambda g, c: (0, c[0] * heads + low + g)),
-                pl.BlockSpec((blk, GROUP * HD), lambda g, c: (0, low + g)),
+                pl.BlockSpec((1, 2, span, lanes), lambda g, c: (g, 0, 0, 0)),
+                pl.BlockSpec((1, 2, 1, lanes), lambda g, c: (g, 0, 0, 0)),
+                pl.BlockSpec((1, 2, HD, lanes), lambda g, c: (g, 0, 0, 0)),
+                own,
+                pl.BlockSpec((blk, GROUP * HD), lambda g, c: (0, g)),
             ]
             + [head] * (2 * n_arr),
-            out_specs=[group_out, group_out, pl.BlockSpec((2, blk, GROUP * HD), lambda g, c: (0, 0, g))]
-            + [head_out] * n_arr,
+            out_specs=[own, own, pl.BlockSpec((2, blk, GROUP * HD), lambda g, c: (0, 0, g))] + [head] * n_arr,
             scratch_shapes=[
                 pltpu.VMEM((WINDOW + rows, HD), F32),
                 pltpu.VMEM((2, blk, GROUP * HD), BF16),
@@ -222,9 +218,8 @@
                 pltpu.VMEM((2, blk, GROUP * HD), BF16),
             ],
         ),
-        out_shape=[jax.ShapeDtypeStruct((blk, GROUP * HD * count), BF16)] * 2
-        + [jax.ShapeDtypeStruct((2, blk, GROUP * HD * count), BF16)]
-        + [jax.ShapeDtypeStruct((rows, HD * count), BF16)] * n_arr,
+        out_shape=[full, full, jax.ShapeDtypeStruct((2, blk, GROUP * width), BF16)]
+        + [jax.ShapeDtypeStruct((rows, width), BF16)] * n_arr,
         compiler_params=pltpu.CompilerParams(vmem_limit_bytes=40 * 1024 * 1024),
         cost_estimate=small_cost(),
         name="grads",
@@ -273,30 +268,37 @@
     )(at, tokens)
 
 
-def product_kernel(at_ref, x_ref, w_ref, o_ref):
-    o_ref[...] = dot(x_ref[...], w_ref[...]).astype(o_ref.dtype)
-
-
-def run_product(at, x, w, kind):
-    rows = x.shape[0]
+def product_kernel(at_ref, *refs):
+    *x_refs, w_ref, o_ref = refs
+    total, first = None, 0
+    for x in x_refs:
+        term = dot(x[...], w_ref[first : first + x.shape[1], :])
+        total = term if total is None else total + term
+        first += x.shape[1]
+    o_ref[...] = total.astype(o_ref.dtype)
+
+
+def run_product(at, parts, w, kind):
+    rows = parts[0].shape[0]
     depth, width = w.shape
     tile = 512
+    if len(parts) == 1:
+        x_specs = [pl.BlockSpec((rows, depth), lambda j, at: (0, at[0]))]
+    else:
+        x_specs = [pl.BlockSpec(x.shape, lambda j, at: (0, 0)) for x in parts]
     return pl.pallas_call(
         product_kernel,
         grid_spec=pltpu.PrefetchScalarGridSpec(
             num_scalar_prefetch=1,
             grid=(width // tile,),
-            in_specs=[
-                pl.BlockSpec((rows, depth), lambda j, at: (0, at[0])),
-                pl.BlockSpec((depth, tile), lambda j, at: (0, j)),
-            ],
+            in_specs=x_specs + [pl.BlockSpec((depth, tile), lambda j, at: (0, j))],
             out_specs=pl.BlockSpec((rows, tile), lambda j, at: (0, j)),
         ),
         out_shape=jax.ShapeDtypeStruct((rows, width), kind),
         compiler_params=pltpu.CompilerParams(vmem_limit_bytes=32 * 1024 * 1024),
         cost_estimate=small_cost(),
         name="product",
-    )(at, x, w)
+    )(at, *parts, w)
 
 
 def weight_kernel(n_z, n, at_ref, *refs):
@@ -459,14 +461,22 @@
     out_rows = model // (n_ctx * n_fsdp)
     places = [(flip, s) for flip in range(2) for s in range(n_fsdp)]
 
-    slabs = [cols(tokens, (my_fsdp + s) % n_fsdp, slab) for s in range(1, n_fsdp)]
-    sent = [rotated(x, s + 1) for s, x in enumerate(slabs)]
+    cut = slab // HD // 2 * HD if aligned else slab
+    parts_at = [(0, cut), (cut, slab)] if aligned else [(0, slab)]
+    slabs = [
+        [
+            lax.dynamic_slice_in_dim(tokens, (my_fsdp + s) % n_fsdp * slab + low, high - low, 1)
+            for low, high in parts_at
+        ]
+        for s in range(1, n_fsdp)
+    ]
+    sent = [[rotated(x, s + 1) for x in parts] for s, parts in enumerate(slabs)]
 
     own_tags = segments[0].astype(BF16)
     tag_row = lax.dynamic_update_slice_in_dim(jnp.zeros((half_kv,), BF16), own_tags, core * shard_rows, 0)
     tag_rows = jnp.concatenate([tag_row[None], jnp.zeros((15, half_kv), BF16)], 0)
     k_sent = jnp.concatenate([cols(key_heads[0], 1 - core, half_kv), tag_rows], 0)
-    got = swapped(after(k_sent, *slabs))
+    got = swapped(after(k_sent, *[parts[0] for parts in slabs]))
 
     if out_rows % 8 == 0:
         at = jnp.stack([my_y, my_fsdp]).astype(jnp.int32)
@@ -493,10 +503,12 @@
     q_sent = jnp.concatenate([cols(queries[0], 1 - core, half_q), cols(d_out[0], 1 - core, half_q)], 1)
     q_other = swapped(after(q_sent, k_own))
     if aligned:
-        value_own = run_product(after(fsdp_arg, q_sent), tokens, w_value, F32)
+        value_own = run_product(after(fsdp_arg, q_sent), [tokens], w_value, F32)
     else:
         value_own = dot(cols(tokens, my_fsdp, slab), w_value)
-    k_far, over_y, _ = lax.optimization_barrier((k_far, over_y, value_own))
+    firsts = [parts[0] for parts in sent]
+    k_far, over_y, firsts, _ = lax.optimization_barrier((k_far, over_y, firsts, value_own))
+    sent = [[x, *parts[1:]] for x, parts in zip(firsts, sent)]
     k_near = flipped(jnp.where(my_y == 0, k_own, k_far))
     keys = [k_far, k_near, k_own]
 
@@ -508,9 +520,9 @@
     low = jnp.maximum(low, jnp.arange(1, chip_rows + 1, dtype=jnp.int32))[None, :]
 
     if aligned:
-        partial = [run_product(zero_arg, x, w_value, BF16) for x in sent]
+        partial = [run_product(zero_arg, parts, w_value, BF16) for parts in sent]
     else:
-        partial = [dot(x, w_value).astype(BF16) for x in sent]
+        partial = [dot(parts[0], w_value).astype(BF16) for parts in sent]
     low = after(low, *partial)
     e, inv, do_t, dv_far, dv_near, dv_mine = run_probs(
         core_arg, low, queries[0], q_other, d_out[0], keys, chip_rows, half_kv
@@ -518,7 +530,8 @@
     dv_got = flipped(dv_near)
 
     value_back = [rotated(x, -s - 1) for s, x in enumerate(partial)]
-    *value_back, _ = lax.optimization_barrier((*value_back, dv_near))
+    over_fsdp = {s: rotated(after(by_place[0, s], *partial), s) for s in range(1, n_fsdp)}
+    value_back, over_fsdp, _ = lax.optimization_barrier((value_back, over_fsdp, dv_near))
     value_sum = value_own
     for x in value_back:
         value_sum = value_sum + x.astype(F32)
@@ -530,33 +543,32 @@
     v_far = shifted(v_own, 4)
     own_pairs = [jnp.concatenate([by_place[0, 0], over_y[0]], 1)]
     other_pairs = [swapped(after(own_pairs[0], v_own))]
-    for s in range(1, n_fsdp):
-        both = jnp.concatenate([by_place[0, s], over_y[s]], 1)
-        own_pairs.append(rotated(after(both, own_values), s))
+    relayed_y = {s: rotated(after(over_y[s], own_values), s) for s in range(1, n_fsdp)}
 
     dv_got = after(dv_got, v_own)
-    dv_back = shifted(relayed(my_y, dv_far, dv_got), -4)
-    v_sent = jnp.where(my_y == 0, v_own, v_far)
+    dv_sent = relayed(my_y, dv_far, dv_got)
+    dv_back = shifted(dv_sent, -4)
+    v_sent = after(jnp.where(my_y == 0, v_own, v_far), dv_sent)
     v_near = flipped(v_sent)
     vals = [v_far, v_near, v_own]
     dv_chip = gathered_terms(my_y, dv_mine, dv_got, after(dv_back, v_sent))
     dv_fsdp = [dv_chip] + [rotated(dv_chip, s) for s in range(1, n_fsdp)]
-    dv_over_y = [flipped(dv_chip)]
-    n_heads = half_kv // HD
-    grad_args = (e, inv, do_t, queries[0], q_other, keys, vals, chip_rows, half_kv)
-    early = run_grads(after(core_arg, *own_pairs), *grad_args, 0, n_heads // 2)
-    dv_fsdp[1:], dv_over_y[0], _ = lax.optimization_barrier((dv_fsdp[1:], dv_over_y[0], early[0]))
-    dv_over_y += [flipped(x) for x in dv_fsdp[1:]]
-    core_late = after(core_arg, dv_over_y[0], *dv_fsdp)
-    late = run_grads(core_late, *grad_args, n_heads // 2, n_heads)
-    dk_got = [flipped(early[4]), flipped(late[4])]
-
+    dv_over_y = [moved(dv_chip, 1, s) for s in range(n_fsdp)]
+    relayed_y, v_near = lax.optimization_barrier((relayed_y, v_near))
+    for s in range(1, n_fsdp):
+        own_pairs.append(jnp.concatenate([over_fsdp[s], relayed_y[s]], 1))
+        other_pairs.append(swapped(own_pairs[s]))
+    vals = [v_far, v_near, v_own]
+    out, dq, other, dk_far, dk_near, dk_mine = run_grads(
+        after(core_arg, dv_chip, *own_pairs), e, inv, do_t, queries[0], q_other, keys, vals, chip_rows, half_kv
+    )
+    dk_got = flipped(dk_near)
+
+    dv_fsdp, dv_over_y, other_pairs, _ = lax.optimization_barrier((dv_fsdp, dv_over_y, other_pairs, dk_near))
     dv_other = swapped(jnp.concatenate([rows_of(x, 1 - core, shard_rows) for x in dv_fsdp], 0))
     dv_rows = placed(
         core, jnp.concatenate([rows_of(x, core, shard_rows) for x in dv_fsdp], 0), dv_other, 1
     )
-    other_pairs += [swapped(after(x, early[0])) for x in own_pairs[1:]]
-    dv_rows, dv_over_y, _ = lax.optimization_barrier((dv_rows, dv_over_y, late[0]))
     if aligned:
         d_tokens, *made = run_tokens(fsdp_arg, dv_rows, w_value, n_fsdp)
     else:
@@ -570,7 +582,7 @@
 
     dv_pairs = list(zip(dv_fsdp, dv_over_y))
     if out_rows % 8 == 0:
-        at = after(jnp.stack([core, my_z]).astype(jnp.int32), *made)
+        at = after(jnp.stack([core, my_z]).astype(jnp.int32), dk_got, *made)
         by_z = run_weight(at, own_pairs, other_pairs, dv_pairs, n_z)
     else:
         weight_term = 0.0
@@ -588,8 +600,7 @@
         lax.ppermute(by_z[d], "ctx", [(i, (i + 4 * d) % n_ctx) for i in range(n_ctx)]) for d in range(1, n_z)
     ]
 
-    *dk_got, _ = lax.optimization_barrier((*dk_got, by_z[0]))
-    dk_got, dk_far, dk_mine = [jnp.concatenate(x, 1) for x in (dk_got, (early[3], late[3]), (early[5], late[5]))]
+    dk_got = after(dk_got, by_z[0])
     dk_sent = relayed(my_y, dk_far, dk_got)
     dk_back = shifted(dk_sent, -4)
 
@@ -601,11 +612,9 @@
 
     dk_chip = gathered_terms(my_y, dk_mine, dk_got, dk_back)
     d_keys = placed(core, rows_of(dk_chip, core, shard_rows), swapped(rows_of(dk_chip, 1 - core, shard_rows)), 1)
-    early, late, _ = lax.optimization_barrier((early, late, made))
-    out, dq, other = [jnp.concatenate((early[i], late[i]), early[i].ndim - 1) for i in range(3)]
-    other = swapped(other)
-    out = placed(core, out, other[0], 1)
-    dq = placed(core, dq, other[1], 1)
+    other = swapped(after(other, *made))
+    out = lax.dynamic_update_slice_in_dim(out, other[0], (1 - core) * half_q, 1)
+    dq = lax.dynamic_update_slice_in_dim(dq, other[1], (1 - core) * half_q, 1)
     return (out[None], dq[None], d_keys[None], d_tokens[None], d_weight)
 
 

time: 215 us -> 223 us (1.037)
  starting transfers between devices: 42.3 us -> 59.7 us
  waiting for transfers between devices: 85.3 us -> 74 us
  local copies, waits for them, and re-layouts: 24.3 us -> 27.6 us
    ppermute x3, waiting for transfers between devices: 24.8 us -> 8.45 us  [shards(): lax.ppermute(by_z[d], 'ctx', [(i, (i + 4 * d) % n_ctx) for i in range(n_c...]
    ppermute x9, starting transfers between devices: 13.5 us -> 28.9 us  [swapped(): lax.ppermute(x, 'ctx', [(i, i ^ 1) for i in range(lax.axis_size('ctx'))])]
    ppermute x5 -> x7, waiting for transfers between devices: 24.5 us -> 11.4 us  [rotated(): lax.ppermute(x, 'fsdp', [(i, (i + by) % length) for i in range(length)])]
    ppermute x9 -> x6, waiting for transfers between devices: 10.7 us -> 23.7 us  [flipped(): lax.ppermute(x, 'ctx', [(i, i ^ 2) for i in range(lax.axis_size('ctx'))])]
    unnamed x101 -> x120, local copies, waits for them, and re-layouts: 12 us -> 19 us
    ppermute x4, waiting for transfers between devices: 23 us -> 26.3 us  [shifted(): lax.ppermute(x, 'ctx', [(i, i + by) for i in range(length) if 0 <= i + by...]
    dynamic_update_slice x6 -> x5, local copies, waits for them, and re-layouts: 3.36 us -> 0.16 us  [placed(): lax.dynamic_update_slice_in_dim(both, other, (1 - core) * own.shape[axis]...]
    dynamic_slice x0 -> x2, local copies, waits for them, and re-layouts: none -> 3.04 us  [shards(): lax.dynamic_slice_in_dim(tokens, (my_fsdp + s) % n_fsdp * slab + low, hig...]
  transfers between devices with their start and end apart: 30 -> 31, of which waited for: 14 -> 17; matrix products, arithmetic and copies ran while one was open for 8% -> 7% of each run, Pallas kernels for 23% -> 19%
where the time goes in v3:
time: 223 us; the launch traced here: 222 us
  waiting for transfers between devices  74 us (33%)
  starting transfers between devices  59.7 us (27%)
  Pallas kernels  48 us (22%)
  local copies, waits for them, and re-layouts  27.6 us (12%)
  other arithmetic  11 us (5%)
    ppermute x9, starting transfers between devices, swapped(): lax.ppermute(x, 'ctx', [(i, i ^ 1) for i in range(lax.axis_size('ctx'))])  28.9 us
    ppermute x4, waiting for transfers between devices, shifted(): lax.ppermute(x, 'ctx', [(i, i + by) for i in range(length) if 0 <= i + by...  26.3 us
    ppermute x6, waiting for transfers between devices, flipped(): lax.ppermute(x, 'ctx', [(i, i ^ 2) for i in range(lax.axis_size('ctx'))])  23.7 us
    unnamed x120, local copies, waits for them, and re-layouts  19 us
    pallas_call x1, Pallas kernels, run_grads(): pl.pallas_call(functools.partial(grads_kernel, blk, n_arr - 1), grid_spec...  15.8 us
    pallas_call x1, Pallas kernels, run_probs(): pl.pallas_call(functools.partial(probs_kernel, blk, n_arr - 1), grid_spec...  14.1 us
    ppermute x4, starting transfers between devices, shifted(): lax.ppermute(x, 'ctx', [(i, i + by) for i in range(length) if 0 <= i + by...  12.9 us
    ppermute x7, waiting for transfers between devices, rotated(): lax.ppermute(x, 'fsdp', [(i, (i + by) % length) for i in range(length)])  11.4 us
  transfers between devices with their start and end apart: 31, of which 17 were waited for; matrix products, arithmetic and copies ran while one was open for 7% of the time, Pallas kernels for 19%

profile of v3, /device:TPU:9, one launch (start us, length us, event | category | flops | bytes accessed | tf_op | source)
XLA Modules:
  0.0 221.8 jit_solution(18235074969821924504)
XLA Ops:
  0.8 2.1 dynamic-slice_bitcast_fusion.1
  6.2 1.2 collective-permute-start.3
  7.5 2.4 %pieces.1 = (bf16[1344,256]{1,0:T(8,128)(2,1)S(1)}, bf16[1344,256]{1,0:T(8,128)(2,1)S(1)}, bf16[1344,256]{1,0:T(8,128)(2,1)S(1)}, bf16[1344,256]{1,0:T(8,128)(2,1)}) custom-call(s32[2]{0:T(128)S(1)} %pad_add_fusion.at_ref, bf16[256,5376]{1,0:T(8,128)(2,1)S(1)} %bitcast.29), custom_call_target="tpu_custom_call" | custom-call | flops 1048576 | bytes 4096 | tf_op jit(solution)/shard_map/pieces/pallas_call | solution.py:259
  11.0 3.2 %collective-permute-start.1 = (bf16[528,512]{1,0:T(8,128)(2,1)S(1)}, bf16[528,512]{1,0:T(8,128)(2,1)}, u32[]{:S(2)}, u32[]{:S(2)}) collective-permute-start(bf16[528,512]{1,0:T(8,128)(2,1)S(1)} %pad_maximum_fusion.2.refs_2_), channel_id=1, source_target_pairs={{0,8},{2,10},{4,12},{6,14},{8,16},{10,18},{12,20},{14,22},{16,24},... | collective-permute-start | bytes 1622024 | tf_op jit(solution)/shard_map/ppermute | solution.py:385
  14.2 1.3 collective-permute-start.2
  19.9 2.6 %copy-done = bf16[2688,1024]{1,0:T(8,128)(2,1)S(1)} copy-done((bf16[2688,1024]{1,0:T(8,128)(2,1)S(1)}, bf16[2688,1024]{1,0:T(8,128)(2,1)}, u32[]{:S(2)}) %copy-start) | copy-done | bytes 5505048
  22.5 2.4 %product.2 = f32[256,1024]{1,0:T(8,128)S(1)} custom-call(s32[1]{0:T(128)} %bitcast.5.at_ref, bf16[256,5376]{1,0:T(8,128)(2,1)S(1)} %bitcast.30, bf16[2688,1024]{1,0:T(8,128)(2,1)S(1)} %copy-done), custom_call_target="tpu_custom_call" | custom-call | flops 1048576 | bytes 4096 | tf_op jit(solution)/shard_map/product/pallas_call | solution.py:289
  24.9 1.7 collective-permute-done.1.refs_0_
  26.6 4.4 %collective-permute-done.2 = bf16[1344,256]{1,0:T(8,128)(2,1)} collective-permute-done((bf16[1344,256]{1,0:T(8,128)(2,1)}, bf16[1344,256]{1,0:T(8,128)(2,1)}, u32[]{:S(2)}, u32[]{:S(2)}) %collective-permute-start.2) | collective-permute-done | bytes 688160 | tf_op jit(solution)/shard_map/ppermute | solution.py:429
  31.9 2.3 %collective-permute-start.4 = (bf16[528,512]{1,0:T(8,128)(2,1)}, bf16[528,512]{1,0:T(8,128)(2,1)}, u32[]{:S(2)}, u32[]{:S(2)}) collective-permute-start(bf16[528,512]{1,0:T(8,128)(2,1)} %broadcast_select_fusion), channel_id=1, source_target_pairs={{0,4},{2,6},{4,0},{6,2},{8,12},{10,14},{12,8},{14,10},{16,20},{18,... | collective-permute-start | bytes 1622024 | tf_op jit(solution)/shard_map/ppermute | solution.py:429
  34.2 1.7 collective-permute-start.6
  35.9 2.4 %collective-permute-done.5.refs_1_ = bf16[256,1408]{1,0:T(8,128)(2,1)} collective-permute-done((bf16[256,1408]{1,0:T(8,128)(2,1)}, bf16[256,1408]{1,0:T(8,128)(2,1)}, u32[]{:S(2)}, u32[]{:S(2)}) %collective-permute-start.5) | collective-permute-done | bytes 720928 | tf_op jit(solution)/shard_map/ppermute | solution.py:394
  38.3 2.6 %copy-done.1 = bf16[2688,1024]{1,0:T(8,128)(2,1)S(1)} copy-done((bf16[2688,1024]{1,0:T(8,128)(2,1)S(1)}, bf16[2688,1024]{1,0:T(8,128)(2,1)}, u32[]{:S(2)}) %copy-start.1) | copy-done | bytes 5505048
  40.9 3.5 %product.3 = bf16[256,1024]{1,0:T(8,128)(2,1)S(1)} custom-call(s32[1]{0:T(128)} %constant.87.clone.1.at_ref, bf16[256,1280]{1,0:T(8,128)(2,1)} %collective-permute-done.3.refs_0_, bf16[256,1408]{1,0:T(8,128)(2,1)} %collective-permute-done.5.refs_1_, bf16[2688,1024]{1,0:T(8,128)(2,1)S(1)} %copy-done.1), custom_call_target="tpu_custom_call" | custom-call | flops 1048576 | bytes 4096 | tf_op jit(solution)/shard_map/product/pallas_call | solution.py:289
  44.4 1.3 collective-permute-start.8
  48.0 1.3 collective-permute-start.11
  49.3 14.1 %probs.1 = (bf16[4,2,1280,512]{3,2,1,0:T(8,128)(2,1)}, f32[4,2,1,512]{3,2,1,0:T(1,128)S(1)}, bf16[4,2,128,512]{3,2,1,0:T(8,128)(2,1)S(1)}, bf16[512,512]{1,0:T(8...) custom-call(s32[1]{0:T(128)} %bitcast.core_ref, s32[1,512]{1,0:T(1,128)S(1)} %add_maximum_fusion.low_ref, ...), custom_call_target="tpu_custom_call" | custom-call | flops 1048576 | bytes 4096 | tf_op jit(solution)/shard_map/probs/pallas_call | solution.py:157
  63.5 8.4 %collective-permute-done.9 = bf16[1344,256]{1,0:T(8,128)(2,1)S(1)} collective-permute-done((bf16[1344,256]{1,0:T(8,128)(2,1)S(1)}, bf16[1344,256]{1,0:T(8,128)(2,1)S(1)}, u32[]{:S(2)}, u32[]{:S(2)}) %collective-permute-start.9) | collective-permute-done | bytes 688160 | tf_op jit(solution)/shard_map/ppermute | solution.py:394
  72.1 1.7 collective-permute-start.10
  73.8 1.3 collective-permute-start.7
  76.1 3.2 %collective-permute-start.13 = (bf16[512,512]{1,0:T(8,128)(2,1)S(1)}, bf16[512,512]{1,0:T(8,128)(2,1)S(1)}, u32[]{:S(2)}, u32[]{:S(2)}) collective-permute-start(bf16[512,512]{1,0:T(8,128)(2,1)S(1)} %constant_dynamic-update-slice_fusion.6.refs_5_), channel_id=1, source_target_pairs={{0,8},{2,10},{4,12},{6,14},{8,16},{10,18},{12,20},{14,22},{16,24},... | collective-permute-start | bytes 1572872 | tf_op jit(solution)/shard_map/ppermute | solution.py:385
  79.3 1.3 collective-permute-start.14
  80.6 6.9 %collective-permute-done.7 = bf16[512,512]{1,0:T(8,128)(2,1)S(1)} collective-permute-done((bf16[512,512]{1,0:T(8,128)(2,1)}, bf16[512,512]{1,0:T(8,128)(2,1)S(1)}, u32[]{:S(2)}, u32[]{:S(2)}) %collective-permute-start.7) | collective-permute-done | bytes 524320 | tf_op jit(solution)/shard_map/ppermute | solution.py:429
  87.5 1.4 fusion.1
  89.0 2.2 collective-permute-done.13.refs_3_
  93.7 1.5 collective-permute-start.19
  96.0 7.6 %collective-permute-done.15.refs_4_ = bf16[512,512]{1,0:T(8,128)(2,1)S(1)} collective-permute-done((bf16[512,512]{1,0:T(8,128)(2,1)S(1)}, bf16[512,512]{1,0:T(8,128)(2,1)S(1)}, u32[]{:S(2)}, u32[]{:S(2)}) %collective-permute-start.15) | collective-permute-done | bytes 524320 | tf_op jit(solution)/shard_map/ppermute | solution.py:429
  103.6 2.2 collective-permute-start.20
  105.8 2.1 collective-permute-start.12
  107.9 13.3 %collective-permute-done.12 = bf16[512,512]{1,0:T(8,128)(2,1)S(1)} collective-permute-done((bf16[512,512]{1,0:T(8,128)(2,1)S(1)}, bf16[512,512]{1,0:T(8,128)(2,1)S(1)}, u32[]{:S(2)}, u32[]{:S(2)}) %collective-permute-start.12) | collective-permute-done | bytes 524320 | tf_op jit(solution)/shard_map/ppermute | solution.py:385
  121.2 1.3 fusion.3.refs_4_
  122.5 1.3 collective-permute-start.16
  125.2 15.8 %grads.1 = (bf16[256,2048]{1,0:T(8,128)(2,1)}, bf16[256,2048]{1,0:T(8,128)(2,1)}, bf16[2,256,1024]{2,1,0:T(8,128)(2,1)S(1)}, bf16[512,512]{1,0:T(8,128)(2,1)S(1)...) custom-call(s32[1]{0:T(128)} %bitcast.core_ref, bf16[4,2,1280,512]{3,2,1,0:T(8,128)(2,1)} %get-tuple-element.92.e_ref, ...), custom_call_target="tpu_custom_call" | custom-call | flops 1048576 | bytes 4096 | tf_op jit(solution)/shard_map/grads/pallas_call | solution.py:200
  144.5 2.8 %collective-permute-done.18.refs_7_ = bf16[512,512]{1,0:T(8,128)(2,1)S(1)} collective-permute-done((bf16[512,512]{1,0:T(8,128)(2,1)S(1)}, bf16[512,512]{1,0:T(8,128)(2,1)S(1)}, u32[]{:S(2)}, u32[]{:S(2)}) %collective-permute-start.18) | collective-permute-done | bytes 524320 | tf_op jit(solution)/shard_map/ppermute | solution.py:404
  149.6 3.0 %collective-permute-start.21 = (bf16[512,512]{1,0:T(8,128)(2,1)S(1)}, bf16[512,512]{1,0:T(8,128)(2,1)S(1)}, u32[]{:S(2)}, u32[]{:S(2)}) collective-permute-start(bf16[512,512]{1,0:T(8,128)(2,1)S(1)} %pad_maximum_fusion.5), channel_id=1, source_target_pairs={{0,2},{2,0},{4,6},{6,4},{8,10},{10,8},{12,14},{14,12},{16,18},{18,... | collective-permute-start | bytes 1572872 | tf_op jit(solution)/shard_map/ppermute | solution.py:389
  154.2 2.6 %copy-done.2 = bf16[2688,1024]{1,0:T(8,128)(2,1)S(1)} copy-done((bf16[2688,1024]{1,0:T(8,128)(2,1)S(1)}, bf16[2688,1024]{1,0:T(8,128)(2,1)}, u32[]{:S(2)}) %copy-start.2) | copy-done | bytes 5505048
  156.8 4.7 %tokens.1 = (bf16[256,5376]{1,0:T(8,128)(2,1)}, bf16[256,2688]{1,0:T(8,128)(2,1)S(1)}) custom-call(s32[1]{0:T(128)} %bitcast.5.at_ref, bf16[512,1024]{1,0:T(8,128)(2,1)S(1)} %constant_dynamic-update-slice_fusion.5.dv_ref, bf16[2688,1024]{1,0:T(8,128)(2,1)S(1)} %copy-done.2), custom_call_target="tpu_custom_call" | custom-call | flops 1048576 | bytes 4096 | tf_op jit(solution)/shard_map/tokens/pallas_call | solution.py:363
  161.5 4.8 %collective-permute-done.23 = bf16[512,512]{1,0:T(8,128)(2,1)S(1)} collective-permute-done((bf16[512,512]{1,0:T(8,128)(2,1)}, bf16[512,512]{1,0:T(8,128)(2,1)S(1)}, u32[]{:S(2)}, u32[]{:S(2)}) %collective-permute-start.23) | collective-permute-done | bytes 524320 | tf_op jit(solution)/shard_map/ppermute | solution.py:429
  166.3 5.0 %weight.1 = (f32[336,512]{1,0:T(8,128)S(1)}, bf16[336,512]{1,0:T(8,128)(2,1)}, bf16[336,512]{1,0:T(8,128)(2,1)S(1)}, bf16[336,512]{1,0:T(8,128)(2,1)S(1)}) custom-call(s32[2]{0:T(128)S(1)} %pad_add_fusion.1.at_ref, bf16[1344,512]{1,0:T(8,128)(2,1)S(1)} %copy-done.15, bf16[1344,512]{1,0:T(8,128)(2,1)S(1)} %copy-done.13, bf16[1344,512]{1,0:T(8,128)(2,1)S(1)} %copy-done.22, ...), custom_call_target="tpu_custom_call" | custom-call | flops 1048576 | bytes 4096 | tf_op jit(solution)/shard_map/weight/pallas_call | solution.py:335
  171.3 1.3 collective-permute-start.27
  174.8 4.4 %collective-permute-start.24 = (bf16[512,512]{1,0:T(8,128)(2,1)}, bf16[512,512]{1,0:T(8,128)(2,1)}, u32[]{:S(2)}, u32[]{:S(2)}) collective-permute-start(bf16[512,512]{1,0:T(8,128)(2,1)} %fusion.5), channel_id=1, source_target_pairs={{8,0},{10,2},{12,4},{14,6},{16,8},{18,10},{20,12},{22,14},{24,16},... | collective-permute-start | bytes 1572872 | tf_op jit(solution)/shard_map/ppermute | solution.py:385
  180.4 16.9 %collective-permute-start.22 = (bf16[2,256,1024]{2,1,0:T(8,128)(2,1)}, bf16[2,256,1024]{2,1,0:T(8,128)(2,1)S(1)}, u32[]{:S(2)}, u32[]{:S(2)}) collective-permute-start(bf16[2,256,1024]{2,1,0:T(8,128)(2,1)} %copy-done.39), channel_id=1, source_target_pairs={{0,2},{2,0},{4,6},{6,4},{8,10},{10,8},{12,14},{14,12},{16,18},{18,... | collective-permute-start | bytes 3145736 | tf_op jit(solution)/shard_map/ppermute | solution.py:389
  197.3 4.2 %collective-permute-done.28 = bf16[336,512]{1,0:T(8,128)(2,1)} collective-permute-done((bf16[336,512]{1,0:T(8,128)(2,1)S(1)}, bf16[336,512]{1,0:T(8,128)(2,1)}, u32[]{:S(2)}, u32[]{:S(2)}) %collective-permute-start.28) | collective-permute-done | bytes 344096 | tf_op jit(solution)/shard_map/ppermute | solution.py:600
  201.5 3.2 %collective-permute-done.29 = bf16[336,512]{1,0:T(8,128)(2,1)} collective-permute-done((bf16[336,512]{1,0:T(8,128)(2,1)S(1)}, bf16[336,512]{1,0:T(8,128)(2,1)}, u32[]{:S(2)}, u32[]{:S(2)}) %collective-permute-start.29) | collective-permute-done | bytes 344096 | tf_op jit(solution)/shard_map/ppermute | solution.py:600
  204.7 1.4 convert_add_fusion
  206.7 9.2 %collective-permute-done.24 = bf16[512,512]{1,0:T(8,128)(2,1)} collective-permute-done((bf16[512,512]{1,0:T(8,128)(2,1)}, bf16[512,512]{1,0:T(8,128)(2,1)}, u32[]{:S(2)}, u32[]{:S(2)}) %collective-permute-start.24) | collective-permute-done | bytes 524320 | tf_op jit(solution)/shard_map/ppermute | solution.py:385
  215.9 1.3 fusion.7
  220.5 1.3 copy-done.54
  (190 shorter events, 32.5 us)
Async XLA Ops:
  5.5 4.5 %collective-permute-start = (bf16[272,512]{1,0:T(8,128)(2,1)}, bf16[272,512]{1,0:T(8,128)(2,1)S(1)}, u32[]{:S(2)}, u32[]{:S(2)}) collective-permute-start(bf16[272,512]{1,0:T(8,128)(2,1)} %maximum_maximum_fusion.1), channel_id=1, source_target_pairs={{0,2},{2,0},{4,6},{6,4},{8,10},{10,8},{12,14},{14,12},{16,18},{18,... | collective-permute-start | bytes 835592 | tf_op jit(solution)/shard_map/ppermute | solution.py:389
  6.2 18.8 %collective-permute-start.3 = (bf16[256,1280]{1,0:T(8,128)(2,1)}, bf16[256,1280]{1,0:T(8,128)(2,1)}, u32[]{:S(2)}, u32[]{:S(2)}) collective-permute-start(bf16[256,1280]{1,0:T(8,128)(2,1)} %dynamic-slice_bitcast_fusion.1), channel_id=1, source_target_pairs={{0,1},{1,0},{2,3},{3,2},{4,5},{5,4},{6,7},{7,6},{8,9},{9,8},{10,11... | collective-permute-start | bytes 1966088 | tf_op jit(solution)/shard_map/ppermute | solution.py:394
  11.0 15.6 %collective-permute-start.1 = (bf16[528,512]{1,0:T(8,128)(2,1)S(1)}, bf16[528,512]{1,0:T(8,128)(2,1)}, u32[]{:S(2)}, u32[]{:S(2)}) collective-permute-start(bf16[528,512]{1,0:T(8,128)(2,1)S(1)} %pad_maximum_fusion.2.refs_2_), channel_id=1, source_target_pairs={{0,8},{2,10},{4,12},{6,14},{8,16},{10,18},{12,20},{14,22},{16,24},... | collective-permute-start | bytes 1622024 | tf_op jit(solution)/shard_map/ppermute | solution.py:385
  14.2 16.8 %collective-permute-start.2 = (bf16[1344,256]{1,0:T(8,128)(2,1)}, bf16[1344,256]{1,0:T(8,128)(2,1)}, u32[]{:S(2)}, u32[]{:S(2)}) collective-permute-start(bf16[1344,256]{1,0:T(8,128)(2,1)} %get-tuple-element.70), channel_id=1, source_target_pairs={{0,4},{2,6},{4,0},{6,2},{8,12},{10,14},{12,8},{14,10},{16,20},{18,... | collective-permute-start | bytes 2064392 | tf_op jit(solution)/shard_map/ppermute | solution.py:429
  16.5 21.8 %collective-permute-start.5 = (bf16[256,1408]{1,0:T(8,128)(2,1)}, bf16[256,1408]{1,0:T(8,128)(2,1)}, u32[]{:S(2)}, u32[]{:S(2)}) collective-permute-start(bf16[256,1408]{1,0:T(8,128)(2,1)} %dynamic-slice_bitcast_fusion), channel_id=1, source_target_pairs={{0,1},{1,0},{2,3},{3,2},{4,5},{5,4},{6,7},{7,6},{8,9},{9,8},{10,11... | collective-permute-start | bytes 2162696 | tf_op jit(solution)/shard_map/ppermute | solution.py:394
  31.9 14.7 %collective-permute-start.4 = (bf16[528,512]{1,0:T(8,128)(2,1)}, bf16[528,512]{1,0:T(8,128)(2,1)}, u32[]{:S(2)}, u32[]{:S(2)}) collective-permute-start(bf16[528,512]{1,0:T(8,128)(2,1)} %broadcast_select_fusion), channel_id=1, source_target_pairs={{0,4},{2,6},{4,0},{6,2},{8,12},{10,14},{12,8},{14,10},{16,20},{18,... | collective-permute-start | bytes 1622024 | tf_op jit(solution)/shard_map/ppermute | solution.py:429
  34.2 15.1 %collective-permute-start.6 = (bf16[256,2048]{1,0:T(8,128)(2,1)}, bf16[256,2048]{1,0:T(8,128)(2,1)S(1)}, u32[]{:S(2)}, u32[]{:S(2)}) collective-permute-start(bf16[256,2048]{1,0:T(8,128)(2,1)} %pad_maximum_fusion), channel_id=1, source_target_pairs={{0,2},{2,0},{4,6},{6,4},{8,10},{10,8},{12,14},{14,12},{16,18},{18,... | collective-permute-start | bytes 3145736 | tf_op jit(solution)/shard_map/ppermute | solution.py:389
  44.4 19.1 %collective-permute-start.8 = (bf16[256,1024]{1,0:T(8,128)(2,1)S(1)}, bf16[256,1024]{1,0:T(8,128)(2,1)S(1)}, u32[]{:S(2)}, u32[]{:S(2)}) collective-permute-start(bf16[256,1024]{1,0:T(8,128)(2,1)S(1)} %product.3), channel_id=1, source_target_pairs={{0,1},{1,0},{2,3},{3,2},{4,5},{5,4},{6,7},{7,6},{8,9},{9,8},{10,11... | collective-permute-start | bytes 1572872 | tf_op jit(solution)/shard_map/ppermute | solution.py:394
  45.7 26.2 %collective-permute-start.9 = (bf16[1344,256]{1,0:T(8,128)(2,1)S(1)}, bf16[1344,256]{1,0:T(8,128)(2,1)S(1)}, u32[]{:S(2)}, u32[]{:S(2)}) collective-permute-start(bf16[1344,256]{1,0:T(8,128)(2,1)S(1)} %copy-done.43), channel_id=1, source_target_pairs={{0,1},{1,0},{2,3},{3,2},{4,5},{5,4},{6,7},{7,6},{8,9},{9,8},{10,11... | collective-permute-start | bytes 2064392 | tf_op jit(solution)/shard_map/ppermute | solution.py:394
  48.0 27.2 %collective-permute-start.11 = (bf16[1344,256]{1,0:T(8,128)(2,1)S(1)}, bf16[1344,256]{1,0:T(8,128)(2,1)S(1)}, u32[]{:S(2)}, u32[]{:S(2)}) collective-permute-start(bf16[1344,256]{1,0:T(8,128)(2,1)S(1)} %copy-done.41), channel_id=1, source_target_pairs={{0,4},{2,6},{4,0},{6,2},{8,12},{10,14},{12,8},{14,10},{16,20},{18,... | collective-permute-start | bytes 2064392 | tf_op jit(solution)/shard_map/ppermute | solution.py:429
  49.3 22.5 %copy-start.11 = (f32[256,1024]{1,0:T(8,128)S(1)}, f32[256,1024]{1,0:T(8,128)}, u32[]{:S(2)}) copy-start(f32[256,1024]{1,0:T(8,128)} %copy-done.10) | copy-start | bytes 3145732
  63.5 11.7 %copy-start.25 = (bf16[4,2,128,512]{3,2,1,0:T(8,128)(2,1)}, bf16[4,2,128,512]{3,2,1,0:T(8,128)(2,1)S(1)}, u32[]{:S(2)}) copy-start(bf16[4,2,128,512]{3,2,1,0:T(8,128)(2,1)S(1)} %get-tuple-element.94.dot_ref) | copy-start | bytes 3145732
  63.5 11.7 %copy-start.30 = (bf16[512,512]{1,0:T(8,128)(2,1)}, bf16[512,512]{1,0:T(8,128)(2,1)S(1)}, u32[]{:S(2)}) copy-start(bf16[512,512]{1,0:T(8,128)(2,1)S(1)} %get-tuple-element.76) | copy-start | bytes 1572868
  63.5 11.7 %copy-start.34 = (bf16[512,512]{1,0:T(8,128)(2,1)}, bf16[512,512]{1,0:T(8,128)(2,1)S(1)}, u32[]{:S(2)}) copy-start(bf16[512,512]{1,0:T(8,128)(2,1)S(1)} %get-tuple-element.77) | copy-start | bytes 1572868
  72.1 3.0 %collective-permute-start.10 = (bf16[256,512]{1,0:T(8,128)(2,1)S(1)}, bf16[256,512]{1,0:T(8,128)(2,1)S(1)}, u32[]{:S(2)}, u32[]{:S(2)}) collective-permute-start(bf16[256,512]{1,0:T(8,128)(2,1)S(1)} %get-tuple-element.131), channel_id=1, source_target_pairs={{0,2},{2,0},{4,6},{6,4},{8,10},{10,8},{12,14},{14,12},{16,18},{18,... | collective-permute-start | bytes 786440 | tf_op jit(solution)/shard_map/ppermute | solution.py:389
  73.8 13.7 %collective-permute-start.7 = (bf16[512,512]{1,0:T(8,128)(2,1)}, bf16[512,512]{1,0:T(8,128)(2,1)S(1)}, u32[]{:S(2)}, u32[]{:S(2)}) collective-permute-start(bf16[512,512]{1,0:T(8,128)(2,1)} %get-tuple-element.78), channel_id=1, source_target_pairs={{0,4},{2,6},{4,0},{6,2},{8,12},{10,14},{12,8},{14,10},{16,20},{18,... | collective-permute-start | bytes 1572872 | tf_op jit(solution)/shard_map/ppermute | solution.py:429
  75.2 18.3 %copy-start.6 = (bf16[512,512]{1,0:T(8,128)(2,1)}, bf16[512,512]{1,0:T(8,128)(2,1)S(1)}, u32[]{:S(2)}) copy-start(bf16[512,512]{1,0:T(8,128)(2,1)S(1)} %constant_dynamic-update-slice_fusion.6.refs_5_) | copy-start | bytes 1572868
  76.1 15.0 %collective-permute-start.13 = (bf16[512,512]{1,0:T(8,128)(2,1)S(1)}, bf16[512,512]{1,0:T(8,128)(2,1)S(1)}, u32[]{:S(2)}, u32[]{:S(2)}) collective-permute-start(bf16[512,512]{1,0:T(8,128)(2,1)S(1)} %constant_dynamic-update-slice_fusion.6.refs_5_), channel_id=1, source_target_pairs={{0,8},{2,10},{4,12},{6,14},{8,16},{10,18},{12,20},{14,22},{16,24},... | collective-permute-start | bytes 1572872 | tf_op jit(solution)/shard_map/ppermute | solution.py:385
  79.3 16.6 %collective-permute-start.14 = (bf16[1344,256]{1,0:T(8,128)(2,1)}, bf16[1344,256]{1,0:T(8,128)(2,1)S(1)}, u32[]{:S(2)}, u32[]{:S(2)}) collective-permute-start(bf16[1344,256]{1,0:T(8,128)(2,1)} %collective-permute-done.2), channel_id=1, source_target_pairs={{0,1},{1,0},{2,3},{3,2},{4,5},{5,4},{6,7},{7,6},{8,9},{9,8},{10,11... | collective-permute-start | bytes 2064392 | tf_op jit(solution)/shard_map/ppermute | solution.py:394
  91.2 12.3 %collective-permute-start.15 = (bf16[512,512]{1,0:T(8,128)(2,1)S(1)}, bf16[512,512]{1,0:T(8,128)(2,1)S(1)}, u32[]{:S(2)}, u32[]{:S(2)}) collective-permute-start(bf16[512,512]{1,0:T(8,128)(2,1)S(1)} %broadcast_select_fusion.1), channel_id=1, source_target_pairs={{0,4},{2,6},{4,0},{6,2},{8,12},{10,14},{12,8},{14,10},{16,20},{18,... | collective-permute-start | bytes 1572872 | tf_op jit(solution)/shard_map/ppermute | solution.py:429
  93.5 27.6 %copy-start.31 = (bf16[512,512]{1,0:T(8,128)(2,1)S(1)}, bf16[512,512]{1,0:T(8,128)(2,1)}, u32[]{:S(2)}) copy-start(bf16[512,512]{1,0:T(8,128)(2,1)} %copy-done.30) | copy-start | bytes 1572868
  93.6 31.6 %copy-start.5 = (bf16[1,256,2048]{2,1,0:T(8,128)(2,1)S(1)}, bf16[1,256,2048]{2,1,0:T(8,128)(2,1)}, u32[]{:S(2)}) copy-start(bf16[1,256,2048]{2,1,0:T(8,128)(2,1)} %param.7) | copy-start | bytes 3145732
  93.6 31.5 %copy-start.7 = (bf16[512,512]{1,0:T(8,128)(2,1)S(1)}, bf16[512,512]{1,0:T(8,128)(2,1)}, u32[]{:S(2)}) copy-start(bf16[512,512]{1,0:T(8,128)(2,1)} %copy-done.6) | copy-start | bytes 1572868
  93.6 31.5 %copy-start.26 = (bf16[4,2,128,512]{3,2,1,0:T(8,128)(2,1)S(1)}, bf16[4,2,128,512]{3,2,1,0:T(8,128)(2,1)}, u32[]{:S(2)}) copy-start(bf16[4,2,128,512]{3,2,1,0:T(8,128)(2,1)} %copy-done.25) | copy-start | bytes 3145732
  93.7 47.3 %copy-start.14 = (bf16[1344,512]{1,0:T(8,128)(2,1)}, bf16[1344,512]{1,0:T(8,128)(2,1)S(1)}, u32[]{:S(2)}) copy-start(bf16[1344,512]{1,0:T(8,128)(2,1)S(1)} %constant_dynamic-update-slice_fusion.refs_0_) | copy-start | bytes 4128772
  93.7 31.5 %copy-start.18 = (bf16[512,512]{1,0:T(8,128)(2,1)S(1)}, bf16[512,512]{1,0:T(8,128)(2,1)}, u32[]{:S(2)}) copy-start(bf16[512,512]{1,0:T(8,128)(2,1)} %copy-done.17) | copy-start | bytes 1572868
  93.7 54.3 %collective-permute-start.19 = (bf16[1344,512]{1,0:T(8,128)(2,1)S(1)}, bf16[1344,512]{1,0:T(8,128)(2,1)S(1)}, u32[]{:S(2)}, u32[]{:S(2)}) collective-permute-start(bf16[1344,512]{1,0:T(8,128)(2,1)S(1)} %constant_dynamic-update-slice_fusion.refs_0_), channel_id=1, source_target_pairs={{0,2},{2,0},{4,6},{6,4},{8,10},{10,8},{12,14},{14,12},{16,18},{18,... | collective-permute-start | bytes 4128776 | tf_op jit(solution)/shard_map/ppermute | solution.py:389
  103.6 37.4 %copy-start.12 = (bf16[1344,512]{1,0:T(8,128)(2,1)}, bf16[1344,512]{1,0:T(8,128)(2,1)S(1)}, u32[]{:S(2)}) copy-start(bf16[1344,512]{1,0:T(8,128)(2,1)S(1)} %constant_dynamic-update-slice_fusion.2.refs_1_) | copy-start | bytes 4128772
  103.6 44.4 %collective-permute-start.20 = (bf16[1344,512]{1,0:T(8,128)(2,1)S(1)}, bf16[1344,512]{1,0:T(8,128)(2,1)S(1)}, u32[]{:S(2)}, u32[]{:S(2)}) collective-permute-start(bf16[1344,512]{1,0:T(8,128)(2,1)S(1)} %constant_dynamic-update-slice_fusion.2.refs_1_), channel_id=1, source_target_pairs={{0,2},{2,0},{4,6},{6,4},{8,10},{10,8},{12,14},{14,12},{16,18},{18,... | collective-permute-start | bytes 4128776 | tf_op jit(solution)/shard_map/ppermute | solution.py:389
  105.8 15.4 %collective-permute-start.12 = (bf16[512,512]{1,0:T(8,128)(2,1)S(1)}, bf16[512,512]{1,0:T(8,128)(2,1)S(1)}, u32[]{:S(2)}, u32[]{:S(2)}) collective-permute-start(bf16[512,512]{1,0:T(8,128)(2,1)S(1)} %fusion.1), channel_id=1, source_target_pairs={{8,0},{10,2},{12,4},{14,6},{16,8},{18,10},{20,12},{22,14},{24,16},... | collective-permute-start | bytes 1572872 | tf_op jit(solution)/shard_map/ppermute | solution.py:385
  122.4 26.7 %copy-start.8 = (bf16[512,512]{1,0:T(8,128)(2,1)}, bf16[512,512]{1,0:T(8,128)(2,1)S(1)}, u32[]{:S(2)}) copy-start(bf16[512,512]{1,0:T(8,128)(2,1)S(1)} %fusion.3.refs_4_) | copy-start | bytes 1572868
  122.5 21.1 %collective-permute-start.16 = (bf16[512,512]{1,0:T(8,128)(2,1)S(1)}, bf16[512,512]{1,0:T(8,128)(2,1)S(1)}, u32[]{:S(2)}, u32[]{:S(2)}) collective-permute-start(bf16[512,512]{1,0:T(8,128)(2,1)S(1)} %fusion.3.refs_4_), channel_id=1, source_target_pairs={{0,1},{1,0},{2,3},{3,2},{4,5},{5,4},{6,7},{7,6},{8,9},{9,8},{10,11... | collective-permute-start | bytes 1572872 | tf_op jit(solution)/shard_map/ppermute | solution.py:394
  123.7 19.9 %collective-permute-start.17 = (bf16[512,512]{1,0:T(8,128)(2,1)S(1)}, bf16[512,512]{1,0:T(8,128)(2,1)S(1)}, u32[]{:S(2)}, u32[]{:S(2)}) collective-permute-start(bf16[512,512]{1,0:T(8,128)(2,1)S(1)} %fusion.3.refs_4_), channel_id=1, source_target_pairs={{0,4},{1,5},{2,6},{3,7},{4,0},{5,1},{6,2},{7,3},{8,12},{9,13},{10,... | collective-permute-start | bytes 1572872 | tf_op jit(solution)/shard_map/ppermute | solution.py:404
  124.8 22.4 %collective-permute-start.18 = (bf16[512,512]{1,0:T(8,128)(2,1)S(1)}, bf16[512,512]{1,0:T(8,128)(2,1)S(1)}, u32[]{:S(2)}, u32[]{:S(2)}) collective-permute-start(bf16[512,512]{1,0:T(8,128)(2,1)S(1)} %fusion.3.refs_4_), channel_id=1, source_target_pairs={{0,5},{1,4},{2,7},{3,6},{4,1},{5,0},{6,3},{7,2},{8,13},{9,12},{10,... | collective-permute-start | bytes 1572872 | tf_op jit(solution)/shard_map/ppermute | solution.py:404
  149.6 4.5 %collective-permute-start.21 = (bf16[512,512]{1,0:T(8,128)(2,1)S(1)}, bf16[512,512]{1,0:T(8,128)(2,1)S(1)}, u32[]{:S(2)}, u32[]{:S(2)}) collective-permute-start(bf16[512,512]{1,0:T(8,128)(2,1)S(1)} %pad_maximum_fusion.5), channel_id=1, source_target_pairs={{0,2},{2,0},{4,6},{6,4},{8,10},{10,8},{12,14},{14,12},{16,18},{18,... | collective-permute-start | bytes 1572872 | tf_op jit(solution)/shard_map/ppermute | solution.py:389
  152.5 13.7 %collective-permute-start.23 = (bf16[512,512]{1,0:T(8,128)(2,1)}, bf16[512,512]{1,0:T(8,128)(2,1)S(1)}, u32[]{:S(2)}, u32[]{:S(2)}) collective-permute-start(bf16[512,512]{1,0:T(8,128)(2,1)} %get-tuple-element.99), channel_id=1, source_target_pairs={{0,4},{2,6},{4,0},{6,2},{8,12},{10,14},{12,8},{14,10},{16,20},{18,... | collective-permute-start | bytes 1572872 | tf_op jit(solution)/shard_map/ppermute | solution.py:429
  154.1 12.2 %copy-start.36 = (bf16[512,512]{1,0:T(8,128)(2,1)S(1)}, bf16[512,512]{1,0:T(8,128)(2,1)}, u32[]{:S(2)}) copy-start(bf16[512,512]{1,0:T(8,128)(2,1)} %copy-done.35) | copy-start | bytes 1572868
  154.1 12.2 %copy-start.38 = (bf16[512,512]{1,0:T(8,128)(2,1)S(1)}, bf16[512,512]{1,0:T(8,128)(2,1)}, u32[]{:S(2)}) copy-start(bf16[512,512]{1,0:T(8,128)(2,1)} %copy-done.37) | copy-start | bytes 1572868
  171.3 9.0 %collective-permute-start.27 = (bf16[336,512]{1,0:T(8,128)(2,1)}, bf16[336,512]{1,0:T(8,128)(2,1)}, u32[]{:S(2)}, u32[]{:S(2)}) collective-permute-start(bf16[336,512]{1,0:T(8,128)(2,1)} %get-tuple-element.115), channel_id=1, source_target_pairs={{0,8},{2,10},{4,12},{6,14},{8,16},{10,18},{12,20},{14,22},{16,24},... | collective-permute-start | bytes 1032200 | tf_op jit(solution)/shard_map/ppermute | solution.py:600
  172.6 28.9 %collective-permute-start.28 = (bf16[336,512]{1,0:T(8,128)(2,1)S(1)}, bf16[336,512]{1,0:T(8,128)(2,1)}, u32[]{:S(2)}, u32[]{:S(2)}) collective-permute-start(bf16[336,512]{1,0:T(8,128)(2,1)S(1)} %get-tuple-element.116), channel_id=1, source_target_pairs={{0,16},{2,18},{4,20},{6,22},{8,24},{10,26},{12,28},{14,30},{16,0},... | collective-permute-start | bytes 1032200 | tf_op jit(solution)/shard_map/ppermute | solution.py:600
  173.6 31.0 %collective-permute-start.29 = (bf16[336,512]{1,0:T(8,128)(2,1)S(1)}, bf16[336,512]{1,0:T(8,128)(2,1)}, u32[]{:S(2)}, u32[]{:S(2)}) collective-permute-start(bf16[336,512]{1,0:T(8,128)(2,1)S(1)} %get-tuple-element.117), channel_id=1, source_target_pairs={{0,24},{2,26},{4,28},{6,30},{8,0},{10,2},{12,4},{14,6},{16,8},{18,... | collective-permute-start | bytes 1032200 | tf_op jit(solution)/shard_map/ppermute | solution.py:600
  174.8 41.1 %copy-start.29 = (bf16[512,512]{1,0:T(8,128)(2,1)S(1)}, bf16[512,512]{1,0:T(8,128)(2,1)}, u32[]{:S(2)}) copy-start(bf16[512,512]{1,0:T(8,128)(2,1)} %copy-done.28) | copy-start | bytes 1572868
  174.8 41.1 %collective-permute-start.24 = (bf16[512,512]{1,0:T(8,128)(2,1)}, bf16[512,512]{1,0:T(8,128)(2,1)}, u32[]{:S(2)}, u32[]{:S(2)}) collective-permute-start(bf16[512,512]{1,0:T(8,128)(2,1)} %fusion.5), channel_id=1, source_target_pairs={{8,0},{10,2},{12,4},{14,6},{16,8},{18,10},{20,12},{22,14},{24,16},... | collective-permute-start | bytes 1572872 | tf_op jit(solution)/shard_map/ppermute | solution.py:385
  179.2 36.7 %copy-start.45 = (bf16[512,512]{1,0:T(8,128)(2,1)S(1)}, bf16[512,512]{1,0:T(8,128)(2,1)}, u32[]{:S(2)}) copy-start(bf16[512,512]{1,0:T(8,128)(2,1)} %copy-done.44) | copy-start | bytes 1572868
  179.2 40.0 %collective-permute-start.26 = (bf16[256,2688]{1,0:T(8,128)(2,1)S(1)}, bf16[256,2688]{1,0:T(8,128)(2,1)S(1)}, u32[]{:S(2)}, u32[]{:S(2)}) collective-permute-start(bf16[256,2688]{1,0:T(8,128)(2,1)S(1)} %get-tuple-element.102), channel_id=1, source_target_pairs={{0,1},{1,0},{2,3},{3,2},{4,5},{5,4},{6,7},{7,6},{8,9},{9,8},{10,11... | collective-permute-start | bytes 4128776 | tf_op jit(solution)/shard_map/ppermute | solution.py:394
  180.4 38.6 %collective-permute-start.22 = (bf16[2,256,1024]{2,1,0:T(8,128)(2,1)}, bf16[2,256,1024]{2,1,0:T(8,128)(2,1)S(1)}, u32[]{:S(2)}, u32[]{:S(2)}) collective-permute-start(bf16[2,256,1024]{2,1,0:T(8,128)(2,1)} %copy-done.39), channel_id=1, source_target_pairs={{0,2},{2,0},{4,6},{6,4},{8,10},{10,8},{12,14},{14,12},{16,18},{18,... | collective-permute-start | bytes 3145736 | tf_op jit(solution)/shard_map/ppermute | solution.py:389
  206.1 11.9 %collective-permute-start.30 = (f32[168,512]{1,0:T(8,128)S(1)}, f32[168,512]{1,0:T(8,128)S(1)}, u32[]{:S(2)}, u32[]{:S(2)}) collective-permute-start(f32[168,512]{1,0:T(8,128)S(1)} %get-tuple-element.123), channel_id=1, source_target_pairs={{0,2},{2,0},{4,6},{6,4},{8,10},{10,8},{12,14},{14,12},{16,18},{18,... | collective-permute-start | bytes 1032200 | tf_op jit(solution)/shard_map/ppermute | solution.py:389
  217.2 1.7 collective-permute-start.25
  (42 other events, 178.0 us)

commit v4 on v3

--- a/solution.py
+++ b/solution.py
@@ -14,6 +14,7 @@
 WINDOW = 1024
 GROUP = 2
 NEG = -1e30
+VMEM_BYTES = 58 * 1024 * 1024
 
 score_scale = 1.0 / math.sqrt(168.0)
 exp2_scale = score_scale / math.log(2.0)
@@ -187,7 +188,7 @@
             jax.ShapeDtypeStruct((heads, 2, HD, lanes), BF16),
         ]
         + [jax.ShapeDtypeStruct((rows, width), BF16)] * n_arr,
-        compiler_params=pltpu.CompilerParams(vmem_limit_bytes=40 * 1024 * 1024),
+        compiler_params=pltpu.CompilerParams(vmem_limit_bytes=VMEM_BYTES),
         cost_estimate=small_cost(),
         name="probs",
     )(core, low, q, q_other, do, q_other, *keys)
@@ -220,7 +221,7 @@
         ),
         out_shape=[full, full, jax.ShapeDtypeStruct((2, blk, GROUP * width), BF16)]
         + [jax.ShapeDtypeStruct((rows, width), BF16)] * n_arr,
-        compiler_params=pltpu.CompilerParams(vmem_limit_bytes=40 * 1024 * 1024),
+        compiler_params=pltpu.CompilerParams(vmem_limit_bytes=VMEM_BYTES),
         cost_estimate=small_cost(),
         name="grads",
     )(core, e, inv, do_t, q, q_other, *keys, *values)
@@ -262,7 +263,7 @@
         out_specs=[whole()] * (2 * n_fsdp),
         out_shape=[shape] * (2 * n_fsdp),
         scratch_shapes=[pltpu.VMEM((model, rows), F32)],
-        compiler_params=pltpu.CompilerParams(vmem_limit_bytes=32 * 1024 * 1024),
+        compiler_params=pltpu.CompilerParams(vmem_limit_bytes=VMEM_BYTES),
         cost_estimate=small_cost(),
         name="pieces",
     )(at, tokens)
@@ -295,7 +296,7 @@
             out_specs=pl.BlockSpec((rows, tile), lambda j, at: (0, j)),
         ),
         out_shape=jax.ShapeDtypeStruct((rows, width), kind),
-        compiler_params=pltpu.CompilerParams(vmem_limit_bytes=32 * 1024 * 1024),
+        compiler_params=pltpu.CompilerParams(vmem_limit_bytes=VMEM_BYTES),
         cost_estimate=small_cost(),
         name="product",
     )(at, *parts, w)
@@ -341,7 +342,7 @@
             out_specs=[pl.BlockSpec((count, width), lambda d, at: (0, 0))] * n_z,
         ),
         out_shape=shapes,
-        compiler_params=pltpu.CompilerParams(vmem_limit_bytes=40 * 1024 * 1024),
+        compiler_params=pltpu.CompilerParams(vmem_limit_bytes=VMEM_BYTES),
         cost_estimate=small_cost(),
         name="weight",
     )(at, *own_pairs, *other_pairs, *dvs)
@@ -374,7 +375,7 @@
         ),
         out_shape=[jax.ShapeDtypeStruct((rows, slab * n_fsdp), BF16)]
         + [jax.ShapeDtypeStruct((rows, slab), BF16)] * (n_fsdp - 1),
-        compiler_params=pltpu.CompilerParams(vmem_limit_bytes=40 * 1024 * 1024),
+        compiler_params=pltpu.CompilerParams(vmem_limit_bytes=VMEM_BYTES),
         cost_estimate=small_cost(),
         name="tokens",
     )(at, dv_rows, w)
@@ -530,8 +531,7 @@
     dv_got = flipped(dv_near)
 
     value_back = [rotated(x, -s - 1) for s, x in enumerate(partial)]
-    over_fsdp = {s: rotated(after(by_place[0, s], *partial), s) for s in range(1, n_fsdp)}
-    value_back, over_fsdp, _ = lax.optimization_barrier((value_back, over_fsdp, dv_near))
+    *value_back, _ = lax.optimization_barrier((*value_back, dv_near))
     value_sum = value_own
     for x in value_back:
         value_sum = value_sum + x.astype(F32)
@@ -543,7 +543,9 @@
     v_far = shifted(v_own, 4)
     own_pairs = [jnp.concatenate([by_place[0, 0], over_y[0]], 1)]
     other_pairs = [swapped(after(own_pairs[0], v_own))]
-    relayed_y = {s: rotated(after(over_y[s], own_values), s) for s in range(1, n_fsdp)}
+    for s in range(1, n_fsdp):
+        both = jnp.concatenate([by_place[0, s], over_y[s]], 1)
+        own_pairs.append(rotated(after(both, own_values), s))
 
     dv_got = after(dv_got, v_own)
     dv_sent = relayed(my_y, dv_far, dv_got)
@@ -554,17 +556,17 @@
     dv_chip = gathered_terms(my_y, dv_mine, dv_got, after(dv_back, v_sent))
     dv_fsdp = [dv_chip] + [rotated(dv_chip, s) for s in range(1, n_fsdp)]
     dv_over_y = [moved(dv_chip, 1, s) for s in range(n_fsdp)]
-    relayed_y, v_near = lax.optimization_barrier((relayed_y, v_near))
-    for s in range(1, n_fsdp):
-        own_pairs.append(jnp.concatenate([over_fsdp[s], relayed_y[s]], 1))
-        other_pairs.append(swapped(own_pairs[s]))
+    own_pairs[1:] = [after(x, dv_chip) for x in own_pairs[1:]]
+    v_near = after(v_near, dv_chip)
+    other_pairs += [swapped(x) for x in own_pairs[1:]]
     vals = [v_far, v_near, v_own]
     out, dq, other, dk_far, dk_near, dk_mine = run_grads(
-        after(core_arg, dv_chip, *own_pairs), e, inv, do_t, queries[0], q_other, keys, vals, chip_rows, half_kv
+        core_arg, e, inv, do_t, queries[0], q_other, keys, vals, chip_rows, half_kv
     )
     dk_got = flipped(dk_near)
 
-    dv_fsdp, dv_over_y, other_pairs, _ = lax.optimization_barrier((dv_fsdp, dv_over_y, other_pairs, dk_near))
+    dv_fsdp = [after(x, dk_near) for x in dv_fsdp]
+    dv_over_y = [after(x, dk_near) for x in dv_over_y]
     dv_other = swapped(jnp.concatenate([rows_of(x, 1 - core, shard_rows) for x in dv_fsdp], 0))
     dv_rows = placed(
         core, jnp.concatenate([rows_of(x, core, shard_rows) for x in dv_fsdp], 0), dv_other, 1
@@ -582,7 +584,7 @@
 
     dv_pairs = list(zip(dv_fsdp, dv_over_y))
     if out_rows % 8 == 0:
-        at = after(jnp.stack([core, my_z]).astype(jnp.int32), dk_got, *made)
+        at = after(jnp.stack([core, my_z]).astype(jnp.int32), *made)
         by_z = run_weight(at, own_pairs, other_pairs, dv_pairs, n_z)
     else:
         weight_term = 0.0

time: 223 us -> 194 us (0.87)
  starting transfers between devices: 59.7 us -> 43 us
  local copies, waits for them, and re-layouts: 27.6 us -> 12 us
  Pallas kernels: 48 us -> 59.4 us
  waiting for transfers between devices: 74 us -> 67.1 us
    ppermute x6, waiting for transfers between devices: 23.7 us -> 8.68 us  [flipped(): lax.ppermute(x, 'ctx', [(i, i ^ 2) for i in range(lax.axis_size('ctx'))])]
    ppermute x3, waiting for transfers between devices: 8.45 us -> 22.6 us  [shards(): lax.ppermute(by_z[d], 'ctx', [(i, (i + 4 * d) % n_ctx) for i in range(n_c...]
    unnamed x120 -> x67, local copies, waits for them, and re-layouts: 19 us -> 4.93 us
    ppermute x9, starting transfers between devices: 28.9 us -> 16 us  [swapped(): lax.ppermute(x, 'ctx', [(i, i ^ 1) for i in range(lax.axis_size('ctx'))])]
    ppermute x4, waiting for transfers between devices: 26.3 us -> 19.8 us  [shifted(): lax.ppermute(x, 'ctx', [(i, i + by) for i in range(length) if 0 <= i + by...]
    pallas_call x2, Pallas kernels: 5.92 us -> 9.56 us  [run_product(): pl.pallas_call(product_kernel, grid_spec=pltpu.PrefetchScalarGridSpec(num...]
    pallas_call x1, Pallas kernels: 4.98 us -> 8.26 us  [run_weight(): pl.pallas_call(functools.partial(weight_kernel, n_z, n), grid_spec=pltpu....]
    ppermute x6, starting transfers between devices: 8.34 us -> 5.61 us  [flipped(): lax.ppermute(x, 'ctx', [(i, i ^ 2) for i in range(lax.axis_size('ctx'))])]
  transfers between devices with their start and end apart: 31 -> 30, of which waited for: 17 -> 15; matrix products, arithmetic and copies ran while one was open for 7% -> 7% of each run, Pallas kernels for 19% -> 31%
where the time goes in v4:
time: 194 us; the launch traced here: 192 us
  waiting for transfers between devices  67.1 us (35%)
  Pallas kernels  59.4 us (31%)
  starting transfers between devices  43 us (22%)
  local copies, waits for them, and re-layouts  12 us (6%)
  other arithmetic  9.72 us (5%)
    ppermute x3, waiting for transfers between devices, shards(): lax.ppermute(by_z[d], 'ctx', [(i, (i + 4 * d) % n_ctx) for i in range(n_c...  22.6 us
    ppermute x4, waiting for transfers between devices, shifted(): lax.ppermute(x, 'ctx', [(i, i + by) for i in range(length) if 0 <= i + by...  19.8 us
    pallas_call x1, Pallas kernels, run_grads(): pl.pallas_call(functools.partial(grads_kernel, blk, n_arr - 1), grid_spec...  16 us
    ppermute x9, starting transfers between devices, swapped(): lax.ppermute(x, 'ctx', [(i, i ^ 1) for i in range(lax.axis_size('ctx'))])  16 us
    pallas_call x1, Pallas kernels, run_probs(): pl.pallas_call(functools.partial(probs_kernel, blk, n_arr - 1), grid_spec...  14.3 us
    ppermute x4, starting transfers between devices, shifted(): lax.ppermute(x, 'ctx', [(i, i + by) for i in range(length) if 0 <= i + by...  12.8 us
    ppermute x6, waiting for transfers between devices, rotated(): lax.ppermute(x, 'fsdp', [(i, (i + by) % length) for i in range(length)])  9.92 us
    pallas_call x2, Pallas kernels, run_product(): pl.pallas_call(product_kernel, grid_spec=pltpu.PrefetchScalarGridSpec(num...  9.56 us
  transfers between devices with their start and end apart: 30, of which 15 were waited for; matrix products, arithmetic and copies ran while one was open for 7% of the time, Pallas kernels for 31%

profile of v4, /device:TPU:9, one launch (start us, length us, event | category | flops | bytes accessed | tf_op | source)
XLA Modules:
  0.0 192.5 jit_solution(6670225338357029237)
XLA Ops:
  0.8 2.0 %dynamic-slice_bitcast_fusion.1 = bf16[256,1280]{1,0:T(8,128)(2,1)} fusion(bf16[1,256,5376]{2,1,0:T(8,128)(2,1)} %param.6, s32[]{:T(128)S(6)} %select_n.110), kind=kLoop, calls=%fused_computation.21 | loop fusion | bytes 1310724 | tf_op jit(solution)/shard_map/dynamic_slice | solution.py:469
  3.4 1.1 dynamic-slice_bitcast_fusion.5
  5.3 1.2 collective-permute-start.3
  7.2 4.2 %pieces.1 = (bf16[1344,256]{1,0:T(8,128)(2,1)}, bf16[1344,256]{1,0:T(8,128)(2,1)}, bf16[1344,256]{1,0:T(8,128)(2,1)}, bf16[1344,256]{1,0:T(8,128)(2,1)}) custom-call(s32[2]{0:T(128)} %pad_add_fusion.at_ref, bf16[256,5376]{1,0:T(8,128)(2,1)} %bitcast.29), custom_call_target="tpu_custom_call" | custom-call | flops 1048576 | bytes 4096 | tf_op jit(solution)/shard_map/pieces/pallas_call | solution.py:260
  11.5 3.3 %collective-permute-start.1 = (bf16[528,512]{1,0:T(8,128)(2,1)S(1)}, bf16[528,512]{1,0:T(8,128)(2,1)S(1)}, u32[]{:S(2)}, u32[]{:S(2)}) collective-permute-start(bf16[528,512]{1,0:T(8,128)(2,1)S(1)} %pad_maximum_fusion.3.refs_2_), channel_id=1, source_target_pairs={{0,8},{2,10},{4,12},{6,14},{8,16},{10,18},{12,20},{14,22},{16,24},... | collective-permute-start | bytes 1622024 | tf_op jit(solution)/shard_map/ppermute | solution.py:386
  14.9 1.3 collective-permute-start.2
  16.2 2.0 %dynamic-slice_bitcast_fusion = bf16[256,1408]{1,0:T(8,128)(2,1)} fusion(bf16[1,256,5376]{2,1,0:T(8,128)(2,1)} %param.6, s32[]{:T(128)S(6)} %select_n.117), kind=kLoop, calls=%fused_computation.18 | loop fusion | bytes 1441796 | tf_op jit(solution)/shard_map/dynamic_slice | solution.py:469
  18.6 1.1 pad_maximum_fusion.1
  19.6 4.9 %product.2 = f32[256,1024]{1,0:T(8,128)} custom-call(s32[1]{0:T(128)} %bitcast.5.at_ref, bf16[256,5376]{1,0:T(8,128)(2,1)} %bitcast.30, bf16[2688,1024]{1,0:T(8,128)(2,1)} %w_ref.1), custom_call_target="tpu_custom_call" | custom-call | flops 1048576 | bytes 4096 | tf_op jit(solution)/shard_map/product/pallas_call | solution.py:290
  24.5 2.7 %collective-permute-done.1.refs_0_ = bf16[528,512]{1,0:T(8,128)(2,1)S(1)} collective-permute-done((bf16[528,512]{1,0:T(8,128)(2,1)S(1)}, bf16[528,512]{1,0:T(8,128)(2,1)S(1)}, u32[]{:S(2)}, u32[]{:S(2)}) %collective-permute-start.1) | collective-permute-done | bytes 540704 | tf_op jit(solution)/shard_map/ppermute | solution.py:386
  27.2 4.4 %collective-permute-done.2 = bf16[1344,256]{1,0:T(8,128)(2,1)} collective-permute-done((bf16[1344,256]{1,0:T(8,128)(2,1)}, bf16[1344,256]{1,0:T(8,128)(2,1)}, u32[]{:S(2)}, u32[]{:S(2)}) %collective-permute-start.2) | collective-permute-done | bytes 688160 | tf_op jit(solution)/shard_map/ppermute | solution.py:430
  32.5 1.2 collective-permute-start.4
  33.7 1.8 collective-permute-start.6
  35.5 1.9 collective-permute-done.5.refs_1_
  37.4 4.7 %product.3 = bf16[256,1024]{1,0:T(8,128)(2,1)} custom-call(s32[1]{0:T(128)} %constant.87.clone.1.at_ref, bf16[256,1280]{1,0:T(8,128)(2,1)} %collective-permute-done.3.refs_0_, bf16[256,1408]{1,0:T(8,128)(2,1)} %collective-permute-done.5.refs_1_, bf16[2688,1024]{1,0:T(8,128)(2,1)} %w_ref.1), custom_call_target="tpu_custom_call" | custom-call | flops 1048576 | bytes 4096 | tf_op jit(solution)/shard_map/product/pallas_call | solution.py:290
  42.1 1.2 collective-permute-start.7
  43.4 1.6 collective-permute-done.4.refs_1_
  46.2 1.2 collective-permute-start.9
  48.4 14.3 %probs.1 = (bf16[4,2,1280,512]{3,2,1,0:T(8,128)(2,1)}, f32[4,2,1,512]{3,2,1,0:T(1,128)}, bf16[4,2,128,512]{3,2,1,0:T(8,128)(2,1)}, bf16[512,512]{1,0:T(8,128)(2,...) custom-call(s32[1]{0:T(128)} %bitcast.core_ref, s32[1,512]{1,0:T(1,128)} %add_maximum_fusion.low_ref, ...), custom_call_target="tpu_custom_call" | custom-call | flops 1048576 | bytes 4096 | tf_op jit(solution)/shard_map/probs/pallas_call | solution.py:158
  63.3 3.0 %collective-permute-start.8 = (bf16[256,512]{1,0:T(8,128)(2,1)S(1)}, bf16[256,512]{1,0:T(8,128)(2,1)S(1)}, u32[]{:S(2)}, u32[]{:S(2)}) collective-permute-start(bf16[256,512]{1,0:T(8,128)(2,1)S(1)} %get-tuple-element.121), channel_id=1, source_target_pairs={{0,2},{2,0},{4,6},{6,4},{8,10},{10,8},{12,14},{14,12},{16,18},{18,... | collective-permute-start | bytes 786440 | tf_op jit(solution)/shard_map/ppermute | solution.py:390
  66.3 1.2 pad_maximum_fusion
  68.0 3.2 %collective-permute-start.10 = (bf16[512,512]{1,0:T(8,128)(2,1)S(1)}, bf16[512,512]{1,0:T(8,128)(2,1)S(1)}, u32[]{:S(2)}, u32[]{:S(2)}) collective-permute-start(bf16[512,512]{1,0:T(8,128)(2,1)S(1)} %constant_dynamic-update-slice_fusion.2.refs_5_), channel_id=1, source_target_pairs={{0,8},{2,10},{4,12},{6,14},{8,16},{10,18},{12,20},{14,22},{16,24},... | collective-permute-start | bytes 1572872 | tf_op jit(solution)/shard_map/ppermute | solution.py:386
  71.2 2.7 %collective-permute-done.11 = bf16[512,512]{1,0:T(8,128)(2,1)S(1)} collective-permute-done((bf16[512,512]{1,0:T(8,128)(2,1)}, bf16[512,512]{1,0:T(8,128)(2,1)S(1)}, u32[]{:S(2)}, u32[]{:S(2)}) %collective-permute-start.11) | collective-permute-done | bytes 524320 | tf_op jit(solution)/shard_map/ppermute | solution.py:430
  74.0 2.3 %collective-permute-start.13 = (bf16[512,512]{1,0:T(8,128)(2,1)S(1)}, bf16[512,512]{1,0:T(8,128)(2,1)S(1)}, u32[]{:S(2)}, u32[]{:S(2)}) collective-permute-start(bf16[512,512]{1,0:T(8,128)(2,1)S(1)} %fusion.1), channel_id=1, source_target_pairs={{8,0},{10,2},{12,4},{14,6},{16,8},{18,10},{20,12},{22,14},{24,16},... | collective-permute-start | bytes 1572872 | tf_op jit(solution)/shard_map/ppermute | solution.py:386
  76.4 6.5 %collective-permute-done.10.refs_3_ = bf16[512,512]{1,0:T(8,128)(2,1)S(1)} collective-permute-done((bf16[512,512]{1,0:T(8,128)(2,1)S(1)}, bf16[512,512]{1,0:T(8,128)(2,1)S(1)}, u32[]{:S(2)}, u32[]{:S(2)}) %collective-permute-start.10) | collective-permute-done | bytes 524320 | tf_op jit(solution)/shard_map/ppermute | solution.py:386
  83.0 1.5 collective-permute-start.12
  84.5 1.4 collective-permute-done.13
  86.6 4.7 %collective-permute-start.19 = (bf16[1344,512]{1,0:T(8,128)(2,1)S(1)}, bf16[1344,512]{1,0:T(8,128)(2,1)}, u32[]{:S(2)}, u32[]{:S(2)}) collective-permute-start(bf16[1344,512]{1,0:T(8,128)(2,1)S(1)} %constant_dynamic-update-slice_fusion.4.refs_0_), channel_id=1, source_target_pairs={{0,2},{2,0},{4,6},{6,4},{8,10},{10,8},{12,14},{14,12},{16,18},{18,... | collective-permute-start | bytes 4128776 | tf_op jit(solution)/shard_map/ppermute | solution.py:390
  91.3 8.0 %collective-permute-done.18.refs_1_ = bf16[1344,512]{1,0:T(8,128)(2,1)} collective-permute-done((bf16[1344,512]{1,0:T(8,128)(2,1)S(1)}, bf16[1344,512]{1,0:T(8,128)(2,1)}, u32[]{:S(2)}, u32[]{:S(2)}) %collective-permute-start.18) | collective-permute-done | bytes 1376288 | tf_op jit(solution)/shard_map/ppermute | solution.py:395
  99.3 1.7 collective-permute-start.20
  100.9 1.0 collective-permute-start.22
  102.8 16.0 %grads.1 = (bf16[256,2048]{1,0:T(8,128)(2,1)}, bf16[256,2048]{1,0:T(8,128)(2,1)}, bf16[2,256,1024]{2,1,0:T(8,128)(2,1)}, bf16[512,512]{1,0:T(8,128)(2,1)}, bf16[...) custom-call(s32[1]{0:T(128)} %bitcast.core_ref, bf16[4,2,1280,512]{3,2,1,0:T(8,128)(2,1)} %get-tuple-element.71.e_ref, ...), custom_call_target="tpu_custom_call" | custom-call | flops 1048576 | bytes 4096 | tf_op jit(solution)/shard_map/grads/pallas_call | solution.py:201
  120.0 2.8 %collective-permute-done.22.refs_7_ = bf16[512,512]{1,0:T(8,128)(2,1)S(1)} collective-permute-done((bf16[512,512]{1,0:T(8,128)(2,1)S(1)}, bf16[512,512]{1,0:T(8,128)(2,1)S(1)}, u32[]{:S(2)}, u32[]{:S(2)}) %collective-permute-start.22) | collective-permute-done | bytes 524320 | tf_op jit(solution)/shard_map/ppermute | solution.py:405
  124.2 2.3 %collective-permute-done.21.refs_5_ = bf16[512,512]{1,0:T(8,128)(2,1)} collective-permute-done((bf16[512,512]{1,0:T(8,128)(2,1)S(1)}, bf16[512,512]{1,0:T(8,128)(2,1)}, u32[]{:S(2)}, u32[]{:S(2)}) %collective-permute-start.21) | collective-permute-done | bytes 524320 | tf_op jit(solution)/shard_map/ppermute | solution.py:405
  126.7 1.1 constant_dynamic-update-slice_fusion.1.dv_ref
  128.8 7.1 %tokens.1 = (bf16[256,5376]{1,0:T(8,128)(2,1)}, bf16[256,2688]{1,0:T(8,128)(2,1)}) custom-call(s32[1]{0:T(128)} %bitcast.5.at_ref, bf16[512,1024]{1,0:T(8,128)(2,1)} %copy-done.7, bf16[2688,1024]{1,0:T(8,128)(2,1)} %w_ref.1), custom_call_target="tpu_custom_call" | custom-call | flops 1048576 | bytes 4096 | tf_op jit(solution)/shard_map/tokens/pallas_call | solution.py:364
  135.8 8.3 %weight.1 = (f32[336,512]{1,0:T(8,128)}, bf16[336,512]{1,0:T(8,128)(2,1)}, bf16[336,512]{1,0:T(8,128)(2,1)}, bf16[336,512]{1,0:T(8,128)(2,1)}) custom-call(s32[2]{0:T(128)} %pad_add_fusion.1.at_ref, bf16[1344,512]{1,0:T(8,128)(2,1)} %copy-done.8, bf16[1344,512]{1,0:T(8,128)(2,1)} %collective-permute-done.18.refs_1_, ...), custom_call_target="tpu_custom_call" | custom-call | flops 1048576 | bytes 4096 | tf_op jit(solution)/shard_map/weight/pallas_call | solution.py:336
  144.1 1.3 collective-permute-start.26
  145.4 1.0 collective-permute-start.27
  146.7 1.2 collective-permute-start.25
  147.9 2.6 %collective-permute-start.16 = (bf16[2,256,1024]{2,1,0:T(8,128)(2,1)S(1)}, bf16[2,256,1024]{2,1,0:T(8,128)(2,1)S(1)}, u32[]{:S(2)}, u32[]{:S(2)}) collective-permute-start(bf16[2,256,1024]{2,1,0:T(8,128)(2,1)S(1)} %copy-done.31), channel_id=1, source_target_pairs={{0,2},{2,0},{4,6},{6,4},{8,10},{10,8},{12,14},{14,12},{16,18},{18,... | collective-permute-start | bytes 3145736 | tf_op jit(solution)/shard_map/ppermute | solution.py:390
  150.7 1.5 collective-permute-done.26
  152.2 4.0 %collective-permute-start.23 = (bf16[512,512]{1,0:T(8,128)(2,1)S(1)}, bf16[512,512]{1,0:T(8,128)(2,1)S(1)}, u32[]{:S(2)}, u32[]{:S(2)}) collective-permute-start(bf16[512,512]{1,0:T(8,128)(2,1)S(1)} %fusion.5), channel_id=1, source_target_pairs={{8,0},{10,2},{12,4},{14,6},{16,8},{18,10},{20,12},{22,14},{24,16},... | collective-permute-start | bytes 1572872 | tf_op jit(solution)/shard_map/ppermute | solution.py:386
  156.2 17.3 %collective-permute-done.27 = bf16[336,512]{1,0:T(8,128)(2,1)S(1)} collective-permute-done((bf16[336,512]{1,0:T(8,128)(2,1)}, bf16[336,512]{1,0:T(8,128)(2,1)S(1)}, u32[]{:S(2)}, u32[]{:S(2)}) %collective-permute-start.27) | collective-permute-done | bytes 344096 | tf_op jit(solution)/shard_map/ppermute | solution.py:602
  173.5 3.8 %collective-permute-done.28 = bf16[336,512]{1,0:T(8,128)(2,1)S(1)} collective-permute-done((bf16[336,512]{1,0:T(8,128)(2,1)}, bf16[336,512]{1,0:T(8,128)(2,1)S(1)}, u32[]{:S(2)}, u32[]{:S(2)}) %collective-permute-start.28) | collective-permute-done | bytes 344096 | tf_op jit(solution)/shard_map/ppermute | solution.py:602
  177.3 1.3 convert_add_fusion
  179.4 9.2 %collective-permute-done.23 = bf16[512,512]{1,0:T(8,128)(2,1)S(1)} collective-permute-done((bf16[512,512]{1,0:T(8,128)(2,1)S(1)}, bf16[512,512]{1,0:T(8,128)(2,1)S(1)}, u32[]{:S(2)}, u32[]{:S(2)}) %collective-permute-start.23) | collective-permute-done | bytes 524320 | tf_op jit(solution)/shard_map/ppermute | solution.py:386
  191.4 1.1 copy-done.26
  (135 shorter events, 16.0 us)
Async XLA Ops:
  4.6 6.8 %collective-permute-start = (bf16[272,512]{1,0:T(8,128)(2,1)S(1)}, bf16[272,512]{1,0:T(8,128)(2,1)S(1)}, u32[]{:S(2)}, u32[]{:S(2)}) collective-permute-start(bf16[272,512]{1,0:T(8,128)(2,1)S(1)} %maximum_maximum_fusion.1), channel_id=1, source_target_pairs={{0,2},{2,0},{4,6},{6,4},{8,10},{10,8},{12,14},{14,12},{16,18},{18,... | collective-permute-start | bytes 835592 | tf_op jit(solution)/shard_map/ppermute | solution.py:390
  5.3 19.1 %collective-permute-start.3 = (bf16[256,1280]{1,0:T(8,128)(2,1)}, bf16[256,1280]{1,0:T(8,128)(2,1)}, u32[]{:S(2)}, u32[]{:S(2)}) collective-permute-start(bf16[256,1280]{1,0:T(8,128)(2,1)} %dynamic-slice_bitcast_fusion.1), channel_id=1, source_target_pairs={{0,1},{1,0},{2,3},{3,2},{4,5},{5,4},{6,7},{7,6},{8,9},{9,8},{10,11... | collective-permute-start | bytes 1966088 | tf_op jit(solution)/shard_map/ppermute | solution.py:395
  11.4 7.1 %copy-start.9 = (bf16[1,256,2048]{2,1,0:T(8,128)(2,1)S(1)}, bf16[1,256,2048]{2,1,0:T(8,128)(2,1)}, u32[]{:S(2)}) copy-start(bf16[1,256,2048]{2,1,0:T(8,128)(2,1)} %param.10) | copy-start | bytes 3145732
  11.5 24.0 %copy-start.1 = (bf16[528,512]{1,0:T(8,128)(2,1)}, bf16[528,512]{1,0:T(8,128)(2,1)S(1)}, u32[]{:S(2)}) copy-start(bf16[528,512]{1,0:T(8,128)(2,1)S(1)} %pad_maximum_fusion.3.refs_2_) | copy-start | bytes 1622020
  11.5 15.6 %collective-permute-start.1 = (bf16[528,512]{1,0:T(8,128)(2,1)S(1)}, bf16[528,512]{1,0:T(8,128)(2,1)S(1)}, u32[]{:S(2)}, u32[]{:S(2)}) collective-permute-start(bf16[528,512]{1,0:T(8,128)(2,1)S(1)} %pad_maximum_fusion.3.refs_2_), channel_id=1, source_target_pairs={{0,8},{2,10},{4,12},{6,14},{8,16},{10,18},{12,20},{14,22},{16,24},... | collective-permute-start | bytes 1622024 | tf_op jit(solution)/shard_map/ppermute | solution.py:386
  14.9 16.7 %collective-permute-start.2 = (bf16[1344,256]{1,0:T(8,128)(2,1)}, bf16[1344,256]{1,0:T(8,128)(2,1)}, u32[]{:S(2)}, u32[]{:S(2)}) collective-permute-start(bf16[1344,256]{1,0:T(8,128)(2,1)} %get-tuple-element.65), channel_id=1, source_target_pairs={{0,4},{2,6},{4,0},{6,2},{8,12},{10,14},{12,8},{14,10},{16,20},{18,... | collective-permute-start | bytes 2064392 | tf_op jit(solution)/shard_map/ppermute | solution.py:430
  18.2 19.2 %collective-permute-start.5 = (bf16[256,1408]{1,0:T(8,128)(2,1)}, bf16[256,1408]{1,0:T(8,128)(2,1)}, u32[]{:S(2)}, u32[]{:S(2)}) collective-permute-start(bf16[256,1408]{1,0:T(8,128)(2,1)} %dynamic-slice_bitcast_fusion), channel_id=1, source_target_pairs={{0,1},{1,0},{2,3},{3,2},{4,5},{5,4},{6,7},{7,6},{8,9},{9,8},{10,11... | collective-permute-start | bytes 2162696 | tf_op jit(solution)/shard_map/ppermute | solution.py:395
  27.2 16.2 %copy-start.3 = (bf16[528,512]{1,0:T(8,128)(2,1)}, bf16[528,512]{1,0:T(8,128)(2,1)S(1)}, u32[]{:S(2)}) copy-start(bf16[528,512]{1,0:T(8,128)(2,1)S(1)} %collective-permute-done.1.refs_0_) | copy-start | bytes 1622020
  32.5 12.5 %collective-permute-start.4 = (bf16[528,512]{1,0:T(8,128)(2,1)}, bf16[528,512]{1,0:T(8,128)(2,1)S(1)}, u32[]{:S(2)}, u32[]{:S(2)}) collective-permute-start(bf16[528,512]{1,0:T(8,128)(2,1)} %broadcast_select_fusion), channel_id=1, source_target_pairs={{0,4},{2,6},{4,0},{6,2},{8,12},{10,14},{12,8},{14,10},{16,20},{18,... | collective-permute-start | bytes 1622024 | tf_op jit(solution)/shard_map/ppermute | solution.py:430
  33.7 13.8 %collective-permute-start.6 = (bf16[256,2048]{1,0:T(8,128)(2,1)}, bf16[256,2048]{1,0:T(8,128)(2,1)S(1)}, u32[]{:S(2)}, u32[]{:S(2)}) collective-permute-start(bf16[256,2048]{1,0:T(8,128)(2,1)} %pad_maximum_fusion.1), channel_id=1, source_target_pairs={{0,2},{2,0},{4,6},{6,4},{8,10},{10,8},{12,14},{14,12},{16,18},{18,... | collective-permute-start | bytes 3145736 | tf_op jit(solution)/shard_map/ppermute | solution.py:390
  35.5 10.7 %copy-start.32 = (bf16[1344,256]{1,0:T(8,128)(2,1)S(1)}, bf16[1344,256]{1,0:T(8,128)(2,1)}, u32[]{:S(2)}) copy-start(bf16[1344,256]{1,0:T(8,128)(2,1)} %get-tuple-element.76) | copy-start | bytes 2064388
  42.1 20.9 %collective-permute-start.7 = (bf16[256,1024]{1,0:T(8,128)(2,1)}, bf16[256,1024]{1,0:T(8,128)(2,1)S(1)}, u32[]{:S(2)}, u32[]{:S(2)}) collective-permute-start(bf16[256,1024]{1,0:T(8,128)(2,1)} %product.3), channel_id=1, source_target_pairs={{0,1},{1,0},{2,3},{3,2},{4,5},{5,4},{6,7},{7,6},{8,9},{9,8},{10,11... | collective-permute-start | bytes 1572872 | tf_op jit(solution)/shard_map/ppermute | solution.py:395
  46.2 21.8 %collective-permute-start.9 = (bf16[1344,256]{1,0:T(8,128)(2,1)S(1)}, bf16[1344,256]{1,0:T(8,128)(2,1)S(1)}, u32[]{:S(2)}, u32[]{:S(2)}) collective-permute-start(bf16[1344,256]{1,0:T(8,128)(2,1)S(1)} %copy-done.32), channel_id=1, source_target_pairs={{0,4},{2,6},{4,0},{6,2},{8,12},{10,14},{12,8},{14,10},{16,20},{18,... | collective-permute-start | bytes 2064392 | tf_op jit(solution)/shard_map/ppermute | solution.py:430
  48.4 14.7 %copy-start.6 = (f32[256,1024]{1,0:T(8,128)S(1)}, f32[256,1024]{1,0:T(8,128)}, u32[]{:S(2)}) copy-start(f32[256,1024]{1,0:T(8,128)} %product.2) | copy-start | bytes 3145732
  62.8 11.1 %collective-permute-start.11 = (bf16[512,512]{1,0:T(8,128)(2,1)}, bf16[512,512]{1,0:T(8,128)(2,1)S(1)}, u32[]{:S(2)}, u32[]{:S(2)}) collective-permute-start(bf16[512,512]{1,0:T(8,128)(2,1)} %get-tuple-element.74), channel_id=1, source_target_pairs={{0,4},{2,6},{4,0},{6,2},{8,12},{10,14},{12,8},{14,10},{16,20},{18,... | collective-permute-start | bytes 1572872 | tf_op jit(solution)/shard_map/ppermute | solution.py:430
  63.3 10.6 %copy-start.23 = (bf16[512,512]{1,0:T(8,128)(2,1)S(1)}, bf16[512,512]{1,0:T(8,128)(2,1)}, u32[]{:S(2)}) copy-start(bf16[512,512]{1,0:T(8,128)(2,1)} %get-tuple-element.78) | copy-start | bytes 1572868
  63.3 4.6 %collective-permute-start.8 = (bf16[256,512]{1,0:T(8,128)(2,1)S(1)}, bf16[256,512]{1,0:T(8,128)(2,1)S(1)}, u32[]{:S(2)}, u32[]{:S(2)}) collective-permute-start(bf16[256,512]{1,0:T(8,128)(2,1)S(1)} %get-tuple-element.121), channel_id=1, source_target_pairs={{0,2},{2,0},{4,6},{6,4},{8,10},{10,8},{12,14},{14,12},{16,18},{18,... | collective-permute-start | bytes 786440 | tf_op jit(solution)/shard_map/ppermute | solution.py:390
  67.5 8.8 %copy-start.13 = (bf16[1344,256]{1,0:T(8,128)(2,1)S(1)}, bf16[1344,256]{1,0:T(8,128)(2,1)}, u32[]{:S(2)}) copy-start(bf16[1344,256]{1,0:T(8,128)(2,1)} %get-tuple-element.60) | copy-start | bytes 2064388
  67.5 31.7 %collective-permute-start.18 = (bf16[1344,512]{1,0:T(8,128)(2,1)S(1)}, bf16[1344,512]{1,0:T(8,128)(2,1)}, u32[]{:S(2)}, u32[]{:S(2)}) collective-permute-start(bf16[1344,512]{1,0:T(8,128)(2,1)S(1)} %pad_maximum_fusion), channel_id=1, source_target_pairs={{0,1},{1,0},{2,3},{3,2},{4,5},{5,4},{6,7},{7,6},{8,9},{9,8},{10,11... | collective-permute-start | bytes 4128776 | tf_op jit(solution)/shard_map/ppermute | solution.py:395
  67.9 15.1 %copy-start.4 = (bf16[512,512]{1,0:T(8,128)(2,1)}, bf16[512,512]{1,0:T(8,128)(2,1)S(1)}, u32[]{:S(2)}) copy-start(bf16[512,512]{1,0:T(8,128)(2,1)S(1)} %constant_dynamic-update-slice_fusion.2.refs_5_) | copy-start | bytes 1572868
  68.0 15.0 %collective-permute-start.10 = (bf16[512,512]{1,0:T(8,128)(2,1)S(1)}, bf16[512,512]{1,0:T(8,128)(2,1)S(1)}, u32[]{:S(2)}, u32[]{:S(2)}) collective-permute-start(bf16[512,512]{1,0:T(8,128)(2,1)S(1)} %constant_dynamic-update-slice_fusion.2.refs_5_), channel_id=1, source_target_pairs={{0,8},{2,10},{4,12},{6,14},{8,16},{10,18},{12,20},{14,22},{16,24},... | collective-permute-start | bytes 1572872 | tf_op jit(solution)/shard_map/ppermute | solution.py:386
  73.9 12.1 %copy-start.19 = (bf16[512,512]{1,0:T(8,128)(2,1)S(1)}, bf16[512,512]{1,0:T(8,128)(2,1)}, u32[]{:S(2)}) copy-start(bf16[512,512]{1,0:T(8,128)(2,1)} %get-tuple-element.81) | copy-start | bytes 1572868
  74.0 11.9 %collective-permute-start.13 = (bf16[512,512]{1,0:T(8,128)(2,1)S(1)}, bf16[512,512]{1,0:T(8,128)(2,1)S(1)}, u32[]{:S(2)}, u32[]{:S(2)}) collective-permute-start(bf16[512,512]{1,0:T(8,128)(2,1)S(1)} %fusion.1), channel_id=1, source_target_pairs={{8,0},{10,2},{12,4},{14,6},{16,8},{18,10},{20,12},{22,14},{24,16},... | collective-permute-start | bytes 1572872 | tf_op jit(solution)/shard_map/ppermute | solution.py:386
  76.4 10.1 %copy-start.16 = (bf16[1344,256]{1,0:T(8,128)(2,1)S(1)}, bf16[1344,256]{1,0:T(8,128)(2,1)}, u32[]{:S(2)}) copy-start(bf16[1344,256]{1,0:T(8,128)(2,1)} %copy-done.15) | copy-start | bytes 2064388
  83.0 19.0 %collective-permute-start.12 = (bf16[512,512]{1,0:T(8,128)(2,1)S(1)}, bf16[512,512]{1,0:T(8,128)(2,1)S(1)}, u32[]{:S(2)}, u32[]{:S(2)}) collective-permute-start(bf16[512,512]{1,0:T(8,128)(2,1)S(1)} %broadcast_select_fusion.1), channel_id=1, source_target_pairs={{0,4},{2,6},{4,0},{6,2},{8,12},{10,14},{12,8},{14,10},{16,20},{18,... | collective-permute-start | bytes 1572872 | tf_op jit(solution)/shard_map/ppermute | solution.py:430
  86.2 32.6 %copy-start.5 = (bf16[512,512]{1,0:T(8,128)(2,1)}, bf16[512,512]{1,0:T(8,128)(2,1)S(1)}, u32[]{:S(2)}) copy-start(bf16[512,512]{1,0:T(8,128)(2,1)S(1)} %fusion.3.refs_4_) | copy-start | bytes 1572868
  86.2 32.6 %collective-permute-start.14 = (bf16[512,512]{1,0:T(8,128)(2,1)S(1)}, bf16[512,512]{1,0:T(8,128)(2,1)S(1)}, u32[]{:S(2)}, u32[]{:S(2)}) collective-permute-start(bf16[512,512]{1,0:T(8,128)(2,1)S(1)} %fusion.3.refs_4_), channel_id=1, source_target_pairs={{0,1},{1,0},{2,3},{3,2},{4,5},{5,4},{6,7},{7,6},{8,9},{9,8},{10,11... | collective-permute-start | bytes 1572872 | tf_op jit(solution)/shard_map/ppermute | solution.py:395
  86.6 32.2 %copy-start.8 = (bf16[1344,512]{1,0:T(8,128)(2,1)}, bf16[1344,512]{1,0:T(8,128)(2,1)S(1)}, u32[]{:S(2)}) copy-start(bf16[1344,512]{1,0:T(8,128)(2,1)S(1)} %constant_dynamic-update-slice_fusion.4.refs_0_) | copy-start | bytes 4128772
  86.6 49.3 %collective-permute-start.19 = (bf16[1344,512]{1,0:T(8,128)(2,1)S(1)}, bf16[1344,512]{1,0:T(8,128)(2,1)}, u32[]{:S(2)}, u32[]{:S(2)}) collective-permute-start(bf16[1344,512]{1,0:T(8,128)(2,1)S(1)} %constant_dynamic-update-slice_fusion.4.refs_0_), channel_id=1, source_target_pairs={{0,2},{2,0},{4,6},{6,4},{8,10},{10,8},{12,14},{14,12},{16,18},{18,... | collective-permute-start | bytes 4128776 | tf_op jit(solution)/shard_map/ppermute | solution.py:390
  99.3 36.6 %collective-permute-start.20 = (bf16[1344,512]{1,0:T(8,128)(2,1)}, bf16[1344,512]{1,0:T(8,128)(2,1)}, u32[]{:S(2)}, u32[]{:S(2)}) collective-permute-start(bf16[1344,512]{1,0:T(8,128)(2,1)} %collective-permute-done.18.refs_1_), channel_id=1, source_target_pairs={{0,2},{2,0},{4,6},{6,4},{8,10},{10,8},{12,14},{14,12},{16,18},{18,... | collective-permute-start | bytes 4128776 | tf_op jit(solution)/shard_map/ppermute | solution.py:390
  100.9 21.9 %collective-permute-start.22 = (bf16[512,512]{1,0:T(8,128)(2,1)S(1)}, bf16[512,512]{1,0:T(8,128)(2,1)S(1)}, u32[]{:S(2)}, u32[]{:S(2)}) collective-permute-start(bf16[512,512]{1,0:T(8,128)(2,1)S(1)} %fusion.3.refs_4_), channel_id=1, source_target_pairs={{0,5},{1,4},{2,7},{3,6},{4,1},{5,0},{6,3},{7,2},{8,13},{9,12},{10,... | collective-permute-start | bytes 1572872 | tf_op jit(solution)/shard_map/ppermute | solution.py:405
  102.0 24.6 %collective-permute-start.21 = (bf16[512,512]{1,0:T(8,128)(2,1)S(1)}, bf16[512,512]{1,0:T(8,128)(2,1)}, u32[]{:S(2)}, u32[]{:S(2)}) collective-permute-start(bf16[512,512]{1,0:T(8,128)(2,1)S(1)} %fusion.3.refs_4_), channel_id=1, source_target_pairs={{0,4},{1,5},{2,6},{3,7},{4,0},{5,1},{6,2},{7,3},{8,12},{9,13},{10,... | collective-permute-start | bytes 1572872 | tf_op jit(solution)/shard_map/ppermute | solution.py:405
  118.8 7.8 %copy-start.12 = (bf16[512,512]{1,0:T(8,128)(2,1)}, bf16[512,512]{1,0:T(8,128)(2,1)S(1)}, u32[]{:S(2)}) copy-start(bf16[512,512]{1,0:T(8,128)(2,1)S(1)} %collective-permute-done.14.refs_6_) | copy-start | bytes 1572868
  119.8 6.9 %collective-permute-start.15 = (bf16[512,512]{1,0:T(8,128)(2,1)}, bf16[512,512]{1,0:T(8,128)(2,1)}, u32[]{:S(2)}, u32[]{:S(2)}) collective-permute-start(bf16[512,512]{1,0:T(8,128)(2,1)} %pad_maximum_fusion.6), channel_id=1, source_target_pairs={{0,2},{2,0},{4,6},{6,4},{8,10},{10,8},{12,14},{14,12},{16,18},{18,... | collective-permute-start | bytes 1572872 | tf_op jit(solution)/shard_map/ppermute | solution.py:390
  123.6 24.3 %collective-permute-start.17 = (bf16[512,512]{1,0:T(8,128)(2,1)}, bf16[512,512]{1,0:T(8,128)(2,1)S(1)}, u32[]{:S(2)}, u32[]{:S(2)}) collective-permute-start(bf16[512,512]{1,0:T(8,128)(2,1)} %get-tuple-element.86), channel_id=1, source_target_pairs={{0,4},{2,6},{4,0},{6,2},{8,12},{10,14},{12,8},{14,10},{16,20},{18,... | collective-permute-start | bytes 1572872 | tf_op jit(solution)/shard_map/ppermute | solution.py:430
  135.8 12.0 %copy-start.31 = (bf16[2,256,1024]{2,1,0:T(8,128)(2,1)S(1)}, bf16[2,256,1024]{2,1,0:T(8,128)(2,1)}, u32[]{:S(2)}) copy-start(bf16[2,256,1024]{2,1,0:T(8,128)(2,1)} %get-tuple-element.90) | copy-start | bytes 3145732
  135.8 14.7 %copy-start.22 = (bf16[512,512]{1,0:T(8,128)(2,1)S(1)}, bf16[512,512]{1,0:T(8,128)(2,1)}, u32[]{:S(2)}) copy-start(bf16[512,512]{1,0:T(8,128)(2,1)} %get-tuple-element.93) | copy-start | bytes 1572868
  144.1 8.1 %collective-permute-start.26 = (bf16[336,512]{1,0:T(8,128)(2,1)}, bf16[336,512]{1,0:T(8,128)(2,1)S(1)}, u32[]{:S(2)}, u32[]{:S(2)}) collective-permute-start(bf16[336,512]{1,0:T(8,128)(2,1)} %get-tuple-element.105), channel_id=1, source_target_pairs={{0,8},{2,10},{4,12},{6,14},{8,16},{10,18},{12,20},{14,22},{16,24},... | collective-permute-start | bytes 1032200 | tf_op jit(solution)/shard_map/ppermute | solution.py:602
  145.4 28.1 %collective-permute-start.27 = (bf16[336,512]{1,0:T(8,128)(2,1)}, bf16[336,512]{1,0:T(8,128)(2,1)S(1)}, u32[]{:S(2)}, u32[]{:S(2)}) collective-permute-start(bf16[336,512]{1,0:T(8,128)(2,1)} %get-tuple-element.106), channel_id=1, source_target_pairs={{0,16},{2,18},{4,20},{6,22},{8,24},{10,26},{12,28},{14,30},{16,0},... | collective-permute-start | bytes 1032200 | tf_op jit(solution)/shard_map/ppermute | solution.py:602
  146.4 30.9 %collective-permute-start.28 = (bf16[336,512]{1,0:T(8,128)(2,1)}, bf16[336,512]{1,0:T(8,128)(2,1)S(1)}, u32[]{:S(2)}, u32[]{:S(2)}) collective-permute-start(bf16[336,512]{1,0:T(8,128)(2,1)} %get-tuple-element.107), channel_id=1, source_target_pairs={{0,24},{2,26},{4,28},{6,30},{8,0},{10,2},{12,4},{14,6},{16,8},{18,... | collective-permute-start | bytes 1032200 | tf_op jit(solution)/shard_map/ppermute | solution.py:602
  146.7 44.0 %collective-permute-start.25 = (bf16[256,2688]{1,0:T(8,128)(2,1)}, bf16[256,2688]{1,0:T(8,128)(2,1)S(1)}, u32[]{:S(2)}, u32[]{:S(2)}) collective-permute-start(bf16[256,2688]{1,0:T(8,128)(2,1)} %get-tuple-element.89), channel_id=1, source_target_pairs={{0,1},{1,0},{2,3},{3,2},{4,5},{5,4},{6,7},{7,6},{8,9},{9,8},{10,11... | collective-permute-start | bytes 4128776 | tf_op jit(solution)/shard_map/ppermute | solution.py:395
  147.9 41.6 %collective-permute-start.16 = (bf16[2,256,1024]{2,1,0:T(8,128)(2,1)S(1)}, bf16[2,256,1024]{2,1,0:T(8,128)(2,1)S(1)}, u32[]{:S(2)}, u32[]{:S(2)}) collective-permute-start(bf16[2,256,1024]{2,1,0:T(8,128)(2,1)S(1)} %copy-done.31), channel_id=1, source_target_pairs={{0,2},{2,0},{4,6},{6,4},{8,10},{10,8},{12,14},{14,12},{16,18},{18,... | collective-permute-start | bytes 3145736 | tf_op jit(solution)/shard_map/ppermute | solution.py:390
  150.7 37.9 %copy-start.18 = (bf16[512,512]{1,0:T(8,128)(2,1)S(1)}, bf16[512,512]{1,0:T(8,128)(2,1)}, u32[]{:S(2)}) copy-start(bf16[512,512]{1,0:T(8,128)(2,1)} %get-tuple-element.92) | copy-start | bytes 1572868
  152.2 36.3 %collective-permute-start.23 = (bf16[512,512]{1,0:T(8,128)(2,1)S(1)}, bf16[512,512]{1,0:T(8,128)(2,1)S(1)}, u32[]{:S(2)}, u32[]{:S(2)}) collective-permute-start(bf16[512,512]{1,0:T(8,128)(2,1)S(1)} %fusion.5), channel_id=1, source_target_pairs={{8,0},{10,2},{12,4},{14,6},{16,8},{18,10},{20,12},{22,14},{24,16},... | collective-permute-start | bytes 1572872 | tf_op jit(solution)/shard_map/ppermute | solution.py:386
  178.7 11.0 %collective-permute-start.29 = (f32[168,512]{1,0:T(8,128)S(1)}, f32[168,512]{1,0:T(8,128)S(1)}, u32[]{:S(2)}, u32[]{:S(2)}) collective-permute-start(f32[168,512]{1,0:T(8,128)S(1)} %get-tuple-element.113), channel_id=1, source_target_pairs={{0,2},{2,0},{4,6},{6,4},{8,10},{10,8},{12,14},{14,12},{16,18},{18,... | collective-permute-start | bytes 1032200 | tf_op jit(solution)/shard_map/ppermute | solution.py:390
  179.4 10.1 %copy-start.27 = (bf16[256,2048]{1,0:T(8,128)(2,1)S(1)}, bf16[256,2048]{1,0:T(8,128)(2,1)}, u32[]{:S(2)}) copy-start(bf16[256,2048]{1,0:T(8,128)(2,1)} %get-tuple-element.84) | copy-start | bytes 3145732
  179.4 10.1 %copy-start.29 = (bf16[256,2048]{1,0:T(8,128)(2,1)S(1)}, bf16[256,2048]{1,0:T(8,128)(2,1)}, u32[]{:S(2)}) copy-start(bf16[256,2048]{1,0:T(8,128)(2,1)} %get-tuple-element.91) | copy-start | bytes 3145732
  188.9 1.7 collective-permute-start.24
  (15 other events, 34.8 us)

commit v5 on v4

--- a/solution.py
+++ b/solution.py
@@ -282,7 +282,7 @@
 def run_product(at, parts, w, kind):
     rows = parts[0].shape[0]
     depth, width = w.shape
-    tile = 512
+    tile = 256
     if len(parts) == 1:
         x_specs = [pl.BlockSpec((rows, depth), lambda j, at: (0, at[0]))]
     else:
@@ -359,7 +359,7 @@
 def run_tokens(at, dv_rows, w, n_fsdp):
     slab, width = w.shape
     rows = dv_rows.shape[0] // n_fsdp
-    tile = slab // 3 if slab % (3 * HD) == 0 else slab
+    tile = 3 * HD if slab % (3 * HD) == 0 else slab
     n_tiles = slab // tile
     return pl.pallas_call(
         functools.partial(tokens_kernel, n_fsdp),
@@ -481,7 +481,7 @@
 
     if out_rows % 8 == 0:
         at = jnp.stack([my_y, my_fsdp]).astype(jnp.int32)
-        pieces = run_pieces(after(at, k_sent), tokens, n_z, n_fsdp, out_rows)
+        pieces = run_pieces(after(at, k_sent, got), tokens, n_z, n_fsdp, out_rows)
     else:
         turned = tokens.T.reshape(n_z, 2, 2, n_fsdp, out_rows, shard_rows)
         pieces = []
@@ -498,8 +498,8 @@
         ],
         0,
     )
-    k_own = after(k_own, *pieces)
     k_far = shifted(k_own, 4)
+    k_near = shifted(k_own, 2)
     over_y = {s: flipped(after(by_place[1, s], k_own)) for s in range(1, n_fsdp)}
     q_sent = jnp.concatenate([cols(queries[0], 1 - core, half_q), cols(d_out[0], 1 - core, half_q)], 1)
     q_other = swapped(after(q_sent, k_own))
@@ -507,10 +507,6 @@
         value_own = run_product(after(fsdp_arg, q_sent), [tokens], w_value, F32)
     else:
         value_own = dot(cols(tokens, my_fsdp, slab), w_value)
-    firsts = [parts[0] for parts in sent]
-    k_far, over_y, firsts, _ = lax.optimization_barrier((k_far, over_y, firsts, value_own))
-    sent = [[x, *parts[1:]] for x, parts in zip(firsts, sent)]
-    k_near = flipped(jnp.where(my_y == 0, k_own, k_far))
     keys = [k_far, k_near, k_own]
 
     span_tags = jnp.concatenate([k[chip_rows, :chip_rows] for k in keys], 0)
@@ -524,7 +520,7 @@
         partial = [run_product(zero_arg, parts, w_value, BF16) for parts in sent]
     else:
         partial = [dot(parts[0], w_value).astype(BF16) for parts in sent]
-    low = after(low, *partial)
+    low = after(low, *partial, *over_y.values())
     e, inv, do_t, dv_far, dv_near, dv_mine = run_probs(
         core_arg, low, queries[0], q_other, d_out[0], keys, chip_rows, half_kv
     )
@@ -539,13 +535,14 @@
     v_own = placed(core, cols(own_values, core, half_kv), swapped(cols(own_values, 1 - core, half_kv)), 0)
 
     over_y[0] = flipped(after(by_place[1, 0], k_near))
-    v_own, over_y[0] = lax.optimization_barrier((v_own, over_y[0]))
+    both_y = [
+        after(jnp.concatenate([by_place[0, s], over_y[s]], 1), own_values) for s in range(1, n_fsdp)
+    ]
+    v_own, over_y[0], both_y = lax.optimization_barrier((v_own, over_y[0], both_y))
     v_far = shifted(v_own, 4)
     own_pairs = [jnp.concatenate([by_place[0, 0], over_y[0]], 1)]
     other_pairs = [swapped(after(own_pairs[0], v_own))]
-    for s in range(1, n_fsdp):
-        both = jnp.concatenate([by_place[0, s], over_y[s]], 1)
-        own_pairs.append(rotated(after(both, own_values), s))
+    own_pairs += [rotated(x, s + 1) for s, x in enumerate(both_y)]
 
     dv_got = after(dv_got, v_own)
     dv_sent = relayed(my_y, dv_far, dv_got)
@@ -556,14 +553,14 @@
     dv_chip = gathered_terms(my_y, dv_mine, dv_got, after(dv_back, v_sent))
     dv_fsdp = [dv_chip] + [rotated(dv_chip, s) for s in range(1, n_fsdp)]
     dv_over_y = [moved(dv_chip, 1, s) for s in range(n_fsdp)]
-    own_pairs[1:] = [after(x, dv_chip) for x in own_pairs[1:]]
     v_near = after(v_near, dv_chip)
-    other_pairs += [swapped(x) for x in own_pairs[1:]]
     vals = [v_far, v_near, v_own]
     out, dq, other, dk_far, dk_near, dk_mine = run_grads(
         core_arg, e, inv, do_t, queries[0], q_other, keys, vals, chip_rows, half_kv
     )
     dk_got = flipped(dk_near)
+    own_pairs[1:] = [after(x, dk_near) for x in own_pairs[1:]]
+    other_pairs += [swapped(x) for x in own_pairs[1:]]
 
     dv_fsdp = [after(x, dk_near) for x in dv_fsdp]
     dv_over_y = [after(x, dk_near) for x in dv_over_y]
@@ -571,6 +568,7 @@
     dv_rows = placed(
         core, jnp.concatenate([rows_of(x, core, shard_rows) for x in dv_fsdp], 0), dv_other, 1
     )
+    dv_rows = after(dv_rows, *dv_over_y)
     if aligned:
         d_tokens, *made = run_tokens(fsdp_arg, dv_rows, w_value, n_fsdp)
     else:
@@ -582,9 +580,12 @@
         back = rotated(made[s - 1], -s)
         d_tokens = lax.dynamic_update_slice_in_dim(d_tokens, back, ((my_fsdp + s) % n_fsdp) * slab, 1)
 
+    dk_sent = relayed(my_y, dk_far, after(dk_got, *made))
+    dk_back = shifted(dk_sent, -4)
+
     dv_pairs = list(zip(dv_fsdp, dv_over_y))
     if out_rows % 8 == 0:
-        at = after(jnp.stack([core, my_z]).astype(jnp.int32), *made)
+        at = after(jnp.stack([core, my_z]).astype(jnp.int32), dk_sent)
         by_z = run_weight(at, own_pairs, other_pairs, dv_pairs, n_z)
     else:
         weight_term = 0.0
@@ -602,17 +603,12 @@
         lax.ppermute(by_z[d], "ctx", [(i, (i + 4 * d) % n_ctx) for i in range(n_ctx)]) for d in range(1, n_z)
     ]
 
-    dk_got = after(dk_got, by_z[0])
-    dk_sent = relayed(my_y, dk_far, dk_got)
-    dk_back = shifted(dk_sent, -4)
-
-    over_z, _ = lax.optimization_barrier((over_z, dk_sent))
     row_sum = by_z[0]
     for x in over_z:
         row_sum = row_sum + x.astype(F32)
     d_weight = placed(core, rows_of(row_sum, core, out_rows), swapped(rows_of(row_sum, 1 - core, out_rows)), 1)
 
-    dk_chip = gathered_terms(my_y, dk_mine, dk_got, dk_back)
+    dk_chip = gathered_terms(my_y, dk_mine, dk_got, after(dk_back, *over_z[:1]))
     d_keys = placed(core, rows_of(dk_chip, core, shard_rows), swapped(rows_of(dk_chip, 1 - core, shard_rows)), 1)
     other = swapped(after(other, *made))
     out = lax.dynamic_update_slice_in_dim(out, other[0], (1 - core) * half_q, 1)

time: 194 us -> 219 us (1.13)
  waiting for transfers between devices: 67.1 us -> 81.5 us
  other arithmetic: 9.72 us -> 13.2 us
  Pallas kernels: 59.4 us -> 62.7 us
  local copies, waits for them, and re-layouts: 12 us -> 14.9 us
    ppermute x6 -> x5, waiting for transfers between devices: 8.68 us -> 24.5 us  [flipped(): lax.ppermute(x, 'ctx', [(i, i ^ 2) for i in range(lax.axis_size('ctx'))])]
    convert_element_type x2, other arithmetic: 0.32 us -> 2.94 us  [relayed(): (far.astype(F32) + jnp.where(my_y == 1, got.astype(F32), 0.0)).astype(BF16)]
    unnamed x67 -> x53, local copies, waits for them, and re-layouts: 4.93 us -> 6.6 us
    ppermute x6 -> x5, starting transfers between devices: 5.61 us -> 4.37 us  [flipped(): lax.ppermute(x, 'ctx', [(i, i ^ 2) for i in range(lax.axis_size('ctx'))])]
    ppermute x4 -> x5, waiting for transfers between devices: 19.8 us -> 18.8 us  [shifted(): lax.ppermute(x, 'ctx', [(i, i + by) for i in range(length) if 0 <= i + by...]
    ppermute x4 -> x5, starting transfers between devices: 12.8 us -> 13.7 us  [shifted(): lax.ppermute(x, 'ctx', [(i, i + by) for i in range(length) if 0 <= i + by...]
  transfers between devices with their start and end apart: 30 -> 30, of which waited for: 15 -> 12; matrix products, arithmetic and copies ran while one was open for 7% -> 9% of each run, Pallas kernels for 31% -> 29%
where the time goes in v5:
time: 219 us; the launch traced here: 218 us
  waiting for transfers between devices  81.5 us (37%)
  Pallas kernels  62.7 us (29%)
  starting transfers between devices  44.6 us (20%)
  local copies, waits for them, and re-layouts  14.9 us (7%)
  other arithmetic  13.2 us (6%)
    ppermute x5, waiting for transfers between devices, flipped(): lax.ppermute(x, 'ctx', [(i, i ^ 2) for i in range(lax.axis_size('ctx'))])  24.5 us
    ppermute x3, waiting for transfers between devices, shards(): lax.ppermute(by_z[d], 'ctx', [(i, (i + 4 * d) % n_ctx) for i in range(n_c...  23.1 us
    ppermute x5, waiting for transfers between devices, shifted(): lax.ppermute(x, 'ctx', [(i, i + by) for i in range(length) if 0 <= i + by...  18.8 us
    pallas_call x1, Pallas kernels, run_grads(): pl.pallas_call(functools.partial(grads_kernel, blk, n_arr - 1), grid_spec...  16 us
    ppermute x9, starting transfers between devices, swapped(): lax.ppermute(x, 'ctx', [(i, i ^ 1) for i in range(lax.axis_size('ctx'))])  14.7 us
    pallas_call x1, Pallas kernels, run_probs(): pl.pallas_call(functools.partial(probs_kernel, blk, n_arr - 1), grid_spec...  14.3 us
    ppermute x5, starting transfers between devices, shifted(): lax.ppermute(x, 'ctx', [(i, i + by) for i in range(length) if 0 <= i + by...  13.7 us
    pallas_call x2, Pallas kernels, run_product(): pl.pallas_call(product_kernel, grid_spec=pltpu.PrefetchScalarGridSpec(num...  11.3 us
  transfers between devices with their start and end apart: 30, of which 12 were waited for; matrix products, arithmetic and copies ran while one was open for 9% of the time, Pallas kernels for 29%

profile of v5, /device:TPU:9, one launch (start us, length us, event | category | flops | bytes accessed | tf_op | source)
XLA Modules:
  0.0 218.1 jit_solution(6627654472891976298)
XLA Ops:
  0.7 1.2 dynamic-slice_bitcast_fusion.1
  1.9 1.3 collective-permute-start.3
  4.0 1.1 dynamic-slice_bitcast_fusion.5
  6.8 2.0 dynamic-slice_bitcast_fusion
  11.0 3.1 %collective-permute-start.2 = (bf16[528,512]{1,0:T(8,128)(2,1)S(1)}, bf16[528,512]{1,0:T(8,128)(2,1)S(1)}, u32[]{:S(2)}, u32[]{:S(2)}) collective-permute-start(bf16[528,512]{1,0:T(8,128)(2,1)S(1)} %pad_maximum_fusion.3.refs_2_), channel_id=1, source_target_pairs={{0,4},{2,6},{4,8},{6,10},{8,12},{10,14},{12,16},{14,18},{16,20},{1... | collective-permute-start | bytes 1622024 | tf_op jit(solution)/shard_map/ppermute | solution.py:386
  14.2 3.2 %collective-permute-start.1 = (bf16[528,512]{1,0:T(8,128)(2,1)S(1)}, bf16[528,512]{1,0:T(8,128)(2,1)S(1)}, u32[]{:S(2)}, u32[]{:S(2)}) collective-permute-start(bf16[528,512]{1,0:T(8,128)(2,1)S(1)} %pad_maximum_fusion.3.refs_2_), channel_id=1, source_target_pairs={{0,8},{2,10},{4,12},{6,14},{8,16},{10,18},{12,20},{14,22},{16,24},... | collective-permute-start | bytes 1622024 | tf_op jit(solution)/shard_map/ppermute | solution.py:386
  18.4 5.8 %product.3 = f32[256,1024]{1,0:T(8,128)} custom-call(s32[1]{0:T(128)} %bitcast.7.at_ref, bf16[256,5376]{1,0:T(8,128)(2,1)} %bitcast.29, bf16[2688,1024]{1,0:T(8,128)(2,1)} %w_ref.1), custom_call_target="tpu_custom_call" | custom-call | flops 1048576 | bytes 4096 | tf_op jit(solution)/shard_map/product/pallas_call | solution.py:290
  25.7 4.2 %pieces.1 = (bf16[1344,256]{1,0:T(8,128)(2,1)}, bf16[1344,256]{1,0:T(8,128)(2,1)}, bf16[1344,256]{1,0:T(8,128)(2,1)}, bf16[1344,256]{1,0:T(8,128)(2,1)}) custom-call(s32[2]{0:T(128)} %pad_add_fusion.at_ref, bf16[256,5376]{1,0:T(8,128)(2,1)} %bitcast.30), custom_call_target="tpu_custom_call" | custom-call | flops 1048576 | bytes 4096 | tf_op jit(solution)/shard_map/pieces/pallas_call | solution.py:260
  29.9 1.3 collective-permute-start.5
  31.2 1.9 collective-permute-done.4.refs_1_
  33.1 5.5 %product.2 = bf16[256,1024]{1,0:T(8,128)(2,1)} custom-call(s32[1]{0:T(128)} %constant.86.clone.1.at_ref, bf16[256,1280]{1,0:T(8,128)(2,1)} %collective-permute-done.3.refs_0_, bf16[256,1408]{1,0:T(8,128)(2,1)} %collective-permute-done.4.refs_1_, bf16[2688,1024]{1,0:T(8,128)(2,1)} %w_ref.1), custom_call_target="tpu_custom_call" | custom-call | flops 1048576 | bytes 4096 | tf_op jit(solution)/shard_map/product/pallas_call | solution.py:290
  38.7 1.2 collective-permute-start.7
  39.9 1.2 collective-permute-start.9
  42.4 4.8 %collective-permute-done.5 = bf16[1344,256]{1,0:T(8,128)(2,1)S(1)} collective-permute-done((bf16[1344,256]{1,0:T(8,128)(2,1)}, bf16[1344,256]{1,0:T(8,128)(2,1)S(1)}, u32[]{:S(2)}, u32[]{:S(2)}) %collective-permute-start.5) | collective-permute-done | bytes 688160 | tf_op jit(solution)/shard_map/ppermute | solution.py:430
  48.2 14.3 %probs.1 = (bf16[4,2,1280,512]{3,2,1,0:T(8,128)(2,1)}, f32[4,2,1,512]{3,2,1,0:T(1,128)}, bf16[4,2,128,512]{3,2,1,0:T(8,128)(2,1)}, bf16[512,512]{1,0:T(8,128)(2,...) custom-call(s32[1]{0:T(128)} %bitcast.core_ref, s32[1,512]{1,0:T(1,128)} %add_maximum_fusion.low_ref, ...), custom_call_target="tpu_custom_call" | custom-call | flops 1048576 | bytes 4096 | tf_op jit(solution)/shard_map/probs/pallas_call | solution.py:158
  62.5 1.3 collective-permute-start.11
  64.0 1.5 collective-permute-start.8
  65.6 1.2 pad_maximum_fusion
  66.9 1.9 collective-permute-start.10
  68.8 6.2 %collective-permute-done.11 = bf16[512,512]{1,0:T(8,128)(2,1)S(1)} collective-permute-done((bf16[512,512]{1,0:T(8,128)(2,1)}, bf16[512,512]{1,0:T(8,128)(2,1)S(1)}, u32[]{:S(2)}, u32[]{:S(2)}) %collective-permute-start.11) | collective-permute-done | bytes 524320 | tf_op jit(solution)/shard_map/ppermute | solution.py:430
  76.0 2.4 %collective-permute-start.13 = (bf16[512,512]{1,0:T(8,128)(2,1)}, bf16[512,512]{1,0:T(8,128)(2,1)}, u32[]{:S(2)}, u32[]{:S(2)}) collective-permute-start(bf16[512,512]{1,0:T(8,128)(2,1)} %fusion.1), channel_id=1, source_target_pairs={{8,0},{10,2},{12,4},{14,6},{16,8},{18,10},{20,12},{22,14},{24,16},... | collective-permute-start | bytes 1572872 | tf_op jit(solution)/shard_map/ppermute | solution.py:386
  78.4 1.3 collective-permute-start.21
  79.7 2.3 %collective-permute-done.10.refs_3_ = bf16[512,512]{1,0:T(8,128)(2,1)S(1)} collective-permute-done((bf16[512,512]{1,0:T(8,128)(2,1)S(1)}, bf16[512,512]{1,0:T(8,128)(2,1)S(1)}, u32[]{:S(2)}, u32[]{:S(2)}) %collective-permute-start.10) | collective-permute-done | bytes 524320 | tf_op jit(solution)/shard_map/ppermute | solution.py:386
  82.4 7.3 %collective-permute-done.13 = bf16[512,512]{1,0:T(8,128)(2,1)} collective-permute-done((bf16[512,512]{1,0:T(8,128)(2,1)}, bf16[512,512]{1,0:T(8,128)(2,1)}, u32[]{:S(2)}, u32[]{:S(2)}) %collective-permute-start.13) | collective-permute-done | bytes 524320 | tf_op jit(solution)/shard_map/ppermute | solution.py:386
  89.6 1.4 fusion.3.refs_4_
  91.1 1.3 collective-permute-start.14
  92.4 1.2 collective-permute-start.17
  95.3 16.0 %grads.1 = (bf16[256,2048]{1,0:T(8,128)(2,1)}, bf16[256,2048]{1,0:T(8,128)(2,1)}, bf16[2,256,1024]{2,1,0:T(8,128)(2,1)}, bf16[512,512]{1,0:T(8,128)(2,1)}, bf16[...) custom-call(s32[1]{0:T(128)} %bitcast.core_ref, bf16[4,2,1280,512]{3,2,1,0:T(8,128)(2,1)} %get-tuple-element.60.e_ref, ...), custom_call_target="tpu_custom_call" | custom-call | flops 1048576 | bytes 4096 | tf_op jit(solution)/shard_map/grads/pallas_call | solution.py:201
  111.3 7.9 %collective-permute-done.14.refs_6_ = bf16[512,512]{1,0:T(8,128)(2,1)S(1)} collective-permute-done((bf16[512,512]{1,0:T(8,128)(2,1)S(1)}, bf16[512,512]{1,0:T(8,128)(2,1)S(1)}, u32[]{:S(2)}, u32[]{:S(2)}) %collective-permute-start.14) | collective-permute-done | bytes 524320 | tf_op jit(solution)/shard_map/ppermute | solution.py:395
  119.4 6.3 %collective-permute-start.15 = (bf16[512,512]{1,0:T(8,128)(2,1)S(1)}, bf16[512,512]{1,0:T(8,128)(2,1)S(1)}, u32[]{:S(2)}, u32[]{:S(2)}) collective-permute-start(bf16[512,512]{1,0:T(8,128)(2,1)S(1)} %pad_maximum_fusion.6), channel_id=1, source_target_pairs={{0,2},{2,0},{4,6},{6,4},{8,10},{10,8},{12,14},{14,12},{16,18},{18,... | collective-permute-start | bytes 1572872 | tf_op jit(solution)/shard_map/ppermute | solution.py:390
  126.3 5.2 %collective-permute-done.17.refs_7_ = bf16[512,512]{1,0:T(8,128)(2,1)} collective-permute-done((bf16[512,512]{1,0:T(8,128)(2,1)S(1)}, bf16[512,512]{1,0:T(8,128)(2,1)}, u32[]{:S(2)}, u32[]{:S(2)}) %collective-permute-start.17) | collective-permute-done | bytes 524320 | tf_op jit(solution)/shard_map/ppermute | solution.py:405
  132.7 8.8 %tokens.1 = (bf16[256,5376]{1,0:T(8,128)(2,1)}, bf16[256,2688]{1,0:T(8,128)(2,1)}) custom-call(s32[1]{0:T(128)} %bitcast.7.at_ref, bf16[512,1024]{1,0:T(8,128)(2,1)} %copy-done.6, bf16[2688,1024]{1,0:T(8,128)(2,1)} %w_ref.1), custom_call_target="tpu_custom_call" | custom-call | flops 1048576 | bytes 4096 | tf_op jit(solution)/shard_map/tokens/pallas_call | solution.py:364
  141.5 3.3 %collective-permute-start.18 = (bf16[2,256,1024]{2,1,0:T(8,128)(2,1)}, bf16[2,256,1024]{2,1,0:T(8,128)(2,1)}, u32[]{:S(2)}, u32[]{:S(2)}) collective-permute-start(bf16[2,256,1024]{2,1,0:T(8,128)(2,1)} %get-tuple-element.86), channel_id=1, source_target_pairs={{0,2},{2,0},{4,6},{6,4},{8,10},{10,8},{12,14},{14,12},{16,18},{18,... | collective-permute-start | bytes 3145736 | tf_op jit(solution)/shard_map/ppermute | solution.py:390
  145.7 12.8 %collective-permute-done.19 = bf16[512,512]{1,0:T(8,128)(2,1)S(1)} collective-permute-done((bf16[512,512]{1,0:T(8,128)(2,1)}, bf16[512,512]{1,0:T(8,128)(2,1)S(1)}, u32[]{:S(2)}, u32[]{:S(2)}) %collective-permute-start.19) | collective-permute-done | bytes 524320 | tf_op jit(solution)/shard_map/ppermute | solution.py:430
  158.5 2.0 add_convert_fusion.1
  160.5 1.1 copy-done.13
  161.6 8.1 %weight.1 = (f32[336,512]{1,0:T(8,128)}, bf16[336,512]{1,0:T(8,128)(2,1)}, bf16[336,512]{1,0:T(8,128)(2,1)}, bf16[336,512]{1,0:T(8,128)(2,1)}) custom-call(s32[2]{0:T(128)} %pad_add_fusion.1.at_ref, bf16[1344,512]{1,0:T(8,128)(2,1)} %copy-done.7, bf16[1344,512]{1,0:T(8,128)(2,1)} %collective-permute-done.21.refs_1_, bf16[1344,512]{1,0:T(8,128)(2,1)} %copy-done.13, ...), custom_call_target="tpu_custom_call" | custom-call | flops 1048576 | bytes 4096 | tf_op jit(solution)/shard_map/weight/pallas_call | solution.py:336
  169.7 1.3 collective-permute-start.24
  171.0 1.1 collective-permute-start.27
  172.1 1.4 collective-permute-start.28
  173.5 1.2 collective-permute-start.26
  174.7 3.0 %collective-permute-start.20 = (bf16[512,512]{1,0:T(8,128)(2,1)}, bf16[512,512]{1,0:T(8,128)(2,1)S(1)}, u32[]{:S(2)}, u32[]{:S(2)}) collective-permute-start(bf16[512,512]{1,0:T(8,128)(2,1)} %add_convert_fusion.1), channel_id=1, source_target_pairs={{8,0},{10,2},{12,4},{14,6},{16,8},{18,10},{20,12},{22,14},{24,16},... | collective-permute-start | bytes 1572872 | tf_op jit(solution)/shard_map/ppermute | solution.py:386
  177.7 2.2 %slice_dynamic-update-slice_fusion = (bf16[1,256,2048]{2,1,0:T(8,128)(2,1)}, bf16[1,256,2048]{2,1,0:T(8,128)(2,1)}) fusion(bf16[1,256,2048]{2,1,0:T(8,128)(2,1)} %bitcast.37, s32[]{:T(128)S(6)} %select_n.107, bf16[2,256,1024]{2,1,0:T(8,128)(2,1)} %collective-permute-done.18, bf16[1,256,2048]{2,1,0:T(8,128)(2,1)} %bitcast.36), kind=kLoop, calls=%fused_computation.19 | loop fusion | bytes 2097156 | tf_op jit(solution)/shard_map/dynamic_update_slice | solution.py:615
  180.0 20.0 %collective-permute-done.27 = bf16[336,512]{1,0:T(8,128)(2,1)S(1)} collective-permute-done((bf16[336,512]{1,0:T(8,128)(2,1)}, bf16[336,512]{1,0:T(8,128)(2,1)S(1)}, u32[]{:S(2)}, u32[]{:S(2)}) %collective-permute-start.27) | collective-permute-done | bytes 344096 | tf_op jit(solution)/shard_map/ppermute | solution.py:603
  200.0 3.1 %collective-permute-done.28 = bf16[336,512]{1,0:T(8,128)(2,1)} collective-permute-done((bf16[336,512]{1,0:T(8,128)(2,1)}, bf16[336,512]{1,0:T(8,128)(2,1)}, u32[]{:S(2)}, u32[]{:S(2)}) %collective-permute-start.28) | collective-permute-done | bytes 344096 | tf_op jit(solution)/shard_map/ppermute | solution.py:603
  203.1 1.2 convert_add_fusion
  205.0 9.3 %collective-permute-done.20 = bf16[512,512]{1,0:T(8,128)(2,1)S(1)} collective-permute-done((bf16[512,512]{1,0:T(8,128)(2,1)}, bf16[512,512]{1,0:T(8,128)(2,1)S(1)}, u32[]{:S(2)}, u32[]{:S(2)}) %collective-permute-start.20) | collective-permute-done | bytes 524320 | tf_op jit(solution)/shard_map/ppermute | solution.py:386
  216.3 1.4 copy-done.25
  (120 shorter events, 18.7 us)
Async XLA Ops:
  0.7 8.4 %copy-start.1 = (bf16[1,256,2048]{2,1,0:T(8,128)(2,1)S(1)}, bf16[1,256,2048]{2,1,0:T(8,128)(2,1)}, u32[]{:S(2)}) copy-start(bf16[1,256,2048]{2,1,0:T(8,128)(2,1)} %param.7) | copy-start | bytes 3145732
  1.9 7.3 %copy-start.8 = (bf16[1,256,2048]{2,1,0:T(8,128)(2,1)S(1)}, bf16[1,256,2048]{2,1,0:T(8,128)(2,1)}, u32[]{:S(2)}) copy-start(bf16[1,256,2048]{2,1,0:T(8,128)(2,1)} %param.10) | copy-start | bytes 3145732
  1.9 28.0 %collective-permute-start.3 = (bf16[256,1280]{1,0:T(8,128)(2,1)S(1)}, bf16[256,1280]{1,0:T(8,128)(2,1)}, u32[]{:S(2)}, u32[]{:S(2)}) collective-permute-start(bf16[256,1280]{1,0:T(8,128)(2,1)S(1)} %dynamic-slice_bitcast_fusion.1), channel_id=1, source_target_pairs={{0,1},{1,0},{2,3},{3,2},{4,5},{5,4},{6,7},{7,6},{8,9},{9,8},{10,11... | collective-permute-start | bytes 1966088 | tf_op jit(solution)/shard_map/ppermute | solution.py:395
  4.0 1.9 copy-start.23
  5.9 3.4 %collective-permute-start = (bf16[272,512]{1,0:T(8,128)(2,1)}, bf16[272,512]{1,0:T(8,128)(2,1)}, u32[]{:S(2)}, u32[]{:S(2)}) collective-permute-start(bf16[272,512]{1,0:T(8,128)(2,1)} %maximum_maximum_fusion.1), channel_id=1, source_target_pairs={{0,2},{2,0},{4,6},{6,4},{8,10},{10,8},{12,14},{14,12},{16,18},{18,... | collective-permute-start | bytes 835592 | tf_op jit(solution)/shard_map/ppermute | solution.py:390
  8.8 24.3 %collective-permute-start.4 = (bf16[256,1408]{1,0:T(8,128)(2,1)}, bf16[256,1408]{1,0:T(8,128)(2,1)}, u32[]{:S(2)}, u32[]{:S(2)}) collective-permute-start(bf16[256,1408]{1,0:T(8,128)(2,1)} %dynamic-slice_bitcast_fusion), channel_id=1, source_target_pairs={{0,1},{1,0},{2,3},{3,2},{4,5},{5,4},{6,7},{7,6},{8,9},{9,8},{10,11... | collective-permute-start | bytes 2162696 | tf_op jit(solution)/shard_map/ppermute | solution.py:395
  11.0 13.2 %copy-start.2 = (bf16[528,512]{1,0:T(8,128)(2,1)}, bf16[528,512]{1,0:T(8,128)(2,1)S(1)}, u32[]{:S(2)}) copy-start(bf16[528,512]{1,0:T(8,128)(2,1)S(1)} %pad_maximum_fusion.3.refs_2_) | copy-start | bytes 1622020
  11.0 28.9 %collective-permute-start.2 = (bf16[528,512]{1,0:T(8,128)(2,1)S(1)}, bf16[528,512]{1,0:T(8,128)(2,1)S(1)}, u32[]{:S(2)}, u32[]{:S(2)}) collective-permute-start(bf16[528,512]{1,0:T(8,128)(2,1)S(1)} %pad_maximum_fusion.3.refs_2_), channel_id=1, source_target_pairs={{0,4},{2,6},{4,8},{6,10},{8,12},{10,14},{12,16},{14,18},{16,20},{1... | collective-permute-start | bytes 1622024 | tf_op jit(solution)/shard_map/ppermute | solution.py:386
  14.2 27.0 %collective-permute-start.1 = (bf16[528,512]{1,0:T(8,128)(2,1)S(1)}, bf16[528,512]{1,0:T(8,128)(2,1)S(1)}, u32[]{:S(2)}, u32[]{:S(2)}) collective-permute-start(bf16[528,512]{1,0:T(8,128)(2,1)S(1)} %pad_maximum_fusion.3.refs_2_), channel_id=1, source_target_pairs={{0,8},{2,10},{4,12},{6,14},{8,16},{10,18},{12,20},{14,22},{16,24},... | collective-permute-start | bytes 1622024 | tf_op jit(solution)/shard_map/ppermute | solution.py:386
  18.4 5.8 %copy-start.14 = (bf16[256,2048]{1,0:T(8,128)(2,1)S(1)}, bf16[256,2048]{1,0:T(8,128)(2,1)}, u32[]{:S(2)}) copy-start(bf16[256,2048]{1,0:T(8,128)(2,1)} %pad_maximum_fusion.1) | copy-start | bytes 3145732
  24.3 23.0 %collective-permute-start.6 = (bf16[256,2048]{1,0:T(8,128)(2,1)S(1)}, bf16[256,2048]{1,0:T(8,128)(2,1)S(1)}, u32[]{:S(2)}, u32[]{:S(2)}) collective-permute-start(bf16[256,2048]{1,0:T(8,128)(2,1)S(1)} %copy-done.14), channel_id=1, source_target_pairs={{0,2},{2,0},{4,6},{6,4},{8,10},{10,8},{12,14},{14,12},{16,18},{18,... | collective-permute-start | bytes 3145736 | tf_op jit(solution)/shard_map/ppermute | solution.py:390
  29.9 17.3 %collective-permute-start.5 = (bf16[1344,256]{1,0:T(8,128)(2,1)}, bf16[1344,256]{1,0:T(8,128)(2,1)S(1)}, u32[]{:S(2)}, u32[]{:S(2)}) collective-permute-start(bf16[1344,256]{1,0:T(8,128)(2,1)} %get-tuple-element.57), channel_id=1, source_target_pairs={{0,4},{2,6},{4,0},{6,2},{8,12},{10,14},{12,8},{14,10},{16,20},{18,... | collective-permute-start | bytes 2064392 | tf_op jit(solution)/shard_map/ppermute | solution.py:430
  38.7 25.2 %collective-permute-start.7 = (bf16[256,1024]{1,0:T(8,128)(2,1)}, bf16[256,1024]{1,0:T(8,128)(2,1)S(1)}, u32[]{:S(2)}, u32[]{:S(2)}) collective-permute-start(bf16[256,1024]{1,0:T(8,128)(2,1)} %product.2), channel_id=1, source_target_pairs={{0,1},{1,0},{2,3},{3,2},{4,5},{5,4},{6,7},{7,6},{8,9},{9,8},{10,11... | collective-permute-start | bytes 1572872 | tf_op jit(solution)/shard_map/ppermute | solution.py:395
  39.9 7.3 %copy-start.9 = (bf16[528,512]{1,0:T(8,128)(2,1)}, bf16[528,512]{1,0:T(8,128)(2,1)S(1)}, u32[]{:S(2)}) copy-start(bf16[528,512]{1,0:T(8,128)(2,1)S(1)} %collective-permute-done.2.refs_1_) | copy-start | bytes 1622020
  39.9 27.0 %collective-permute-start.9 = (bf16[1344,256]{1,0:T(8,128)(2,1)}, bf16[1344,256]{1,0:T(8,128)(2,1)S(1)}, u32[]{:S(2)}, u32[]{:S(2)}) collective-permute-start(bf16[1344,256]{1,0:T(8,128)(2,1)} %get-tuple-element.67), channel_id=1, source_target_pairs={{0,4},{2,6},{4,0},{6,2},{8,12},{10,14},{12,8},{14,10},{16,20},{18,... | collective-permute-start | bytes 2064392 | tf_op jit(solution)/shard_map/ppermute | solution.py:430
  41.1 6.1 %copy-start.10 = (bf16[528,512]{1,0:T(8,128)(2,1)}, bf16[528,512]{1,0:T(8,128)(2,1)S(1)}, u32[]{:S(2)}) copy-start(bf16[528,512]{1,0:T(8,128)(2,1)S(1)} %collective-permute-done.1.refs_0_) | copy-start | bytes 1622020
  48.2 15.6 %copy-start.5 = (f32[256,1024]{1,0:T(8,128)S(1)}, f32[256,1024]{1,0:T(8,128)}, u32[]{:S(2)}) copy-start(f32[256,1024]{1,0:T(8,128)} %product.3) | copy-start | bytes 3145732
  62.5 3.1 %copy-start.16 = (bf16[1344,256]{1,0:T(8,128)(2,1)S(1)}, bf16[1344,256]{1,0:T(8,128)(2,1)}, u32[]{:S(2)}) copy-start(bf16[1344,256]{1,0:T(8,128)(2,1)} %get-tuple-element.68) | copy-start | bytes 2064388
  62.5 12.5 %collective-permute-start.11 = (bf16[512,512]{1,0:T(8,128)(2,1)}, bf16[512,512]{1,0:T(8,128)(2,1)S(1)}, u32[]{:S(2)}, u32[]{:S(2)}) collective-permute-start(bf16[512,512]{1,0:T(8,128)(2,1)} %get-tuple-element.64), channel_id=1, source_target_pairs={{0,4},{2,6},{4,0},{6,2},{8,12},{10,14},{12,8},{14,10},{16,20},{18,... | collective-permute-start | bytes 1572872 | tf_op jit(solution)/shard_map/ppermute | solution.py:430
  64.0 11.0 %copy-start.22 = (bf16[512,512]{1,0:T(8,128)(2,1)S(1)}, bf16[512,512]{1,0:T(8,128)(2,1)}, u32[]{:S(2)}) copy-start(bf16[512,512]{1,0:T(8,128)(2,1)} %get-tuple-element.71) | copy-start | bytes 1572868
  64.0 2.8 %collective-permute-start.8 = (bf16[256,512]{1,0:T(8,128)(2,1)S(1)}, bf16[256,512]{1,0:T(8,128)(2,1)S(1)}, u32[]{:S(2)}, u32[]{:S(2)}) collective-permute-start(bf16[256,512]{1,0:T(8,128)(2,1)S(1)} %get-tuple-element.113), channel_id=1, source_target_pairs={{0,2},{2,0},{4,6},{6,4},{8,10},{10,8},{12,14},{14,12},{16,18},{18,... | collective-permute-start | bytes 786440 | tf_op jit(solution)/shard_map/ppermute | solution.py:390
  66.9 24.2 %copy-start.3 = (bf16[512,512]{1,0:T(8,128)(2,1)}, bf16[512,512]{1,0:T(8,128)(2,1)S(1)}, u32[]{:S(2)}) copy-start(bf16[512,512]{1,0:T(8,128)(2,1)S(1)} %constant_dynamic-update-slice_fusion.2.refs_5_) | copy-start | bytes 1572868
  66.9 15.1 %collective-permute-start.10 = (bf16[512,512]{1,0:T(8,128)(2,1)S(1)}, bf16[512,512]{1,0:T(8,128)(2,1)S(1)}, u32[]{:S(2)}, u32[]{:S(2)}) collective-permute-start(bf16[512,512]{1,0:T(8,128)(2,1)S(1)} %constant_dynamic-update-slice_fusion.2.refs_5_), channel_id=1, source_target_pairs={{0,8},{2,10},{4,12},{6,14},{8,16},{10,18},{12,20},{14,22},{16,24},... | collective-permute-start | bytes 1572872 | tf_op jit(solution)/shard_map/ppermute | solution.py:386
  76.0 16.4 %copy-start.15 = (bf16[1344,256]{1,0:T(8,128)(2,1)S(1)}, bf16[1344,256]{1,0:T(8,128)(2,1)}, u32[]{:S(2)}) copy-start(bf16[1344,256]{1,0:T(8,128)(2,1)} %get-tuple-element.92) | copy-start | bytes 2064388
  76.0 13.6 %collective-permute-start.13 = (bf16[512,512]{1,0:T(8,128)(2,1)}, bf16[512,512]{1,0:T(8,128)(2,1)}, u32[]{:S(2)}, u32[]{:S(2)}) collective-permute-start(bf16[512,512]{1,0:T(8,128)(2,1)} %fusion.1), channel_id=1, source_target_pairs={{8,0},{10,2},{12,4},{14,6},{16,8},{18,10},{20,12},{22,14},{24,16},... | collective-permute-start | bytes 1572872 | tf_op jit(solution)/shard_map/ppermute | solution.py:386
  78.4 47.8 %collective-permute-start.21 = (bf16[1344,512]{1,0:T(8,128)(2,1)}, bf16[1344,512]{1,0:T(8,128)(2,1)}, u32[]{:S(2)}, u32[]{:S(2)}) collective-permute-start(bf16[1344,512]{1,0:T(8,128)(2,1)} %pad_maximum_fusion), channel_id=1, source_target_pairs={{0,1},{1,0},{2,3},{3,2},{4,5},{5,4},{6,7},{7,6},{8,9},{9,8},{10,11... | collective-permute-start | bytes 4128776 | tf_op jit(solution)/shard_map/ppermute | solution.py:395
  82.0 10.4 %copy-start.11 = (bf16[512,512]{1,0:T(8,128)(2,1)}, bf16[512,512]{1,0:T(8,128)(2,1)S(1)}, u32[]{:S(2)}) copy-start(bf16[512,512]{1,0:T(8,128)(2,1)S(1)} %collective-permute-done.10.refs_3_) | copy-start | bytes 1572868
  82.1 12.5 %collective-permute-start.12 = (bf16[512,512]{1,0:T(8,128)(2,1)S(1)}, bf16[512,512]{1,0:T(8,128)(2,1)S(1)}, u32[]{:S(2)}, u32[]{:S(2)}) collective-permute-start(bf16[512,512]{1,0:T(8,128)(2,1)S(1)} %broadcast_select_fusion), channel_id=1, source_target_pairs={{0,4},{2,6},{4,0},{6,2},{8,12},{10,14},{12,8},{14,10},{16,20},{18,... | collective-permute-start | bytes 1572872 | tf_op jit(solution)/shard_map/ppermute | solution.py:430
  91.1 28.2 %copy-start.4 = (bf16[512,512]{1,0:T(8,128)(2,1)}, bf16[512,512]{1,0:T(8,128)(2,1)S(1)}, u32[]{:S(2)}) copy-start(bf16[512,512]{1,0:T(8,128)(2,1)S(1)} %fusion.3.refs_4_) | copy-start | bytes 1572868
  91.1 28.2 %collective-permute-start.14 = (bf16[512,512]{1,0:T(8,128)(2,1)S(1)}, bf16[512,512]{1,0:T(8,128)(2,1)S(1)}, u32[]{:S(2)}, u32[]{:S(2)}) collective-permute-start(bf16[512,512]{1,0:T(8,128)(2,1)S(1)} %fusion.3.refs_4_), channel_id=1, source_target_pairs={{0,1},{1,0},{2,3},{3,2},{4,5},{5,4},{6,7},{7,6},{8,9},{9,8},{10,11... | collective-permute-start | bytes 1572872 | tf_op jit(solution)/shard_map/ppermute | solution.py:395
  92.4 39.1 %collective-permute-start.17 = (bf16[512,512]{1,0:T(8,128)(2,1)S(1)}, bf16[512,512]{1,0:T(8,128)(2,1)}, u32[]{:S(2)}, u32[]{:S(2)}) collective-permute-start(bf16[512,512]{1,0:T(8,128)(2,1)S(1)} %fusion.3.refs_4_), channel_id=1, source_target_pairs={{0,5},{1,4},{2,7},{3,6},{4,1},{5,0},{6,3},{7,2},{8,13},{9,12},{10,... | collective-permute-start | bytes 1572872 | tf_op jit(solution)/shard_map/ppermute | solution.py:405
  93.7 37.8 %collective-permute-start.16 = (bf16[512,512]{1,0:T(8,128)(2,1)S(1)}, bf16[512,512]{1,0:T(8,128)(2,1)}, u32[]{:S(2)}, u32[]{:S(2)}) collective-permute-start(bf16[512,512]{1,0:T(8,128)(2,1)S(1)} %fusion.3.refs_4_), channel_id=1, source_target_pairs={{0,4},{1,5},{2,6},{3,7},{4,0},{5,1},{6,2},{7,3},{8,12},{9,13},{10,... | collective-permute-start | bytes 1572872 | tf_op jit(solution)/shard_map/ppermute | solution.py:405
  119.2 6.4 %copy-start.12 = (bf16[512,512]{1,0:T(8,128)(2,1)}, bf16[512,512]{1,0:T(8,128)(2,1)S(1)}, u32[]{:S(2)}) copy-start(bf16[512,512]{1,0:T(8,128)(2,1)S(1)} %collective-permute-done.14.refs_6_) | copy-start | bytes 1572868
  119.4 12.3 %collective-permute-start.15 = (bf16[512,512]{1,0:T(8,128)(2,1)S(1)}, bf16[512,512]{1,0:T(8,128)(2,1)S(1)}, u32[]{:S(2)}, u32[]{:S(2)}) collective-permute-start(bf16[512,512]{1,0:T(8,128)(2,1)S(1)} %pad_maximum_fusion.6), channel_id=1, source_target_pairs={{0,2},{2,0},{4,6},{6,4},{8,10},{10,8},{12,14},{14,12},{16,18},{18,... | collective-permute-start | bytes 1572872 | tf_op jit(solution)/shard_map/ppermute | solution.py:390
  125.7 15.8 %copy-start.7 = (bf16[1344,512]{1,0:T(8,128)(2,1)}, bf16[1344,512]{1,0:T(8,128)(2,1)S(1)}, u32[]{:S(2)}) copy-start(bf16[1344,512]{1,0:T(8,128)(2,1)S(1)} %constant_dynamic-update-slice_fusion.4.refs_0_) | copy-start | bytes 4128772
  125.7 34.8 %collective-permute-start.22 = (bf16[1344,512]{1,0:T(8,128)(2,1)S(1)}, bf16[1344,512]{1,0:T(8,128)(2,1)S(1)}, u32[]{:S(2)}, u32[]{:S(2)}) collective-permute-start(bf16[1344,512]{1,0:T(8,128)(2,1)S(1)} %constant_dynamic-update-slice_fusion.4.refs_0_), channel_id=1, source_target_pairs={{0,2},{2,0},{4,6},{6,4},{8,10},{10,8},{12,14},{14,12},{16,18},{18,... | collective-permute-start | bytes 4128776 | tf_op jit(solution)/shard_map/ppermute | solution.py:390
  126.2 34.3 %collective-permute-start.23 = (bf16[1344,512]{1,0:T(8,128)(2,1)}, bf16[1344,512]{1,0:T(8,128)(2,1)}, u32[]{:S(2)}, u32[]{:S(2)}) collective-permute-start(bf16[1344,512]{1,0:T(8,128)(2,1)} %collective-permute-done.21.refs_1_), channel_id=1, source_target_pairs={{0,2},{2,0},{4,6},{6,4},{8,10},{10,8},{12,14},{14,12},{16,18},{18,... | collective-permute-start | bytes 4128776 | tf_op jit(solution)/shard_map/ppermute | solution.py:390
  141.5 33.2 %collective-permute-start.18 = (bf16[2,256,1024]{2,1,0:T(8,128)(2,1)}, bf16[2,256,1024]{2,1,0:T(8,128)(2,1)}, u32[]{:S(2)}, u32[]{:S(2)}) collective-permute-start(bf16[2,256,1024]{2,1,0:T(8,128)(2,1)} %get-tuple-element.86), channel_id=1, source_target_pairs={{0,2},{2,0},{4,6},{6,4},{8,10},{10,8},{12,14},{14,12},{16,18},{18,... | collective-permute-start | bytes 3145736 | tf_op jit(solution)/shard_map/ppermute | solution.py:390
  144.8 13.7 %collective-permute-start.19 = (bf16[512,512]{1,0:T(8,128)(2,1)}, bf16[512,512]{1,0:T(8,128)(2,1)S(1)}, u32[]{:S(2)}, u32[]{:S(2)}) collective-permute-start(bf16[512,512]{1,0:T(8,128)(2,1)} %get-tuple-element.79), channel_id=1, source_target_pairs={{0,4},{2,6},{4,0},{6,2},{8,12},{10,14},{12,8},{14,10},{16,20},{18,... | collective-permute-start | bytes 1572872 | tf_op jit(solution)/shard_map/ppermute | solution.py:430
  169.7 33.3 %copy-start.17 = (f32[336,512]{1,0:T(8,128)S(1)}, f32[336,512]{1,0:T(8,128)}, u32[]{:S(2)}) copy-start(f32[336,512]{1,0:T(8,128)} %get-tuple-element.100) | copy-start | bytes 2064388
  169.7 10.2 %collective-permute-start.24 = (bf16[336,512]{1,0:T(8,128)(2,1)}, bf16[336,512]{1,0:T(8,128)(2,1)S(1)}, u32[]{:S(2)}, u32[]{:S(2)}) collective-permute-start(bf16[336,512]{1,0:T(8,128)(2,1)} %get-tuple-element.97), channel_id=1, source_target_pairs={{0,8},{2,10},{4,12},{6,14},{8,16},{10,18},{12,20},{14,22},{16,24},... | collective-permute-start | bytes 1032200 | tf_op jit(solution)/shard_map/ppermute | solution.py:603
  171.0 29.0 %collective-permute-start.27 = (bf16[336,512]{1,0:T(8,128)(2,1)}, bf16[336,512]{1,0:T(8,128)(2,1)S(1)}, u32[]{:S(2)}, u32[]{:S(2)}) collective-permute-start(bf16[336,512]{1,0:T(8,128)(2,1)} %get-tuple-element.101), channel_id=1, source_target_pairs={{0,16},{2,18},{4,20},{6,22},{8,24},{10,26},{12,28},{14,30},{16,0},... | collective-permute-start | bytes 1032200 | tf_op jit(solution)/shard_map/ppermute | solution.py:603
  172.1 31.0 %collective-permute-start.28 = (bf16[336,512]{1,0:T(8,128)(2,1)}, bf16[336,512]{1,0:T(8,128)(2,1)}, u32[]{:S(2)}, u32[]{:S(2)}) collective-permute-start(bf16[336,512]{1,0:T(8,128)(2,1)} %get-tuple-element.102), channel_id=1, source_target_pairs={{0,24},{2,26},{4,28},{6,30},{8,0},{10,2},{12,4},{14,6},{16,8},{18,... | collective-permute-start | bytes 1032200 | tf_op jit(solution)/shard_map/ppermute | solution.py:603
  173.5 41.7 %collective-permute-start.26 = (bf16[256,2688]{1,0:T(8,128)(2,1)}, bf16[256,2688]{1,0:T(8,128)(2,1)S(1)}, u32[]{:S(2)}, u32[]{:S(2)}) collective-permute-start(bf16[256,2688]{1,0:T(8,128)(2,1)} %get-tuple-element.85), channel_id=1, source_target_pairs={{0,1},{1,0},{2,3},{3,2},{4,5},{5,4},{6,7},{7,6},{8,9},{9,8},{10,11... | collective-permute-start | bytes 4128776 | tf_op jit(solution)/shard_map/ppermute | solution.py:395
  174.7 39.5 %collective-permute-start.20 = (bf16[512,512]{1,0:T(8,128)(2,1)}, bf16[512,512]{1,0:T(8,128)(2,1)S(1)}, u32[]{:S(2)}, u32[]{:S(2)}) collective-permute-start(bf16[512,512]{1,0:T(8,128)(2,1)} %add_convert_fusion.1), channel_id=1, source_target_pairs={{8,0},{10,2},{12,4},{14,6},{16,8},{18,10},{20,12},{22,14},{24,16},... | collective-permute-start | bytes 1572872 | tf_op jit(solution)/shard_map/ppermute | solution.py:386
  180.0 34.3 %copy-start.19 = (bf16[512,512]{1,0:T(8,128)(2,1)S(1)}, bf16[512,512]{1,0:T(8,128)(2,1)}, u32[]{:S(2)}) copy-start(bf16[512,512]{1,0:T(8,128)(2,1)} %get-tuple-element.88) | copy-start | bytes 1572868
  204.3 12.0 %collective-permute-start.29 = (f32[168,512]{1,0:T(8,128)S(1)}, f32[168,512]{1,0:T(8,128)S(1)}, u32[]{:S(2)}, u32[]{:S(2)}) collective-permute-start(f32[168,512]{1,0:T(8,128)S(1)} %get-tuple-element.105), channel_id=1, source_target_pairs={{0,2},{2,0},{4,6},{6,4},{8,10},{10,8},{12,14},{14,12},{16,18},{18,... | collective-permute-start | bytes 1032200 | tf_op jit(solution)/shard_map/ppermute | solution.py:390
  214.5 1.7 collective-permute-start.25
  (8 other events, 10.6 us)

commit v6 on v5

--- a/solution.py
+++ b/solution.py
@@ -282,7 +282,7 @@
 def run_product(at, parts, w, kind):
     rows = parts[0].shape[0]
     depth, width = w.shape
-    tile = 256
+    tile = 512
     if len(parts) == 1:
         x_specs = [pl.BlockSpec((rows, depth), lambda j, at: (0, at[0]))]
     else:
@@ -359,7 +359,7 @@
 def run_tokens(at, dv_rows, w, n_fsdp):
     slab, width = w.shape
     rows = dv_rows.shape[0] // n_fsdp
-    tile = 3 * HD if slab % (3 * HD) == 0 else slab
+    tile = slab // 3 if slab % (3 * HD) == 0 else slab
     n_tiles = slab // tile
     return pl.pallas_call(
         functools.partial(tokens_kernel, n_fsdp),
@@ -504,7 +504,7 @@
     q_sent = jnp.concatenate([cols(queries[0], 1 - core, half_q), cols(d_out[0], 1 - core, half_q)], 1)
     q_other = swapped(after(q_sent, k_own))
     if aligned:
-        value_own = run_product(after(fsdp_arg, q_sent), [tokens], w_value, F32)
+        value_own = run_product(after(fsdp_arg, q_sent, *pieces), [tokens], w_value, F32)
     else:
         value_own = dot(cols(tokens, my_fsdp, slab), w_value)
     keys = [k_far, k_near, k_own]
@@ -527,7 +527,9 @@
     dv_got = flipped(dv_near)
 
     value_back = [rotated(x, -s - 1) for s, x in enumerate(partial)]
-    *value_back, _ = lax.optimization_barrier((*value_back, dv_near))
+    over_fsdp = {s: rotated(after(by_place[0, s], sent), s) for s in range(1, n_fsdp)}
+    value_back = [after(x, dv_near) for x in value_back]
+    value_back[0] = after(value_back[0], over_fsdp)
     value_sum = value_own
     for x in value_back:
         value_sum = value_sum + x.astype(F32)
@@ -535,14 +537,11 @@
     v_own = placed(core, cols(own_values, core, half_kv), swapped(cols(own_values, 1 - core, half_kv)), 0)
 
     over_y[0] = flipped(after(by_place[1, 0], k_near))
-    both_y = [
-        after(jnp.concatenate([by_place[0, s], over_y[s]], 1), own_values) for s in range(1, n_fsdp)
-    ]
-    v_own, over_y[0], both_y = lax.optimization_barrier((v_own, over_y[0], both_y))
+    v_own, over_y[0] = lax.optimization_barrier((v_own, over_y[0]))
     v_far = shifted(v_own, 4)
     own_pairs = [jnp.concatenate([by_place[0, 0], over_y[0]], 1)]
     other_pairs = [swapped(after(own_pairs[0], v_own))]
-    own_pairs += [rotated(x, s + 1) for s, x in enumerate(both_y)]
+    relayed_y = {s: rotated(after(over_y[s], own_values), s) for s in range(1, n_fsdp)}
 
     dv_got = after(dv_got, v_own)
     dv_sent = relayed(my_y, dv_far, dv_got)
@@ -553,14 +552,15 @@
     dv_chip = gathered_terms(my_y, dv_mine, dv_got, after(dv_back, v_sent))
     dv_fsdp = [dv_chip] + [rotated(dv_chip, s) for s in range(1, n_fsdp)]
     dv_over_y = [moved(dv_chip, 1, s) for s in range(n_fsdp)]
+    for s in range(1, n_fsdp):
+        own_pairs.append(jnp.concatenate([over_fsdp[s], after(relayed_y[s], dv_chip)], 1))
+        other_pairs.append(swapped(own_pairs[s]))
     v_near = after(v_near, dv_chip)
     vals = [v_far, v_near, v_own]
     out, dq, other, dk_far, dk_near, dk_mine = run_grads(
         core_arg, e, inv, do_t, queries[0], q_other, keys, vals, chip_rows, half_kv
     )
-    dk_got = flipped(dk_near)
-    own_pairs[1:] = [after(x, dk_near) for x in own_pairs[1:]]
-    other_pairs += [swapped(x) for x in own_pairs[1:]]
+    dk_back = [shifted(dk_near, -2), shifted(dk_far, -4)]
 
     dv_fsdp = [after(x, dk_near) for x in dv_fsdp]
     dv_over_y = [after(x, dk_near) for x in dv_over_y]
@@ -580,12 +580,9 @@
         back = rotated(made[s - 1], -s)
         d_tokens = lax.dynamic_update_slice_in_dim(d_tokens, back, ((my_fsdp + s) % n_fsdp) * slab, 1)
 
-    dk_sent = relayed(my_y, dk_far, after(dk_got, *made))
-    dk_back = shifted(dk_sent, -4)
-
     dv_pairs = list(zip(dv_fsdp, dv_over_y))
     if out_rows % 8 == 0:
-        at = after(jnp.stack([core, my_z]).astype(jnp.int32), dk_sent)
+        at = after(jnp.stack([core, my_z]).astype(jnp.int32), *made)
         by_z = run_weight(at, own_pairs, other_pairs, dv_pairs, n_z)
     else:
         weight_term = 0.0
@@ -599,6 +596,7 @@
             lax.dynamic_index_in_dim(weight_term, (my_z + d) % n_z, 0, keepdims=False).astype(BF16 if d else F32)
             for d in range(n_z)
         ]
+    by_z, dk_back = lax.optimization_barrier((list(by_z), dk_back))
     over_z = [
         lax.ppermute(by_z[d], "ctx", [(i, (i + 4 * d) % n_ctx) for i in range(n_ctx)]) for d in range(1, n_z)
     ]
@@ -608,7 +606,7 @@
         row_sum = row_sum + x.astype(F32)
     d_weight = placed(core, rows_of(row_sum, core, out_rows), swapped(rows_of(row_sum, 1 - core, out_rows)), 1)
 
-    dk_chip = gathered_terms(my_y, dk_mine, dk_got, after(dk_back, *over_z[:1]))
+    dk_chip = (dk_mine.astype(F32) + dk_back[0].astype(F32) + dk_back[1].astype(F32)).astype(BF16)
     d_keys = placed(core, rows_of(dk_chip, core, shard_rows), swapped(rows_of(dk_chip, 1 - core, shard_rows)), 1)
     other = swapped(after(other, *made))
     out = lax.dynamic_update_slice_in_dim(out, other[0], (1 - core) * half_q, 1)

time: 219 us -> 187 us (0.85)
  waiting for transfers between devices: 81.5 us -> 46.7 us
  starting transfers between devices: 44.6 us -> 58.3 us
  other arithmetic: 13.2 us -> 6.6 us
  Pallas kernels: 62.7 us -> 59.2 us
    ppermute x5 -> x4, waiting for transfers between devices: 24.5 us -> 6.11 us  [flipped(): lax.ppermute(x, 'ctx', [(i, i ^ 2) for i in range(lax.axis_size('ctx'))])]
    ppermute x5 -> x6, waiting for transfers between devices: 18.8 us -> 7.99 us  [shifted(): lax.ppermute(x, 'ctx', [(i, i + by) for i in range(length) if 0 <= i + by...]
    ppermute x9, starting transfers between devices: 14.7 us -> 21.8 us  [swapped(): lax.ppermute(x, 'ctx', [(i, i ^ 1) for i in range(lax.axis_size('ctx'))])]
    ppermute x2, waiting for transfers between devices: 5.21 us -> 0.01 us  [moved(): return lax.ppermute(x, ('ctx', 'fsdp'), pairs)]
    ppermute x3, starting transfers between devices: 3.76 us -> 6.81 us  [shards(): lax.ppermute(by_z[d], 'ctx', [(i, (i + 4 * d) % n_ctx) for i in range(n_c...]
    convert_element_type x2 -> x1, other arithmetic: 2.94 us -> 0.16 us  [relayed(): (far.astype(F32) + jnp.where(my_y == 1, got.astype(F32), 0.0)).astype(BF16)]
    ppermute x3, waiting for transfers between devices: 23.1 us -> 20.5 us  [shards(): lax.ppermute(by_z[d], 'ctx', [(i, (i + 4 * d) % n_ctx) for i in range(n_c...]
    ppermute x5 -> x6, starting transfers between devices: 13.7 us -> 15.8 us  [shifted(): lax.ppermute(x, 'ctx', [(i, i + by) for i in range(length) if 0 <= i + by...]
  transfers between devices with their start and end apart: 30 -> 31, of which waited for: 12 -> 10; matrix products, arithmetic and copies ran while one was open for 9% -> 7% of each run, Pallas kernels for 29% -> 32%
where the time goes in v6:
time: 187 us; the launch traced here: 186 us
  Pallas kernels  59.2 us (32%)
  starting transfers between devices  58.3 us (31%)
  waiting for transfers between devices  46.7 us (25%)
  local copies, waits for them, and re-layouts  13.2 us (7%)
  other arithmetic  6.6 us (4%)
    ppermute x9, starting transfers between devices, swapped(): lax.ppermute(x, 'ctx', [(i, i ^ 1) for i in range(lax.axis_size('ctx'))])  21.8 us
    ppermute x3, waiting for transfers between devices, shards(): lax.ppermute(by_z[d], 'ctx', [(i, (i + 4 * d) % n_ctx) for i in range(n_c...  20.5 us
    pallas_call x1, Pallas kernels, run_grads(): pl.pallas_call(functools.partial(grads_kernel, blk, n_arr - 1), grid_spec...  16 us
    ppermute x6, starting transfers between devices, shifted(): lax.ppermute(x, 'ctx', [(i, i + by) for i in range(length) if 0 <= i + by...  15.8 us
    pallas_call x1, Pallas kernels, run_probs(): pl.pallas_call(functools.partial(probs_kernel, blk, n_arr - 1), grid_spec...  14.3 us
    ppermute x7, waiting for transfers between devices, rotated(): lax.ppermute(x, 'fsdp', [(i, (i + by) % length) for i in range(length)])  10.9 us
    pallas_call x2, Pallas kernels, run_product(): pl.pallas_call(product_kernel, grid_spec=pltpu.PrefetchScalarGridSpec(num...  9.53 us
    pallas_call x1, Pallas kernels, run_weight(): pl.pallas_call(functools.partial(weight_kernel, n_z, n), grid_spec=pltpu....  8.14 us
  transfers between devices with their start and end apart: 31, of which 10 were waited for; matrix products, arithmetic and copies ran while one was open for 7% of the time, Pallas kernels for 32%

profile of v6, /device:TPU:9, one launch (start us, length us, event | category | flops | bytes accessed | tf_op | source)
XLA Modules:
  0.0 185.5 jit_solution(8611303543354731142)
XLA Ops:
  0.7 2.0 %dynamic-slice_bitcast_fusion.1 = bf16[256,1280]{1,0:T(8,128)(2,1)} fusion(bf16[1,256,5376]{2,1,0:T(8,128)(2,1)} %param.6, s32[]{:T(128)S(6)} %select_n.94), kind=kLoop, calls=%fused_computation.15 | loop fusion | bytes 1310724 | tf_op jit(solution)/shard_map/dynamic_slice | solution.py:469
  2.6 1.2 collective-permute-start.3
  4.6 1.1 dynamic-slice_bitcast_fusion.5
  5.8 1.0 collective-permute-start
  6.9 2.0 %dynamic-slice_bitcast_fusion = bf16[256,1408]{1,0:T(8,128)(2,1)} fusion(bf16[1,256,5376]{2,1,0:T(8,128)(2,1)} %param.6, s32[]{:T(128)S(6)} %select_n.97), kind=kLoop, calls=%fused_computation.12 | loop fusion | bytes 1441796 | tf_op jit(solution)/shard_map/dynamic_slice | solution.py:469
  9.4 3.1 %collective-permute-start.2 = (bf16[528,512]{1,0:T(8,128)(2,1)S(1)}, bf16[528,512]{1,0:T(8,128)(2,1)S(1)}, u32[]{:S(2)}, u32[]{:S(2)}) collective-permute-start(bf16[528,512]{1,0:T(8,128)(2,1)S(1)} %pad_maximum_fusion.2.refs_2_), channel_id=1, source_target_pairs={{0,4},{2,6},{4,8},{6,10},{8,12},{10,14},{12,16},{14,18},{16,20},{1... | collective-permute-start | bytes 1622024 | tf_op jit(solution)/shard_map/ppermute | solution.py:386
  12.6 3.2 %collective-permute-start.1 = (bf16[528,512]{1,0:T(8,128)(2,1)S(1)}, bf16[528,512]{1,0:T(8,128)(2,1)S(1)}, u32[]{:S(2)}, u32[]{:S(2)}) collective-permute-start(bf16[528,512]{1,0:T(8,128)(2,1)S(1)} %pad_maximum_fusion.2.refs_2_), channel_id=1, source_target_pairs={{0,8},{2,10},{4,12},{6,14},{8,16},{10,18},{12,20},{14,22},{16,24},... | collective-permute-start | bytes 1622024 | tf_op jit(solution)/shard_map/ppermute | solution.py:386
  15.9 1.1 collective-permute-start.6
  17.6 4.2 %pieces.1 = (bf16[1344,256]{1,0:T(8,128)(2,1)}, bf16[1344,256]{1,0:T(8,128)(2,1)}, bf16[1344,256]{1,0:T(8,128)(2,1)}, bf16[1344,256]{1,0:T(8,128)(2,1)}) custom-call(s32[2]{0:T(128)} %pad_add_fusion.at_ref, bf16[256,5376]{1,0:T(8,128)(2,1)} %bitcast.29), custom_call_target="tpu_custom_call" | custom-call | flops 1048576 | bytes 4096 | tf_op jit(solution)/shard_map/pieces/pallas_call | solution.py:260
  21.7 4.9 %product.3 = f32[256,1024]{1,0:T(8,128)} custom-call(s32[1]{0:T(128)} %bitcast.7.at_ref, bf16[256,5376]{1,0:T(8,128)(2,1)} %bitcast.30, bf16[2688,1024]{1,0:T(8,128)(2,1)} %w_ref.1), custom_call_target="tpu_custom_call" | custom-call | flops 1048576 | bytes 4096 | tf_op jit(solution)/shard_map/product/pallas_call | solution.py:290
  26.6 1.3 collective-permute-start.5
  27.9 6.1 %collective-permute-done.4.refs_1_ = bf16[256,1408]{1,0:T(8,128)(2,1)} collective-permute-done((bf16[256,1408]{1,0:T(8,128)(2,1)}, bf16[256,1408]{1,0:T(8,128)(2,1)}, u32[]{:S(2)}, u32[]{:S(2)}) %collective-permute-start.4) | collective-permute-done | bytes 720928 | tf_op jit(solution)/shard_map/ppermute | solution.py:395
  34.0 4.7 %product.2 = bf16[256,1024]{1,0:T(8,128)(2,1)} custom-call(s32[1]{0:T(128)} %constant.86.clone.1.at_ref, bf16[256,1280]{1,0:T(8,128)(2,1)} %collective-permute-done.3.refs_0_, bf16[256,1408]{1,0:T(8,128)(2,1)} %collective-permute-done.4.refs_1_, bf16[2688,1024]{1,0:T(8,128)(2,1)} %w_ref.1), custom_call_target="tpu_custom_call" | custom-call | flops 1048576 | bytes 4096 | tf_op jit(solution)/shard_map/product/pallas_call | solution.py:290
  38.7 1.2 collective-permute-start.7
  40.2 1.3 collective-permute-start.10
  42.7 1.3 collective-permute-done.5
  45.0 14.3 %probs.1 = (bf16[4,2,1280,512]{3,2,1,0:T(8,128)(2,1)}, f32[4,2,1,512]{3,2,1,0:T(1,128)}, bf16[4,2,128,512]{3,2,1,0:T(8,128)(2,1)}, bf16[512,512]{1,0:T(8,128)(2,...) custom-call(s32[1]{0:T(128)} %bitcast.core_ref, s32[1,512]{1,0:T(1,128)} %add_maximum_fusion.low_ref, ...), custom_call_target="tpu_custom_call" | custom-call | flops 1048576 | bytes 4096 | tf_op jit(solution)/shard_map/probs/pallas_call | solution.py:158
  59.4 1.3 collective-permute-start.12
  60.7 4.8 %collective-permute-done.8 = bf16[1344,256]{1,0:T(8,128)(2,1)S(1)} collective-permute-done((bf16[1344,256]{1,0:T(8,128)(2,1)}, bf16[1344,256]{1,0:T(8,128)(2,1)S(1)}, u32[]{:S(2)}, u32[]{:S(2)}) %collective-permute-start.8) | collective-permute-done | bytes 688160 | tf_op jit(solution)/shard_map/ppermute | solution.py:395
  65.7 2.5 %collective-permute-start.9 = (bf16[256,512]{1,0:T(8,128)(2,1)S(1)}, bf16[256,512]{1,0:T(8,128)(2,1)S(1)}, u32[]{:S(2)}, u32[]{:S(2)}) collective-permute-start(bf16[256,512]{1,0:T(8,128)(2,1)S(1)} %get-tuple-element.123), channel_id=1, source_target_pairs={{0,2},{2,0},{4,6},{6,4},{8,10},{10,8},{12,14},{14,12},{16,18},{18,... | collective-permute-start | bytes 786440 | tf_op jit(solution)/shard_map/ppermute | solution.py:390
  68.3 1.3 collective-permute-start.20
  69.7 3.2 %collective-permute-start.11 = (bf16[512,512]{1,0:T(8,128)(2,1)S(1)}, bf16[512,512]{1,0:T(8,128)(2,1)S(1)}, u32[]{:S(2)}, u32[]{:S(2)}) collective-permute-start(bf16[512,512]{1,0:T(8,128)(2,1)S(1)} %constant_dynamic-update-slice_fusion.6.refs_5_), channel_id=1, source_target_pairs={{0,8},{2,10},{4,12},{6,14},{8,16},{10,18},{12,20},{14,22},{16,24},... | collective-permute-start | bytes 1572872 | tf_op jit(solution)/shard_map/ppermute | solution.py:386
  73.1 2.4 %collective-permute-start.14 = (bf16[512,512]{1,0:T(8,128)(2,1)S(1)}, bf16[512,512]{1,0:T(8,128)(2,1)S(1)}, u32[]{:S(2)}, u32[]{:S(2)}) collective-permute-start(bf16[512,512]{1,0:T(8,128)(2,1)S(1)} %fusion.1), channel_id=1, source_target_pairs={{8,0},{10,2},{12,4},{14,6},{16,8},{18,10},{20,12},{22,14},{24,16},... | collective-permute-start | bytes 1572872 | tf_op jit(solution)/shard_map/ppermute | solution.py:386
  75.6 1.1 constant_dynamic-update-slice_fusion.refs_0_
  76.8 1.4 collective-permute-start.21
  78.2 6.7 %collective-permute-done.11.refs_3_ = bf16[512,512]{1,0:T(8,128)(2,1)S(1)} collective-permute-done((bf16[512,512]{1,0:T(8,128)(2,1)S(1)}, bf16[512,512]{1,0:T(8,128)(2,1)S(1)}, u32[]{:S(2)}, u32[]{:S(2)}) %collective-permute-start.11) | collective-permute-done | bytes 524320 | tf_op jit(solution)/shard_map/ppermute | solution.py:386
  84.9 1.3 collective-permute-start.13
  86.2 1.3 collective-permute-done.14
  88.7 2.5 %collective-permute-start.22 = (bf16[1344,512]{1,0:T(8,128)(2,1)S(1)}, bf16[1344,512]{1,0:T(8,128)(2,1)}, u32[]{:S(2)}, u32[]{:S(2)}) collective-permute-start(bf16[1344,512]{1,0:T(8,128)(2,1)S(1)} %constant_dynamic-update-slice_fusion.2.refs_1_), channel_id=1, source_target_pairs={{0,2},{2,0},{4,6},{6,4},{8,10},{10,8},{12,14},{14,12},{16,18},{18,... | collective-permute-start | bytes 4128776 | tf_op jit(solution)/shard_map/ppermute | solution.py:390
  91.2 1.3 collective-permute-start.17
  92.5 4.8 %collective-permute-done.13.refs_4_ = bf16[512,512]{1,0:T(8,128)(2,1)S(1)} collective-permute-done((bf16[512,512]{1,0:T(8,128)(2,1)S(1)}, bf16[512,512]{1,0:T(8,128)(2,1)S(1)}, u32[]{:S(2)}, u32[]{:S(2)}) %collective-permute-start.13) | collective-permute-done | bytes 524320 | tf_op jit(solution)/shard_map/ppermute | solution.py:430
  97.3 1.8 collective-permute-start.18
  99.0 16.0 %grads.1 = (bf16[256,2048]{1,0:T(8,128)(2,1)}, bf16[256,2048]{1,0:T(8,128)(2,1)}, bf16[2,256,1024]{2,1,0:T(8,128)(2,1)}, bf16[512,512]{1,0:T(8,128)(2,1)}, bf16[...) custom-call(s32[1]{0:T(128)} %bitcast.core_ref, bf16[4,2,1280,512]{3,2,1,0:T(8,128)(2,1)} %get-tuple-element.65.e_ref, ...), custom_call_target="tpu_custom_call" | custom-call | flops 1048576 | bytes 4096 | tf_op jit(solution)/shard_map/grads/pallas_call | solution.py:201
  116.0 4.1 %collective-permute-start.16 = (bf16[512,512]{1,0:T(8,128)(2,1)}, bf16[512,512]{1,0:T(8,128)(2,1)}, u32[]{:S(2)}, u32[]{:S(2)}) collective-permute-start(bf16[512,512]{1,0:T(8,128)(2,1)} %pad_maximum_fusion.5), channel_id=1, source_target_pairs={{0,2},{2,0},{4,6},{6,4},{8,10},{10,8},{12,14},{14,12},{16,18},{18,... | collective-permute-start | bytes 1572872 | tf_op jit(solution)/shard_map/ppermute | solution.py:390
  120.1 1.9 %collective-permute-start.23 = (bf16[512,512]{1,0:T(8,128)(2,1)}, bf16[512,512]{1,0:T(8,128)(2,1)}, u32[]{:S(2)}, u32[]{:S(2)}) collective-permute-start(bf16[512,512]{1,0:T(8,128)(2,1)} %get-tuple-element.86), channel_id=1, source_target_pairs={{4,0},{6,2},{8,4},{10,6},{12,8},{14,10},{16,12},{18,14},{20,16},{2... | collective-permute-start | bytes 1572872 | tf_op jit(solution)/shard_map/ppermute | solution.py:386
  122.8 1.9 %collective-permute-start.24 = (bf16[512,512]{1,0:T(8,128)(2,1)}, bf16[512,512]{1,0:T(8,128)(2,1)}, u32[]{:S(2)}, u32[]{:S(2)}) collective-permute-start(bf16[512,512]{1,0:T(8,128)(2,1)} %get-tuple-element.105), channel_id=1, source_target_pairs={{8,0},{10,2},{12,4},{14,6},{16,8},{18,10},{20,12},{22,14},{24,16},... | collective-permute-start | bytes 1572872 | tf_op jit(solution)/shard_map/ppermute | solution.py:386
  125.5 1.1 constant_dynamic-update-slice_fusion.5.dv_ref
  127.6 7.0 %tokens.1 = (bf16[256,5376]{1,0:T(8,128)(2,1)}, bf16[256,2688]{1,0:T(8,128)(2,1)}) custom-call(s32[1]{0:T(128)} %bitcast.7.at_ref, bf16[512,1024]{1,0:T(8,128)(2,1)} %copy-done.6, bf16[2688,1024]{1,0:T(8,128)(2,1)} %w_ref.1), custom_call_target="tpu_custom_call" | custom-call | flops 1048576 | bytes 4096 | tf_op jit(solution)/shard_map/tokens/pallas_call | solution.py:364
  135.3 2.7 %collective-permute-start.19 = (bf16[2,256,1024]{2,1,0:T(8,128)(2,1)}, bf16[2,256,1024]{2,1,0:T(8,128)(2,1)S(1)}, u32[]{:S(2)}, u32[]{:S(2)}) collective-permute-start(bf16[2,256,1024]{2,1,0:T(8,128)(2,1)} %get-tuple-element.93), channel_id=1, source_target_pairs={{0,2},{2,0},{4,6},{6,4},{8,10},{10,8},{12,14},{14,12},{16,18},{18,... | collective-permute-start | bytes 3145736 | tf_op jit(solution)/shard_map/ppermute | solution.py:390
  138.0 8.1 %weight.1 = (f32[336,512]{1,0:T(8,128)}, bf16[336,512]{1,0:T(8,128)(2,1)}, bf16[336,512]{1,0:T(8,128)(2,1)}, bf16[336,512]{1,0:T(8,128)(2,1)}) custom-call(s32[2]{0:T(128)} %pad_add_fusion.1.at_ref, bf16[1344,512]{1,0:T(8,128)(2,1)} %copy-done.7, bf16[1344,512]{1,0:T(8,128)(2,1)} %copy-done.8, bf16[1344,512]{1,0:T(8,128)(2,1)} %collective-permute-done.21.refs_2_, ...), custom_call_target="tpu_custom_call" | custom-call | flops 1048576 | bytes 4096 | tf_op jit(solution)/shard_map/weight/pallas_call | solution.py:336
  146.2 4.5 %collective-permute-start.28 = (bf16[336,512]{1,0:T(8,128)(2,1)}, bf16[336,512]{1,0:T(8,128)(2,1)S(1)}, u32[]{:S(2)}, u32[]{:S(2)}) collective-permute-start(bf16[336,512]{1,0:T(8,128)(2,1)} %get-tuple-element.111), channel_id=1, source_target_pairs={{0,16},{2,18},{4,20},{6,22},{8,24},{10,26},{12,28},{14,30},{16,0},... | collective-permute-start | bytes 1032200 | tf_op jit(solution)/shard_map/ppermute | solution.py:601
  150.7 2.3 %collective-permute-start.27 = (bf16[336,512]{1,0:T(8,128)(2,1)}, bf16[336,512]{1,0:T(8,128)(2,1)S(1)}, u32[]{:S(2)}, u32[]{:S(2)}) collective-permute-start(bf16[336,512]{1,0:T(8,128)(2,1)} %get-tuple-element.110), channel_id=1, source_target_pairs={{0,8},{2,10},{4,12},{6,14},{8,16},{10,18},{12,20},{14,22},{16,24},... | collective-permute-start | bytes 1032200 | tf_op jit(solution)/shard_map/ppermute | solution.py:601
  152.9 1.4 add_convert_fusion
  155.1 5.2 %collective-permute-start.25 = (bf16[256,512]{1,0:T(8,128)(2,1)S(1)}, bf16[256,512]{1,0:T(8,128)(2,1)S(1)}, u32[]{:S(2)}, u32[]{:S(2)}) collective-permute-start(bf16[256,512]{1,0:T(8,128)(2,1)S(1)} %get-tuple-element.117), channel_id=1, source_target_pairs={{0,2},{2,0},{4,6},{6,4},{8,10},{10,8},{12,14},{14,12},{16,18},{18,... | collective-permute-start | bytes 786440 | tf_op jit(solution)/shard_map/ppermute | solution.py:390
  160.3 12.4 %collective-permute-done.28 = bf16[336,512]{1,0:T(8,128)(2,1)S(1)} collective-permute-done((bf16[336,512]{1,0:T(8,128)(2,1)}, bf16[336,512]{1,0:T(8,128)(2,1)S(1)}, u32[]{:S(2)}, u32[]{:S(2)}) %collective-permute-start.28) | collective-permute-done | bytes 344096 | tf_op jit(solution)/shard_map/ppermute | solution.py:601
  172.7 7.4 %collective-permute-done.27 = bf16[336,512]{1,0:T(8,128)(2,1)S(1)} collective-permute-done((bf16[336,512]{1,0:T(8,128)(2,1)}, bf16[336,512]{1,0:T(8,128)(2,1)S(1)}, u32[]{:S(2)}, u32[]{:S(2)}) %collective-permute-start.27) | collective-permute-done | bytes 344096 | tf_op jit(solution)/shard_map/ppermute | solution.py:601
  180.4 1.4 collective-permute-start.30
  181.9 1.2 collective-permute-done.30
  (132 shorter events, 14.0 us)
Async XLA Ops:
  2.6 6.5 %copy-start.9 = (bf16[1,256,2048]{2,1,0:T(8,128)(2,1)S(1)}, bf16[1,256,2048]{2,1,0:T(8,128)(2,1)}, u32[]{:S(2)}) copy-start(bf16[1,256,2048]{2,1,0:T(8,128)(2,1)} %param.10) | copy-start | bytes 3145732
  2.6 24.0 %collective-permute-start.3 = (bf16[256,1280]{1,0:T(8,128)(2,1)}, bf16[256,1280]{1,0:T(8,128)(2,1)}, u32[]{:S(2)}, u32[]{:S(2)}) collective-permute-start(bf16[256,1280]{1,0:T(8,128)(2,1)} %dynamic-slice_bitcast_fusion.1), channel_id=1, source_target_pairs={{0,1},{1,0},{2,3},{3,2},{4,5},{5,4},{6,7},{7,6},{8,9},{9,8},{10,11... | collective-permute-start | bytes 1966088 | tf_op jit(solution)/shard_map/ppermute | solution.py:395
  5.8 3.5 %collective-permute-start = (bf16[272,512]{1,0:T(8,128)(2,1)S(1)}, bf16[272,512]{1,0:T(8,128)(2,1)S(1)}, u32[]{:S(2)}, u32[]{:S(2)}) collective-permute-start(bf16[272,512]{1,0:T(8,128)(2,1)S(1)} %maximum_maximum_fusion.1), channel_id=1, source_target_pairs={{0,2},{2,0},{4,6},{6,4},{8,10},{10,8},{12,14},{14,12},{16,18},{18,... | collective-permute-start | bytes 835592 | tf_op jit(solution)/shard_map/ppermute | solution.py:390
  8.9 25.1 %collective-permute-start.4 = (bf16[256,1408]{1,0:T(8,128)(2,1)}, bf16[256,1408]{1,0:T(8,128)(2,1)}, u32[]{:S(2)}, u32[]{:S(2)}) collective-permute-start(bf16[256,1408]{1,0:T(8,128)(2,1)} %dynamic-slice_bitcast_fusion), channel_id=1, source_target_pairs={{0,1},{1,0},{2,3},{3,2},{4,5},{5,4},{6,7},{7,6},{8,9},{9,8},{10,11... | collective-permute-start | bytes 2162696 | tf_op jit(solution)/shard_map/ppermute | solution.py:395
  9.4 12.3 %copy-start.2 = (bf16[528,512]{1,0:T(8,128)(2,1)}, bf16[528,512]{1,0:T(8,128)(2,1)S(1)}, u32[]{:S(2)}) copy-start(bf16[528,512]{1,0:T(8,128)(2,1)S(1)} %pad_maximum_fusion.2.refs_2_) | copy-start | bytes 1622020
  9.4 30.5 %collective-permute-start.2 = (bf16[528,512]{1,0:T(8,128)(2,1)S(1)}, bf16[528,512]{1,0:T(8,128)(2,1)S(1)}, u32[]{:S(2)}, u32[]{:S(2)}) collective-permute-start(bf16[528,512]{1,0:T(8,128)(2,1)S(1)} %pad_maximum_fusion.2.refs_2_), channel_id=1, source_target_pairs={{0,4},{2,6},{4,8},{6,10},{8,12},{10,14},{12,16},{14,18},{16,20},{1... | collective-permute-start | bytes 1622024 | tf_op jit(solution)/shard_map/ppermute | solution.py:386
  12.6 27.6 %collective-permute-start.1 = (bf16[528,512]{1,0:T(8,128)(2,1)S(1)}, bf16[528,512]{1,0:T(8,128)(2,1)S(1)}, u32[]{:S(2)}, u32[]{:S(2)}) collective-permute-start(bf16[528,512]{1,0:T(8,128)(2,1)S(1)} %pad_maximum_fusion.2.refs_2_), channel_id=1, source_target_pairs={{0,8},{2,10},{4,12},{6,14},{8,16},{10,18},{12,20},{14,22},{16,24},... | collective-permute-start | bytes 1622024 | tf_op jit(solution)/shard_map/ppermute | solution.py:386
  15.9 28.1 %collective-permute-start.6 = (bf16[256,2048]{1,0:T(8,128)(2,1)S(1)}, bf16[256,2048]{1,0:T(8,128)(2,1)S(1)}, u32[]{:S(2)}, u32[]{:S(2)}) collective-permute-start(bf16[256,2048]{1,0:T(8,128)(2,1)S(1)} %pad_maximum_fusion), channel_id=1, source_target_pairs={{0,2},{2,0},{4,6},{6,4},{8,10},{10,8},{12,14},{14,12},{16,18},{18,... | collective-permute-start | bytes 3145736 | tf_op jit(solution)/shard_map/ppermute | solution.py:390
  26.6 13.6 %copy-start.30 = (bf16[1344,256]{1,0:T(8,128)(2,1)S(1)}, bf16[1344,256]{1,0:T(8,128)(2,1)}, u32[]{:S(2)}) copy-start(bf16[1344,256]{1,0:T(8,128)(2,1)} %get-tuple-element.76) | copy-start | bytes 2064388
  26.6 17.4 %collective-permute-start.5 = (bf16[1344,256]{1,0:T(8,128)(2,1)}, bf16[1344,256]{1,0:T(8,128)(2,1)}, u32[]{:S(2)}, u32[]{:S(2)}) collective-permute-start(bf16[1344,256]{1,0:T(8,128)(2,1)} %get-tuple-element.62), channel_id=1, source_target_pairs={{0,4},{2,6},{4,0},{6,2},{8,12},{10,14},{12,8},{14,10},{16,20},{18,... | collective-permute-start | bytes 2064392 | tf_op jit(solution)/shard_map/ppermute | solution.py:430
  38.7 22.0 %collective-permute-start.7 = (bf16[256,1024]{1,0:T(8,128)(2,1)}, bf16[256,1024]{1,0:T(8,128)(2,1)S(1)}, u32[]{:S(2)}, u32[]{:S(2)}) collective-permute-start(bf16[256,1024]{1,0:T(8,128)(2,1)} %product.2), channel_id=1, source_target_pairs={{0,1},{1,0},{2,3},{3,2},{4,5},{5,4},{6,7},{7,6},{8,9},{9,8},{10,11... | collective-permute-start | bytes 1572872 | tf_op jit(solution)/shard_map/ppermute | solution.py:395
  39.9 4.2 %copy-start.10 = (bf16[528,512]{1,0:T(8,128)(2,1)}, bf16[528,512]{1,0:T(8,128)(2,1)S(1)}, u32[]{:S(2)}) copy-start(bf16[528,512]{1,0:T(8,128)(2,1)S(1)} %collective-permute-done.2.refs_1_) | copy-start | bytes 1622020
  39.9 25.6 %collective-permute-start.8 = (bf16[1344,256]{1,0:T(8,128)(2,1)}, bf16[1344,256]{1,0:T(8,128)(2,1)S(1)}, u32[]{:S(2)}, u32[]{:S(2)}) collective-permute-start(bf16[1344,256]{1,0:T(8,128)(2,1)} %get-tuple-element.74), channel_id=1, source_target_pairs={{0,1},{1,0},{2,3},{3,2},{4,5},{5,4},{6,7},{7,6},{8,9},{9,8},{10,11... | collective-permute-start | bytes 2064392 | tf_op jit(solution)/shard_map/ppermute | solution.py:395
  40.2 3.9 %copy-start.11 = (bf16[528,512]{1,0:T(8,128)(2,1)}, bf16[528,512]{1,0:T(8,128)(2,1)S(1)}, u32[]{:S(2)}) copy-start(bf16[528,512]{1,0:T(8,128)(2,1)S(1)} %collective-permute-done.1.refs_0_) | copy-start | bytes 1622020
  40.2 29.5 %collective-permute-start.10 = (bf16[1344,256]{1,0:T(8,128)(2,1)S(1)}, bf16[1344,256]{1,0:T(8,128)(2,1)}, u32[]{:S(2)}, u32[]{:S(2)}) collective-permute-start(bf16[1344,256]{1,0:T(8,128)(2,1)S(1)} %copy-done.30), channel_id=1, source_target_pairs={{0,4},{2,6},{4,0},{6,2},{8,12},{10,14},{12,8},{14,10},{16,20},{18,... | collective-permute-start | bytes 2064392 | tf_op jit(solution)/shard_map/ppermute | solution.py:430
  45.0 20.5 %copy-start.5 = (f32[256,1024]{1,0:T(8,128)S(1)}, f32[256,1024]{1,0:T(8,128)}, u32[]{:S(2)}) copy-start(f32[256,1024]{1,0:T(8,128)} %product.3) | copy-start | bytes 3145732
  59.4 8.9 %copy-start.14 = (bf16[1344,256]{1,0:T(8,128)(2,1)S(1)}, bf16[1344,256]{1,0:T(8,128)(2,1)}, u32[]{:S(2)}) copy-start(bf16[1344,256]{1,0:T(8,128)(2,1)} %get-tuple-element.68) | copy-start | bytes 2064388
  59.4 13.5 %collective-permute-start.12 = (bf16[512,512]{1,0:T(8,128)(2,1)}, bf16[512,512]{1,0:T(8,128)(2,1)S(1)}, u32[]{:S(2)}, u32[]{:S(2)}) collective-permute-start(bf16[512,512]{1,0:T(8,128)(2,1)} %get-tuple-element.72), channel_id=1, source_target_pairs={{0,4},{2,6},{4,0},{6,2},{8,12},{10,14},{12,8},{14,10},{16,20},{18,... | collective-permute-start | bytes 1572872 | tf_op jit(solution)/shard_map/ppermute | solution.py:430
  65.7 7.3 %copy-start.20 = (bf16[512,512]{1,0:T(8,128)(2,1)S(1)}, bf16[512,512]{1,0:T(8,128)(2,1)}, u32[]{:S(2)}) copy-start(bf16[512,512]{1,0:T(8,128)(2,1)} %get-tuple-element.78) | copy-start | bytes 1572868
  65.7 3.9 %collective-permute-start.9 = (bf16[256,512]{1,0:T(8,128)(2,1)S(1)}, bf16[256,512]{1,0:T(8,128)(2,1)S(1)}, u32[]{:S(2)}, u32[]{:S(2)}) collective-permute-start(bf16[256,512]{1,0:T(8,128)(2,1)S(1)} %get-tuple-element.123), channel_id=1, source_target_pairs={{0,2},{2,0},{4,6},{6,4},{8,10},{10,8},{12,14},{14,12},{16,18},{18,... | collective-permute-start | bytes 786440 | tf_op jit(solution)/shard_map/ppermute | solution.py:390
  68.3 20.3 %collective-permute-start.20 = (bf16[1344,256]{1,0:T(8,128)(2,1)}, bf16[1344,256]{1,0:T(8,128)(2,1)S(1)}, u32[]{:S(2)}, u32[]{:S(2)}) collective-permute-start(bf16[1344,256]{1,0:T(8,128)(2,1)} %collective-permute-done.5), channel_id=1, source_target_pairs={{0,1},{1,0},{2,3},{3,2},{4,5},{5,4},{6,7},{7,6},{8,9},{9,8},{10,11... | collective-permute-start | bytes 2064392 | tf_op jit(solution)/shard_map/ppermute | solution.py:395
  69.7 15.1 %copy-start.3 = (bf16[512,512]{1,0:T(8,128)(2,1)}, bf16[512,512]{1,0:T(8,128)(2,1)S(1)}, u32[]{:S(2)}) copy-start(bf16[512,512]{1,0:T(8,128)(2,1)S(1)} %constant_dynamic-update-slice_fusion.6.refs_5_) | copy-start | bytes 1572868
  69.7 15.1 %collective-permute-start.11 = (bf16[512,512]{1,0:T(8,128)(2,1)S(1)}, bf16[512,512]{1,0:T(8,128)(2,1)S(1)}, u32[]{:S(2)}, u32[]{:S(2)}) collective-permute-start(bf16[512,512]{1,0:T(8,128)(2,1)S(1)} %constant_dynamic-update-slice_fusion.6.refs_5_), channel_id=1, source_target_pairs={{0,8},{2,10},{4,12},{6,14},{8,16},{10,18},{12,20},{14,22},{16,24},... | collective-permute-start | bytes 1572872 | tf_op jit(solution)/shard_map/ppermute | solution.py:386
  73.1 14.4 %copy-start.17 = (bf16[512,512]{1,0:T(8,128)(2,1)S(1)}, bf16[512,512]{1,0:T(8,128)(2,1)}, u32[]{:S(2)}) copy-start(bf16[512,512]{1,0:T(8,128)(2,1)} %get-tuple-element.81) | copy-start | bytes 1572868
  73.1 14.4 %collective-permute-start.14 = (bf16[512,512]{1,0:T(8,128)(2,1)S(1)}, bf16[512,512]{1,0:T(8,128)(2,1)S(1)}, u32[]{:S(2)}, u32[]{:S(2)}) collective-permute-start(bf16[512,512]{1,0:T(8,128)(2,1)S(1)} %fusion.1), channel_id=1, source_target_pairs={{8,0},{10,2},{12,4},{14,6},{16,8},{18,10},{20,12},{22,14},{24,16},... | collective-permute-start | bytes 1572872 | tf_op jit(solution)/shard_map/ppermute | solution.py:386
  76.8 11.9 %copy-start.7 = (bf16[1344,512]{1,0:T(8,128)(2,1)}, bf16[1344,512]{1,0:T(8,128)(2,1)S(1)}, u32[]{:S(2)}) copy-start(bf16[1344,512]{1,0:T(8,128)(2,1)S(1)} %constant_dynamic-update-slice_fusion.refs_0_) | copy-start | bytes 4128772
  76.8 58.5 %collective-permute-start.21 = (bf16[1344,512]{1,0:T(8,128)(2,1)S(1)}, bf16[1344,512]{1,0:T(8,128)(2,1)}, u32[]{:S(2)}, u32[]{:S(2)}) collective-permute-start(bf16[1344,512]{1,0:T(8,128)(2,1)S(1)} %constant_dynamic-update-slice_fusion.refs_0_), channel_id=1, source_target_pairs={{0,2},{2,0},{4,6},{6,4},{8,10},{10,8},{12,14},{14,12},{16,18},{18,... | collective-permute-start | bytes 4128776 | tf_op jit(solution)/shard_map/ppermute | solution.py:390
  84.8 3.9 %copy-start.12 = (bf16[512,512]{1,0:T(8,128)(2,1)}, bf16[512,512]{1,0:T(8,128)(2,1)S(1)}, u32[]{:S(2)}) copy-start(bf16[512,512]{1,0:T(8,128)(2,1)S(1)} %collective-permute-done.11.refs_3_) | copy-start | bytes 1572868
  84.9 12.4 %collective-permute-start.13 = (bf16[512,512]{1,0:T(8,128)(2,1)S(1)}, bf16[512,512]{1,0:T(8,128)(2,1)S(1)}, u32[]{:S(2)}, u32[]{:S(2)}) collective-permute-start(bf16[512,512]{1,0:T(8,128)(2,1)S(1)} %broadcast_select_fusion), channel_id=1, source_target_pairs={{0,4},{2,6},{4,0},{6,2},{8,12},{10,14},{12,8},{14,10},{16,20},{18,... | collective-permute-start | bytes 1572872 | tf_op jit(solution)/shard_map/ppermute | solution.py:430
  87.7 27.3 %copy-start.4 = (bf16[512,512]{1,0:T(8,128)(2,1)}, bf16[512,512]{1,0:T(8,128)(2,1)S(1)}, u32[]{:S(2)}) copy-start(bf16[512,512]{1,0:T(8,128)(2,1)S(1)} %fusion.3.refs_4_) | copy-start | bytes 1572868
  87.8 27.3 %collective-permute-start.15 = (bf16[512,512]{1,0:T(8,128)(2,1)S(1)}, bf16[512,512]{1,0:T(8,128)(2,1)S(1)}, u32[]{:S(2)}, u32[]{:S(2)}) collective-permute-start(bf16[512,512]{1,0:T(8,128)(2,1)S(1)} %fusion.3.refs_4_), channel_id=1, source_target_pairs={{0,1},{1,0},{2,3},{3,2},{4,5},{5,4},{6,7},{7,6},{8,9},{9,8},{10,11... | collective-permute-start | bytes 1572872 | tf_op jit(solution)/shard_map/ppermute | solution.py:395
  88.7 26.3 %copy-start.8 = (bf16[1344,512]{1,0:T(8,128)(2,1)}, bf16[1344,512]{1,0:T(8,128)(2,1)S(1)}, u32[]{:S(2)}) copy-start(bf16[1344,512]{1,0:T(8,128)(2,1)S(1)} %constant_dynamic-update-slice_fusion.2.refs_1_) | copy-start | bytes 4128772
  88.7 49.3 %collective-permute-start.22 = (bf16[1344,512]{1,0:T(8,128)(2,1)S(1)}, bf16[1344,512]{1,0:T(8,128)(2,1)}, u32[]{:S(2)}, u32[]{:S(2)}) collective-permute-start(bf16[1344,512]{1,0:T(8,128)(2,1)S(1)} %constant_dynamic-update-slice_fusion.2.refs_1_), channel_id=1, source_target_pairs={{0,2},{2,0},{4,6},{6,4},{8,10},{10,8},{12,14},{14,12},{16,18},{18,... | collective-permute-start | bytes 4128776 | tf_op jit(solution)/shard_map/ppermute | solution.py:390
  91.2 28.9 %collective-permute-start.17 = (bf16[512,512]{1,0:T(8,128)(2,1)S(1)}, bf16[512,512]{1,0:T(8,128)(2,1)S(1)}, u32[]{:S(2)}, u32[]{:S(2)}) collective-permute-start(bf16[512,512]{1,0:T(8,128)(2,1)S(1)} %fusion.3.refs_4_), channel_id=1, source_target_pairs={{0,4},{1,5},{2,6},{3,7},{4,0},{5,1},{6,2},{7,3},{8,12},{9,13},{10,... | collective-permute-start | bytes 1572872 | tf_op jit(solution)/shard_map/ppermute | solution.py:405
  97.3 24.8 %collective-permute-start.18 = (bf16[512,512]{1,0:T(8,128)(2,1)S(1)}, bf16[512,512]{1,0:T(8,128)(2,1)S(1)}, u32[]{:S(2)}, u32[]{:S(2)}) collective-permute-start(bf16[512,512]{1,0:T(8,128)(2,1)S(1)} %fusion.3.refs_4_), channel_id=1, source_target_pairs={{0,5},{1,4},{2,7},{3,6},{4,1},{5,0},{6,3},{7,2},{8,13},{9,12},{10,... | collective-permute-start | bytes 1572872 | tf_op jit(solution)/shard_map/ppermute | solution.py:405
  115.1 7.0 %copy-start.13 = (bf16[512,512]{1,0:T(8,128)(2,1)}, bf16[512,512]{1,0:T(8,128)(2,1)S(1)}, u32[]{:S(2)}) copy-start(bf16[512,512]{1,0:T(8,128)(2,1)S(1)} %collective-permute-done.15.refs_6_) | copy-start | bytes 1572868
  116.0 9.5 %collective-permute-start.16 = (bf16[512,512]{1,0:T(8,128)(2,1)}, bf16[512,512]{1,0:T(8,128)(2,1)}, u32[]{:S(2)}, u32[]{:S(2)}) collective-permute-start(bf16[512,512]{1,0:T(8,128)(2,1)} %pad_maximum_fusion.5), channel_id=1, source_target_pairs={{0,2},{2,0},{4,6},{6,4},{8,10},{10,8},{12,14},{14,12},{16,18},{18,... | collective-permute-start | bytes 1572872 | tf_op jit(solution)/shard_map/ppermute | solution.py:390
  120.1 26.0 %collective-permute-start.23 = (bf16[512,512]{1,0:T(8,128)(2,1)}, bf16[512,512]{1,0:T(8,128)(2,1)}, u32[]{:S(2)}, u32[]{:S(2)}) collective-permute-start(bf16[512,512]{1,0:T(8,128)(2,1)} %get-tuple-element.86), channel_id=1, source_target_pairs={{4,0},{6,2},{8,4},{10,6},{12,8},{14,10},{16,12},{18,14},{20,16},{2... | collective-permute-start | bytes 1572872 | tf_op jit(solution)/shard_map/ppermute | solution.py:386
  122.8 23.3 %collective-permute-start.24 = (bf16[512,512]{1,0:T(8,128)(2,1)}, bf16[512,512]{1,0:T(8,128)(2,1)}, u32[]{:S(2)}, u32[]{:S(2)}) collective-permute-start(bf16[512,512]{1,0:T(8,128)(2,1)} %get-tuple-element.105), channel_id=1, source_target_pairs={{8,0},{10,2},{12,4},{14,6},{16,8},{18,10},{20,12},{22,14},{24,16},... | collective-permute-start | bytes 1572872 | tf_op jit(solution)/shard_map/ppermute | solution.py:386
  134.6 48.6 %collective-permute-start.26 = (bf16[256,2688]{1,0:T(8,128)(2,1)}, bf16[256,2688]{1,0:T(8,128)(2,1)S(1)}, u32[]{:S(2)}, u32[]{:S(2)}) collective-permute-start(bf16[256,2688]{1,0:T(8,128)(2,1)} %get-tuple-element.92), channel_id=1, source_target_pairs={{0,1},{1,0},{2,3},{3,2},{4,5},{5,4},{6,7},{7,6},{8,9},{9,8},{10,11... | collective-permute-start | bytes 4128776 | tf_op jit(solution)/shard_map/ppermute | solution.py:395
  135.3 17.7 %copy-start.21 = (bf16[512,512]{1,0:T(8,128)(2,1)S(1)}, bf16[512,512]{1,0:T(8,128)(2,1)}, u32[]{:S(2)}) copy-start(bf16[512,512]{1,0:T(8,128)(2,1)} %get-tuple-element.95) | copy-start | bytes 1572868
  135.3 47.8 %collective-permute-start.19 = (bf16[2,256,1024]{2,1,0:T(8,128)(2,1)}, bf16[2,256,1024]{2,1,0:T(8,128)(2,1)S(1)}, u32[]{:S(2)}, u32[]{:S(2)}) collective-permute-start(bf16[2,256,1024]{2,1,0:T(8,128)(2,1)} %get-tuple-element.93), channel_id=1, source_target_pairs={{0,2},{2,0},{4,6},{6,4},{8,10},{10,8},{12,14},{14,12},{16,18},{18,... | collective-permute-start | bytes 3145736 | tf_op jit(solution)/shard_map/ppermute | solution.py:390
  146.1 34.0 %copy-start.15 = (f32[336,512]{1,0:T(8,128)S(1)}, f32[336,512]{1,0:T(8,128)}, u32[]{:S(2)}) copy-start(f32[336,512]{1,0:T(8,128)} %get-tuple-element.109) | copy-start | bytes 2064388
  146.1 9.0 %collective-permute-start.29 = (bf16[336,512]{1,0:T(8,128)(2,1)}, bf16[336,512]{1,0:T(8,128)(2,1)S(1)}, u32[]{:S(2)}, u32[]{:S(2)}) collective-permute-start(bf16[336,512]{1,0:T(8,128)(2,1)} %get-tuple-element.112), channel_id=1, source_target_pairs={{0,24},{2,26},{4,28},{6,30},{8,0},{10,2},{12,4},{14,6},{16,8},{18,... | collective-permute-start | bytes 1032200 | tf_op jit(solution)/shard_map/ppermute | solution.py:601
  146.2 26.5 %collective-permute-start.28 = (bf16[336,512]{1,0:T(8,128)(2,1)}, bf16[336,512]{1,0:T(8,128)(2,1)S(1)}, u32[]{:S(2)}, u32[]{:S(2)}) collective-permute-start(bf16[336,512]{1,0:T(8,128)(2,1)} %get-tuple-element.111), channel_id=1, source_target_pairs={{0,16},{2,18},{4,20},{6,22},{8,24},{10,26},{12,28},{14,30},{16,0},... | collective-permute-start | bytes 1032200 | tf_op jit(solution)/shard_map/ppermute | solution.py:601
  150.7 29.4 %collective-permute-start.27 = (bf16[336,512]{1,0:T(8,128)(2,1)}, bf16[336,512]{1,0:T(8,128)(2,1)S(1)}, u32[]{:S(2)}, u32[]{:S(2)}) collective-permute-start(bf16[336,512]{1,0:T(8,128)(2,1)} %get-tuple-element.110), channel_id=1, source_target_pairs={{0,8},{2,10},{4,12},{6,14},{8,16},{10,18},{12,20},{14,22},{16,24},... | collective-permute-start | bytes 1032200 | tf_op jit(solution)/shard_map/ppermute | solution.py:601
  155.1 26.6 %collective-permute-start.25 = (bf16[256,512]{1,0:T(8,128)(2,1)S(1)}, bf16[256,512]{1,0:T(8,128)(2,1)S(1)}, u32[]{:S(2)}, u32[]{:S(2)}) collective-permute-start(bf16[256,512]{1,0:T(8,128)(2,1)S(1)} %get-tuple-element.117), channel_id=1, source_target_pairs={{0,2},{2,0},{4,6},{6,4},{8,10},{10,8},{12,14},{14,12},{16,18},{18,... | collective-permute-start | bytes 786440 | tf_op jit(solution)/shard_map/ppermute | solution.py:390
  180.4 2.7 %collective-permute-start.30 = (f32[168,512]{1,0:T(8,128)S(1)}, f32[168,512]{1,0:T(8,128)S(1)}, u32[]{:S(2)}, u32[]{:S(2)}) collective-permute-start(f32[168,512]{1,0:T(8,128)S(1)} %get-tuple-element.115), channel_id=1, source_target_pairs={{0,2},{2,0},{4,6},{6,4},{8,10},{10,8},{12,14},{14,12},{16,18},{18,... | collective-permute-start | bytes 1032200 | tf_op jit(solution)/shard_map/ppermute | solution.py:390
  (14 other events, 25.1 us)

commit v7 on v6

--- a/solution.py
+++ b/solution.py
@@ -529,7 +529,6 @@
     value_back = [rotated(x, -s - 1) for s, x in enumerate(partial)]
     over_fsdp = {s: rotated(after(by_place[0, s], sent), s) for s in range(1, n_fsdp)}
     value_back = [after(x, dv_near) for x in value_back]
-    value_back[0] = after(value_back[0], over_fsdp)
     value_sum = value_own
     for x in value_back:
         value_sum = value_sum + x.astype(F32)
@@ -537,7 +536,7 @@
     v_own = placed(core, cols(own_values, core, half_kv), swapped(cols(own_values, 1 - core, half_kv)), 0)
 
     over_y[0] = flipped(after(by_place[1, 0], k_near))
-    v_own, over_y[0] = lax.optimization_barrier((v_own, over_y[0]))
+    v_own, over_y[0], over_fsdp = lax.optimization_barrier((v_own, over_y[0], over_fsdp))
     v_far = shifted(v_own, 4)
     own_pairs = [jnp.concatenate([by_place[0, 0], over_y[0]], 1)]
     other_pairs = [swapped(after(own_pairs[0], v_own))]
@@ -552,37 +551,19 @@
     dv_chip = gathered_terms(my_y, dv_mine, dv_got, after(dv_back, v_sent))
     dv_fsdp = [dv_chip] + [rotated(dv_chip, s) for s in range(1, n_fsdp)]
     dv_over_y = [moved(dv_chip, 1, s) for s in range(n_fsdp)]
+    v_near = after(v_near, dv_chip)
     for s in range(1, n_fsdp):
-        own_pairs.append(jnp.concatenate([over_fsdp[s], after(relayed_y[s], dv_chip)], 1))
+        own_pairs.append(jnp.concatenate([over_fsdp[s], after(relayed_y[s], v_near)], 1))
         other_pairs.append(swapped(own_pairs[s]))
-    v_near = after(v_near, dv_chip)
     vals = [v_far, v_near, v_own]
     out, dq, other, dk_far, dk_near, dk_mine = run_grads(
         core_arg, e, inv, do_t, queries[0], q_other, keys, vals, chip_rows, half_kv
     )
     dk_back = [shifted(dk_near, -2), shifted(dk_far, -4)]
 
-    dv_fsdp = [after(x, dk_near) for x in dv_fsdp]
-    dv_over_y = [after(x, dk_near) for x in dv_over_y]
-    dv_other = swapped(jnp.concatenate([rows_of(x, 1 - core, shard_rows) for x in dv_fsdp], 0))
-    dv_rows = placed(
-        core, jnp.concatenate([rows_of(x, core, shard_rows) for x in dv_fsdp], 0), dv_other, 1
-    )
-    dv_rows = after(dv_rows, *dv_over_y)
-    if aligned:
-        d_tokens, *made = run_tokens(fsdp_arg, dv_rows, w_value, n_fsdp)
-    else:
-        made = dot(dv_rows, w_value, NT).astype(BF16)
-        made = [made[s * shard_rows : (s + 1) * shard_rows] for s in range(n_fsdp)]
-        d_tokens = jnp.concatenate([made[0]] * n_fsdp, 1)
-        made = made[1:]
-    for s in range(1, n_fsdp):
-        back = rotated(made[s - 1], -s)
-        d_tokens = lax.dynamic_update_slice_in_dim(d_tokens, back, ((my_fsdp + s) % n_fsdp) * slab, 1)
-
     dv_pairs = list(zip(dv_fsdp, dv_over_y))
     if out_rows % 8 == 0:
-        at = after(jnp.stack([core, my_z]).astype(jnp.int32), *made)
+        at = after(jnp.stack([core, my_z]).astype(jnp.int32), dk_near)
         by_z = run_weight(at, own_pairs, other_pairs, dv_pairs, n_z)
     else:
         weight_term = 0.0
@@ -596,16 +577,33 @@
             lax.dynamic_index_in_dim(weight_term, (my_z + d) % n_z, 0, keepdims=False).astype(BF16 if d else F32)
             for d in range(n_z)
         ]
-    by_z, dk_back = lax.optimization_barrier((list(by_z), dk_back))
     over_z = [
         lax.ppermute(by_z[d], "ctx", [(i, (i + 4 * d) % n_ctx) for i in range(n_ctx)]) for d in range(1, n_z)
     ]
+
+    dv_fsdp = [after(x, dk_near) for x in dv_fsdp]
+    dv_over_y = [after(x, dk_near) for x in dv_over_y]
+    dv_fsdp = [after(x, by_z[0]) for x in dv_fsdp]
+    dv_other = swapped(jnp.concatenate([rows_of(x, 1 - core, shard_rows) for x in dv_fsdp], 0))
+    dv_rows = placed(
+        core, jnp.concatenate([rows_of(x, core, shard_rows) for x in dv_fsdp], 0), dv_other, 1
+    )
+    if aligned:
+        d_tokens, *made = run_tokens(fsdp_arg, dv_rows, w_value, n_fsdp)
+    else:
+        made = dot(dv_rows, w_value, NT).astype(BF16)
+        made = [made[s * shard_rows : (s + 1) * shard_rows] for s in range(n_fsdp)]
+        d_tokens = jnp.concatenate([made[0]] * n_fsdp, 1)
+        made = made[1:]
+    for s in range(1, n_fsdp):
+        back = rotated(made[s - 1], -s)
+        d_tokens = lax.dynamic_update_slice_in_dim(d_tokens, back, ((my_fsdp + s) % n_fsdp) * slab, 1)
 
     row_sum = by_z[0]
     for x in over_z:
         row_sum = row_sum + x.astype(F32)
     d_weight = placed(core, rows_of(row_sum, core, out_rows), swapped(rows_of(row_sum, 1 - core, out_rows)), 1)
-
+    dk_back = [after(x, *made) for x in dk_back]
     dk_chip = (dk_mine.astype(F32) + dk_back[0].astype(F32) + dk_back[1].astype(F32)).astype(BF16)
     d_keys = placed(core, rows_of(dk_chip, core, shard_rows), swapped(rows_of(dk_chip, 1 - core, shard_rows)), 1)
     other = swapped(after(other, *made))

time: 187 us -> 211 us (1.13)
  waiting for transfers between devices: 46.7 us -> 81 us
  starting transfers between devices: 58.3 us -> 42.9 us
  other arithmetic: 6.6 us -> 11.4 us
    ppermute x9, starting transfers between devices: 21.8 us -> 9.15 us  [swapped(): lax.ppermute(x, 'ctx', [(i, i ^ 1) for i in range(lax.axis_size('ctx'))])]
    ppermute x6, waiting for transfers between devices: 7.99 us -> 18.4 us  [shifted(): lax.ppermute(x, 'ctx', [(i, i + by) for i in range(length) if 0 <= i + by...]
    ppermute x4, waiting for transfers between devices: 6.11 us -> 15.2 us  [flipped(): lax.ppermute(x, 'ctx', [(i, i ^ 2) for i in range(lax.axis_size('ctx'))])]
    ppermute x7, waiting for transfers between devices: 10.9 us -> 19.1 us  [rotated(): lax.ppermute(x, 'fsdp', [(i, (i + by) % length) for i in range(length)])]
    ppermute x2, waiting for transfers between devices: 0.01 us -> 7.35 us  [moved(): return lax.ppermute(x, ('ctx', 'fsdp'), pairs)]
    ppermute x3, starting transfers between devices: 6.81 us -> 2.6 us  [shards(): lax.ppermute(by_z[d], 'ctx', [(i, (i + 4 * d) % n_ctx) for i in range(n_c...]
    unnamed x64 -> x66, local copies, waits for them, and re-layouts: 4.99 us -> 5.38 us
  transfers between devices with their start and end apart: 31 -> 31, of which waited for: 10 -> 12; matrix products, arithmetic and copies ran while one was open for 7% -> 9% of each run, Pallas kernels for 32% -> 24%
where the time goes in v7:
time: 211 us; the launch traced here: 210 us
  waiting for transfers between devices  81 us (38%)
  Pallas kernels  59.3 us (28%)
  starting transfers between devices  42.9 us (20%)
  local copies, waits for them, and re-layouts  13.8 us (7%)
  other arithmetic  11.4 us (5%)
    ppermute x3, waiting for transfers between devices, shards(): lax.ppermute(by_z[d], 'ctx', [(i, (i + 4 * d) % n_ctx) for i in range(n_c...  19.9 us
    ppermute x7, waiting for transfers between devices, rotated(): lax.ppermute(x, 'fsdp', [(i, (i + by) % length) for i in range(length)])  19.1 us
    ppermute x6, waiting for transfers between devices, shifted(): lax.ppermute(x, 'ctx', [(i, i + by) for i in range(length) if 0 <= i + by...  18.4 us
    ppermute x6, starting transfers between devices, shifted(): lax.ppermute(x, 'ctx', [(i, i + by) for i in range(length) if 0 <= i + by...  17.8 us
    pallas_call x1, Pallas kernels, run_grads(): pl.pallas_call(functools.partial(grads_kernel, blk, n_arr - 1), grid_spec...  15.9 us
    ppermute x4, waiting for transfers between devices, flipped(): lax.ppermute(x, 'ctx', [(i, i ^ 2) for i in range(lax.axis_size('ctx'))])  15.2 us
    pallas_call x1, Pallas kernels, run_probs(): pl.pallas_call(functools.partial(probs_kernel, blk, n_arr - 1), grid_spec...  14.3 us
    pallas_call x2, Pallas kernels, run_product(): pl.pallas_call(product_kernel, grid_spec=pltpu.PrefetchScalarGridSpec(num...  9.54 us
  transfers between devices with their start and end apart: 31, of which 12 were waited for; matrix products, arithmetic and copies ran while one was open for 9% of the time, Pallas kernels for 24%

profile of v7, /device:TPU:9, one launch (start us, length us, event | category | flops | bytes accessed | tf_op | source)
XLA Modules:
  0.0 209.6 jit_solution(7922218937068117020)
XLA Ops:
  0.7 1.2 dynamic-slice_bitcast_fusion.1
  1.9 1.3 collective-permute-start.3
  4.0 1.1 dynamic-slice_bitcast_fusion.5
  6.8 2.0 dynamic-slice_bitcast_fusion
  11.0 3.1 %collective-permute-start.2 = (bf16[528,512]{1,0:T(8,128)(2,1)S(1)}, bf16[528,512]{1,0:T(8,128)(2,1)S(1)}, u32[]{:S(2)}, u32[]{:S(2)}) collective-permute-start(bf16[528,512]{1,0:T(8,128)(2,1)S(1)} %pad_maximum_fusion.2.refs_2_), channel_id=1, source_target_pairs={{0,4},{2,6},{4,8},{6,10},{8,12},{10,14},{12,16},{14,18},{16,20},{1... | collective-permute-start | bytes 1622024 | tf_op jit(solution)/shard_map/ppermute | solution.py:386
  14.2 3.2 %collective-permute-start.1 = (bf16[528,512]{1,0:T(8,128)(2,1)S(1)}, bf16[528,512]{1,0:T(8,128)(2,1)S(1)}, u32[]{:S(2)}, u32[]{:S(2)}) collective-permute-start(bf16[528,512]{1,0:T(8,128)(2,1)S(1)} %pad_maximum_fusion.2.refs_2_), channel_id=1, source_target_pairs={{0,8},{2,10},{4,12},{6,14},{8,16},{10,18},{12,20},{14,22},{16,24},... | collective-permute-start | bytes 1622024 | tf_op jit(solution)/shard_map/ppermute | solution.py:386
  19.9 4.2 %pieces.1 = (bf16[1344,256]{1,0:T(8,128)(2,1)}, bf16[1344,256]{1,0:T(8,128)(2,1)}, bf16[1344,256]{1,0:T(8,128)(2,1)}, bf16[1344,256]{1,0:T(8,128)(2,1)}) custom-call(s32[2]{0:T(128)} %pad_add_fusion.at_ref, bf16[256,5376]{1,0:T(8,128)(2,1)} %bitcast.29), custom_call_target="tpu_custom_call" | custom-call | flops 1048576 | bytes 4096 | tf_op jit(solution)/shard_map/pieces/pallas_call | solution.py:260
  24.1 4.9 %product.3 = f32[256,1024]{1,0:T(8,128)} custom-call(s32[1]{0:T(128)} %bitcast.7.at_ref, bf16[256,5376]{1,0:T(8,128)(2,1)} %bitcast.30, bf16[2688,1024]{1,0:T(8,128)(2,1)} %w_ref.1), custom_call_target="tpu_custom_call" | custom-call | flops 1048576 | bytes 4096 | tf_op jit(solution)/shard_map/product/pallas_call | solution.py:290
  29.0 1.3 collective-permute-start.5
  30.3 2.8 %collective-permute-done.4.refs_1_ = bf16[256,1408]{1,0:T(8,128)(2,1)} collective-permute-done((bf16[256,1408]{1,0:T(8,128)(2,1)}, bf16[256,1408]{1,0:T(8,128)(2,1)}, u32[]{:S(2)}, u32[]{:S(2)}) %collective-permute-start.4) | collective-permute-done | bytes 720928 | tf_op jit(solution)/shard_map/ppermute | solution.py:395
  33.1 4.7 %product.2 = bf16[256,1024]{1,0:T(8,128)(2,1)} custom-call(s32[1]{0:T(128)} %constant.86.clone.1.at_ref, bf16[256,1280]{1,0:T(8,128)(2,1)} %collective-permute-done.3.refs_0_, bf16[256,1408]{1,0:T(8,128)(2,1)} %collective-permute-done.4.refs_1_, bf16[2688,1024]{1,0:T(8,128)(2,1)} %w_ref.1), custom_call_target="tpu_custom_call" | custom-call | flops 1048576 | bytes 4096 | tf_op jit(solution)/shard_map/product/pallas_call | solution.py:290
  37.8 1.2 collective-permute-start.7
  39.3 1.3 collective-permute-start.9
  41.9 4.2 %collective-permute-done.5 = bf16[1344,256]{1,0:T(8,128)(2,1)S(1)} collective-permute-done((bf16[1344,256]{1,0:T(8,128)(2,1)S(1)}, bf16[1344,256]{1,0:T(8,128)(2,1)S(1)}, u32[]{:S(2)}, u32[]{:S(2)}) %collective-permute-start.5) | collective-permute-done | bytes 688160 | tf_op jit(solution)/shard_map/ppermute | solution.py:430
  47.3 14.3 %probs.1 = (bf16[4,2,1280,512]{3,2,1,0:T(8,128)(2,1)}, f32[4,2,1,512]{3,2,1,0:T(1,128)}, bf16[4,2,128,512]{3,2,1,0:T(8,128)(2,1)}, bf16[512,512]{1,0:T(8,128)(2,...) custom-call(s32[1]{0:T(128)} %bitcast.core_ref, s32[1,512]{1,0:T(1,128)} %add_maximum_fusion.low_ref, ...), custom_call_target="tpu_custom_call" | custom-call | flops 1048576 | bytes 4096 | tf_op jit(solution)/shard_map/probs/pallas_call | solution.py:158
  62.4 1.2 add_convert_fusion.1
  63.8 1.2 collective-permute-start.8
  65.0 1.3 collective-permute-start.12
  66.4 3.1 %collective-permute-start.11 = (bf16[512,512]{1,0:T(8,128)(2,1)S(1)}, bf16[512,512]{1,0:T(8,128)(2,1)S(1)}, u32[]{:S(2)}, u32[]{:S(2)}) collective-permute-start(bf16[512,512]{1,0:T(8,128)(2,1)S(1)} %constant_dynamic-update-slice_fusion.6.refs_5_), channel_id=1, source_target_pairs={{0,8},{2,10},{4,12},{6,14},{8,16},{10,18},{12,20},{14,22},{16,24},... | collective-permute-start | bytes 1572872 | tf_op jit(solution)/shard_map/ppermute | solution.py:386
  69.5 1.3 collective-permute-start.15
  70.8 7.9 %collective-permute-done.12 = bf16[512,512]{1,0:T(8,128)(2,1)S(1)} collective-permute-done((bf16[512,512]{1,0:T(8,128)(2,1)}, bf16[512,512]{1,0:T(8,128)(2,1)S(1)}, u32[]{:S(2)}, u32[]{:S(2)}) %collective-permute-start.12) | collective-permute-done | bytes 524320 | tf_op jit(solution)/shard_map/ppermute | solution.py:430
  78.7 1.4 fusion.1
  80.1 2.4 %collective-permute-start.14 = (bf16[512,512]{1,0:T(8,128)(2,1)S(1)}, bf16[512,512]{1,0:T(8,128)(2,1)S(1)}, u32[]{:S(2)}, u32[]{:S(2)}) collective-permute-start(bf16[512,512]{1,0:T(8,128)(2,1)S(1)} %fusion.1), channel_id=1, source_target_pairs={{8,0},{10,2},{12,4},{14,6},{16,8},{18,10},{20,12},{22,14},{24,16},... | collective-permute-start | bytes 1572872 | tf_op jit(solution)/shard_map/ppermute | solution.py:386
  82.5 1.1 constant_dynamic-update-slice_fusion.refs_0_
  83.7 1.2 collective-permute-start.16
  85.7 1.2 collective-permute-start.13
  87.0 7.7 %collective-permute-done.14 = bf16[512,512]{1,0:T(8,128)(2,1)S(1)} collective-permute-done((bf16[512,512]{1,0:T(8,128)(2,1)S(1)}, bf16[512,512]{1,0:T(8,128)(2,1)S(1)}, u32[]{:S(2)}, u32[]{:S(2)}) %collective-permute-start.14) | collective-permute-done | bytes 524320 | tf_op jit(solution)/shard_map/ppermute | solution.py:386
  94.7 1.3 fusion.3.refs_4_
  96.0 3.1 %collective-permute-done.13.refs_4_ = bf16[512,512]{1,0:T(8,128)(2,1)S(1)} collective-permute-done((bf16[512,512]{1,0:T(8,128)(2,1)S(1)}, bf16[512,512]{1,0:T(8,128)(2,1)S(1)}, u32[]{:S(2)}, u32[]{:S(2)}) %collective-permute-start.13) | collective-permute-done | bytes 524320 | tf_op jit(solution)/shard_map/ppermute | solution.py:430
  100.2 1.2 collective-permute-start.19
  101.4 1.2 collective-permute-start.20
  103.5 15.9 %grads.1 = (bf16[256,2048]{1,0:T(8,128)(2,1)}, bf16[256,2048]{1,0:T(8,128)(2,1)}, bf16[2,256,1024]{2,1,0:T(8,128)(2,1)}, bf16[512,512]{1,0:T(8,128)(2,1)}, bf16[...) custom-call(s32[1]{0:T(128)} %bitcast.core_ref, bf16[4,2,1280,512]{3,2,1,0:T(8,128)(2,1)} %get-tuple-element.60.e_ref, ...), custom_call_target="tpu_custom_call" | custom-call | flops 1048576 | bytes 4096 | tf_op jit(solution)/shard_map/grads/pallas_call | solution.py:201
  119.4 6.6 %collective-permute-done.20.refs_7_ = bf16[512,512]{1,0:T(8,128)(2,1)} collective-permute-done((bf16[512,512]{1,0:T(8,128)(2,1)S(1)}, bf16[512,512]{1,0:T(8,128)(2,1)}, u32[]{:S(2)}, u32[]{:S(2)}) %collective-permute-start.20) | collective-permute-done | bytes 524320 | tf_op jit(solution)/shard_map/ppermute | solution.py:405
  126.8 8.1 %weight.1 = (f32[336,512]{1,0:T(8,128)}, bf16[336,512]{1,0:T(8,128)(2,1)}, bf16[336,512]{1,0:T(8,128)(2,1)}, bf16[336,512]{1,0:T(8,128)(2,1)}) custom-call(s32[2]{0:T(128)} %pad_add_fusion.1.at_ref, bf16[1344,512]{1,0:T(8,128)(2,1)} %copy-done.9, bf16[1344,512]{1,0:T(8,128)(2,1)} %copy-done.8, bf16[1344,512]{1,0:T(8,128)(2,1)} %collective-permute-done.16.refs_2_, ...), custom_call_target="tpu_custom_call" | custom-call | flops 1048576 | bytes 4096 | tf_op jit(solution)/shard_map/weight/pallas_call | solution.py:336
  134.9 1.3 collective-permute-start.27
  136.2 1.3 collective-permute-start.29
  137.5 1.1 constant_dynamic-slice_fusion.4
  138.7 2.4 %collective-permute-start.21 = (bf16[512,512]{1,0:T(8,128)(2,1)S(1)}, bf16[512,512]{1,0:T(8,128)(2,1)S(1)}, u32[]{:S(2)}, u32[]{:S(2)}) collective-permute-start(bf16[512,512]{1,0:T(8,128)(2,1)S(1)} %pad_maximum_fusion.5), channel_id=1, source_target_pairs={{0,2},{2,0},{4,6},{6,4},{8,10},{10,8},{12,14},{14,12},{16,18},{18,... | collective-permute-start | bytes 1572872 | tf_op jit(solution)/shard_map/ppermute | solution.py:390
  141.1 4.1 %collective-permute-start.23 = (bf16[512,512]{1,0:T(8,128)(2,1)}, bf16[512,512]{1,0:T(8,128)(2,1)S(1)}, u32[]{:S(2)}, u32[]{:S(2)}) collective-permute-start(bf16[512,512]{1,0:T(8,128)(2,1)} %get-tuple-element.80), channel_id=1, source_target_pairs={{4,0},{6,2},{8,4},{10,6},{12,8},{14,10},{16,12},{18,14},{20,16},{2... | collective-permute-start | bytes 1572872 | tf_op jit(solution)/shard_map/ppermute | solution.py:386
  145.3 1.9 collective-permute-start.24
  147.2 17.2 %collective-permute-done.28 = bf16[336,512]{1,0:T(8,128)(2,1)S(1)} collective-permute-done((bf16[336,512]{1,0:T(8,128)(2,1)}, bf16[336,512]{1,0:T(8,128)(2,1)S(1)}, u32[]{:S(2)}, u32[]{:S(2)}) %collective-permute-start.28) | collective-permute-done | bytes 344096 | tf_op jit(solution)/shard_map/ppermute | solution.py:581
  164.4 2.7 %collective-permute-done.29 = bf16[336,512]{1,0:T(8,128)(2,1)} collective-permute-done((bf16[336,512]{1,0:T(8,128)(2,1)}, bf16[336,512]{1,0:T(8,128)(2,1)}, u32[]{:S(2)}, u32[]{:S(2)}) %collective-permute-start.29) | collective-permute-done | bytes 344096 | tf_op jit(solution)/shard_map/ppermute | solution.py:581
  167.1 1.2 convert_add_fusion
  169.3 7.2 %tokens.1 = (bf16[256,5376]{1,0:T(8,128)(2,1)}, bf16[256,2688]{1,0:T(8,128)(2,1)}) custom-call(s32[1]{0:T(128)} %bitcast.7.at_ref, bf16[512,1024]{1,0:T(8,128)(2,1)} %copy-done.7, bf16[2688,1024]{1,0:T(8,128)(2,1)} %w_ref.1), custom_call_target="tpu_custom_call" | custom-call | flops 1048576 | bytes 4096 | tf_op jit(solution)/shard_map/tokens/pallas_call | solution.py:364
  176.5 1.3 collective-permute-start.26
  178.8 10.7 %collective-permute-done.24 = bf16[512,512]{1,0:T(8,128)(2,1)S(1)} collective-permute-done((bf16[512,512]{1,0:T(8,128)(2,1)}, bf16[512,512]{1,0:T(8,128)(2,1)S(1)}, u32[]{:S(2)}, u32[]{:S(2)}) %collective-permute-start.24) | collective-permute-done | bytes 524320 | tf_op jit(solution)/shard_map/ppermute | solution.py:386
  191.7 16.2 %collective-permute-done.26 = bf16[256,2688]{1,0:T(8,128)(2,1)S(1)} collective-permute-done((bf16[256,2688]{1,0:T(8,128)(2,1)}, bf16[256,2688]{1,0:T(8,128)(2,1)S(1)}, u32[]{:S(2)}, u32[]{:S(2)}) %collective-permute-start.26) | collective-permute-done | bytes 1376288 | tf_op jit(solution)/shard_map/ppermute | solution.py:395
  208.1 1.5 copy-done.24
  (134 shorter events, 18.8 us)
Async XLA Ops:
  0.7 8.4 %copy-start.1 = (bf16[1,256,2048]{2,1,0:T(8,128)(2,1)S(1)}, bf16[1,256,2048]{2,1,0:T(8,128)(2,1)}, u32[]{:S(2)}) copy-start(bf16[1,256,2048]{2,1,0:T(8,128)(2,1)} %param.7) | copy-start | bytes 3145732
  1.9 27.1 %collective-permute-start.3 = (bf16[256,1280]{1,0:T(8,128)(2,1)S(1)}, bf16[256,1280]{1,0:T(8,128)(2,1)}, u32[]{:S(2)}, u32[]{:S(2)}) collective-permute-start(bf16[256,1280]{1,0:T(8,128)(2,1)S(1)} %dynamic-slice_bitcast_fusion.1), channel_id=1, source_target_pairs={{0,1},{1,0},{2,3},{3,2},{4,5},{5,4},{6,7},{7,6},{8,9},{9,8},{10,11... | collective-permute-start | bytes 1966088 | tf_op jit(solution)/shard_map/ppermute | solution.py:395
  5.8 3.4 %collective-permute-start = (bf16[272,512]{1,0:T(8,128)(2,1)}, bf16[272,512]{1,0:T(8,128)(2,1)}, u32[]{:S(2)}, u32[]{:S(2)}) collective-permute-start(bf16[272,512]{1,0:T(8,128)(2,1)} %maximum_maximum_fusion.1), channel_id=1, source_target_pairs={{0,2},{2,0},{4,6},{6,4},{8,10},{10,8},{12,14},{14,12},{16,18},{18,... | collective-permute-start | bytes 835592 | tf_op jit(solution)/shard_map/ppermute | solution.py:390
  8.8 24.3 %collective-permute-start.4 = (bf16[256,1408]{1,0:T(8,128)(2,1)}, bf16[256,1408]{1,0:T(8,128)(2,1)}, u32[]{:S(2)}, u32[]{:S(2)}) collective-permute-start(bf16[256,1408]{1,0:T(8,128)(2,1)} %dynamic-slice_bitcast_fusion), channel_id=1, source_target_pairs={{0,1},{1,0},{2,3},{3,2},{4,5},{5,4},{6,7},{7,6},{8,9},{9,8},{10,11... | collective-permute-start | bytes 2162696 | tf_op jit(solution)/shard_map/ppermute | solution.py:395
  11.0 13.1 %copy-start.2 = (bf16[528,512]{1,0:T(8,128)(2,1)}, bf16[528,512]{1,0:T(8,128)(2,1)S(1)}, u32[]{:S(2)}) copy-start(bf16[528,512]{1,0:T(8,128)(2,1)S(1)} %pad_maximum_fusion.2.refs_2_) | copy-start | bytes 1622020
  11.0 28.0 %collective-permute-start.2 = (bf16[528,512]{1,0:T(8,128)(2,1)S(1)}, bf16[528,512]{1,0:T(8,128)(2,1)S(1)}, u32[]{:S(2)}, u32[]{:S(2)}) collective-permute-start(bf16[528,512]{1,0:T(8,128)(2,1)S(1)} %pad_maximum_fusion.2.refs_2_), channel_id=1, source_target_pairs={{0,4},{2,6},{4,8},{6,10},{8,12},{10,14},{12,16},{14,18},{16,20},{1... | collective-permute-start | bytes 1622024 | tf_op jit(solution)/shard_map/ppermute | solution.py:386
  14.2 25.1 %collective-permute-start.1 = (bf16[528,512]{1,0:T(8,128)(2,1)S(1)}, bf16[528,512]{1,0:T(8,128)(2,1)S(1)}, u32[]{:S(2)}, u32[]{:S(2)}) collective-permute-start(bf16[528,512]{1,0:T(8,128)(2,1)S(1)} %pad_maximum_fusion.2.refs_2_), channel_id=1, source_target_pairs={{0,8},{2,10},{4,12},{6,14},{8,16},{10,18},{12,20},{14,22},{16,24},... | collective-permute-start | bytes 1622024 | tf_op jit(solution)/shard_map/ppermute | solution.py:386
  18.4 27.7 %collective-permute-start.6 = (bf16[256,2048]{1,0:T(8,128)(2,1)}, bf16[256,2048]{1,0:T(8,128)(2,1)S(1)}, u32[]{:S(2)}, u32[]{:S(2)}) collective-permute-start(bf16[256,2048]{1,0:T(8,128)(2,1)} %pad_maximum_fusion), channel_id=1, source_target_pairs={{0,2},{2,0},{4,6},{6,4},{8,10},{10,8},{12,14},{14,12},{16,18},{18,... | collective-permute-start | bytes 3145736 | tf_op jit(solution)/shard_map/ppermute | solution.py:390
  29.0 17.1 %collective-permute-start.5 = (bf16[1344,256]{1,0:T(8,128)(2,1)S(1)}, bf16[1344,256]{1,0:T(8,128)(2,1)S(1)}, u32[]{:S(2)}, u32[]{:S(2)}) collective-permute-start(bf16[1344,256]{1,0:T(8,128)(2,1)S(1)} %copy-done.31), channel_id=1, source_target_pairs={{0,4},{2,6},{4,0},{6,2},{8,12},{10,14},{12,8},{14,10},{16,20},{18,... | collective-permute-start | bytes 2064392 | tf_op jit(solution)/shard_map/ppermute | solution.py:430
  37.8 23.9 %collective-permute-start.7 = (bf16[256,1024]{1,0:T(8,128)(2,1)}, bf16[256,1024]{1,0:T(8,128)(2,1)S(1)}, u32[]{:S(2)}, u32[]{:S(2)}) collective-permute-start(bf16[256,1024]{1,0:T(8,128)(2,1)} %product.2), channel_id=1, source_target_pairs={{0,1},{1,0},{2,3},{3,2},{4,5},{5,4},{6,7},{7,6},{8,9},{9,8},{10,11... | collective-permute-start | bytes 1572872 | tf_op jit(solution)/shard_map/ppermute | solution.py:395
  39.0 27.3 %collective-permute-start.10 = (bf16[1344,256]{1,0:T(8,128)(2,1)}, bf16[1344,256]{1,0:T(8,128)(2,1)S(1)}, u32[]{:S(2)}, u32[]{:S(2)}) collective-permute-start(bf16[1344,256]{1,0:T(8,128)(2,1)} %get-tuple-element.70), channel_id=1, source_target_pairs={{0,1},{1,0},{2,3},{3,2},{4,5},{5,4},{6,7},{7,6},{8,9},{9,8},{10,11... | collective-permute-start | bytes 2064392 | tf_op jit(solution)/shard_map/ppermute | solution.py:395
  39.3 27.1 %collective-permute-start.9 = (bf16[1344,256]{1,0:T(8,128)(2,1)}, bf16[1344,256]{1,0:T(8,128)(2,1)}, u32[]{:S(2)}, u32[]{:S(2)}) collective-permute-start(bf16[1344,256]{1,0:T(8,128)(2,1)} %get-tuple-element.69), channel_id=1, source_target_pairs={{0,4},{2,6},{4,0},{6,2},{8,12},{10,14},{12,8},{14,10},{16,20},{18,... | collective-permute-start | bytes 2064392 | tf_op jit(solution)/shard_map/ppermute | solution.py:430
  47.3 15.1 %copy-start.6 = (f32[256,1024]{1,0:T(8,128)S(1)}, f32[256,1024]{1,0:T(8,128)}, u32[]{:S(2)}) copy-start(f32[256,1024]{1,0:T(8,128)} %product.3) | copy-start | bytes 3145732
  63.8 2.5 %collective-permute-start.8 = (bf16[256,512]{1,0:T(8,128)(2,1)S(1)}, bf16[256,512]{1,0:T(8,128)(2,1)S(1)}, u32[]{:S(2)}, u32[]{:S(2)}) collective-permute-start(bf16[256,512]{1,0:T(8,128)(2,1)S(1)} %get-tuple-element.113), channel_id=1, source_target_pairs={{0,2},{2,0},{4,6},{6,4},{8,10},{10,8},{12,14},{14,12},{16,18},{18,... | collective-permute-start | bytes 786440 | tf_op jit(solution)/shard_map/ppermute | solution.py:390
  65.0 13.7 %collective-permute-start.12 = (bf16[512,512]{1,0:T(8,128)(2,1)}, bf16[512,512]{1,0:T(8,128)(2,1)S(1)}, u32[]{:S(2)}, u32[]{:S(2)}) collective-permute-start(bf16[512,512]{1,0:T(8,128)(2,1)} %get-tuple-element.67), channel_id=1, source_target_pairs={{0,4},{2,6},{4,0},{6,2},{8,12},{10,14},{12,8},{14,10},{16,20},{18,... | collective-permute-start | bytes 1572872 | tf_op jit(solution)/shard_map/ppermute | solution.py:430
  66.3 18.6 %copy-start.3 = (bf16[512,512]{1,0:T(8,128)(2,1)}, bf16[512,512]{1,0:T(8,128)(2,1)S(1)}, u32[]{:S(2)}) copy-start(bf16[512,512]{1,0:T(8,128)(2,1)S(1)} %constant_dynamic-update-slice_fusion.6.refs_5_) | copy-start | bytes 1572868
  66.4 18.5 %collective-permute-start.11 = (bf16[512,512]{1,0:T(8,128)(2,1)S(1)}, bf16[512,512]{1,0:T(8,128)(2,1)S(1)}, u32[]{:S(2)}, u32[]{:S(2)}) collective-permute-start(bf16[512,512]{1,0:T(8,128)(2,1)S(1)} %constant_dynamic-update-slice_fusion.6.refs_5_), channel_id=1, source_target_pairs={{0,8},{2,10},{4,12},{6,14},{8,16},{10,18},{12,20},{14,22},{16,24},... | collective-permute-start | bytes 1572872 | tf_op jit(solution)/shard_map/ppermute | solution.py:386
  69.5 29.6 %collective-permute-start.15 = (bf16[1344,256]{1,0:T(8,128)(2,1)}, bf16[1344,256]{1,0:T(8,128)(2,1)S(1)}, u32[]{:S(2)}, u32[]{:S(2)}) collective-permute-start(bf16[1344,256]{1,0:T(8,128)(2,1)} %copy-done.30), channel_id=1, source_target_pairs={{0,1},{1,0},{2,3},{3,2},{4,5},{5,4},{6,7},{7,6},{8,9},{9,8},{10,11... | collective-permute-start | bytes 2064392 | tf_op jit(solution)/shard_map/ppermute | solution.py:395
  80.1 14.6 %copy-start.18 = (bf16[512,512]{1,0:T(8,128)(2,1)S(1)}, bf16[512,512]{1,0:T(8,128)(2,1)}, u32[]{:S(2)}) copy-start(bf16[512,512]{1,0:T(8,128)(2,1)} %get-tuple-element.75) | copy-start | bytes 1572868
  80.1 14.6 %collective-permute-start.14 = (bf16[512,512]{1,0:T(8,128)(2,1)S(1)}, bf16[512,512]{1,0:T(8,128)(2,1)S(1)}, u32[]{:S(2)}, u32[]{:S(2)}) collective-permute-start(bf16[512,512]{1,0:T(8,128)(2,1)S(1)} %fusion.1), channel_id=1, source_target_pairs={{8,0},{10,2},{12,4},{14,6},{16,8},{18,10},{20,12},{22,14},{24,16},... | collective-permute-start | bytes 1572872 | tf_op jit(solution)/shard_map/ppermute | solution.py:386
  83.7 12.3 %copy-start.9 = (bf16[1344,512]{1,0:T(8,128)(2,1)}, bf16[1344,512]{1,0:T(8,128)(2,1)S(1)}, u32[]{:S(2)}) copy-start(bf16[1344,512]{1,0:T(8,128)(2,1)S(1)} %constant_dynamic-update-slice_fusion.refs_0_) | copy-start | bytes 4128772
  83.7 43.1 %collective-permute-start.16 = (bf16[1344,512]{1,0:T(8,128)(2,1)S(1)}, bf16[1344,512]{1,0:T(8,128)(2,1)}, u32[]{:S(2)}, u32[]{:S(2)}) collective-permute-start(bf16[1344,512]{1,0:T(8,128)(2,1)S(1)} %constant_dynamic-update-slice_fusion.refs_0_), channel_id=1, source_target_pairs={{0,2},{2,0},{4,6},{6,4},{8,10},{10,8},{12,14},{14,12},{16,18},{18,... | collective-permute-start | bytes 4128776 | tf_op jit(solution)/shard_map/ppermute | solution.py:390
  85.7 13.4 %collective-permute-start.13 = (bf16[512,512]{1,0:T(8,128)(2,1)S(1)}, bf16[512,512]{1,0:T(8,128)(2,1)S(1)}, u32[]{:S(2)}, u32[]{:S(2)}) collective-permute-start(bf16[512,512]{1,0:T(8,128)(2,1)S(1)} %broadcast_select_fusion), channel_id=1, source_target_pairs={{0,4},{2,6},{4,0},{6,2},{8,12},{10,14},{12,8},{14,10},{16,20},{18,... | collective-permute-start | bytes 1572872 | tf_op jit(solution)/shard_map/ppermute | solution.py:430
  96.0 23.4 %copy-start.4 = (bf16[512,512]{1,0:T(8,128)(2,1)}, bf16[512,512]{1,0:T(8,128)(2,1)S(1)}, u32[]{:S(2)}) copy-start(bf16[512,512]{1,0:T(8,128)(2,1)S(1)} %fusion.3.refs_4_) | copy-start | bytes 1572868
  99.1 20.2 %copy-start.8 = (bf16[1344,512]{1,0:T(8,128)(2,1)}, bf16[1344,512]{1,0:T(8,128)(2,1)S(1)}, u32[]{:S(2)}) copy-start(bf16[1344,512]{1,0:T(8,128)(2,1)S(1)} %constant_dynamic-update-slice_fusion.2.refs_1_) | copy-start | bytes 4128772
  99.2 27.6 %collective-permute-start.17 = (bf16[1344,512]{1,0:T(8,128)(2,1)S(1)}, bf16[1344,512]{1,0:T(8,128)(2,1)}, u32[]{:S(2)}, u32[]{:S(2)}) collective-permute-start(bf16[1344,512]{1,0:T(8,128)(2,1)S(1)} %constant_dynamic-update-slice_fusion.2.refs_1_), channel_id=1, source_target_pairs={{0,2},{2,0},{4,6},{6,4},{8,10},{10,8},{12,14},{14,12},{16,18},{18,... | collective-permute-start | bytes 4128776 | tf_op jit(solution)/shard_map/ppermute | solution.py:390
  100.2 19.2 %collective-permute-start.19 = (bf16[512,512]{1,0:T(8,128)(2,1)S(1)}, bf16[512,512]{1,0:T(8,128)(2,1)}, u32[]{:S(2)}, u32[]{:S(2)}) collective-permute-start(bf16[512,512]{1,0:T(8,128)(2,1)S(1)} %fusion.3.refs_4_), channel_id=1, source_target_pairs={{0,1},{1,0},{2,3},{3,2},{4,5},{5,4},{6,7},{7,6},{8,9},{9,8},{10,11... | collective-permute-start | bytes 1572872 | tf_op jit(solution)/shard_map/ppermute | solution.py:395
  101.4 24.6 %collective-permute-start.20 = (bf16[512,512]{1,0:T(8,128)(2,1)S(1)}, bf16[512,512]{1,0:T(8,128)(2,1)}, u32[]{:S(2)}, u32[]{:S(2)}) collective-permute-start(bf16[512,512]{1,0:T(8,128)(2,1)S(1)} %fusion.3.refs_4_), channel_id=1, source_target_pairs={{0,5},{1,4},{2,7},{3,6},{4,1},{5,0},{6,3},{7,2},{8,13},{9,12},{10,... | collective-permute-start | bytes 1572872 | tf_op jit(solution)/shard_map/ppermute | solution.py:405
  102.6 24.1 %collective-permute-start.18 = (bf16[512,512]{1,0:T(8,128)(2,1)S(1)}, bf16[512,512]{1,0:T(8,128)(2,1)}, u32[]{:S(2)}, u32[]{:S(2)}) collective-permute-start(bf16[512,512]{1,0:T(8,128)(2,1)S(1)} %fusion.3.refs_4_), channel_id=1, source_target_pairs={{0,4},{1,5},{2,6},{3,7},{4,0},{5,1},{6,2},{7,3},{8,12},{9,13},{10,... | collective-permute-start | bytes 1572872 | tf_op jit(solution)/shard_map/ppermute | solution.py:405
  119.4 18.1 %copy-start.5 = (bf16[512,512]{1,0:T(8,128)(2,1)S(1)}, bf16[512,512]{1,0:T(8,128)(2,1)}, u32[]{:S(2)}) copy-start(bf16[512,512]{1,0:T(8,128)(2,1)} %copy-done.4) | copy-start | bytes 1572868
  134.9 10.4 %collective-permute-start.27 = (bf16[336,512]{1,0:T(8,128)(2,1)}, bf16[336,512]{1,0:T(8,128)(2,1)S(1)}, u32[]{:S(2)}, u32[]{:S(2)}) collective-permute-start(bf16[336,512]{1,0:T(8,128)(2,1)} %get-tuple-element.100), channel_id=1, source_target_pairs={{0,8},{2,10},{4,12},{6,14},{8,16},{10,18},{12,20},{14,22},{16,24},... | collective-permute-start | bytes 1032200 | tf_op jit(solution)/shard_map/ppermute | solution.py:581
  136.1 28.2 %collective-permute-start.28 = (bf16[336,512]{1,0:T(8,128)(2,1)}, bf16[336,512]{1,0:T(8,128)(2,1)S(1)}, u32[]{:S(2)}, u32[]{:S(2)}) collective-permute-start(bf16[336,512]{1,0:T(8,128)(2,1)} %get-tuple-element.101), channel_id=1, source_target_pairs={{0,16},{2,18},{4,20},{6,22},{8,24},{10,26},{12,28},{14,30},{16,0},... | collective-permute-start | bytes 1032200 | tf_op jit(solution)/shard_map/ppermute | solution.py:581
  136.2 31.0 %copy-start.16 = (f32[336,512]{1,0:T(8,128)S(1)}, f32[336,512]{1,0:T(8,128)}, u32[]{:S(2)}) copy-start(f32[336,512]{1,0:T(8,128)} %get-tuple-element.88) | copy-start | bytes 2064388
  136.2 31.0 %collective-permute-start.29 = (bf16[336,512]{1,0:T(8,128)(2,1)}, bf16[336,512]{1,0:T(8,128)(2,1)}, u32[]{:S(2)}, u32[]{:S(2)}) collective-permute-start(bf16[336,512]{1,0:T(8,128)(2,1)} %get-tuple-element.102), channel_id=1, source_target_pairs={{0,24},{2,26},{4,28},{6,30},{8,0},{10,2},{12,4},{14,6},{16,8},{18,... | collective-permute-start | bytes 1032200 | tf_op jit(solution)/shard_map/ppermute | solution.py:581
  138.7 29.6 %collective-permute-start.21 = (bf16[512,512]{1,0:T(8,128)(2,1)S(1)}, bf16[512,512]{1,0:T(8,128)(2,1)S(1)}, u32[]{:S(2)}, u32[]{:S(2)}) collective-permute-start(bf16[512,512]{1,0:T(8,128)(2,1)S(1)} %pad_maximum_fusion.5), channel_id=1, source_target_pairs={{0,2},{2,0},{4,6},{6,4},{8,10},{10,8},{12,14},{14,12},{16,18},{18,... | collective-permute-start | bytes 1572872 | tf_op jit(solution)/shard_map/ppermute | solution.py:390
  141.1 48.4 %collective-permute-start.23 = (bf16[512,512]{1,0:T(8,128)(2,1)}, bf16[512,512]{1,0:T(8,128)(2,1)S(1)}, u32[]{:S(2)}, u32[]{:S(2)}) collective-permute-start(bf16[512,512]{1,0:T(8,128)(2,1)} %get-tuple-element.80), channel_id=1, source_target_pairs={{4,0},{6,2},{8,4},{10,6},{12,8},{14,10},{16,12},{18,14},{20,16},{2... | collective-permute-start | bytes 1572872 | tf_op jit(solution)/shard_map/ppermute | solution.py:386
  145.3 44.2 %collective-permute-start.24 = (bf16[512,512]{1,0:T(8,128)(2,1)}, bf16[512,512]{1,0:T(8,128)(2,1)S(1)}, u32[]{:S(2)}, u32[]{:S(2)}) collective-permute-start(bf16[512,512]{1,0:T(8,128)(2,1)} %get-tuple-element.97), channel_id=1, source_target_pairs={{8,0},{10,2},{12,4},{14,6},{16,8},{18,10},{20,12},{22,14},{24,16},... | collective-permute-start | bytes 1572872 | tf_op jit(solution)/shard_map/ppermute | solution.py:386
  169.3 8.4 %copy-start.29 = (bf16[2,256,1024]{2,1,0:T(8,128)(2,1)S(1)}, bf16[2,256,1024]{2,1,0:T(8,128)(2,1)}, u32[]{:S(2)}) copy-start(bf16[2,256,1024]{2,1,0:T(8,128)(2,1)} %get-tuple-element.93) | copy-start | bytes 3145732
  169.3 20.1 %copy-start.21 = (bf16[512,512]{1,0:T(8,128)(2,1)S(1)}, bf16[512,512]{1,0:T(8,128)(2,1)}, u32[]{:S(2)}) copy-start(bf16[512,512]{1,0:T(8,128)(2,1)} %get-tuple-element.95) | copy-start | bytes 1572868
  176.5 31.4 %collective-permute-start.26 = (bf16[256,2688]{1,0:T(8,128)(2,1)}, bf16[256,2688]{1,0:T(8,128)(2,1)S(1)}, u32[]{:S(2)}, u32[]{:S(2)}) collective-permute-start(bf16[256,2688]{1,0:T(8,128)(2,1)} %get-tuple-element.92), channel_id=1, source_target_pairs={{0,1},{1,0},{2,3},{3,2},{4,5},{5,4},{6,7},{7,6},{8,9},{9,8},{10,11... | collective-permute-start | bytes 4128776 | tf_op jit(solution)/shard_map/ppermute | solution.py:395
  177.8 13.7 %collective-permute-start.22 = (bf16[2,256,1024]{2,1,0:T(8,128)(2,1)S(1)}, bf16[2,256,1024]{2,1,0:T(8,128)(2,1)S(1)}, u32[]{:S(2)}, u32[]{:S(2)}) collective-permute-start(bf16[2,256,1024]{2,1,0:T(8,128)(2,1)S(1)} %copy-done.29), channel_id=1, source_target_pairs={{0,2},{2,0},{4,6},{6,4},{8,10},{10,8},{12,14},{14,12},{16,18},{18,... | collective-permute-start | bytes 3145736 | tf_op jit(solution)/shard_map/ppermute | solution.py:390
  178.7 11.8 %collective-permute-start.30 = (f32[168,512]{1,0:T(8,128)S(1)}, f32[168,512]{1,0:T(8,128)S(1)}, u32[]{:S(2)}, u32[]{:S(2)}) collective-permute-start(f32[168,512]{1,0:T(8,128)S(1)} %get-tuple-element.105), channel_id=1, source_target_pairs={{0,2},{2,0},{4,6},{6,4},{8,10},{10,8},{12,14},{14,12},{16,18},{18,... | collective-permute-start | bytes 1032200 | tf_op jit(solution)/shard_map/ppermute | solution.py:390
  189.8 1.7 collective-permute-start.25
  190.4 17.5 %copy-start.23 = (bf16[256,5376]{1,0:T(8,128)(2,1)S(1)}, bf16[256,5376]{1,0:T(8,128)(2,1)}, u32[]{:S(2)}) copy-start(bf16[256,5376]{1,0:T(8,128)(2,1)} %get-tuple-element.99) | copy-start | bytes 8257540
  190.5 17.6 %copy-start.17 = (f32[168,1024]{1,0:T(8,128)}, f32[168,1024]{1,0:T(8,128)S(1)}, u32[]{:S(2)}) copy-start(f32[168,1024]{1,0:T(8,128)S(1)} %constant_dynamic-update-slice_fusion.4) | copy-start | bytes 2064388
  191.5 16.6 %copy-start.20 = (bf16[1,256,1024]{2,1,0:T(8,128)(2,1)}, bf16[1,256,1024]{2,1,0:T(8,128)(2,1)S(1)}, u32[]{:S(2)}) copy-start(bf16[1,256,1024]{2,1,0:T(8,128)(2,1)S(1)} %bitcast_dynamic-update-slice_fusion.1) | copy-start | bytes 1572868
  191.7 16.4 %copy-start.26 = (bf16[1,256,2048]{2,1,0:T(8,128)(2,1)}, bf16[1,256,2048]{2,1,0:T(8,128)(2,1)S(1)}, u32[]{:S(2)}) copy-start(bf16[1,256,2048]{2,1,0:T(8,128)(2,1)S(1)} %get-tuple-element.104) | copy-start | bytes 3145732
  191.7 16.4 %copy-start.28 = (bf16[1,256,2048]{2,1,0:T(8,128)(2,1)}, bf16[1,256,2048]{2,1,0:T(8,128)(2,1)S(1)}, u32[]{:S(2)}) copy-start(bf16[1,256,2048]{2,1,0:T(8,128)(2,1)S(1)} %get-tuple-element.103) | copy-start | bytes 3145732
  (15 other events, 53.4 us)

commit v8 on v6

--- a/solution.py
+++ b/solution.py
@@ -520,7 +520,7 @@
         partial = [run_product(zero_arg, parts, w_value, BF16) for parts in sent]
     else:
         partial = [dot(parts[0], w_value).astype(BF16) for parts in sent]
-    low = after(low, *partial, *over_y.values())
+    low = after(low, *partial)
     e, inv, do_t, dv_far, dv_near, dv_mine = run_probs(
         core_arg, low, queries[0], q_other, d_out[0], keys, chip_rows, half_kv
     )
@@ -528,18 +528,17 @@
 
     value_back = [rotated(x, -s - 1) for s, x in enumerate(partial)]
     over_fsdp = {s: rotated(after(by_place[0, s], sent), s) for s in range(1, n_fsdp)}
-    value_back = [after(x, dv_near) for x in value_back]
-    value_back[0] = after(value_back[0], over_fsdp)
+    value_back = [after(x, dv_near, over_y) for x in value_back]
     value_sum = value_own
     for x in value_back:
         value_sum = value_sum + x.astype(F32)
     own_values = value_sum.astype(BF16)
     v_own = placed(core, cols(own_values, core, half_kv), swapped(cols(own_values, 1 - core, half_kv)), 0)
 
-    over_y[0] = flipped(after(by_place[1, 0], k_near))
-    v_own, over_y[0] = lax.optimization_barrier((v_own, over_y[0]))
+    late_y = flipped(after(by_place[1, 0], k_near))
+    v_own, late_y, over_fsdp = lax.optimization_barrier((v_own, late_y, over_fsdp))
     v_far = shifted(v_own, 4)
-    own_pairs = [jnp.concatenate([by_place[0, 0], over_y[0]], 1)]
+    own_pairs = [jnp.concatenate([by_place[0, 0], late_y], 1)]
     other_pairs = [swapped(after(own_pairs[0], v_own))]
     relayed_y = {s: rotated(after(over_y[s], own_values), s) for s in range(1, n_fsdp)}
 
@@ -553,21 +552,22 @@
     dv_fsdp = [dv_chip] + [rotated(dv_chip, s) for s in range(1, n_fsdp)]
     dv_over_y = [moved(dv_chip, 1, s) for s in range(n_fsdp)]
     for s in range(1, n_fsdp):
-        own_pairs.append(jnp.concatenate([over_fsdp[s], after(relayed_y[s], dv_chip)], 1))
+        own_pairs.append(jnp.concatenate([over_fsdp[s], relayed_y[s]], 1))
         other_pairs.append(swapped(own_pairs[s]))
-    v_near = after(v_near, dv_chip)
     vals = [v_far, v_near, v_own]
+    v_near, dv_fsdp[1:] = lax.optimization_barrier((v_near, dv_fsdp[1:]))
+    vals = [v_far, v_near, v_own]
+    dv_sides = [
+        jnp.concatenate([rows_of(x, at, shard_rows) for x in dv_fsdp], 0) for at in (core, 1 - core)
+    ]
+    dv_other = swapped(dv_sides[1])
     out, dq, other, dk_far, dk_near, dk_mine = run_grads(
-        core_arg, e, inv, do_t, queries[0], q_other, keys, vals, chip_rows, half_kv
+        after(core_arg, *dv_sides), e, inv, do_t, queries[0], q_other, keys, vals, chip_rows, half_kv
     )
     dk_back = [shifted(dk_near, -2), shifted(dk_far, -4)]
 
-    dv_fsdp = [after(x, dk_near) for x in dv_fsdp]
     dv_over_y = [after(x, dk_near) for x in dv_over_y]
-    dv_other = swapped(jnp.concatenate([rows_of(x, 1 - core, shard_rows) for x in dv_fsdp], 0))
-    dv_rows = placed(
-        core, jnp.concatenate([rows_of(x, core, shard_rows) for x in dv_fsdp], 0), dv_other, 1
-    )
+    dv_rows = placed(core, dv_sides[0], after(dv_other, dk_near), 1)
     dv_rows = after(dv_rows, *dv_over_y)
     if aligned:
         d_tokens, *made = run_tokens(fsdp_arg, dv_rows, w_value, n_fsdp)
@@ -605,7 +605,6 @@
     for x in over_z:
         row_sum = row_sum + x.astype(F32)
     d_weight = placed(core, rows_of(row_sum, core, out_rows), swapped(rows_of(row_sum, 1 - core, out_rows)), 1)
-
     dk_chip = (dk_mine.astype(F32) + dk_back[0].astype(F32) + dk_back[1].astype(F32)).astype(BF16)
     d_keys = placed(core, rows_of(dk_chip, core, shard_rows), swapped(rows_of(dk_chip, 1 - core, shard_rows)), 1)
     other = swapped(after(other, *made))

time: 187 us -> 190 us (1.016); the launches traced: 186 us -> 186 us
  waiting for transfers between devices: 46.7 us -> 40.3 us
  starting transfers between devices: 58.3 us -> 63.2 us
  other arithmetic: 6.6 us -> 8.5 us
    ppermute x9, starting transfers between devices: 21.8 us -> 28.4 us  [swapped(): lax.ppermute(x, 'ctx', [(i, i ^ 1) for i in range(lax.axis_size('ctx'))])]
    ppermute x4, waiting for transfers between devices: 6.11 us -> 0.59 us  [flipped(): lax.ppermute(x, 'ctx', [(i, i ^ 2) for i in range(lax.axis_size('ctx'))])]
    ppermute x3, waiting for transfers between devices: 20.5 us -> 25.1 us  [shards(): lax.ppermute(by_z[d], 'ctx', [(i, (i + 4 * d) % n_ctx) for i in range(n_c...]
    ppermute x7, waiting for transfers between devices: 10.9 us -> 7.89 us  [rotated(): lax.ppermute(x, 'fsdp', [(i, (i + by) % length) for i in range(length)])]
    ppermute x6, waiting for transfers between devices: 7.99 us -> 5.59 us  [shifted(): lax.ppermute(x, 'ctx', [(i, i + by) for i in range(length) if 0 <= i + by...]
    unnamed x64 -> x60, local copies, waits for them, and re-layouts: 4.99 us -> 5.05 us
  transfers between devices with their start and end apart: 31 -> 31, of which waited for: 10 -> 10; matrix products, arithmetic and copies ran while one was open for 7% -> 8% of each run, Pallas kernels for 32% -> 32%
where the time goes in v8:
time: 190 us; the launch traced here: 186 us
  starting transfers between devices  63.2 us (33%)
  Pallas kernels  59.2 us (31%)
  waiting for transfers between devices  40.3 us (21%)
  local copies, waits for them, and re-layouts  13.3 us (7%)
  other arithmetic  8.5 us (4%)
    ppermute x9, starting transfers between devices, swapped(): lax.ppermute(x, 'ctx', [(i, i ^ 1) for i in range(lax.axis_size('ctx'))])  28.4 us
    ppermute x3, waiting for transfers between devices, shards(): lax.ppermute(by_z[d], 'ctx', [(i, (i + 4 * d) % n_ctx) for i in range(n_c...  25.1 us
    pallas_call x1, Pallas kernels, run_grads(): pl.pallas_call(functools.partial(grads_kernel, blk, n_arr - 1), grid_spec...  16 us
    ppermute x6, starting transfers between devices, shifted(): lax.ppermute(x, 'ctx', [(i, i + by) for i in range(length) if 0 <= i + by...  15.8 us
    pallas_call x1, Pallas kernels, run_probs(): pl.pallas_call(functools.partial(probs_kernel, blk, n_arr - 1), grid_spec...  14.3 us
    pallas_call x2, Pallas kernels, run_product(): pl.pallas_call(product_kernel, grid_spec=pltpu.PrefetchScalarGridSpec(num...  9.54 us
    pallas_call x1, Pallas kernels, run_weight(): pl.pallas_call(functools.partial(weight_kernel, n_z, n), grid_spec=pltpu....  8.12 us
    ppermute x7, waiting for transfers between devices, rotated(): lax.ppermute(x, 'fsdp', [(i, (i + by) % length) for i in range(length)])  7.89 us
  transfers between devices with their start and end apart: 31, of which 10 were waited for; matrix products, arithmetic and copies ran while one was open for 8% of the time, Pallas kernels for 32%

profile of v8, /device:TPU:9, one launch (start us, length us, event | category | flops | bytes accessed | tf_op | source)
XLA Modules:
  0.0 185.8 jit_solution(13787818840547860903)
XLA Ops:
  0.7 2.0 %dynamic-slice_bitcast_fusion.1 = bf16[256,1280]{1,0:T(8,128)(2,1)} fusion(bf16[1,256,5376]{2,1,0:T(8,128)(2,1)} %param.6, s32[]{:T(128)S(6)} %select_n.94), kind=kLoop, calls=%fused_computation.15 | loop fusion | bytes 1310724 | tf_op jit(solution)/shard_map/dynamic_slice | solution.py:469
  2.6 1.2 collective-permute-start.3
  4.6 1.1 dynamic-slice_bitcast_fusion.5
  6.5 1.0 collective-permute-start
  7.5 2.0 %dynamic-slice_bitcast_fusion = bf16[256,1408]{1,0:T(8,128)(2,1)} fusion(bf16[1,256,5376]{2,1,0:T(8,128)(2,1)} %param.6, s32[]{:T(128)S(6)} %select_n.97), kind=kLoop, calls=%fused_computation.12 | loop fusion | bytes 1441796 | tf_op jit(solution)/shard_map/dynamic_slice | solution.py:469
  10.0 3.1 %collective-permute-start.2 = (bf16[528,512]{1,0:T(8,128)(2,1)S(1)}, bf16[528,512]{1,0:T(8,128)(2,1)S(1)}, u32[]{:S(2)}, u32[]{:S(2)}) collective-permute-start(bf16[528,512]{1,0:T(8,128)(2,1)S(1)} %pad_maximum_fusion.2.refs_2_), channel_id=1, source_target_pairs={{0,4},{2,6},{4,8},{6,10},{8,12},{10,14},{12,16},{14,18},{16,20},{1... | collective-permute-start | bytes 1622024 | tf_op jit(solution)/shard_map/ppermute | solution.py:386
  13.2 3.2 %collective-permute-start.1 = (bf16[528,512]{1,0:T(8,128)(2,1)S(1)}, bf16[528,512]{1,0:T(8,128)(2,1)S(1)}, u32[]{:S(2)}, u32[]{:S(2)}) collective-permute-start(bf16[528,512]{1,0:T(8,128)(2,1)S(1)} %pad_maximum_fusion.2.refs_2_), channel_id=1, source_target_pairs={{0,8},{2,10},{4,12},{6,14},{8,16},{10,18},{12,20},{14,22},{16,24},... | collective-permute-start | bytes 1622024 | tf_op jit(solution)/shard_map/ppermute | solution.py:386
  16.5 0.9 collective-permute-start.5
  18.0 4.2 %pieces.1 = (bf16[1344,256]{1,0:T(8,128)(2,1)}, bf16[1344,256]{1,0:T(8,128)(2,1)}, bf16[1344,256]{1,0:T(8,128)(2,1)}, bf16[1344,256]{1,0:T(8,128)(2,1)}) custom-call(s32[2]{0:T(128)} %pad_add_fusion.at_ref, bf16[256,5376]{1,0:T(8,128)(2,1)} %bitcast.29), custom_call_target="tpu_custom_call" | custom-call | flops 1048576 | bytes 4096 | tf_op jit(solution)/shard_map/pieces/pallas_call | solution.py:260
  22.3 4.9 %product.3 = f32[256,1024]{1,0:T(8,128)} custom-call(s32[1]{0:T(128)} %bitcast.10.at_ref, bf16[256,5376]{1,0:T(8,128)(2,1)} %bitcast.30, bf16[2688,1024]{1,0:T(8,128)(2,1)} %w_ref.1), custom_call_target="tpu_custom_call" | custom-call | flops 1048576 | bytes 4096 | tf_op jit(solution)/shard_map/product/pallas_call | solution.py:290
  27.1 1.3 collective-permute-start.8
  28.5 5.5 %collective-permute-done.4.refs_1_ = bf16[256,1408]{1,0:T(8,128)(2,1)S(1)} collective-permute-done((bf16[256,1408]{1,0:T(8,128)(2,1)}, bf16[256,1408]{1,0:T(8,128)(2,1)S(1)}, u32[]{:S(2)}, u32[]{:S(2)}) %collective-permute-start.4) | collective-permute-done | bytes 720928 | tf_op jit(solution)/shard_map/ppermute | solution.py:395
  34.0 0.9 copy-done.14
  34.9 4.7 %product.2 = bf16[256,1024]{1,0:T(8,128)(2,1)} custom-call(s32[1]{0:T(128)} %constant.86.clone.1.at_ref, bf16[256,1280]{1,0:T(8,128)(2,1)} %collective-permute-done.3.refs_0_, bf16[256,1408]{1,0:T(8,128)(2,1)} %copy-done.14, bf16[2688,1024]{1,0:T(8,128)(2,1)} %w_ref.1), custom_call_target="tpu_custom_call" | custom-call | flops 1048576 | bytes 4096 | tf_op jit(solution)/shard_map/product/pallas_call | solution.py:290
  39.5 1.2 collective-permute-start.7
  42.3 1.2 collective-permute-start.10
  43.5 1.0 copy-done
  44.5 14.3 %probs.1 = (bf16[4,2,1280,512]{3,2,1,0:T(8,128)(2,1)}, f32[4,2,1,512]{3,2,1,0:T(1,128)}, bf16[4,2,128,512]{3,2,1,0:T(8,128)(2,1)}, bf16[512,512]{1,0:T(8,128)(2,...) custom-call(s32[1]{0:T(128)} %bitcast.core_ref, s32[1,512]{1,0:T(1,128)} %add_maximum_fusion.low_ref, ...), custom_call_target="tpu_custom_call" | custom-call | flops 1048576 | bytes 4096 | tf_op jit(solution)/shard_map/probs/pallas_call | solution.py:158
  59.1 1.2 add_convert_fusion.1
  60.4 2.6 %collective-permute-start.9 = (bf16[256,512]{1,0:T(8,128)(2,1)S(1)}, bf16[256,512]{1,0:T(8,128)(2,1)S(1)}, u32[]{:S(2)}, u32[]{:S(2)}) collective-permute-start(bf16[256,512]{1,0:T(8,128)(2,1)S(1)} %get-tuple-element.123), channel_id=1, source_target_pairs={{0,2},{2,0},{4,6},{6,4},{8,10},{10,8},{12,14},{14,12},{16,18},{18,... | collective-permute-start | bytes 786440 | tf_op jit(solution)/shard_map/ppermute | solution.py:390
  63.1 1.3 collective-permute-start.20
  64.5 2.0 %collective-permute-done.11 = bf16[1344,256]{1,0:T(8,128)(2,1)S(1)} collective-permute-done((bf16[1344,256]{1,0:T(8,128)(2,1)}, bf16[1344,256]{1,0:T(8,128)(2,1)S(1)}, u32[]{:S(2)}, u32[]{:S(2)}) %collective-permute-start.11) | collective-permute-done | bytes 688160 | tf_op jit(solution)/shard_map/ppermute | solution.py:395
  66.5 3.2 %collective-permute-start.13 = (bf16[512,512]{1,0:T(8,128)(2,1)S(1)}, bf16[512,512]{1,0:T(8,128)(2,1)S(1)}, u32[]{:S(2)}, u32[]{:S(2)}) collective-permute-start(bf16[512,512]{1,0:T(8,128)(2,1)S(1)} %constant_dynamic-update-slice_fusion.6.refs_5_), channel_id=1, source_target_pairs={{0,8},{2,10},{4,12},{6,14},{8,16},{10,18},{12,20},{14,22},{16,24},... | collective-permute-start | bytes 1572872 | tf_op jit(solution)/shard_map/ppermute | solution.py:386
  70.4 2.4 %collective-permute-start.12 = (bf16[512,512]{1,0:T(8,128)(2,1)S(1)}, bf16[512,512]{1,0:T(8,128)(2,1)S(1)}, u32[]{:S(2)}, u32[]{:S(2)}) collective-permute-start(bf16[512,512]{1,0:T(8,128)(2,1)S(1)} %fusion.1), channel_id=1, source_target_pairs={{8,0},{10,2},{12,4},{14,6},{16,8},{18,10},{20,12},{22,14},{24,16},... | collective-permute-start | bytes 1572872 | tf_op jit(solution)/shard_map/ppermute | solution.py:386
  72.8 1.1 constant_dynamic-update-slice_fusion.refs_0_
  74.0 4.4 %collective-permute-start.21 = (bf16[1344,512]{1,0:T(8,128)(2,1)S(1)}, bf16[1344,512]{1,0:T(8,128)(2,1)}, u32[]{:S(2)}, u32[]{:S(2)}) collective-permute-start(bf16[1344,512]{1,0:T(8,128)(2,1)S(1)} %constant_dynamic-update-slice_fusion.refs_0_), channel_id=1, source_target_pairs={{0,2},{2,0},{4,6},{6,4},{8,10},{10,8},{12,14},{14,12},{16,18},{18,... | collective-permute-start | bytes 4128776 | tf_op jit(solution)/shard_map/ppermute | solution.py:390
  78.6 1.3 collective-permute-start.14
  79.9 1.9 %collective-permute-done.12 = bf16[512,512]{1,0:T(8,128)(2,1)S(1)} collective-permute-done((bf16[512,512]{1,0:T(8,128)(2,1)S(1)}, bf16[512,512]{1,0:T(8,128)(2,1)S(1)}, u32[]{:S(2)}, u32[]{:S(2)}) %collective-permute-start.12) | collective-permute-done | bytes 524320 | tf_op jit(solution)/shard_map/ppermute | solution.py:386
  82.1 1.3 collective-permute-start.15
  83.4 5.3 %collective-permute-start.22 = (bf16[1344,512]{1,0:T(8,128)(2,1)S(1)}, bf16[1344,512]{1,0:T(8,128)(2,1)}, u32[]{:S(2)}, u32[]{:S(2)}) collective-permute-start(bf16[1344,512]{1,0:T(8,128)(2,1)S(1)} %constant_dynamic-update-slice_fusion.2.refs_1_), channel_id=1, source_target_pairs={{0,2},{2,0},{4,6},{6,4},{8,10},{10,8},{12,14},{14,12},{16,18},{18,... | collective-permute-start | bytes 4128776 | tf_op jit(solution)/shard_map/ppermute | solution.py:390
  90.6 0.9 pad_maximum_fusion.5
  91.6 10.9 %collective-permute-start.16 = (bf16[512,512]{1,0:T(8,128)(2,1)}, bf16[512,512]{1,0:T(8,128)(2,1)}, u32[]{:S(2)}, u32[]{:S(2)}) collective-permute-start(bf16[512,512]{1,0:T(8,128)(2,1)} %pad_maximum_fusion.5), channel_id=1, source_target_pairs={{0,2},{2,0},{4,6},{6,4},{8,10},{10,8},{12,14},{14,12},{16,18},{18,... | collective-permute-start | bytes 1572872 | tf_op jit(solution)/shard_map/ppermute | solution.py:390
  102.5 16.0 %grads.1 = (bf16[256,2048]{1,0:T(8,128)(2,1)}, bf16[256,2048]{1,0:T(8,128)(2,1)}, bf16[2,256,1024]{2,1,0:T(8,128)(2,1)}, bf16[512,512]{1,0:T(8,128)(2,1)}, bf16[...) custom-call(s32[1]{0:T(128)} %bitcast.core_ref, bf16[4,2,1280,512]{3,2,1,0:T(8,128)(2,1)} %get-tuple-element.81.e_ref, ...), custom_call_target="tpu_custom_call" | custom-call | flops 1048576 | bytes 4096 | tf_op jit(solution)/shard_map/grads/pallas_call | solution.py:201
  118.5 1.9 %collective-permute-start.23 = (bf16[512,512]{1,0:T(8,128)(2,1)}, bf16[512,512]{1,0:T(8,128)(2,1)}, u32[]{:S(2)}, u32[]{:S(2)}) collective-permute-start(bf16[512,512]{1,0:T(8,128)(2,1)} %get-tuple-element.87), channel_id=1, source_target_pairs={{4,0},{6,2},{8,4},{10,6},{12,8},{14,10},{16,12},{18,14},{20,16},{2... | collective-permute-start | bytes 1572872 | tf_op jit(solution)/shard_map/ppermute | solution.py:386
  120.4 1.9 %collective-permute-start.24 = (bf16[512,512]{1,0:T(8,128)(2,1)}, bf16[512,512]{1,0:T(8,128)(2,1)}, u32[]{:S(2)}, u32[]{:S(2)}) collective-permute-start(bf16[512,512]{1,0:T(8,128)(2,1)} %get-tuple-element.105), channel_id=1, source_target_pairs={{8,0},{10,2},{12,4},{14,6},{16,8},{18,10},{20,12},{22,14},{24,16},... | collective-permute-start | bytes 1572872 | tf_op jit(solution)/shard_map/ppermute | solution.py:386
  123.2 1.1 constant_dynamic-update-slice_fusion.5.dv_ref
  124.3 1.0 copy-done.6
  125.3 7.0 %tokens.1 = (bf16[256,5376]{1,0:T(8,128)(2,1)}, bf16[256,2688]{1,0:T(8,128)(2,1)}) custom-call(s32[1]{0:T(128)} %bitcast.10.at_ref, bf16[512,1024]{1,0:T(8,128)(2,1)} %copy-done.6, bf16[2688,1024]{1,0:T(8,128)(2,1)} %w_ref.1), custom_call_target="tpu_custom_call" | custom-call | flops 1048576 | bytes 4096 | tf_op jit(solution)/shard_map/tokens/pallas_call | solution.py:364
  133.5 8.1 %weight.1 = (f32[336,512]{1,0:T(8,128)}, bf16[336,512]{1,0:T(8,128)(2,1)}, bf16[336,512]{1,0:T(8,128)(2,1)}, bf16[336,512]{1,0:T(8,128)(2,1)}) custom-call(s32[2]{0:T(128)} %pad_add_fusion.1.at_ref, bf16[1344,512]{1,0:T(8,128)(2,1)} %copy-done.7, bf16[1344,512]{1,0:T(8,128)(2,1)} %copy-done.8, bf16[1344,512]{1,0:T(8,128)(2,1)} %collective-permute-done.21.refs_2_, ...), custom_call_target="tpu_custom_call" | custom-call | flops 1048576 | bytes 4096 | tf_op jit(solution)/shard_map/weight/pallas_call | solution.py:336
  141.7 3.6 %collective-permute-done.24 = bf16[512,512]{1,0:T(8,128)(2,1)} collective-permute-done((bf16[512,512]{1,0:T(8,128)(2,1)}, bf16[512,512]{1,0:T(8,128)(2,1)}, u32[]{:S(2)}, u32[]{:S(2)}) %collective-permute-start.24) | collective-permute-done | bytes 524320 | tf_op jit(solution)/shard_map/ppermute | solution.py:386
  145.8 6.5 %collective-permute-start.28 = (bf16[336,512]{1,0:T(8,128)(2,1)}, bf16[336,512]{1,0:T(8,128)(2,1)S(1)}, u32[]{:S(2)}, u32[]{:S(2)}) collective-permute-start(bf16[336,512]{1,0:T(8,128)(2,1)} %get-tuple-element.111), channel_id=1, source_target_pairs={{0,16},{2,18},{4,20},{6,22},{8,24},{10,26},{12,28},{14,30},{16,0},... | collective-permute-start | bytes 1032200 | tf_op jit(solution)/shard_map/ppermute | solution.py:601
  152.5 1.4 add_convert_fusion
  154.0 5.3 %collective-permute-done.29 = bf16[336,512]{1,0:T(8,128)(2,1)S(1)} collective-permute-done((bf16[336,512]{1,0:T(8,128)(2,1)}, bf16[336,512]{1,0:T(8,128)(2,1)S(1)}, u32[]{:S(2)}, u32[]{:S(2)}) %collective-permute-start.29) | collective-permute-done | bytes 344096 | tf_op jit(solution)/shard_map/ppermute | solution.py:601
  159.3 2.2 %collective-permute-start.25 = (bf16[256,512]{1,0:T(8,128)(2,1)S(1)}, bf16[256,512]{1,0:T(8,128)(2,1)S(1)}, u32[]{:S(2)}, u32[]{:S(2)}) collective-permute-start(bf16[256,512]{1,0:T(8,128)(2,1)S(1)} %get-tuple-element.117), channel_id=1, source_target_pairs={{0,2},{2,0},{4,6},{6,4},{8,10},{10,8},{12,14},{14,12},{16,18},{18,... | collective-permute-start | bytes 786440 | tf_op jit(solution)/shard_map/ppermute | solution.py:390
  161.5 12.4 %collective-permute-done.28 = bf16[336,512]{1,0:T(8,128)(2,1)S(1)} collective-permute-done((bf16[336,512]{1,0:T(8,128)(2,1)}, bf16[336,512]{1,0:T(8,128)(2,1)S(1)}, u32[]{:S(2)}, u32[]{:S(2)}) %collective-permute-start.28) | collective-permute-done | bytes 344096 | tf_op jit(solution)/shard_map/ppermute | solution.py:601
  173.9 7.4 %collective-permute-done.27 = bf16[336,512]{1,0:T(8,128)(2,1)S(1)} collective-permute-done((bf16[336,512]{1,0:T(8,128)(2,1)}, bf16[336,512]{1,0:T(8,128)(2,1)S(1)}, u32[]{:S(2)}, u32[]{:S(2)}) %collective-permute-start.27) | collective-permute-done | bytes 344096 | tf_op jit(solution)/shard_map/ppermute | solution.py:601
  182.2 1.2 collective-permute-done.30
  184.9 0.9 copy-done.24
  (128 shorter events, 12.9 us)
Async XLA Ops:
  2.6 7.2 %copy-start.1 = (bf16[1,256,2048]{2,1,0:T(8,128)(2,1)S(1)}, bf16[1,256,2048]{2,1,0:T(8,128)(2,1)}, u32[]{:S(2)}) copy-start(bf16[1,256,2048]{2,1,0:T(8,128)(2,1)} %param.7) | copy-start | bytes 3145732
  2.6 7.2 %copy-start.9 = (bf16[1,256,2048]{2,1,0:T(8,128)(2,1)S(1)}, bf16[1,256,2048]{2,1,0:T(8,128)(2,1)}, u32[]{:S(2)}) copy-start(bf16[1,256,2048]{2,1,0:T(8,128)(2,1)} %param.10) | copy-start | bytes 3145732
  2.6 24.5 %collective-permute-start.3 = (bf16[256,1280]{1,0:T(8,128)(2,1)}, bf16[256,1280]{1,0:T(8,128)(2,1)}, u32[]{:S(2)}, u32[]{:S(2)}) collective-permute-start(bf16[256,1280]{1,0:T(8,128)(2,1)} %dynamic-slice_bitcast_fusion.1), channel_id=1, source_target_pairs={{0,1},{1,0},{2,3},{3,2},{4,5},{5,4},{6,7},{7,6},{8,9},{9,8},{10,11... | collective-permute-start | bytes 1966088 | tf_op jit(solution)/shard_map/ppermute | solution.py:395
  6.5 3.4 %collective-permute-start = (bf16[272,512]{1,0:T(8,128)(2,1)}, bf16[272,512]{1,0:T(8,128)(2,1)S(1)}, u32[]{:S(2)}, u32[]{:S(2)}) collective-permute-start(bf16[272,512]{1,0:T(8,128)(2,1)} %maximum_maximum_fusion.1), channel_id=1, source_target_pairs={{0,2},{2,0},{4,6},{6,4},{8,10},{10,8},{12,14},{14,12},{16,18},{18,... | collective-permute-start | bytes 835592 | tf_op jit(solution)/shard_map/ppermute | solution.py:390
  9.5 24.5 %collective-permute-start.4 = (bf16[256,1408]{1,0:T(8,128)(2,1)}, bf16[256,1408]{1,0:T(8,128)(2,1)S(1)}, u32[]{:S(2)}, u32[]{:S(2)}) collective-permute-start(bf16[256,1408]{1,0:T(8,128)(2,1)} %dynamic-slice_bitcast_fusion), channel_id=1, source_target_pairs={{0,1},{1,0},{2,3},{3,2},{4,5},{5,4},{6,7},{7,6},{8,9},{9,8},{10,11... | collective-permute-start | bytes 2162696 | tf_op jit(solution)/shard_map/ppermute | solution.py:395
  10.0 12.2 %copy-start.2 = (bf16[528,512]{1,0:T(8,128)(2,1)}, bf16[528,512]{1,0:T(8,128)(2,1)S(1)}, u32[]{:S(2)}) copy-start(bf16[528,512]{1,0:T(8,128)(2,1)S(1)} %pad_maximum_fusion.2.refs_2_) | copy-start | bytes 1622020
  10.0 30.7 %collective-permute-start.2 = (bf16[528,512]{1,0:T(8,128)(2,1)S(1)}, bf16[528,512]{1,0:T(8,128)(2,1)S(1)}, u32[]{:S(2)}, u32[]{:S(2)}) collective-permute-start(bf16[528,512]{1,0:T(8,128)(2,1)S(1)} %pad_maximum_fusion.2.refs_2_), channel_id=1, source_target_pairs={{0,4},{2,6},{4,8},{6,10},{8,12},{10,14},{12,16},{14,18},{16,20},{1... | collective-permute-start | bytes 1622024 | tf_op jit(solution)/shard_map/ppermute | solution.py:386
  13.2 27.8 %collective-permute-start.1 = (bf16[528,512]{1,0:T(8,128)(2,1)S(1)}, bf16[528,512]{1,0:T(8,128)(2,1)S(1)}, u32[]{:S(2)}, u32[]{:S(2)}) collective-permute-start(bf16[528,512]{1,0:T(8,128)(2,1)S(1)} %pad_maximum_fusion.2.refs_2_), channel_id=1, source_target_pairs={{0,8},{2,10},{4,12},{6,14},{8,16},{10,18},{12,20},{14,22},{16,24},... | collective-permute-start | bytes 1622024 | tf_op jit(solution)/shard_map/ppermute | solution.py:386
  16.5 27.0 %collective-permute-start.5 = (bf16[256,2048]{1,0:T(8,128)(2,1)S(1)}, bf16[256,2048]{1,0:T(8,128)(2,1)S(1)}, u32[]{:S(2)}, u32[]{:S(2)}) collective-permute-start(bf16[256,2048]{1,0:T(8,128)(2,1)S(1)} %pad_maximum_fusion), channel_id=1, source_target_pairs={{0,2},{2,0},{4,6},{6,4},{8,10},{10,8},{12,14},{14,12},{16,18},{18,... | collective-permute-start | bytes 3145736 | tf_op jit(solution)/shard_map/ppermute | solution.py:390
  27.1 32.0 %collective-permute-start.8 = (bf16[1344,256]{1,0:T(8,128)(2,1)}, bf16[1344,256]{1,0:T(8,128)(2,1)}, u32[]{:S(2)}, u32[]{:S(2)}) collective-permute-start(bf16[1344,256]{1,0:T(8,128)(2,1)} %get-tuple-element.71), channel_id=1, source_target_pairs={{0,4},{2,6},{4,0},{6,2},{8,12},{10,14},{12,8},{14,10},{16,20},{18,... | collective-permute-start | bytes 2064392 | tf_op jit(solution)/shard_map/ppermute | solution.py:430
  39.5 19.6 %collective-permute-start.7 = (bf16[256,1024]{1,0:T(8,128)(2,1)}, bf16[256,1024]{1,0:T(8,128)(2,1)}, u32[]{:S(2)}, u32[]{:S(2)}) collective-permute-start(bf16[256,1024]{1,0:T(8,128)(2,1)} %product.2), channel_id=1, source_target_pairs={{0,1},{1,0},{2,3},{3,2},{4,5},{5,4},{6,7},{7,6},{8,9},{9,8},{10,11... | collective-permute-start | bytes 1572872 | tf_op jit(solution)/shard_map/ppermute | solution.py:395
  40.8 2.8 %copy-start.10 = (bf16[528,512]{1,0:T(8,128)(2,1)}, bf16[528,512]{1,0:T(8,128)(2,1)S(1)}, u32[]{:S(2)}) copy-start(bf16[528,512]{1,0:T(8,128)(2,1)S(1)} %collective-permute-done.2.refs_1_) | copy-start | bytes 1622020
  40.8 25.7 %collective-permute-start.11 = (bf16[1344,256]{1,0:T(8,128)(2,1)}, bf16[1344,256]{1,0:T(8,128)(2,1)S(1)}, u32[]{:S(2)}, u32[]{:S(2)}) collective-permute-start(bf16[1344,256]{1,0:T(8,128)(2,1)} %get-tuple-element.74), channel_id=1, source_target_pairs={{0,1},{1,0},{2,3},{3,2},{4,5},{5,4},{6,7},{7,6},{8,9},{9,8},{10,11... | collective-permute-start | bytes 2064392 | tf_op jit(solution)/shard_map/ppermute | solution.py:395
  42.3 24.2 %collective-permute-start.10 = (bf16[1344,256]{1,0:T(8,128)(2,1)}, bf16[1344,256]{1,0:T(8,128)(2,1)}, u32[]{:S(2)}, u32[]{:S(2)}) collective-permute-start(bf16[1344,256]{1,0:T(8,128)(2,1)} %get-tuple-element.73), channel_id=1, source_target_pairs={{0,4},{2,6},{4,0},{6,2},{8,12},{10,14},{12,8},{14,10},{16,20},{18,... | collective-permute-start | bytes 2064392 | tf_op jit(solution)/shard_map/ppermute | solution.py:430
  44.5 14.6 %copy-start.5 = (f32[256,1024]{1,0:T(8,128)S(1)}, f32[256,1024]{1,0:T(8,128)}, u32[]{:S(2)}) copy-start(f32[256,1024]{1,0:T(8,128)} %product.3) | copy-start | bytes 3145732
  58.8 4.2 %copy-start.15 = (bf16[1344,256]{1,0:T(8,128)(2,1)S(1)}, bf16[1344,256]{1,0:T(8,128)(2,1)}, u32[]{:S(2)}) copy-start(bf16[1344,256]{1,0:T(8,128)(2,1)} %get-tuple-element.66) | copy-start | bytes 2064388
  58.8 11.4 %collective-permute-start.6 = (bf16[512,512]{1,0:T(8,128)(2,1)}, bf16[512,512]{1,0:T(8,128)(2,1)S(1)}, u32[]{:S(2)}, u32[]{:S(2)}) collective-permute-start(bf16[512,512]{1,0:T(8,128)(2,1)} %get-tuple-element.64), channel_id=1, source_target_pairs={{0,4},{2,6},{4,0},{6,2},{8,12},{10,14},{12,8},{14,10},{16,20},{18,... | collective-permute-start | bytes 1572872 | tf_op jit(solution)/shard_map/ppermute | solution.py:430
  60.3 9.9 %copy-start.21 = (bf16[512,512]{1,0:T(8,128)(2,1)S(1)}, bf16[512,512]{1,0:T(8,128)(2,1)}, u32[]{:S(2)}) copy-start(bf16[512,512]{1,0:T(8,128)(2,1)} %get-tuple-element.63) | copy-start | bytes 1572868
  60.4 4.0 %collective-permute-start.9 = (bf16[256,512]{1,0:T(8,128)(2,1)S(1)}, bf16[256,512]{1,0:T(8,128)(2,1)S(1)}, u32[]{:S(2)}, u32[]{:S(2)}) collective-permute-start(bf16[256,512]{1,0:T(8,128)(2,1)S(1)} %get-tuple-element.123), channel_id=1, source_target_pairs={{0,2},{2,0},{4,6},{6,4},{8,10},{10,8},{12,14},{14,12},{16,18},{18,... | collective-permute-start | bytes 786440 | tf_op jit(solution)/shard_map/ppermute | solution.py:390
  63.1 20.3 %collective-permute-start.20 = (bf16[1344,256]{1,0:T(8,128)(2,1)}, bf16[1344,256]{1,0:T(8,128)(2,1)S(1)}, u32[]{:S(2)}, u32[]{:S(2)}) collective-permute-start(bf16[1344,256]{1,0:T(8,128)(2,1)} %collective-permute-done.8), channel_id=1, source_target_pairs={{0,1},{1,0},{2,3},{3,2},{4,5},{5,4},{6,7},{7,6},{8,9},{9,8},{10,11... | collective-permute-start | bytes 2064392 | tf_op jit(solution)/shard_map/ppermute | solution.py:395
  64.4 14.0 %copy-start.3 = (bf16[512,512]{1,0:T(8,128)(2,1)}, bf16[512,512]{1,0:T(8,128)(2,1)S(1)}, u32[]{:S(2)}) copy-start(bf16[512,512]{1,0:T(8,128)(2,1)S(1)} %constant_dynamic-update-slice_fusion.6.refs_5_) | copy-start | bytes 1572868
  66.5 12.0 %collective-permute-start.13 = (bf16[512,512]{1,0:T(8,128)(2,1)S(1)}, bf16[512,512]{1,0:T(8,128)(2,1)S(1)}, u32[]{:S(2)}, u32[]{:S(2)}) collective-permute-start(bf16[512,512]{1,0:T(8,128)(2,1)S(1)} %constant_dynamic-update-slice_fusion.6.refs_5_), channel_id=1, source_target_pairs={{0,8},{2,10},{4,12},{6,14},{8,16},{10,18},{12,20},{14,22},{16,24},... | collective-permute-start | bytes 1572872 | tf_op jit(solution)/shard_map/ppermute | solution.py:386
  70.4 11.4 %copy-start.18 = (bf16[512,512]{1,0:T(8,128)(2,1)S(1)}, bf16[512,512]{1,0:T(8,128)(2,1)}, u32[]{:S(2)}) copy-start(bf16[512,512]{1,0:T(8,128)(2,1)} %get-tuple-element.62) | copy-start | bytes 1572868
  70.4 11.4 %collective-permute-start.12 = (bf16[512,512]{1,0:T(8,128)(2,1)S(1)}, bf16[512,512]{1,0:T(8,128)(2,1)S(1)}, u32[]{:S(2)}, u32[]{:S(2)}) collective-permute-start(bf16[512,512]{1,0:T(8,128)(2,1)S(1)} %fusion.1), channel_id=1, source_target_pairs={{8,0},{10,2},{12,4},{14,6},{16,8},{18,10},{20,12},{22,14},{24,16},... | collective-permute-start | bytes 1572872 | tf_op jit(solution)/shard_map/ppermute | solution.py:386
  74.0 8.1 %copy-start.7 = (bf16[1344,512]{1,0:T(8,128)(2,1)}, bf16[1344,512]{1,0:T(8,128)(2,1)S(1)}, u32[]{:S(2)}) copy-start(bf16[1344,512]{1,0:T(8,128)(2,1)S(1)} %constant_dynamic-update-slice_fusion.refs_0_) | copy-start | bytes 4128772
  74.0 59.0 %collective-permute-start.21 = (bf16[1344,512]{1,0:T(8,128)(2,1)S(1)}, bf16[1344,512]{1,0:T(8,128)(2,1)}, u32[]{:S(2)}, u32[]{:S(2)}) collective-permute-start(bf16[1344,512]{1,0:T(8,128)(2,1)S(1)} %constant_dynamic-update-slice_fusion.refs_0_), channel_id=1, source_target_pairs={{0,2},{2,0},{4,6},{6,4},{8,10},{10,8},{12,14},{14,12},{16,18},{18,... | collective-permute-start | bytes 4128776 | tf_op jit(solution)/shard_map/ppermute | solution.py:390
  78.5 4.9 %copy-start.12 = (bf16[512,512]{1,0:T(8,128)(2,1)}, bf16[512,512]{1,0:T(8,128)(2,1)S(1)}, u32[]{:S(2)}) copy-start(bf16[512,512]{1,0:T(8,128)(2,1)S(1)} %collective-permute-done.13.refs_3_) | copy-start | bytes 1572868
  78.6 10.9 %collective-permute-start.14 = (bf16[512,512]{1,0:T(8,128)(2,1)S(1)}, bf16[512,512]{1,0:T(8,128)(2,1)S(1)}, u32[]{:S(2)}, u32[]{:S(2)}) collective-permute-start(bf16[512,512]{1,0:T(8,128)(2,1)S(1)} %broadcast_select_fusion), channel_id=1, source_target_pairs={{0,4},{2,6},{4,0},{6,2},{8,12},{10,14},{12,8},{14,10},{16,20},{18,... | collective-permute-start | bytes 1572872 | tf_op jit(solution)/shard_map/ppermute | solution.py:430
  82.1 9.5 %copy-start.4 = (bf16[512,512]{1,0:T(8,128)(2,1)}, bf16[512,512]{1,0:T(8,128)(2,1)S(1)}, u32[]{:S(2)}) copy-start(bf16[512,512]{1,0:T(8,128)(2,1)S(1)} %fusion.3.refs_4_) | copy-start | bytes 1572868
  82.1 8.5 %collective-permute-start.15 = (bf16[512,512]{1,0:T(8,128)(2,1)S(1)}, bf16[512,512]{1,0:T(8,128)(2,1)S(1)}, u32[]{:S(2)}, u32[]{:S(2)}) collective-permute-start(bf16[512,512]{1,0:T(8,128)(2,1)S(1)} %fusion.3.refs_4_), channel_id=1, source_target_pairs={{0,1},{1,0},{2,3},{3,2},{4,5},{5,4},{6,7},{7,6},{8,9},{9,8},{10,11... | collective-permute-start | bytes 1572872 | tf_op jit(solution)/shard_map/ppermute | solution.py:395
  83.4 35.0 %copy-start.8 = (bf16[1344,512]{1,0:T(8,128)(2,1)}, bf16[1344,512]{1,0:T(8,128)(2,1)S(1)}, u32[]{:S(2)}) copy-start(bf16[1344,512]{1,0:T(8,128)(2,1)S(1)} %constant_dynamic-update-slice_fusion.2.refs_1_) | copy-start | bytes 4128772
  83.4 50.1 %collective-permute-start.22 = (bf16[1344,512]{1,0:T(8,128)(2,1)S(1)}, bf16[1344,512]{1,0:T(8,128)(2,1)}, u32[]{:S(2)}, u32[]{:S(2)}) collective-permute-start(bf16[1344,512]{1,0:T(8,128)(2,1)S(1)} %constant_dynamic-update-slice_fusion.2.refs_1_), channel_id=1, source_target_pairs={{0,2},{2,0},{4,6},{6,4},{8,10},{10,8},{12,14},{14,12},{16,18},{18,... | collective-permute-start | bytes 4128776 | tf_op jit(solution)/shard_map/ppermute | solution.py:390
  88.8 29.7 %collective-permute-start.17 = (bf16[512,512]{1,0:T(8,128)(2,1)S(1)}, bf16[512,512]{1,0:T(8,128)(2,1)}, u32[]{:S(2)}, u32[]{:S(2)}) collective-permute-start(bf16[512,512]{1,0:T(8,128)(2,1)S(1)} %fusion.3.refs_4_), channel_id=1, source_target_pairs={{0,4},{1,5},{2,6},{3,7},{4,0},{5,1},{6,2},{7,3},{8,12},{9,13},{10,... | collective-permute-start | bytes 1572872 | tf_op jit(solution)/shard_map/ppermute | solution.py:405
  89.4 13.0 %copy-start.19 = (bf16[512,512]{1,0:T(8,128)(2,1)}, bf16[512,512]{1,0:T(8,128)(2,1)S(1)}, u32[]{:S(2)}) copy-start(bf16[512,512]{1,0:T(8,128)(2,1)S(1)} %collective-permute-done.14.refs_4_) | copy-start | bytes 1572868
  89.4 31.0 %collective-permute-start.18 = (bf16[512,512]{1,0:T(8,128)(2,1)S(1)}, bf16[512,512]{1,0:T(8,128)(2,1)}, u32[]{:S(2)}, u32[]{:S(2)}) collective-permute-start(bf16[512,512]{1,0:T(8,128)(2,1)S(1)} %fusion.3.refs_4_), channel_id=1, source_target_pairs={{0,5},{1,4},{2,7},{3,6},{4,1},{5,0},{6,3},{7,2},{8,13},{9,12},{10,... | collective-permute-start | bytes 1572872 | tf_op jit(solution)/shard_map/ppermute | solution.py:405
  90.6 27.9 %copy-start.13 = (bf16[512,512]{1,0:T(8,128)(2,1)}, bf16[512,512]{1,0:T(8,128)(2,1)S(1)}, u32[]{:S(2)}) copy-start(bf16[512,512]{1,0:T(8,128)(2,1)S(1)} %collective-permute-done.15.refs_6_) | copy-start | bytes 1572868
  91.6 31.6 %collective-permute-start.16 = (bf16[512,512]{1,0:T(8,128)(2,1)}, bf16[512,512]{1,0:T(8,128)(2,1)}, u32[]{:S(2)}, u32[]{:S(2)}) collective-permute-start(bf16[512,512]{1,0:T(8,128)(2,1)} %pad_maximum_fusion.5), channel_id=1, source_target_pairs={{0,2},{2,0},{4,6},{6,4},{8,10},{10,8},{12,14},{14,12},{16,18},{18,... | collective-permute-start | bytes 1572872 | tf_op jit(solution)/shard_map/ppermute | solution.py:390
  118.5 23.2 %collective-permute-start.23 = (bf16[512,512]{1,0:T(8,128)(2,1)}, bf16[512,512]{1,0:T(8,128)(2,1)}, u32[]{:S(2)}, u32[]{:S(2)}) collective-permute-start(bf16[512,512]{1,0:T(8,128)(2,1)} %get-tuple-element.87), channel_id=1, source_target_pairs={{4,0},{6,2},{8,4},{10,6},{12,8},{14,10},{16,12},{18,14},{20,16},{2... | collective-permute-start | bytes 1572872 | tf_op jit(solution)/shard_map/ppermute | solution.py:386
  120.4 24.9 %collective-permute-start.24 = (bf16[512,512]{1,0:T(8,128)(2,1)}, bf16[512,512]{1,0:T(8,128)(2,1)}, u32[]{:S(2)}, u32[]{:S(2)}) collective-permute-start(bf16[512,512]{1,0:T(8,128)(2,1)} %get-tuple-element.105), channel_id=1, source_target_pairs={{8,0},{10,2},{12,4},{14,6},{16,8},{18,10},{20,12},{22,14},{24,16},... | collective-permute-start | bytes 1572872 | tf_op jit(solution)/shard_map/ppermute | solution.py:386
  132.3 51.3 %collective-permute-start.26 = (bf16[256,2688]{1,0:T(8,128)(2,1)}, bf16[256,2688]{1,0:T(8,128)(2,1)S(1)}, u32[]{:S(2)}, u32[]{:S(2)}) collective-permute-start(bf16[256,2688]{1,0:T(8,128)(2,1)} %get-tuple-element.92), channel_id=1, source_target_pairs={{0,1},{1,0},{2,3},{3,2},{4,5},{5,4},{6,7},{7,6},{8,9},{9,8},{10,11... | collective-permute-start | bytes 4128776 | tf_op jit(solution)/shard_map/ppermute | solution.py:395
  133.0 19.4 %copy-start.22 = (bf16[512,512]{1,0:T(8,128)(2,1)S(1)}, bf16[512,512]{1,0:T(8,128)(2,1)}, u32[]{:S(2)}) copy-start(bf16[512,512]{1,0:T(8,128)(2,1)} %get-tuple-element.95) | copy-start | bytes 1572868
  133.0 50.4 %collective-permute-start.19 = (bf16[2,256,1024]{2,1,0:T(8,128)(2,1)}, bf16[2,256,1024]{2,1,0:T(8,128)(2,1)S(1)}, u32[]{:S(2)}, u32[]{:S(2)}) collective-permute-start(bf16[2,256,1024]{2,1,0:T(8,128)(2,1)} %get-tuple-element.93), channel_id=1, source_target_pairs={{0,2},{2,0},{4,6},{6,4},{8,10},{10,8},{12,14},{14,12},{16,18},{18,... | collective-permute-start | bytes 3145736 | tf_op jit(solution)/shard_map/ppermute | solution.py:390
  141.7 39.6 %copy-start.16 = (f32[336,512]{1,0:T(8,128)S(1)}, f32[336,512]{1,0:T(8,128)}, u32[]{:S(2)}) copy-start(f32[336,512]{1,0:T(8,128)} %get-tuple-element.109) | copy-start | bytes 2064388
  145.3 13.9 %collective-permute-start.29 = (bf16[336,512]{1,0:T(8,128)(2,1)}, bf16[336,512]{1,0:T(8,128)(2,1)S(1)}, u32[]{:S(2)}, u32[]{:S(2)}) collective-permute-start(bf16[336,512]{1,0:T(8,128)(2,1)} %get-tuple-element.112), channel_id=1, source_target_pairs={{0,24},{2,26},{4,28},{6,30},{8,0},{10,2},{12,4},{14,6},{16,8},{18,... | collective-permute-start | bytes 1032200 | tf_op jit(solution)/shard_map/ppermute | solution.py:601
  145.8 28.1 %collective-permute-start.28 = (bf16[336,512]{1,0:T(8,128)(2,1)}, bf16[336,512]{1,0:T(8,128)(2,1)S(1)}, u32[]{:S(2)}, u32[]{:S(2)}) collective-permute-start(bf16[336,512]{1,0:T(8,128)(2,1)} %get-tuple-element.111), channel_id=1, source_target_pairs={{0,16},{2,18},{4,20},{6,22},{8,24},{10,26},{12,28},{14,30},{16,0},... | collective-permute-start | bytes 1032200 | tf_op jit(solution)/shard_map/ppermute | solution.py:601
  152.3 29.0 %collective-permute-start.27 = (bf16[336,512]{1,0:T(8,128)(2,1)}, bf16[336,512]{1,0:T(8,128)(2,1)S(1)}, u32[]{:S(2)}, u32[]{:S(2)}) collective-permute-start(bf16[336,512]{1,0:T(8,128)(2,1)} %get-tuple-element.110), channel_id=1, source_target_pairs={{0,8},{2,10},{4,12},{6,14},{8,16},{10,18},{12,20},{14,22},{16,24},... | collective-permute-start | bytes 1032200 | tf_op jit(solution)/shard_map/ppermute | solution.py:601
  159.3 22.8 %collective-permute-start.25 = (bf16[256,512]{1,0:T(8,128)(2,1)S(1)}, bf16[256,512]{1,0:T(8,128)(2,1)S(1)}, u32[]{:S(2)}, u32[]{:S(2)}) collective-permute-start(bf16[256,512]{1,0:T(8,128)(2,1)S(1)} %get-tuple-element.117), channel_id=1, source_target_pairs={{0,2},{2,0},{4,6},{6,4},{8,10},{10,8},{12,14},{14,12},{16,18},{18,... | collective-permute-start | bytes 786440 | tf_op jit(solution)/shard_map/ppermute | solution.py:390
  181.5 1.8 collective-permute-start.30
  (12 other events, 18.8 us)

commit v9 on v8

--- a/solution.py
+++ b/solution.py
@@ -194,24 +194,28 @@
     )(core, low, q, q_other, do, q_other, *keys)
 
 
-def run_grads(core, e, inv, do_t, q, q_other, keys, values, rows, width):
-    blk, heads, span, lanes, head, own = specs_of(rows, width)
+def run_grads(core, e, inv, do_t, q, q_other, keys, values, rows, width, low, high):
+    blk, heads, span, lanes, _, _ = specs_of(rows, width)
     n_arr = len(keys)
-    full = jax.ShapeDtypeStruct(q.shape, BF16)
+    count = high - low
+    head = pl.BlockSpec((rows, HD), lambda g, c: (0, low + g))
+    head_out = pl.BlockSpec((rows, HD), lambda g, c: (0, g))
+    group_out = pl.BlockSpec((blk, GROUP * HD), lambda g, c: (0, g))
     return pl.pallas_call(
         functools.partial(grads_kernel, blk, n_arr - 1),
         grid_spec=pltpu.PrefetchScalarGridSpec(
             num_scalar_prefetch=1,
-            grid=(heads,),
+            grid=(count,),
             in_specs=[
-                pl.BlockSpec((1, 2, span, lanes), lambda g, c: (g, 0, 0, 0)),
-                pl.BlockSpec((1, 2, 1, lanes), lambda g, c: (g, 0, 0, 0)),
-                pl.BlockSpec((1, 2, HD, lanes), lambda g, c: (g, 0, 0, 0)),
-                own,
-                pl.BlockSpec((blk, GROUP * HD), lambda g, c: (0, g)),
+                pl.BlockSpec((1, 2, span, lanes), lambda g, c: (low + g, 0, 0, 0)),
+                pl.BlockSpec((1, 2, 1, lanes), lambda g, c: (low + g, 0, 0, 0)),
+                pl.BlockSpec((1, 2, HD, lanes), lambda g, c: (low + g, 0, 0, 0)),
+                pl.BlockSpec((blk, GROUP * HD), lambda g, c: (0, c[0] * heads + low + g)),
+                pl.BlockSpec((blk, GROUP * HD), lambda g, c: (0, low + g)),
             ]
             + [head] * (2 * n_arr),
-            out_specs=[own, own, pl.BlockSpec((2, blk, GROUP * HD), lambda g, c: (0, 0, g))] + [head] * n_arr,
+            out_specs=[group_out, group_out, pl.BlockSpec((2, blk, GROUP * HD), lambda g, c: (0, 0, g))]
+            + [head_out] * n_arr,
             scratch_shapes=[
                 pltpu.VMEM((WINDOW + rows, HD), F32),
                 pltpu.VMEM((2, blk, GROUP * HD), BF16),
@@ -219,8 +223,9 @@
                 pltpu.VMEM((2, blk, GROUP * HD), BF16),
             ],
         ),
-        out_shape=[full, full, jax.ShapeDtypeStruct((2, blk, GROUP * width), BF16)]
-        + [jax.ShapeDtypeStruct((rows, width), BF16)] * n_arr,
+        out_shape=[jax.ShapeDtypeStruct((blk, GROUP * HD * count), BF16)] * 2
+        + [jax.ShapeDtypeStruct((2, blk, GROUP * HD * count), BF16)]
+        + [jax.ShapeDtypeStruct((rows, HD * count), BF16)] * n_arr,
         compiler_params=pltpu.CompilerParams(vmem_limit_bytes=VMEM_BYTES),
         cost_estimate=small_cost(),
         name="grads",
@@ -555,19 +560,18 @@
         own_pairs.append(jnp.concatenate([over_fsdp[s], relayed_y[s]], 1))
         other_pairs.append(swapped(own_pairs[s]))
     vals = [v_far, v_near, v_own]
-    v_near, dv_fsdp[1:] = lax.optimization_barrier((v_near, dv_fsdp[1:]))
     vals = [v_far, v_near, v_own]
+    n_heads = half_kv // HD
+    grad_args = (e, inv, do_t, queries[0], q_other, keys, vals, chip_rows, half_kv)
+    early = run_grads(core_arg, *grad_args, 0, n_heads // 2)
+    early_back = [shifted(early[4], -2), shifted(early[3], -4)]
+
+    dv_fsdp[1:] = [after(x, early[4]) for x in dv_fsdp[1:]]
+    dv_over_y = [after(x, early[4]) for x in dv_over_y]
     dv_sides = [
         jnp.concatenate([rows_of(x, at, shard_rows) for x in dv_fsdp], 0) for at in (core, 1 - core)
     ]
-    dv_other = swapped(dv_sides[1])
-    out, dq, other, dk_far, dk_near, dk_mine = run_grads(
-        after(core_arg, *dv_sides), e, inv, do_t, queries[0], q_other, keys, vals, chip_rows, half_kv
-    )
-    dk_back = [shifted(dk_near, -2), shifted(dk_far, -4)]
-
-    dv_over_y = [after(x, dk_near) for x in dv_over_y]
-    dv_rows = placed(core, dv_sides[0], after(dv_other, dk_near), 1)
+    dv_rows = placed(core, dv_sides[0], swapped(dv_sides[1]), 1)
     dv_rows = after(dv_rows, *dv_over_y)
     if aligned:
         d_tokens, *made = run_tokens(fsdp_arg, dv_rows, w_value, n_fsdp)
@@ -596,20 +600,31 @@
             lax.dynamic_index_in_dim(weight_term, (my_z + d) % n_z, 0, keepdims=False).astype(BF16 if d else F32)
             for d in range(n_z)
         ]
-    by_z, dk_back = lax.optimization_barrier((list(by_z), dk_back))
+    by_z, early_back = lax.optimization_barrier((list(by_z), early_back))
     over_z = [
         lax.ppermute(by_z[d], "ctx", [(i, (i + 4 * d) % n_ctx) for i in range(n_ctx)]) for d in range(1, n_z)
     ]
 
+    late = run_grads(after(core_arg, by_z[0]), *grad_args, n_heads // 2, n_heads)
+    late_back = [shifted(late[4], -2), shifted(late[3], -4)]
+    over_z = [after(x, late[4]) for x in over_z]
     row_sum = by_z[0]
     for x in over_z:
         row_sum = row_sum + x.astype(F32)
     d_weight = placed(core, rows_of(row_sum, core, out_rows), swapped(rows_of(row_sum, 1 - core, out_rows)), 1)
-    dk_chip = (dk_mine.astype(F32) + dk_back[0].astype(F32) + dk_back[1].astype(F32)).astype(BF16)
+    late_back = [after(x, over_z[0]) for x in late_back]
+    dk_chip = jnp.concatenate(
+        [
+            (made_by[5].astype(F32) + back[0].astype(F32) + back[1].astype(F32)).astype(BF16)
+            for made_by, back in ((early, early_back), (late, late_back))
+        ],
+        1,
+    )
     d_keys = placed(core, rows_of(dk_chip, core, shard_rows), swapped(rows_of(dk_chip, 1 - core, shard_rows)), 1)
-    other = swapped(after(other, *made))
-    out = lax.dynamic_update_slice_in_dim(out, other[0], (1 - core) * half_q, 1)
-    dq = lax.dynamic_update_slice_in_dim(dq, other[1], (1 - core) * half_q, 1)
+    out, dq, other = [jnp.concatenate((early[i], late[i]), early[i].ndim - 1) for i in range(3)]
+    other = swapped(other)
+    out = placed(core, out, other[0], 1)
+    dq = placed(core, dq, other[1], 1)
     return (out[None], dq[None], d_keys[None], d_tokens[None], d_weight)
 
 

time: 190 us -> 190 us (level)
  waiting for transfers between devices: 40.3 us -> 30.5 us
  starting transfers between devices: 63.2 us -> 69.1 us
  Pallas kernels: 59.2 us -> 62.1 us
  local copies, waits for them, and re-layouts: 13.3 us -> 15.7 us
    ppermute x3, waiting for transfers between devices: 25.1 us -> 7.11 us  [shards(): lax.ppermute(by_z[d], 'ctx', [(i, (i + 4 * d) % n_ctx) for i in range(n_c...]
    ppermute x6 -> x8, starting transfers between devices: 15.8 us -> 26.9 us  [shifted(): lax.ppermute(x, 'ctx', [(i, i + by) for i in range(length) if 0 <= i + by...]
    ppermute x6 -> x8, waiting for transfers between devices: 5.59 us -> 9.78 us  [shifted(): lax.ppermute(x, 'ctx', [(i, i + by) for i in range(length) if 0 <= i + by...]
    ppermute x2, waiting for transfers between devices: 0.01 us -> 3.35 us  [moved(): return lax.ppermute(x, ('ctx', 'fsdp'), pairs)]
    ppermute x9, starting transfers between devices: 28.4 us -> 25.1 us  [swapped(): lax.ppermute(x, 'ctx', [(i, i ^ 1) for i in range(lax.axis_size('ctx'))])]
    pallas_call x1 -> x2, Pallas kernels: 16 us -> 18.8 us  [run_grads(): pl.pallas_call(functools.partial(grads_kernel, blk, n_arr - 1), grid_spec...]
    broadcast_in_dim x1 -> x3, other arithmetic: 0.04 us -> 2.43 us  [shards(): return (out[None], dq[None], d_keys[None], d_tokens[None], d_weight)]
    unnamed x60 -> x72, local copies, waits for them, and re-layouts: 5.05 us -> 6.66 us
  transfers between devices with their start and end apart: 31 -> 33, of which waited for: 10 -> 10; matrix products, arithmetic and copies ran while one was open for 8% -> 9% of each run, Pallas kernels for 32% -> 33%
where the time goes in v9:
time: 190 us; the launch traced here: 187 us
  starting transfers between devices  69.1 us (36%)
  Pallas kernels  62.1 us (33%)
  waiting for transfers between devices  30.5 us (16%)
  local copies, waits for them, and re-layouts  15.7 us (8%)
  other arithmetic  8.2 us (4%)
    ppermute x8, starting transfers between devices, shifted(): lax.ppermute(x, 'ctx', [(i, i + by) for i in range(length) if 0 <= i + by...  26.9 us
    ppermute x9, starting transfers between devices, swapped(): lax.ppermute(x, 'ctx', [(i, i ^ 1) for i in range(lax.axis_size('ctx'))])  25.1 us
    pallas_call x2, Pallas kernels, run_grads(): pl.pallas_call(functools.partial(grads_kernel, blk, n_arr - 1), grid_spec...  18.8 us
    pallas_call x1, Pallas kernels, run_probs(): pl.pallas_call(functools.partial(probs_kernel, blk, n_arr - 1), grid_spec...  14.3 us
    ppermute x8, waiting for transfers between devices, shifted(): lax.ppermute(x, 'ctx', [(i, i + by) for i in range(length) if 0 <= i + by...  9.78 us
    pallas_call x2, Pallas kernels, run_product(): pl.pallas_call(product_kernel, grid_spec=pltpu.PrefetchScalarGridSpec(num...  9.57 us
    ppermute x7, waiting for transfers between devices, rotated(): lax.ppermute(x, 'fsdp', [(i, (i + by) % length) for i in range(length)])  8.3 us
    pallas_call x1, Pallas kernels, run_weight(): pl.pallas_call(functools.partial(weight_kernel, n_z, n), grid_spec=pltpu....  8.13 us
  transfers between devices with their start and end apart: 33, of which 10 were waited for; matrix products, arithmetic and copies ran while one was open for 9% of the time, Pallas kernels for 33%

profile of v9, /device:TPU:9, one launch (start us, length us, event | category | flops | bytes accessed | tf_op | source)
XLA Modules:
  0.0 187.1 jit_solution(16904585982857577487)
XLA Ops:
  0.7 2.0 %dynamic-slice_bitcast_fusion.1 = bf16[256,1280]{1,0:T(8,128)(2,1)} fusion(bf16[1,256,5376]{2,1,0:T(8,128)(2,1)} %param.6, s32[]{:T(128)S(6)} %select_n.94), kind=kLoop, calls=%fused_computation.17 | loop fusion | bytes 1310724 | tf_op jit(solution)/shard_map/dynamic_slice | solution.py:474
  2.6 1.2 collective-permute-start.3
  3.9 1.1 dynamic-slice_bitcast_fusion.5
  5.9 1.0 collective-permute-start
  6.8 2.0 %dynamic-slice_bitcast_fusion = bf16[256,1408]{1,0:T(8,128)(2,1)} fusion(bf16[1,256,5376]{2,1,0:T(8,128)(2,1)} %param.6, s32[]{:T(128)S(6)} %select_n.97), kind=kLoop, calls=%fused_computation.14 | loop fusion | bytes 1441796 | tf_op jit(solution)/shard_map/dynamic_slice | solution.py:474
  9.4 3.1 %collective-permute-start.2 = (bf16[528,512]{1,0:T(8,128)(2,1)S(1)}, bf16[528,512]{1,0:T(8,128)(2,1)S(1)}, u32[]{:S(2)}, u32[]{:S(2)}) collective-permute-start(bf16[528,512]{1,0:T(8,128)(2,1)S(1)} %pad_maximum_fusion.3.refs_2_), channel_id=1, source_target_pairs={{0,4},{2,6},{4,8},{6,10},{8,12},{10,14},{12,16},{14,18},{16,20},{1... | collective-permute-start | bytes 1622024 | tf_op jit(solution)/shard_map/ppermute | solution.py:391
  12.6 3.2 %collective-permute-start.1 = (bf16[528,512]{1,0:T(8,128)(2,1)S(1)}, bf16[528,512]{1,0:T(8,128)(2,1)S(1)}, u32[]{:S(2)}, u32[]{:S(2)}) collective-permute-start(bf16[528,512]{1,0:T(8,128)(2,1)S(1)} %pad_maximum_fusion.3.refs_2_), channel_id=1, source_target_pairs={{0,8},{2,10},{4,12},{6,14},{8,16},{10,18},{12,20},{14,22},{16,24},... | collective-permute-start | bytes 1622024 | tf_op jit(solution)/shard_map/ppermute | solution.py:391
  17.4 4.2 %pieces.1 = (bf16[1344,256]{1,0:T(8,128)(2,1)}, bf16[1344,256]{1,0:T(8,128)(2,1)}, bf16[1344,256]{1,0:T(8,128)(2,1)}, bf16[1344,256]{1,0:T(8,128)(2,1)}) custom-call(s32[2]{0:T(128)} %pad_add_fusion.at_ref, bf16[256,5376]{1,0:T(8,128)(2,1)} %bitcast.31), custom_call_target="tpu_custom_call" | custom-call | flops 1048576 | bytes 4096 | tf_op jit(solution)/shard_map/pieces/pallas_call | solution.py:265
  21.6 4.9 %product.3 = f32[256,1024]{1,0:T(8,128)} custom-call(s32[1]{0:T(128)} %bitcast.10.at_ref, bf16[256,5376]{1,0:T(8,128)(2,1)} %bitcast.32, bf16[2688,1024]{1,0:T(8,128)(2,1)} %w_ref.1), custom_call_target="tpu_custom_call" | custom-call | flops 1048576 | bytes 4096 | tf_op jit(solution)/shard_map/product/pallas_call | solution.py:295
  26.5 1.3 collective-permute-start.7
  27.8 6.2 %collective-permute-done.4.refs_1_ = bf16[256,1408]{1,0:T(8,128)(2,1)S(1)} collective-permute-done((bf16[256,1408]{1,0:T(8,128)(2,1)}, bf16[256,1408]{1,0:T(8,128)(2,1)S(1)}, u32[]{:S(2)}, u32[]{:S(2)}) %collective-permute-start.4) | collective-permute-done | bytes 720928 | tf_op jit(solution)/shard_map/ppermute | solution.py:400
  34.9 4.7 %product.2 = bf16[256,1024]{1,0:T(8,128)(2,1)} custom-call(s32[1]{0:T(128)} %constant.86.clone.1.at_ref, bf16[256,1280]{1,0:T(8,128)(2,1)} %collective-permute-done.3.refs_0_, bf16[256,1408]{1,0:T(8,128)(2,1)} %copy-done.16, bf16[2688,1024]{1,0:T(8,128)(2,1)} %w_ref.1), custom_call_target="tpu_custom_call" | custom-call | flops 1048576 | bytes 4096 | tf_op jit(solution)/shard_map/product/pallas_call | solution.py:295
  39.6 1.2 collective-permute-start.6
  42.3 1.2 collective-permute-start.9
  43.5 1.0 copy-done
  44.5 14.3 %probs.1 = (bf16[4,2,1280,512]{3,2,1,0:T(8,128)(2,1)}, f32[4,2,1,512]{3,2,1,0:T(1,128)}, bf16[4,2,128,512]{3,2,1,0:T(8,128)(2,1)}, bf16[512,512]{1,0:T(8,128)(2,...) custom-call(s32[1]{0:T(128)} %bitcast.core_ref, s32[1,512]{1,0:T(1,128)} %add_maximum_fusion.low_ref, ...), custom_call_target="tpu_custom_call" | custom-call | flops 1048576 | bytes 4096 | tf_op jit(solution)/shard_map/probs/pallas_call | solution.py:158
  59.1 1.2 add_convert_fusion
  60.4 2.6 %collective-permute-start.8 = (bf16[256,512]{1,0:T(8,128)(2,1)S(1)}, bf16[256,512]{1,0:T(8,128)(2,1)S(1)}, u32[]{:S(2)}, u32[]{:S(2)}) collective-permute-start(bf16[256,512]{1,0:T(8,128)(2,1)S(1)} %get-tuple-element.139), channel_id=1, source_target_pairs={{0,2},{2,0},{4,6},{6,4},{8,10},{10,8},{12,14},{14,12},{16,18},{18,... | collective-permute-start | bytes 786440 | tf_op jit(solution)/shard_map/ppermute | solution.py:395
  63.1 1.3 collective-permute-start.19
  64.5 2.1 %collective-permute-done.10 = bf16[1344,256]{1,0:T(8,128)(2,1)S(1)} collective-permute-done((bf16[1344,256]{1,0:T(8,128)(2,1)}, bf16[1344,256]{1,0:T(8,128)(2,1)S(1)}, u32[]{:S(2)}, u32[]{:S(2)}) %collective-permute-start.10) | collective-permute-done | bytes 688160 | tf_op jit(solution)/shard_map/ppermute | solution.py:400
  66.5 3.2 %collective-permute-start.11 = (bf16[512,512]{1,0:T(8,128)(2,1)S(1)}, bf16[512,512]{1,0:T(8,128)(2,1)S(1)}, u32[]{:S(2)}, u32[]{:S(2)}) collective-permute-start(bf16[512,512]{1,0:T(8,128)(2,1)S(1)} %constant_dynamic-update-slice_fusion.6.refs_5_), channel_id=1, source_target_pairs={{0,8},{2,10},{4,12},{6,14},{8,16},{10,18},{12,20},{14,22},{16,24},... | collective-permute-start | bytes 1572872 | tf_op jit(solution)/shard_map/ppermute | solution.py:391
  70.4 2.4 %collective-permute-start.14 = (bf16[512,512]{1,0:T(8,128)(2,1)S(1)}, bf16[512,512]{1,0:T(8,128)(2,1)S(1)}, u32[]{:S(2)}, u32[]{:S(2)}) collective-permute-start(bf16[512,512]{1,0:T(8,128)(2,1)S(1)} %fusion.1), channel_id=1, source_target_pairs={{8,0},{10,2},{12,4},{14,6},{16,8},{18,10},{20,12},{22,14},{24,16},... | collective-permute-start | bytes 1572872 | tf_op jit(solution)/shard_map/ppermute | solution.py:391
  72.8 1.1 constant_dynamic-update-slice_fusion.refs_0_
  74.0 4.5 %collective-permute-start.20 = (bf16[1344,512]{1,0:T(8,128)(2,1)S(1)}, bf16[1344,512]{1,0:T(8,128)(2,1)}, u32[]{:S(2)}, u32[]{:S(2)}) collective-permute-start(bf16[1344,512]{1,0:T(8,128)(2,1)S(1)} %constant_dynamic-update-slice_fusion.refs_0_), channel_id=1, source_target_pairs={{0,2},{2,0},{4,6},{6,4},{8,10},{10,8},{12,14},{14,12},{16,18},{18,... | collective-permute-start | bytes 4128776 | tf_op jit(solution)/shard_map/ppermute | solution.py:395
  79.4 1.3 collective-permute-start.13
  80.7 1.0 collective-permute-done.14
  82.0 1.3 collective-permute-start.15
  84.2 5.3 %collective-permute-start.21 = (bf16[1344,512]{1,0:T(8,128)(2,1)}, bf16[1344,512]{1,0:T(8,128)(2,1)}, u32[]{:S(2)}, u32[]{:S(2)}) collective-permute-start(bf16[1344,512]{1,0:T(8,128)(2,1)} %constant_dynamic-update-slice_fusion.2.refs_1_), channel_id=1, source_target_pairs={{0,2},{2,0},{4,6},{6,4},{8,10},{10,8},{12,14},{14,12},{16,18},{18,... | collective-permute-start | bytes 4128776 | tf_op jit(solution)/shard_map/ppermute | solution.py:395
  91.1 9.4 %grads.2 = (bf16[256,512]{1,0:T(8,128)(2,1)}, bf16[256,512]{1,0:T(8,128)(2,1)}, bf16[2,256,512]{2,1,0:T(8,128)(2,1)}, bf16[512,256]{1,0:T(8,128)(2,1)}, bf16[512...) custom-call(s32[1]{0:T(128)} %bitcast.core_ref, bf16[4,2,1280,512]{3,2,1,0:T(8,128)(2,1)} %get-tuple-element.70.e_ref, ...), custom_call_target="tpu_custom_call" | custom-call | flops 1048576 | bytes 4096 | tf_op jit(solution)/shard_map/grads/pallas_call | solution.py:204
  100.6 6.8 %collective-permute-start.16 = (bf16[512,512]{1,0:T(8,128)(2,1)S(1)}, bf16[512,512]{1,0:T(8,128)(2,1)}, u32[]{:S(2)}, u32[]{:S(2)}) collective-permute-start(bf16[512,512]{1,0:T(8,128)(2,1)S(1)} %pad_maximum_fusion.6), channel_id=1, source_target_pairs={{0,2},{2,0},{4,6},{6,4},{8,10},{10,8},{12,14},{14,12},{16,18},{18,... | collective-permute-start | bytes 1572872 | tf_op jit(solution)/shard_map/ppermute | solution.py:395
  108.1 1.9 %collective-permute-start.22 = (bf16[512,256]{1,0:T(8,128)(2,1)}, bf16[512,256]{1,0:T(8,128)(2,1)S(1)}, u32[]{:S(2)}, u32[]{:S(2)}) collective-permute-start(bf16[512,256]{1,0:T(8,128)(2,1)} %get-tuple-element.91), channel_id=1, source_target_pairs={{4,0},{6,2},{8,4},{10,6},{12,8},{14,10},{16,12},{18,14},{20,16},{2... | collective-permute-start | bytes 786440 | tf_op jit(solution)/shard_map/ppermute | solution.py:391
  110.0 3.3 %collective-permute-done.17.refs_5_ = bf16[512,512]{1,0:T(8,128)(2,1)} collective-permute-done((bf16[512,512]{1,0:T(8,128)(2,1)S(1)}, bf16[512,512]{1,0:T(8,128)(2,1)}, u32[]{:S(2)}, u32[]{:S(2)}) %collective-permute-start.17) | collective-permute-done | bytes 524320 | tf_op jit(solution)/shard_map/ppermute | solution.py:410
  113.3 6.4 %collective-permute-start.23 = (bf16[512,256]{1,0:T(8,128)(2,1)}, bf16[512,256]{1,0:T(8,128)(2,1)S(1)}, u32[]{:S(2)}, u32[]{:S(2)}) collective-permute-start(bf16[512,256]{1,0:T(8,128)(2,1)} %get-tuple-element.106), channel_id=1, source_target_pairs={{8,0},{10,2},{12,4},{14,6},{16,8},{18,10},{20,12},{22,14},{24,16},... | collective-permute-start | bytes 786440 | tf_op jit(solution)/shard_map/ppermute | solution.py:391
  119.9 1.1 constant_dynamic-update-slice_fusion.5.dv_ref
  121.0 1.0 copy-done.9
  122.0 7.1 %tokens.1 = (bf16[256,5376]{1,0:T(8,128)(2,1)}, bf16[256,2688]{1,0:T(8,128)(2,1)}) custom-call(s32[1]{0:T(128)} %bitcast.10.at_ref, bf16[512,1024]{1,0:T(8,128)(2,1)} %copy-done.9, bf16[2688,1024]{1,0:T(8,128)(2,1)} %w_ref.1), custom_call_target="tpu_custom_call" | custom-call | flops 1048576 | bytes 4096 | tf_op jit(solution)/shard_map/tokens/pallas_call | solution.py:369
  129.0 8.1 %weight.1 = (f32[336,512]{1,0:T(8,128)}, bf16[336,512]{1,0:T(8,128)(2,1)}, bf16[336,512]{1,0:T(8,128)(2,1)}, bf16[336,512]{1,0:T(8,128)(2,1)}) custom-call(s32[2]{0:T(128)} %pad_add_fusion.1.at_ref, bf16[1344,512]{1,0:T(8,128)(2,1)} %copy-done.10, bf16[1344,512]{1,0:T(8,128)(2,1)} %constant_dynamic-update-slice_fusion.2.refs_1_, ...), custom_call_target="tpu_custom_call" | custom-call | flops 1048576 | bytes 4096 | tf_op jit(solution)/shard_map/weight/pallas_call | solution.py:341
  137.9 5.9 %collective-permute-start.30 = (bf16[336,512]{1,0:T(8,128)(2,1)}, bf16[336,512]{1,0:T(8,128)(2,1)S(1)}, u32[]{:S(2)}, u32[]{:S(2)}) collective-permute-start(bf16[336,512]{1,0:T(8,128)(2,1)} %get-tuple-element.125), channel_id=1, source_target_pairs={{0,16},{2,18},{4,20},{6,22},{8,24},{10,26},{12,28},{14,30},{16,0},... | collective-permute-start | bytes 1032200 | tf_op jit(solution)/shard_map/ppermute | solution.py:605
  143.7 9.4 %grads.3 = (bf16[256,512]{1,0:T(8,128)(2,1)}, bf16[256,512]{1,0:T(8,128)(2,1)}, bf16[2,256,512]{2,1,0:T(8,128)(2,1)}, bf16[512,256]{1,0:T(8,128)(2,1)}, bf16[512...) custom-call(s32[1]{0:T(128)} %bitcast.core_ref, bf16[4,2,1280,512]{3,2,1,0:T(8,128)(2,1)} %get-tuple-element.70.e_ref, ...), custom_call_target="tpu_custom_call" | custom-call | flops 1048576 | bytes 4096 | tf_op jit(solution)/shard_map/grads/pallas_call | solution.py:204
  153.2 4.7 %collective-permute-start.25 = (bf16[512,256]{1,0:T(8,128)(2,1)}, bf16[512,256]{1,0:T(8,128)(2,1)S(1)}, u32[]{:S(2)}, u32[]{:S(2)}) collective-permute-start(bf16[512,256]{1,0:T(8,128)(2,1)} %get-tuple-element.118), channel_id=1, source_target_pairs={{4,0},{6,2},{8,4},{10,6},{12,8},{14,10},{16,12},{18,14},{20,16},{2... | collective-permute-start | bytes 786440 | tf_op jit(solution)/shard_map/ppermute | solution.py:391
  157.9 1.9 %collective-permute-start.27 = (bf16[512,256]{1,0:T(8,128)(2,1)}, bf16[512,256]{1,0:T(8,128)(2,1)S(1)}, u32[]{:S(2)}, u32[]{:S(2)}) collective-permute-start(bf16[512,256]{1,0:T(8,128)(2,1)} %get-tuple-element.122), channel_id=1, source_target_pairs={{8,0},{10,2},{12,4},{14,6},{16,8},{18,10},{20,12},{22,14},{24,16},... | collective-permute-start | bytes 786440 | tf_op jit(solution)/shard_map/ppermute | solution.py:391
  159.8 1.2 maximum_bitcast_fusion
  161.0 1.2 maximum_bitcast_fusion.1
  162.7 5.0 %collective-permute-done.25 = bf16[512,256]{1,0:T(8,128)(2,1)S(1)} collective-permute-done((bf16[512,256]{1,0:T(8,128)(2,1)}, bf16[512,256]{1,0:T(8,128)(2,1)S(1)}, u32[]{:S(2)}, u32[]{:S(2)}) %collective-permute-start.25) | collective-permute-done | bytes 262176 | tf_op jit(solution)/shard_map/ppermute | solution.py:391
  167.6 1.8 collective-permute-start.24
  169.5 3.8 %collective-permute-done.27 = bf16[512,256]{1,0:T(8,128)(2,1)S(1)} collective-permute-done((bf16[512,256]{1,0:T(8,128)(2,1)}, bf16[512,256]{1,0:T(8,128)(2,1)S(1)}, u32[]{:S(2)}, u32[]{:S(2)}) %collective-permute-start.27) | collective-permute-done | bytes 262176 | tf_op jit(solution)/shard_map/ppermute | solution.py:391
  173.4 7.1 %collective-permute-done.31 = bf16[336,512]{1,0:T(8,128)(2,1)S(1)} collective-permute-done((bf16[336,512]{1,0:T(8,128)(2,1)S(1)}, bf16[336,512]{1,0:T(8,128)(2,1)S(1)}, u32[]{:S(2)}, u32[]{:S(2)}) %collective-permute-start.31) | collective-permute-done | bytes 344096 | tf_op jit(solution)/shard_map/ppermute | solution.py:605
  180.5 2.1 %collective-permute-start.28 = (bf16[256,512]{1,0:T(8,128)(2,1)S(1)}, bf16[256,512]{1,0:T(8,128)(2,1)S(1)}, u32[]{:S(2)}, u32[]{:S(2)}) collective-permute-start(bf16[256,512]{1,0:T(8,128)(2,1)S(1)} %get-tuple-element.133), channel_id=1, source_target_pairs={{0,2},{2,0},{4,6},{6,4},{8,10},{10,8},{12,14},{14,12},{16,18},{18,... | collective-permute-start | bytes 786440 | tf_op jit(solution)/shard_map/ppermute | solution.py:395
  (149 shorter events, 16.5 us)
Async XLA Ops:
  2.6 6.5 %copy-start.11 = (bf16[1,256,2048]{2,1,0:T(8,128)(2,1)S(1)}, bf16[1,256,2048]{2,1,0:T(8,128)(2,1)}, u32[]{:S(2)}) copy-start(bf16[1,256,2048]{2,1,0:T(8,128)(2,1)} %param.10) | copy-start | bytes 3145732
  2.6 23.8 %collective-permute-start.3 = (bf16[256,1280]{1,0:T(8,128)(2,1)}, bf16[256,1280]{1,0:T(8,128)(2,1)}, u32[]{:S(2)}, u32[]{:S(2)}) collective-permute-start(bf16[256,1280]{1,0:T(8,128)(2,1)} %dynamic-slice_bitcast_fusion.1), channel_id=1, source_target_pairs={{0,1},{1,0},{2,3},{3,2},{4,5},{5,4},{6,7},{7,6},{8,9},{9,8},{10,11... | collective-permute-start | bytes 1966088 | tf_op jit(solution)/shard_map/ppermute | solution.py:400
  5.9 3.4 %collective-permute-start = (bf16[272,512]{1,0:T(8,128)(2,1)}, bf16[272,512]{1,0:T(8,128)(2,1)S(1)}, u32[]{:S(2)}, u32[]{:S(2)}) collective-permute-start(bf16[272,512]{1,0:T(8,128)(2,1)} %maximum_maximum_fusion.1), channel_id=1, source_target_pairs={{0,2},{2,0},{4,6},{6,4},{8,10},{10,8},{12,14},{14,12},{16,18},{18,... | collective-permute-start | bytes 835592 | tf_op jit(solution)/shard_map/ppermute | solution.py:395
  8.8 25.2 %collective-permute-start.4 = (bf16[256,1408]{1,0:T(8,128)(2,1)}, bf16[256,1408]{1,0:T(8,128)(2,1)S(1)}, u32[]{:S(2)}, u32[]{:S(2)}) collective-permute-start(bf16[256,1408]{1,0:T(8,128)(2,1)} %dynamic-slice_bitcast_fusion), channel_id=1, source_target_pairs={{0,1},{1,0},{2,3},{3,2},{4,5},{5,4},{6,7},{7,6},{8,9},{9,8},{10,11... | collective-permute-start | bytes 2162696 | tf_op jit(solution)/shard_map/ppermute | solution.py:400
  9.4 12.2 %copy-start.2 = (bf16[528,512]{1,0:T(8,128)(2,1)}, bf16[528,512]{1,0:T(8,128)(2,1)S(1)}, u32[]{:S(2)}) copy-start(bf16[528,512]{1,0:T(8,128)(2,1)S(1)} %pad_maximum_fusion.3.refs_2_) | copy-start | bytes 1622020
  9.4 31.4 %collective-permute-start.2 = (bf16[528,512]{1,0:T(8,128)(2,1)S(1)}, bf16[528,512]{1,0:T(8,128)(2,1)S(1)}, u32[]{:S(2)}, u32[]{:S(2)}) collective-permute-start(bf16[528,512]{1,0:T(8,128)(2,1)S(1)} %pad_maximum_fusion.3.refs_2_), channel_id=1, source_target_pairs={{0,4},{2,6},{4,8},{6,10},{8,12},{10,14},{12,16},{14,18},{16,20},{1... | collective-permute-start | bytes 1622024 | tf_op jit(solution)/shard_map/ppermute | solution.py:391
  12.6 28.5 %collective-permute-start.1 = (bf16[528,512]{1,0:T(8,128)(2,1)S(1)}, bf16[528,512]{1,0:T(8,128)(2,1)S(1)}, u32[]{:S(2)}, u32[]{:S(2)}) collective-permute-start(bf16[528,512]{1,0:T(8,128)(2,1)S(1)} %pad_maximum_fusion.3.refs_2_), channel_id=1, source_target_pairs={{0,8},{2,10},{4,12},{6,14},{8,16},{10,18},{12,20},{14,22},{16,24},... | collective-permute-start | bytes 1622024 | tf_op jit(solution)/shard_map/ppermute | solution.py:391
  15.9 27.6 %collective-permute-start.5 = (bf16[256,2048]{1,0:T(8,128)(2,1)S(1)}, bf16[256,2048]{1,0:T(8,128)(2,1)S(1)}, u32[]{:S(2)}, u32[]{:S(2)}) collective-permute-start(bf16[256,2048]{1,0:T(8,128)(2,1)S(1)} %pad_maximum_fusion), channel_id=1, source_target_pairs={{0,2},{2,0},{4,6},{6,4},{8,10},{10,8},{12,14},{14,12},{16,18},{18,... | collective-permute-start | bytes 3145736 | tf_op jit(solution)/shard_map/ppermute | solution.py:395
  26.5 32.7 %collective-permute-start.7 = (bf16[1344,256]{1,0:T(8,128)(2,1)}, bf16[1344,256]{1,0:T(8,128)(2,1)}, u32[]{:S(2)}, u32[]{:S(2)}) collective-permute-start(bf16[1344,256]{1,0:T(8,128)(2,1)} %get-tuple-element.80), channel_id=1, source_target_pairs={{0,4},{2,6},{4,0},{6,2},{8,12},{10,14},{12,8},{14,10},{16,20},{18,... | collective-permute-start | bytes 2064392 | tf_op jit(solution)/shard_map/ppermute | solution.py:435
  39.6 19.6 %collective-permute-start.6 = (bf16[256,1024]{1,0:T(8,128)(2,1)}, bf16[256,1024]{1,0:T(8,128)(2,1)}, u32[]{:S(2)}, u32[]{:S(2)}) collective-permute-start(bf16[256,1024]{1,0:T(8,128)(2,1)} %product.2), channel_id=1, source_target_pairs={{0,1},{1,0},{2,3},{3,2},{4,5},{5,4},{6,7},{7,6},{8,9},{9,8},{10,11... | collective-permute-start | bytes 1572872 | tf_op jit(solution)/shard_map/ppermute | solution.py:400
  40.8 25.7 %collective-permute-start.10 = (bf16[1344,256]{1,0:T(8,128)(2,1)}, bf16[1344,256]{1,0:T(8,128)(2,1)S(1)}, u32[]{:S(2)}, u32[]{:S(2)}) collective-permute-start(bf16[1344,256]{1,0:T(8,128)(2,1)} %get-tuple-element.83), channel_id=1, source_target_pairs={{0,1},{1,0},{2,3},{3,2},{4,5},{5,4},{6,7},{7,6},{8,9},{9,8},{10,11... | collective-permute-start | bytes 2064392 | tf_op jit(solution)/shard_map/ppermute | solution.py:400
  42.3 24.2 %collective-permute-start.9 = (bf16[1344,256]{1,0:T(8,128)(2,1)}, bf16[1344,256]{1,0:T(8,128)(2,1)}, u32[]{:S(2)}, u32[]{:S(2)}) collective-permute-start(bf16[1344,256]{1,0:T(8,128)(2,1)} %get-tuple-element.82), channel_id=1, source_target_pairs={{0,4},{2,6},{4,0},{6,2},{8,12},{10,14},{12,8},{14,10},{16,20},{18,... | collective-permute-start | bytes 2064392 | tf_op jit(solution)/shard_map/ppermute | solution.py:435
  44.5 14.7 %copy-start.8 = (f32[256,1024]{1,0:T(8,128)S(1)}, f32[256,1024]{1,0:T(8,128)}, u32[]{:S(2)}) copy-start(f32[256,1024]{1,0:T(8,128)} %product.3) | copy-start | bytes 3145732
  58.8 11.4 %collective-permute-start.12 = (bf16[512,512]{1,0:T(8,128)(2,1)}, bf16[512,512]{1,0:T(8,128)(2,1)S(1)}, u32[]{:S(2)}, u32[]{:S(2)}) collective-permute-start(bf16[512,512]{1,0:T(8,128)(2,1)} %get-tuple-element.79), channel_id=1, source_target_pairs={{0,4},{2,6},{4,0},{6,2},{8,12},{10,14},{12,8},{14,10},{16,20},{18,... | collective-permute-start | bytes 1572872 | tf_op jit(solution)/shard_map/ppermute | solution.py:435
  60.3 9.9 %copy-start.22 = (bf16[512,512]{1,0:T(8,128)(2,1)S(1)}, bf16[512,512]{1,0:T(8,128)(2,1)}, u32[]{:S(2)}) copy-start(bf16[512,512]{1,0:T(8,128)(2,1)} %get-tuple-element.85) | copy-start | bytes 1572868
  60.4 4.0 %collective-permute-start.8 = (bf16[256,512]{1,0:T(8,128)(2,1)S(1)}, bf16[256,512]{1,0:T(8,128)(2,1)S(1)}, u32[]{:S(2)}, u32[]{:S(2)}) collective-permute-start(bf16[256,512]{1,0:T(8,128)(2,1)S(1)} %get-tuple-element.139), channel_id=1, source_target_pairs={{0,2},{2,0},{4,6},{6,4},{8,10},{10,8},{12,14},{14,12},{16,18},{18,... | collective-permute-start | bytes 786440 | tf_op jit(solution)/shard_map/ppermute | solution.py:395
  63.1 20.2 %collective-permute-start.19 = (bf16[1344,256]{1,0:T(8,128)(2,1)}, bf16[1344,256]{1,0:T(8,128)(2,1)S(1)}, u32[]{:S(2)}, u32[]{:S(2)}) collective-permute-start(bf16[1344,256]{1,0:T(8,128)(2,1)} %collective-permute-done.7), channel_id=1, source_target_pairs={{0,1},{1,0},{2,3},{3,2},{4,5},{5,4},{6,7},{7,6},{8,9},{9,8},{10,11... | collective-permute-start | bytes 2064392 | tf_op jit(solution)/shard_map/ppermute | solution.py:400
  64.4 14.9 %copy-start.3 = (bf16[512,512]{1,0:T(8,128)(2,1)}, bf16[512,512]{1,0:T(8,128)(2,1)S(1)}, u32[]{:S(2)}) copy-start(bf16[512,512]{1,0:T(8,128)(2,1)S(1)} %constant_dynamic-update-slice_fusion.6.refs_5_) | copy-start | bytes 1572868
  66.5 12.9 %collective-permute-start.11 = (bf16[512,512]{1,0:T(8,128)(2,1)S(1)}, bf16[512,512]{1,0:T(8,128)(2,1)S(1)}, u32[]{:S(2)}, u32[]{:S(2)}) collective-permute-start(bf16[512,512]{1,0:T(8,128)(2,1)S(1)} %constant_dynamic-update-slice_fusion.6.refs_5_), channel_id=1, source_target_pairs={{0,8},{2,10},{4,12},{6,14},{8,16},{10,18},{12,20},{14,22},{16,24},... | collective-permute-start | bytes 1572872 | tf_op jit(solution)/shard_map/ppermute | solution.py:391
  70.4 11.3 %copy-start.20 = (bf16[512,512]{1,0:T(8,128)(2,1)S(1)}, bf16[512,512]{1,0:T(8,128)(2,1)}, u32[]{:S(2)}) copy-start(bf16[512,512]{1,0:T(8,128)(2,1)} %get-tuple-element.89) | copy-start | bytes 1572868
  70.4 11.3 %collective-permute-start.14 = (bf16[512,512]{1,0:T(8,128)(2,1)S(1)}, bf16[512,512]{1,0:T(8,128)(2,1)S(1)}, u32[]{:S(2)}, u32[]{:S(2)}) collective-permute-start(bf16[512,512]{1,0:T(8,128)(2,1)S(1)} %fusion.1), channel_id=1, source_target_pairs={{8,0},{10,2},{12,4},{14,6},{16,8},{18,10},{20,12},{22,14},{24,16},... | collective-permute-start | bytes 1572872 | tf_op jit(solution)/shard_map/ppermute | solution.py:391
  74.0 8.0 %copy-start.10 = (bf16[1344,512]{1,0:T(8,128)(2,1)}, bf16[1344,512]{1,0:T(8,128)(2,1)S(1)}, u32[]{:S(2)}) copy-start(bf16[1344,512]{1,0:T(8,128)(2,1)S(1)} %constant_dynamic-update-slice_fusion.refs_0_) | copy-start | bytes 4128772
  74.0 55.0 %collective-permute-start.20 = (bf16[1344,512]{1,0:T(8,128)(2,1)S(1)}, bf16[1344,512]{1,0:T(8,128)(2,1)}, u32[]{:S(2)}, u32[]{:S(2)}) collective-permute-start(bf16[1344,512]{1,0:T(8,128)(2,1)S(1)} %constant_dynamic-update-slice_fusion.refs_0_), channel_id=1, source_target_pairs={{0,2},{2,0},{4,6},{6,4},{8,10},{10,8},{12,14},{14,12},{16,18},{18,... | collective-permute-start | bytes 4128776 | tf_op jit(solution)/shard_map/ppermute | solution.py:395
  79.4 10.8 %collective-permute-start.13 = (bf16[512,512]{1,0:T(8,128)(2,1)S(1)}, bf16[512,512]{1,0:T(8,128)(2,1)S(1)}, u32[]{:S(2)}, u32[]{:S(2)}) collective-permute-start(bf16[512,512]{1,0:T(8,128)(2,1)S(1)} %broadcast_select_fusion), channel_id=1, source_target_pairs={{0,4},{2,6},{4,0},{6,2},{8,12},{10,14},{12,8},{14,10},{16,20},{18,... | collective-permute-start | bytes 1572872 | tf_op jit(solution)/shard_map/ppermute | solution.py:435
  82.0 18.5 %copy-start.7 = (bf16[512,512]{1,0:T(8,128)(2,1)}, bf16[512,512]{1,0:T(8,128)(2,1)S(1)}, u32[]{:S(2)}) copy-start(bf16[512,512]{1,0:T(8,128)(2,1)S(1)} %fusion.3.refs_4_) | copy-start | bytes 1572868
  82.0 18.5 %collective-permute-start.15 = (bf16[512,512]{1,0:T(8,128)(2,1)S(1)}, bf16[512,512]{1,0:T(8,128)(2,1)S(1)}, u32[]{:S(2)}, u32[]{:S(2)}) collective-permute-start(bf16[512,512]{1,0:T(8,128)(2,1)S(1)} %fusion.3.refs_4_), channel_id=1, source_target_pairs={{0,1},{1,0},{2,3},{3,2},{4,5},{5,4},{6,7},{7,6},{8,9},{9,8},{10,11... | collective-permute-start | bytes 1572872 | tf_op jit(solution)/shard_map/ppermute | solution.py:400
  84.2 44.8 %collective-permute-start.21 = (bf16[1344,512]{1,0:T(8,128)(2,1)}, bf16[1344,512]{1,0:T(8,128)(2,1)}, u32[]{:S(2)}, u32[]{:S(2)}) collective-permute-start(bf16[1344,512]{1,0:T(8,128)(2,1)} %constant_dynamic-update-slice_fusion.2.refs_1_), channel_id=1, source_target_pairs={{0,2},{2,0},{4,6},{6,4},{8,10},{10,8},{12,14},{14,12},{16,18},{18,... | collective-permute-start | bytes 4128776 | tf_op jit(solution)/shard_map/ppermute | solution.py:395
  89.5 18.6 %collective-permute-start.18 = (bf16[512,512]{1,0:T(8,128)(2,1)S(1)}, bf16[512,512]{1,0:T(8,128)(2,1)}, u32[]{:S(2)}, u32[]{:S(2)}) collective-permute-start(bf16[512,512]{1,0:T(8,128)(2,1)S(1)} %fusion.3.refs_4_), channel_id=1, source_target_pairs={{0,5},{1,4},{2,7},{3,6},{4,1},{5,0},{6,3},{7,2},{8,13},{9,12},{10,... | collective-permute-start | bytes 1572872 | tf_op jit(solution)/shard_map/ppermute | solution.py:410
  90.3 23.1 %collective-permute-start.17 = (bf16[512,512]{1,0:T(8,128)(2,1)S(1)}, bf16[512,512]{1,0:T(8,128)(2,1)}, u32[]{:S(2)}, u32[]{:S(2)}) collective-permute-start(bf16[512,512]{1,0:T(8,128)(2,1)S(1)} %fusion.3.refs_4_), channel_id=1, source_target_pairs={{0,4},{1,5},{2,6},{3,7},{4,0},{5,1},{6,2},{7,3},{8,12},{9,13},{10,... | collective-permute-start | bytes 1572872 | tf_op jit(solution)/shard_map/ppermute | solution.py:410
  100.5 20.5 %copy-start.13 = (bf16[512,512]{1,0:T(8,128)(2,1)}, bf16[512,512]{1,0:T(8,128)(2,1)S(1)}, u32[]{:S(2)}) copy-start(bf16[512,512]{1,0:T(8,128)(2,1)S(1)} %collective-permute-done.15.refs_6_) | copy-start | bytes 1572868
  100.6 19.3 %collective-permute-start.16 = (bf16[512,512]{1,0:T(8,128)(2,1)S(1)}, bf16[512,512]{1,0:T(8,128)(2,1)}, u32[]{:S(2)}, u32[]{:S(2)}) collective-permute-start(bf16[512,512]{1,0:T(8,128)(2,1)S(1)} %pad_maximum_fusion.6), channel_id=1, source_target_pairs={{0,2},{2,0},{4,6},{6,4},{8,10},{10,8},{12,14},{14,12},{16,18},{18,... | collective-permute-start | bytes 1572872 | tf_op jit(solution)/shard_map/ppermute | solution.py:395
  108.1 29.1 %collective-permute-start.22 = (bf16[512,256]{1,0:T(8,128)(2,1)}, bf16[512,256]{1,0:T(8,128)(2,1)S(1)}, u32[]{:S(2)}, u32[]{:S(2)}) collective-permute-start(bf16[512,256]{1,0:T(8,128)(2,1)} %get-tuple-element.91), channel_id=1, source_target_pairs={{4,0},{6,2},{8,4},{10,6},{12,8},{14,10},{16,12},{18,14},{20,16},{2... | collective-permute-start | bytes 786440 | tf_op jit(solution)/shard_map/ppermute | solution.py:391
  113.3 23.9 %collective-permute-start.23 = (bf16[512,256]{1,0:T(8,128)(2,1)}, bf16[512,256]{1,0:T(8,128)(2,1)S(1)}, u32[]{:S(2)}, u32[]{:S(2)}) collective-permute-start(bf16[512,256]{1,0:T(8,128)(2,1)} %get-tuple-element.106), channel_id=1, source_target_pairs={{8,0},{10,2},{12,4},{14,6},{16,8},{18,10},{20,12},{22,14},{24,16},... | collective-permute-start | bytes 786440 | tf_op jit(solution)/shard_map/ppermute | solution.py:391
  129.0 55.8 %collective-permute-start.29 = (bf16[256,2688]{1,0:T(8,128)(2,1)}, bf16[256,2688]{1,0:T(8,128)(2,1)S(1)}, u32[]{:S(2)}, u32[]{:S(2)}) collective-permute-start(bf16[256,2688]{1,0:T(8,128)(2,1)} %get-tuple-element.96), channel_id=1, source_target_pairs={{0,1},{1,0},{2,3},{3,2},{4,5},{5,4},{6,7},{7,6},{8,9},{9,8},{10,11... | collective-permute-start | bytes 4128776 | tf_op jit(solution)/shard_map/ppermute | solution.py:400
  137.9 22.0 %copy-start.27 = (bf16[256,512]{1,0:T(8,128)(2,1)S(1)}, bf16[256,512]{1,0:T(8,128)(2,1)}, u32[]{:S(2)}) copy-start(bf16[256,512]{1,0:T(8,128)(2,1)} %get-tuple-element.88) | copy-start | bytes 786436
  137.9 23.1 %copy-start.26 = (bf16[256,512]{1,0:T(8,128)(2,1)S(1)}, bf16[256,512]{1,0:T(8,128)(2,1)}, u32[]{:S(2)}) copy-start(bf16[256,512]{1,0:T(8,128)(2,1)} %get-tuple-element.112) | copy-start | bytes 786436
  137.9 35.5 %collective-permute-start.30 = (bf16[336,512]{1,0:T(8,128)(2,1)}, bf16[336,512]{1,0:T(8,128)(2,1)S(1)}, u32[]{:S(2)}, u32[]{:S(2)}) collective-permute-start(bf16[336,512]{1,0:T(8,128)(2,1)} %get-tuple-element.125), channel_id=1, source_target_pairs={{0,16},{2,18},{4,20},{6,22},{8,24},{10,26},{12,28},{14,30},{16,0},... | collective-permute-start | bytes 1032200 | tf_op jit(solution)/shard_map/ppermute | solution.py:605
  143.7 18.8 %collective-permute-start.26 = (bf16[336,512]{1,0:T(8,128)(2,1)}, bf16[336,512]{1,0:T(8,128)(2,1)S(1)}, u32[]{:S(2)}, u32[]{:S(2)}) collective-permute-start(bf16[336,512]{1,0:T(8,128)(2,1)} %get-tuple-element.119), channel_id=1, source_target_pairs={{0,8},{2,10},{4,12},{6,14},{8,16},{10,18},{12,20},{14,22},{16,24},... | collective-permute-start | bytes 1032200 | tf_op jit(solution)/shard_map/ppermute | solution.py:605
  153.2 9.1 %copy-start.23 = (bf16[2,256,512]{2,1,0:T(8,128)(2,1)S(1)}, bf16[2,256,512]{2,1,0:T(8,128)(2,1)}, u32[]{:S(2)}) copy-start(bf16[2,256,512]{2,1,0:T(8,128)(2,1)} %get-tuple-element.110) | copy-start | bytes 1572868
  153.2 9.1 %copy-start.24 = (bf16[2,256,512]{2,1,0:T(8,128)(2,1)S(1)}, bf16[2,256,512]{2,1,0:T(8,128)(2,1)}, u32[]{:S(2)}) copy-start(bf16[2,256,512]{2,1,0:T(8,128)(2,1)} %get-tuple-element.111) | copy-start | bytes 1572868
  153.2 14.4 %collective-permute-start.25 = (bf16[512,256]{1,0:T(8,128)(2,1)}, bf16[512,256]{1,0:T(8,128)(2,1)S(1)}, u32[]{:S(2)}, u32[]{:S(2)}) collective-permute-start(bf16[512,256]{1,0:T(8,128)(2,1)} %get-tuple-element.118), channel_id=1, source_target_pairs={{4,0},{6,2},{8,4},{10,6},{12,8},{14,10},{16,12},{18,14},{20,16},{2... | collective-permute-start | bytes 786440 | tf_op jit(solution)/shard_map/ppermute | solution.py:391
  157.9 15.4 %collective-permute-start.27 = (bf16[512,256]{1,0:T(8,128)(2,1)}, bf16[512,256]{1,0:T(8,128)(2,1)S(1)}, u32[]{:S(2)}, u32[]{:S(2)}) collective-permute-start(bf16[512,256]{1,0:T(8,128)(2,1)} %get-tuple-element.122), channel_id=1, source_target_pairs={{8,0},{10,2},{12,4},{14,6},{16,8},{18,10},{20,12},{22,14},{24,16},... | collective-permute-start | bytes 786440 | tf_op jit(solution)/shard_map/ppermute | solution.py:391
  161.0 12.2 %copy-start.30 = (bf16[512,256]{1,0:T(8,128)(2,1)S(1)}, bf16[512,256]{1,0:T(8,128)(2,1)}, u32[]{:S(2)}) copy-start(bf16[512,256]{1,0:T(8,128)(2,1)} %get-tuple-element.117) | copy-start | bytes 786436
  162.4 20.2 %copy-start.17 = (f32[336,512]{1,0:T(8,128)S(1)}, f32[336,512]{1,0:T(8,128)}, u32[]{:S(2)}) copy-start(f32[336,512]{1,0:T(8,128)} %get-tuple-element.107) | copy-start | bytes 2064388
  162.6 17.9 %collective-permute-start.31 = (bf16[336,512]{1,0:T(8,128)(2,1)S(1)}, bf16[336,512]{1,0:T(8,128)(2,1)S(1)}, u32[]{:S(2)}, u32[]{:S(2)}) collective-permute-start(bf16[336,512]{1,0:T(8,128)(2,1)S(1)} %copy-done.34), channel_id=1, source_target_pairs={{0,24},{2,26},{4,28},{6,30},{8,0},{10,2},{12,4},{14,6},{16,8},{18,... | collective-permute-start | bytes 1032200 | tf_op jit(solution)/shard_map/ppermute | solution.py:605
  167.6 17.0 %collective-permute-start.24 = (bf16[2,256,1024]{2,1,0:T(8,128)(2,1)S(1)}, bf16[2,256,1024]{2,1,0:T(8,128)(2,1)S(1)}, u32[]{:S(2)}, u32[]{:S(2)}) collective-permute-start(bf16[2,256,1024]{2,1,0:T(8,128)(2,1)S(1)} %pad_maximum_fusion.1), channel_id=1, source_target_pairs={{0,2},{2,0},{4,6},{6,4},{8,10},{10,8},{12,14},{14,12},{16,18},{18,... | collective-permute-start | bytes 3145736 | tf_op jit(solution)/shard_map/ppermute | solution.py:395
  180.5 3.3 %collective-permute-start.28 = (bf16[256,512]{1,0:T(8,128)(2,1)S(1)}, bf16[256,512]{1,0:T(8,128)(2,1)S(1)}, u32[]{:S(2)}, u32[]{:S(2)}) collective-permute-start(bf16[256,512]{1,0:T(8,128)(2,1)S(1)} %get-tuple-element.133), channel_id=1, source_target_pairs={{0,2},{2,0},{4,6},{6,4},{8,10},{10,8},{12,14},{14,12},{16,18},{18,... | collective-permute-start | bytes 786440 | tf_op jit(solution)/shard_map/ppermute | solution.py:395
  182.9 1.7 collective-permute-start.32
  (20 other events, 41.9 us)

commit v10 on v9

--- a/solution.py
+++ b/solution.py
@@ -568,25 +568,9 @@
 
     dv_fsdp[1:] = [after(x, early[4]) for x in dv_fsdp[1:]]
     dv_over_y = [after(x, early[4]) for x in dv_over_y]
-    dv_sides = [
-        jnp.concatenate([rows_of(x, at, shard_rows) for x in dv_fsdp], 0) for at in (core, 1 - core)
-    ]
-    dv_rows = placed(core, dv_sides[0], swapped(dv_sides[1]), 1)
-    dv_rows = after(dv_rows, *dv_over_y)
-    if aligned:
-        d_tokens, *made = run_tokens(fsdp_arg, dv_rows, w_value, n_fsdp)
-    else:
-        made = dot(dv_rows, w_value, NT).astype(BF16)
-        made = [made[s * shard_rows : (s + 1) * shard_rows] for s in range(n_fsdp)]
-        d_tokens = jnp.concatenate([made[0]] * n_fsdp, 1)
-        made = made[1:]
-    for s in range(1, n_fsdp):
-        back = rotated(made[s - 1], -s)
-        d_tokens = lax.dynamic_update_slice_in_dim(d_tokens, back, ((my_fsdp + s) % n_fsdp) * slab, 1)
-
     dv_pairs = list(zip(dv_fsdp, dv_over_y))
     if out_rows % 8 == 0:
-        at = after(jnp.stack([core, my_z]).astype(jnp.int32), *made)
+        at = after(jnp.stack([core, my_z]).astype(jnp.int32), early[4])
         by_z = run_weight(at, own_pairs, other_pairs, dv_pairs, n_z)
     else:
         weight_term = 0.0
@@ -605,14 +589,32 @@
         lax.ppermute(by_z[d], "ctx", [(i, (i + 4 * d) % n_ctx) for i in range(n_ctx)]) for d in range(1, n_z)
     ]
 
-    late = run_grads(after(core_arg, by_z[0]), *grad_args, n_heads // 2, n_heads)
+    dv_sides = [
+        jnp.concatenate([rows_of(x, at, shard_rows) for x in dv_fsdp], 0) for at in (core, 1 - core)
+    ]
+    dv_rows = placed(core, dv_sides[0], swapped(dv_sides[1]), 1)
+    dv_rows = after(dv_rows, by_z[0])
+    if aligned:
+        d_tokens, *made = run_tokens(fsdp_arg, dv_rows, w_value, n_fsdp)
+    else:
+        made = dot(dv_rows, w_value, NT).astype(BF16)
+        made = [made[s * shard_rows : (s + 1) * shard_rows] for s in range(n_fsdp)]
+        d_tokens = jnp.concatenate([made[0]] * n_fsdp, 1)
+        made = made[1:]
+    arrivals = []
+    for s in range(1, n_fsdp):
+        back = rotated(made[s - 1], -s)
+        arrivals.append(back)
+        d_tokens = lax.dynamic_update_slice_in_dim(d_tokens, back, ((my_fsdp + s) % n_fsdp) * slab, 1)
+
+    late = run_grads(after(core_arg, *made), *grad_args, n_heads // 2, n_heads)
     late_back = [shifted(late[4], -2), shifted(late[3], -4)]
-    over_z = [after(x, late[4]) for x in over_z]
+    late_back = [after(x, *arrivals) for x in late_back]
+    over_z = [after(x, *late_back) for x in over_z]
     row_sum = by_z[0]
     for x in over_z:
         row_sum = row_sum + x.astype(F32)
     d_weight = placed(core, rows_of(row_sum, core, out_rows), swapped(rows_of(row_sum, 1 - core, out_rows)), 1)
-    late_back = [after(x, over_z[0]) for x in late_back]
     dk_chip = jnp.concatenate(
         [
             (made_by[5].astype(F32) + back[0].astype(F32) + back[1].astype(F32)).astype(BF16)

time: 190 us -> 213 us (1.12)
  waiting for transfers between devices: 30.5 us -> 58.5 us
  starting transfers between devices: 69.1 us -> 64.5 us
  local copies, waits for them, and re-layouts: 15.7 us -> 13.3 us
    ppermute x8, waiting for transfers between devices: 9.78 us -> 28.6 us  [shifted(): lax.ppermute(x, 'ctx', [(i, i + by) for i in range(length) if 0 <= i + by...]
    ppermute x2, waiting for transfers between devices: 3.35 us -> 14.4 us  [moved(): return lax.ppermute(x, ('ctx', 'fsdp'), pairs)]
    ppermute x9, starting transfers between devices: 25.1 us -> 16.2 us  [swapped(): lax.ppermute(x, 'ctx', [(i, i ^ 1) for i in range(lax.axis_size('ctx'))])]
    ppermute x3, waiting for transfers between devices: 7.11 us -> 0.01 us  [shards(): lax.ppermute(by_z[d], 'ctx', [(i, (i + 4 * d) % n_ctx) for i in range(n_c...]
    ppermute x8, starting transfers between devices: 26.9 us -> 31.9 us  [shifted(): lax.ppermute(x, 'ctx', [(i, i + by) for i in range(length) if 0 <= i + by...]
    ppermute x4, waiting for transfers between devices: 0.53 us -> 4.24 us  [flipped(): lax.ppermute(x, 'ctx', [(i, i ^ 2) for i in range(lax.axis_size('ctx'))])]
    ppermute x3, starting transfers between devices: 5.92 us -> 3.09 us  [shards(): lax.ppermute(by_z[d], 'ctx', [(i, (i + 4 * d) % n_ctx) for i in range(n_c...]
    ppermute x7, waiting for transfers between devices: 8.3 us -> 10.5 us  [rotated(): lax.ppermute(x, 'fsdp', [(i, (i + by) % length) for i in range(length)])]
  transfers between devices with their start and end apart: 33 -> 33, of which waited for: 10 -> 10; matrix products, arithmetic and copies ran while one was open for 9% -> 8% of each run, Pallas kernels for 33% -> 26%
where the time goes in v10:
time: 213 us; the launch traced here: 209 us
  starting transfers between devices  64.5 us (30%)
  Pallas kernels  62.1 us (29%)
  waiting for transfers between devices  58.5 us (27%)
  local copies, waits for them, and re-layouts  13.3 us (6%)
  other arithmetic  9.58 us (4%)
    ppermute x8, starting transfers between devices, shifted(): lax.ppermute(x, 'ctx', [(i, i + by) for i in range(length) if 0 <= i + by...  31.9 us
    ppermute x8, waiting for transfers between devices, shifted(): lax.ppermute(x, 'ctx', [(i, i + by) for i in range(length) if 0 <= i + by...  28.6 us
    pallas_call x2, Pallas kernels, run_grads(): pl.pallas_call(functools.partial(grads_kernel, blk, n_arr - 1), grid_spec...  18.9 us
    ppermute x9, starting transfers between devices, swapped(): lax.ppermute(x, 'ctx', [(i, i ^ 1) for i in range(lax.axis_size('ctx'))])  16.2 us
    ppermute x2, waiting for transfers between devices, moved(): return lax.ppermute(x, ('ctx', 'fsdp'), pairs)  14.4 us
    pallas_call x1, Pallas kernels, run_probs(): pl.pallas_call(functools.partial(probs_kernel, blk, n_arr - 1), grid_spec...  14.3 us
    ppermute x7, waiting for transfers between devices, rotated(): lax.ppermute(x, 'fsdp', [(i, (i + by) % length) for i in range(length)])  10.5 us
    pallas_call x2, Pallas kernels, run_product(): pl.pallas_call(product_kernel, grid_spec=pltpu.PrefetchScalarGridSpec(num...  9.54 us
  transfers between devices with their start and end apart: 33, of which 10 were waited for; matrix products, arithmetic and copies ran while one was open for 8% of the time, Pallas kernels for 26%

profile of v10, /device:TPU:9, one launch (start us, length us, event | category | flops | bytes accessed | tf_op | source)
XLA Modules:
  0.0 209.5 jit_solution(6168786518130566597)
XLA Ops:
  0.7 2.0 dynamic-slice_bitcast_fusion.1
  2.6 1.2 collective-permute-start.3
  6.8 2.0 dynamic-slice_bitcast_fusion
  9.4 3.1 %collective-permute-start.2 = (bf16[528,512]{1,0:T(8,128)(2,1)S(1)}, bf16[528,512]{1,0:T(8,128)(2,1)S(1)}, u32[]{:S(2)}, u32[]{:S(2)}) collective-permute-start(bf16[528,512]{1,0:T(8,128)(2,1)S(1)} %pad_maximum_fusion.3.refs_2_), channel_id=1, source_target_pairs={{0,4},{2,6},{4,8},{6,10},{8,12},{10,14},{12,16},{14,18},{16,20},{1... | collective-permute-start | bytes 1622024 | tf_op jit(solution)/shard_map/ppermute | solution.py:391
  12.6 3.2 %collective-permute-start.1 = (bf16[528,512]{1,0:T(8,128)(2,1)S(1)}, bf16[528,512]{1,0:T(8,128)(2,1)S(1)}, u32[]{:S(2)}, u32[]{:S(2)}) collective-permute-start(bf16[528,512]{1,0:T(8,128)(2,1)S(1)} %pad_maximum_fusion.3.refs_2_), channel_id=1, source_target_pairs={{0,8},{2,10},{4,12},{6,14},{8,16},{10,18},{12,20},{14,22},{16,24},... | collective-permute-start | bytes 1622024 | tf_op jit(solution)/shard_map/ppermute | solution.py:391
  17.4 4.2 %pieces.1 = (bf16[1344,256]{1,0:T(8,128)(2,1)}, bf16[1344,256]{1,0:T(8,128)(2,1)}, bf16[1344,256]{1,0:T(8,128)(2,1)}, bf16[1344,256]{1,0:T(8,128)(2,1)}) custom-call(s32[2]{0:T(128)} %pad_add_fusion.at_ref, bf16[256,5376]{1,0:T(8,128)(2,1)} %bitcast.31), custom_call_target="tpu_custom_call" | custom-call | flops 1048576 | bytes 4096 | tf_op jit(solution)/shard_map/pieces/pallas_call | solution.py:265
  21.6 4.9 %product.3 = f32[256,1024]{1,0:T(8,128)} custom-call(s32[1]{0:T(128)} %bitcast.10.at_ref, bf16[256,5376]{1,0:T(8,128)(2,1)} %bitcast.32, bf16[2688,1024]{1,0:T(8,128)(2,1)} %w_ref.1), custom_call_target="tpu_custom_call" | custom-call | flops 1048576 | bytes 4096 | tf_op jit(solution)/shard_map/product/pallas_call | solution.py:295
  26.5 1.3 collective-permute-start.7
  27.8 6.2 %collective-permute-done.4.refs_1_ = bf16[256,1408]{1,0:T(8,128)(2,1)S(1)} collective-permute-done((bf16[256,1408]{1,0:T(8,128)(2,1)}, bf16[256,1408]{1,0:T(8,128)(2,1)S(1)}, u32[]{:S(2)}, u32[]{:S(2)}) %collective-permute-start.4) | collective-permute-done | bytes 720928 | tf_op jit(solution)/shard_map/ppermute | solution.py:400
  34.9 4.7 %product.2 = bf16[256,1024]{1,0:T(8,128)(2,1)} custom-call(s32[1]{0:T(128)} %constant.86.clone.1.at_ref, bf16[256,1280]{1,0:T(8,128)(2,1)} %collective-permute-done.3.refs_0_, bf16[256,1408]{1,0:T(8,128)(2,1)} %copy-done.16, bf16[2688,1024]{1,0:T(8,128)(2,1)} %w_ref.1), custom_call_target="tpu_custom_call" | custom-call | flops 1048576 | bytes 4096 | tf_op jit(solution)/shard_map/product/pallas_call | solution.py:295
  39.5 1.2 collective-permute-start.6
  42.2 1.2 collective-permute-start.9
  44.5 14.3 %probs.1 = (bf16[4,2,1280,512]{3,2,1,0:T(8,128)(2,1)}, f32[4,2,1,512]{3,2,1,0:T(1,128)}, bf16[4,2,128,512]{3,2,1,0:T(8,128)(2,1)}, bf16[512,512]{1,0:T(8,128)(2,...) custom-call(s32[1]{0:T(128)} %bitcast.core_ref, s32[1,512]{1,0:T(1,128)} %add_maximum_fusion.low_ref, ...), custom_call_target="tpu_custom_call" | custom-call | flops 1048576 | bytes 4096 | tf_op jit(solution)/shard_map/probs/pallas_call | solution.py:158
  59.1 1.2 add_convert_fusion
  60.4 2.6 %collective-permute-start.8 = (bf16[256,512]{1,0:T(8,128)(2,1)S(1)}, bf16[256,512]{1,0:T(8,128)(2,1)S(1)}, u32[]{:S(2)}, u32[]{:S(2)}) collective-permute-start(bf16[256,512]{1,0:T(8,128)(2,1)S(1)} %get-tuple-element.139), channel_id=1, source_target_pairs={{0,2},{2,0},{4,6},{6,4},{8,10},{10,8},{12,14},{14,12},{16,18},{18,... | collective-permute-start | bytes 786440 | tf_op jit(solution)/shard_map/ppermute | solution.py:395
  63.1 1.3 collective-permute-start.17
  64.4 2.1 collective-permute-done.10
  66.5 3.2 %collective-permute-start.11 = (bf16[512,512]{1,0:T(8,128)(2,1)S(1)}, bf16[512,512]{1,0:T(8,128)(2,1)S(1)}, u32[]{:S(2)}, u32[]{:S(2)}) collective-permute-start(bf16[512,512]{1,0:T(8,128)(2,1)S(1)} %constant_dynamic-update-slice_fusion.6.refs_5_), channel_id=1, source_target_pairs={{0,8},{2,10},{4,12},{6,14},{8,16},{10,18},{12,20},{14,22},{16,24},... | collective-permute-start | bytes 1572872 | tf_op jit(solution)/shard_map/ppermute | solution.py:391
  69.7 1.1 constant_dynamic-update-slice_fusion.refs_0_
  70.9 4.7 %collective-permute-start.18 = (bf16[1344,512]{1,0:T(8,128)(2,1)S(1)}, bf16[1344,512]{1,0:T(8,128)(2,1)}, u32[]{:S(2)}, u32[]{:S(2)}) collective-permute-start(bf16[1344,512]{1,0:T(8,128)(2,1)S(1)} %constant_dynamic-update-slice_fusion.refs_0_), channel_id=1, source_target_pairs={{0,2},{2,0},{4,6},{6,4},{8,10},{10,8},{12,14},{14,12},{16,18},{18,... | collective-permute-start | bytes 4128776 | tf_op jit(solution)/shard_map/ppermute | solution.py:395
  75.7 2.4 %collective-permute-start.14 = (bf16[512,512]{1,0:T(8,128)(2,1)S(1)}, bf16[512,512]{1,0:T(8,128)(2,1)S(1)}, u32[]{:S(2)}, u32[]{:S(2)}) collective-permute-start(bf16[512,512]{1,0:T(8,128)(2,1)S(1)} %fusion.1), channel_id=1, source_target_pairs={{8,0},{10,2},{12,4},{14,6},{16,8},{18,10},{20,12},{22,14},{24,16},... | collective-permute-start | bytes 1572872 | tf_op jit(solution)/shard_map/ppermute | solution.py:391
  79.1 2.2 %collective-permute-done.17 = bf16[1344,256]{1,0:T(8,128)(2,1)S(1)} collective-permute-done((bf16[1344,256]{1,0:T(8,128)(2,1)}, bf16[1344,256]{1,0:T(8,128)(2,1)S(1)}, u32[]{:S(2)}, u32[]{:S(2)}) %collective-permute-start.17) | collective-permute-done | bytes 688160 | tf_op jit(solution)/shard_map/ppermute | solution.py:400
  82.2 2.4 %collective-permute-start.19 = (bf16[1344,512]{1,0:T(8,128)(2,1)}, bf16[1344,512]{1,0:T(8,128)(2,1)}, u32[]{:S(2)}, u32[]{:S(2)}) collective-permute-start(bf16[1344,512]{1,0:T(8,128)(2,1)} %constant_dynamic-update-slice_fusion.2.refs_1_), channel_id=1, source_target_pairs={{0,2},{2,0},{4,6},{6,4},{8,10},{10,8},{12,14},{14,12},{16,18},{18,... | collective-permute-start | bytes 4128776 | tf_op jit(solution)/shard_map/ppermute | solution.py:395
  84.6 1.3 collective-permute-start.13
  85.9 5.3 %collective-permute-done.14 = bf16[512,512]{1,0:T(8,128)(2,1)S(1)} collective-permute-done((bf16[512,512]{1,0:T(8,128)(2,1)S(1)}, bf16[512,512]{1,0:T(8,128)(2,1)S(1)}, u32[]{:S(2)}, u32[]{:S(2)}) %collective-permute-start.14) | collective-permute-done | bytes 524320 | tf_op jit(solution)/shard_map/ppermute | solution.py:391
  91.5 1.3 collective-permute-start.15
  92.8 1.2 collective-permute-start.21
  94.0 4.2 %collective-permute-done.13.refs_4_ = bf16[512,512]{1,0:T(8,128)(2,1)S(1)} collective-permute-done((bf16[512,512]{1,0:T(8,128)(2,1)S(1)}, bf16[512,512]{1,0:T(8,128)(2,1)S(1)}, u32[]{:S(2)}, u32[]{:S(2)}) %collective-permute-start.13) | collective-permute-done | bytes 524320 | tf_op jit(solution)/shard_map/ppermute | solution.py:435
  98.2 1.2 collective-permute-start.20
  99.5 9.4 %grads.2 = (bf16[256,512]{1,0:T(8,128)(2,1)}, bf16[256,512]{1,0:T(8,128)(2,1)}, bf16[2,256,512]{2,1,0:T(8,128)(2,1)}, bf16[512,256]{1,0:T(8,128)(2,1)}, bf16[512...) custom-call(s32[1]{0:T(128)} %bitcast.core_ref, bf16[4,2,1280,512]{3,2,1,0:T(8,128)(2,1)} %get-tuple-element.70.e_ref, ...), custom_call_target="tpu_custom_call" | custom-call | flops 1048576 | bytes 4096 | tf_op jit(solution)/shard_map/grads/pallas_call | solution.py:204
  110.2 6.3 %collective-permute-done.21.refs_7_ = bf16[512,512]{1,0:T(8,128)(2,1)} collective-permute-done((bf16[512,512]{1,0:T(8,128)(2,1)S(1)}, bf16[512,512]{1,0:T(8,128)(2,1)}, u32[]{:S(2)}, u32[]{:S(2)}) %collective-permute-start.21) | collective-permute-done | bytes 524320 | tf_op jit(solution)/shard_map/ppermute | solution.py:410
  116.5 2.0 collective-permute-start.22
  118.6 8.0 %collective-permute-done.20.refs_5_ = bf16[512,512]{1,0:T(8,128)(2,1)} collective-permute-done((bf16[512,512]{1,0:T(8,128)(2,1)S(1)}, bf16[512,512]{1,0:T(8,128)(2,1)}, u32[]{:S(2)}, u32[]{:S(2)}) %collective-permute-start.20) | collective-permute-done | bytes 524320 | tf_op jit(solution)/shard_map/ppermute | solution.py:410
  126.6 2.1 collective-permute-start.23
  129.5 8.1 %weight.1 = (f32[336,512]{1,0:T(8,128)}, bf16[336,512]{1,0:T(8,128)(2,1)}, bf16[336,512]{1,0:T(8,128)(2,1)}, bf16[336,512]{1,0:T(8,128)(2,1)}) custom-call(s32[2]{0:T(128)} %pad_add_fusion.1.at_ref, bf16[1344,512]{1,0:T(8,128)(2,1)} %copy-done.10, bf16[1344,512]{1,0:T(8,128)(2,1)} %constant_dynamic-update-slice_fusion.2.refs_1_, ...), custom_call_target="tpu_custom_call" | custom-call | flops 1048576 | bytes 4096 | tf_op jit(solution)/shard_map/weight/pallas_call | solution.py:341
  138.8 7.0 %tokens.1 = (bf16[256,5376]{1,0:T(8,128)(2,1)}, bf16[256,2688]{1,0:T(8,128)(2,1)}) custom-call(s32[1]{0:T(128)} %bitcast.10.at_ref, bf16[512,1024]{1,0:T(8,128)(2,1)} %copy-done.9, bf16[2688,1024]{1,0:T(8,128)(2,1)} %w_ref.1), custom_call_target="tpu_custom_call" | custom-call | flops 1048576 | bytes 4096 | tf_op jit(solution)/shard_map/tokens/pallas_call | solution.py:369
  145.8 1.2 collective-permute-start.26
  147.0 9.5 %grads.3 = (bf16[256,512]{1,0:T(8,128)(2,1)}, bf16[256,512]{1,0:T(8,128)(2,1)}, bf16[2,256,512]{2,1,0:T(8,128)(2,1)}, bf16[512,256]{1,0:T(8,128)(2,1)}, bf16[512...) custom-call(s32[1]{0:T(128)} %bitcast.core_ref, bf16[4,2,1280,512]{3,2,1,0:T(8,128)(2,1)} %get-tuple-element.70.e_ref, ...), custom_call_target="tpu_custom_call" | custom-call | flops 1048576 | bytes 4096 | tf_op jit(solution)/shard_map/grads/pallas_call | solution.py:204
  156.5 1.1 pad_maximum_fusion.1
  157.6 2.4 %collective-permute-start.24 = (bf16[2,256,1024]{2,1,0:T(8,128)(2,1)S(1)}, bf16[2,256,1024]{2,1,0:T(8,128)(2,1)S(1)}, u32[]{:S(2)}, u32[]{:S(2)}) collective-permute-start(bf16[2,256,1024]{2,1,0:T(8,128)(2,1)S(1)} %pad_maximum_fusion.1), channel_id=1, source_target_pairs={{0,2},{2,0},{4,6},{6,4},{8,10},{10,8},{12,14},{14,12},{16,18},{18,... | collective-permute-start | bytes 3145736 | tf_op jit(solution)/shard_map/ppermute | solution.py:395
  160.1 1.3 collective-permute-start.29
  161.4 1.8 collective-permute-start.30
  163.2 5.3 %collective-permute-start.25 = (bf16[512,256]{1,0:T(8,128)(2,1)}, bf16[512,256]{1,0:T(8,128)(2,1)S(1)}, u32[]{:S(2)}, u32[]{:S(2)}) collective-permute-start(bf16[512,256]{1,0:T(8,128)(2,1)} %get-tuple-element.118), channel_id=1, source_target_pairs={{4,0},{6,2},{8,4},{10,6},{12,8},{14,10},{16,12},{18,14},{20,16},{2... | collective-permute-start | bytes 786440 | tf_op jit(solution)/shard_map/ppermute | solution.py:391
  168.5 1.2 add_convert_fusion.2
  169.8 1.4 maximum_bitcast_fusion
  171.2 5.4 %collective-permute-done.25 = bf16[512,256]{1,0:T(8,128)(2,1)S(1)} collective-permute-done((bf16[512,256]{1,0:T(8,128)(2,1)}, bf16[512,256]{1,0:T(8,128)(2,1)S(1)}, u32[]{:S(2)}, u32[]{:S(2)}) %collective-permute-start.25) | collective-permute-done | bytes 262176 | tf_op jit(solution)/shard_map/ppermute | solution.py:391
  176.8 10.5 %collective-permute-start.27 = (bf16[512,256]{1,0:T(8,128)(2,1)S(1)}, bf16[512,256]{1,0:T(8,128)(2,1)S(1)}, u32[]{:S(2)}, u32[]{:S(2)}) collective-permute-start(bf16[512,256]{1,0:T(8,128)(2,1)S(1)} %copy-done.31), channel_id=1, source_target_pairs={{8,0},{10,2},{12,4},{14,6},{16,8},{18,10},{20,12},{22,14},{24,16},... | collective-permute-start | bytes 786440 | tf_op jit(solution)/shard_map/ppermute | solution.py:391
  187.4 17.9 %collective-permute-done.27 = bf16[512,256]{1,0:T(8,128)(2,1)S(1)} collective-permute-done((bf16[512,256]{1,0:T(8,128)(2,1)S(1)}, bf16[512,256]{1,0:T(8,128)(2,1)S(1)}, u32[]{:S(2)}, u32[]{:S(2)}) %collective-permute-start.27) | collective-permute-done | bytes 262176 | tf_op jit(solution)/shard_map/ppermute | solution.py:391
  (143 shorter events, 18.6 us)
Async XLA Ops:
  2.6 23.8 %collective-permute-start.3 = (bf16[256,1280]{1,0:T(8,128)(2,1)}, bf16[256,1280]{1,0:T(8,128)(2,1)}, u32[]{:S(2)}, u32[]{:S(2)}) collective-permute-start(bf16[256,1280]{1,0:T(8,128)(2,1)} %dynamic-slice_bitcast_fusion.1), channel_id=1, source_target_pairs={{0,1},{1,0},{2,3},{3,2},{4,5},{5,4},{6,7},{7,6},{8,9},{9,8},{10,11... | collective-permute-start | bytes 1966088 | tf_op jit(solution)/shard_map/ppermute | solution.py:400
  5.9 3.4 %collective-permute-start = (bf16[272,512]{1,0:T(8,128)(2,1)}, bf16[272,512]{1,0:T(8,128)(2,1)S(1)}, u32[]{:S(2)}, u32[]{:S(2)}) collective-permute-start(bf16[272,512]{1,0:T(8,128)(2,1)} %maximum_maximum_fusion.1), channel_id=1, source_target_pairs={{0,2},{2,0},{4,6},{6,4},{8,10},{10,8},{12,14},{14,12},{16,18},{18,... | collective-permute-start | bytes 835592 | tf_op jit(solution)/shard_map/ppermute | solution.py:395
  8.8 25.2 %collective-permute-start.4 = (bf16[256,1408]{1,0:T(8,128)(2,1)}, bf16[256,1408]{1,0:T(8,128)(2,1)S(1)}, u32[]{:S(2)}, u32[]{:S(2)}) collective-permute-start(bf16[256,1408]{1,0:T(8,128)(2,1)} %dynamic-slice_bitcast_fusion), channel_id=1, source_target_pairs={{0,1},{1,0},{2,3},{3,2},{4,5},{5,4},{6,7},{7,6},{8,9},{9,8},{10,11... | collective-permute-start | bytes 2162696 | tf_op jit(solution)/shard_map/ppermute | solution.py:400
  9.4 12.2 %copy-start.2 = (bf16[528,512]{1,0:T(8,128)(2,1)}, bf16[528,512]{1,0:T(8,128)(2,1)S(1)}, u32[]{:S(2)}) copy-start(bf16[528,512]{1,0:T(8,128)(2,1)S(1)} %pad_maximum_fusion.3.refs_2_) | copy-start | bytes 1622020
  9.4 31.4 %collective-permute-start.2 = (bf16[528,512]{1,0:T(8,128)(2,1)S(1)}, bf16[528,512]{1,0:T(8,128)(2,1)S(1)}, u32[]{:S(2)}, u32[]{:S(2)}) collective-permute-start(bf16[528,512]{1,0:T(8,128)(2,1)S(1)} %pad_maximum_fusion.3.refs_2_), channel_id=1, source_target_pairs={{0,4},{2,6},{4,8},{6,10},{8,12},{10,14},{12,16},{14,18},{16,20},{1... | collective-permute-start | bytes 1622024 | tf_op jit(solution)/shard_map/ppermute | solution.py:391
  12.6 28.5 %collective-permute-start.1 = (bf16[528,512]{1,0:T(8,128)(2,1)S(1)}, bf16[528,512]{1,0:T(8,128)(2,1)S(1)}, u32[]{:S(2)}, u32[]{:S(2)}) collective-permute-start(bf16[528,512]{1,0:T(8,128)(2,1)S(1)} %pad_maximum_fusion.3.refs_2_), channel_id=1, source_target_pairs={{0,8},{2,10},{4,12},{6,14},{8,16},{10,18},{12,20},{14,22},{16,24},... | collective-permute-start | bytes 1622024 | tf_op jit(solution)/shard_map/ppermute | solution.py:391
  15.9 27.6 %collective-permute-start.5 = (bf16[256,2048]{1,0:T(8,128)(2,1)S(1)}, bf16[256,2048]{1,0:T(8,128)(2,1)S(1)}, u32[]{:S(2)}, u32[]{:S(2)}) collective-permute-start(bf16[256,2048]{1,0:T(8,128)(2,1)S(1)} %pad_maximum_fusion), channel_id=1, source_target_pairs={{0,2},{2,0},{4,6},{6,4},{8,10},{10,8},{12,14},{14,12},{16,18},{18,... | collective-permute-start | bytes 3145736 | tf_op jit(solution)/shard_map/ppermute | solution.py:395
  26.5 32.6 %collective-permute-start.7 = (bf16[1344,256]{1,0:T(8,128)(2,1)}, bf16[1344,256]{1,0:T(8,128)(2,1)}, u32[]{:S(2)}, u32[]{:S(2)}) collective-permute-start(bf16[1344,256]{1,0:T(8,128)(2,1)} %get-tuple-element.80), channel_id=1, source_target_pairs={{0,4},{2,6},{4,0},{6,2},{8,12},{10,14},{12,8},{14,10},{16,20},{18,... | collective-permute-start | bytes 2064392 | tf_op jit(solution)/shard_map/ppermute | solution.py:435
  39.5 19.6 %collective-permute-start.6 = (bf16[256,1024]{1,0:T(8,128)(2,1)}, bf16[256,1024]{1,0:T(8,128)(2,1)}, u32[]{:S(2)}, u32[]{:S(2)}) collective-permute-start(bf16[256,1024]{1,0:T(8,128)(2,1)} %product.2), channel_id=1, source_target_pairs={{0,1},{1,0},{2,3},{3,2},{4,5},{5,4},{6,7},{7,6},{8,9},{9,8},{10,11... | collective-permute-start | bytes 1572872 | tf_op jit(solution)/shard_map/ppermute | solution.py:400
  40.8 25.7 %collective-permute-start.10 = (bf16[1344,256]{1,0:T(8,128)(2,1)}, bf16[1344,256]{1,0:T(8,128)(2,1)S(1)}, u32[]{:S(2)}, u32[]{:S(2)}) collective-permute-start(bf16[1344,256]{1,0:T(8,128)(2,1)} %get-tuple-element.83), channel_id=1, source_target_pairs={{0,1},{1,0},{2,3},{3,2},{4,5},{5,4},{6,7},{7,6},{8,9},{9,8},{10,11... | collective-permute-start | bytes 2064392 | tf_op jit(solution)/shard_map/ppermute | solution.py:400
  42.2 24.2 %collective-permute-start.9 = (bf16[1344,256]{1,0:T(8,128)(2,1)}, bf16[1344,256]{1,0:T(8,128)(2,1)}, u32[]{:S(2)}, u32[]{:S(2)}) collective-permute-start(bf16[1344,256]{1,0:T(8,128)(2,1)} %get-tuple-element.82), channel_id=1, source_target_pairs={{0,4},{2,6},{4,0},{6,2},{8,12},{10,14},{12,8},{14,10},{16,20},{18,... | collective-permute-start | bytes 2064392 | tf_op jit(solution)/shard_map/ppermute | solution.py:435
  44.5 14.7 %copy-start.8 = (f32[256,1024]{1,0:T(8,128)S(1)}, f32[256,1024]{1,0:T(8,128)}, u32[]{:S(2)}) copy-start(f32[256,1024]{1,0:T(8,128)} %product.3) | copy-start | bytes 3145732
  58.8 16.7 %collective-permute-start.12 = (bf16[512,512]{1,0:T(8,128)(2,1)}, bf16[512,512]{1,0:T(8,128)(2,1)S(1)}, u32[]{:S(2)}, u32[]{:S(2)}) collective-permute-start(bf16[512,512]{1,0:T(8,128)(2,1)} %get-tuple-element.79), channel_id=1, source_target_pairs={{0,4},{2,6},{4,0},{6,2},{8,12},{10,14},{12,8},{14,10},{16,20},{18,... | collective-permute-start | bytes 1572872 | tf_op jit(solution)/shard_map/ppermute | solution.py:435
  60.4 15.2 %copy-start.22 = (bf16[512,512]{1,0:T(8,128)(2,1)S(1)}, bf16[512,512]{1,0:T(8,128)(2,1)}, u32[]{:S(2)}) copy-start(bf16[512,512]{1,0:T(8,128)(2,1)} %get-tuple-element.85) | copy-start | bytes 1572868
  60.4 4.0 %collective-permute-start.8 = (bf16[256,512]{1,0:T(8,128)(2,1)S(1)}, bf16[256,512]{1,0:T(8,128)(2,1)S(1)}, u32[]{:S(2)}, u32[]{:S(2)}) collective-permute-start(bf16[256,512]{1,0:T(8,128)(2,1)S(1)} %get-tuple-element.139), channel_id=1, source_target_pairs={{0,2},{2,0},{4,6},{6,4},{8,10},{10,8},{12,14},{14,12},{16,18},{18,... | collective-permute-start | bytes 786440 | tf_op jit(solution)/shard_map/ppermute | solution.py:395
  63.1 18.2 %collective-permute-start.17 = (bf16[1344,256]{1,0:T(8,128)(2,1)}, bf16[1344,256]{1,0:T(8,128)(2,1)S(1)}, u32[]{:S(2)}, u32[]{:S(2)}) collective-permute-start(bf16[1344,256]{1,0:T(8,128)(2,1)} %collective-permute-done.7), channel_id=1, source_target_pairs={{0,1},{1,0},{2,3},{3,2},{4,5},{5,4},{6,7},{7,6},{8,9},{9,8},{10,11... | collective-permute-start | bytes 2064392 | tf_op jit(solution)/shard_map/ppermute | solution.py:400
  64.4 20.1 %copy-start.3 = (bf16[512,512]{1,0:T(8,128)(2,1)}, bf16[512,512]{1,0:T(8,128)(2,1)S(1)}, u32[]{:S(2)}) copy-start(bf16[512,512]{1,0:T(8,128)(2,1)S(1)} %constant_dynamic-update-slice_fusion.6.refs_5_) | copy-start | bytes 1572868
  66.5 18.1 %collective-permute-start.11 = (bf16[512,512]{1,0:T(8,128)(2,1)S(1)}, bf16[512,512]{1,0:T(8,128)(2,1)S(1)}, u32[]{:S(2)}, u32[]{:S(2)}) collective-permute-start(bf16[512,512]{1,0:T(8,128)(2,1)S(1)} %constant_dynamic-update-slice_fusion.6.refs_5_), channel_id=1, source_target_pairs={{0,8},{2,10},{4,12},{6,14},{8,16},{10,18},{12,20},{14,22},{16,24},... | collective-permute-start | bytes 1572872 | tf_op jit(solution)/shard_map/ppermute | solution.py:391
  70.9 58.6 %collective-permute-start.18 = (bf16[1344,512]{1,0:T(8,128)(2,1)S(1)}, bf16[1344,512]{1,0:T(8,128)(2,1)}, u32[]{:S(2)}, u32[]{:S(2)}) collective-permute-start(bf16[1344,512]{1,0:T(8,128)(2,1)S(1)} %constant_dynamic-update-slice_fusion.refs_0_), channel_id=1, source_target_pairs={{0,2},{2,0},{4,6},{6,4},{8,10},{10,8},{12,14},{14,12},{16,18},{18,... | collective-permute-start | bytes 4128776 | tf_op jit(solution)/shard_map/ppermute | solution.py:395
  75.7 15.6 %copy-start.20 = (bf16[512,512]{1,0:T(8,128)(2,1)S(1)}, bf16[512,512]{1,0:T(8,128)(2,1)}, u32[]{:S(2)}) copy-start(bf16[512,512]{1,0:T(8,128)(2,1)} %get-tuple-element.89) | copy-start | bytes 1572868
  75.7 15.5 %collective-permute-start.14 = (bf16[512,512]{1,0:T(8,128)(2,1)S(1)}, bf16[512,512]{1,0:T(8,128)(2,1)S(1)}, u32[]{:S(2)}, u32[]{:S(2)}) collective-permute-start(bf16[512,512]{1,0:T(8,128)(2,1)S(1)} %fusion.1), channel_id=1, source_target_pairs={{8,0},{10,2},{12,4},{14,6},{16,8},{18,10},{20,12},{22,14},{24,16},... | collective-permute-start | bytes 1572872 | tf_op jit(solution)/shard_map/ppermute | solution.py:391
  82.2 47.3 %collective-permute-start.19 = (bf16[1344,512]{1,0:T(8,128)(2,1)}, bf16[1344,512]{1,0:T(8,128)(2,1)}, u32[]{:S(2)}, u32[]{:S(2)}) collective-permute-start(bf16[1344,512]{1,0:T(8,128)(2,1)} %constant_dynamic-update-slice_fusion.2.refs_1_), channel_id=1, source_target_pairs={{0,2},{2,0},{4,6},{6,4},{8,10},{10,8},{12,14},{14,12},{16,18},{18,... | collective-permute-start | bytes 4128776 | tf_op jit(solution)/shard_map/ppermute | solution.py:395
  84.5 14.9 %copy-start.6 = (bf16[512,512]{1,0:T(8,128)(2,1)}, bf16[512,512]{1,0:T(8,128)(2,1)S(1)}, u32[]{:S(2)}) copy-start(bf16[512,512]{1,0:T(8,128)(2,1)S(1)} %collective-permute-done.11.refs_3_) | copy-start | bytes 1572868
  84.6 13.6 %collective-permute-start.13 = (bf16[512,512]{1,0:T(8,128)(2,1)S(1)}, bf16[512,512]{1,0:T(8,128)(2,1)S(1)}, u32[]{:S(2)}, u32[]{:S(2)}) collective-permute-start(bf16[512,512]{1,0:T(8,128)(2,1)S(1)} %broadcast_select_fusion), channel_id=1, source_target_pairs={{0,4},{2,6},{4,0},{6,2},{8,12},{10,14},{12,8},{14,10},{16,20},{18,... | collective-permute-start | bytes 1572872 | tf_op jit(solution)/shard_map/ppermute | solution.py:435
  91.5 17.5 %copy-start.7 = (bf16[512,512]{1,0:T(8,128)(2,1)}, bf16[512,512]{1,0:T(8,128)(2,1)S(1)}, u32[]{:S(2)}) copy-start(bf16[512,512]{1,0:T(8,128)(2,1)S(1)} %fusion.3.refs_4_) | copy-start | bytes 1572868
  91.5 17.5 %collective-permute-start.15 = (bf16[512,512]{1,0:T(8,128)(2,1)S(1)}, bf16[512,512]{1,0:T(8,128)(2,1)S(1)}, u32[]{:S(2)}, u32[]{:S(2)}) collective-permute-start(bf16[512,512]{1,0:T(8,128)(2,1)S(1)} %fusion.3.refs_4_), channel_id=1, source_target_pairs={{0,1},{1,0},{2,3},{3,2},{4,5},{5,4},{6,7},{7,6},{8,9},{9,8},{10,11... | collective-permute-start | bytes 1572872 | tf_op jit(solution)/shard_map/ppermute | solution.py:400
  92.8 23.8 %collective-permute-start.21 = (bf16[512,512]{1,0:T(8,128)(2,1)S(1)}, bf16[512,512]{1,0:T(8,128)(2,1)}, u32[]{:S(2)}, u32[]{:S(2)}) collective-permute-start(bf16[512,512]{1,0:T(8,128)(2,1)S(1)} %fusion.3.refs_4_), channel_id=1, source_target_pairs={{0,5},{1,4},{2,7},{3,6},{4,1},{5,0},{6,3},{7,2},{8,13},{9,12},{10,... | collective-permute-start | bytes 1572872 | tf_op jit(solution)/shard_map/ppermute | solution.py:410
  98.2 28.4 %collective-permute-start.20 = (bf16[512,512]{1,0:T(8,128)(2,1)S(1)}, bf16[512,512]{1,0:T(8,128)(2,1)}, u32[]{:S(2)}, u32[]{:S(2)}) collective-permute-start(bf16[512,512]{1,0:T(8,128)(2,1)S(1)} %fusion.3.refs_4_), channel_id=1, source_target_pairs={{0,4},{1,5},{2,6},{3,7},{4,0},{5,1},{6,2},{7,3},{8,12},{9,13},{10,... | collective-permute-start | bytes 1572872 | tf_op jit(solution)/shard_map/ppermute | solution.py:410
  109.0 20.5 %copy-start.13 = (bf16[512,512]{1,0:T(8,128)(2,1)}, bf16[512,512]{1,0:T(8,128)(2,1)S(1)}, u32[]{:S(2)}) copy-start(bf16[512,512]{1,0:T(8,128)(2,1)S(1)} %collective-permute-done.15.refs_6_) | copy-start | bytes 1572868
  109.1 28.6 %collective-permute-start.16 = (bf16[512,512]{1,0:T(8,128)(2,1)S(1)}, bf16[512,512]{1,0:T(8,128)(2,1)S(1)}, u32[]{:S(2)}, u32[]{:S(2)}) collective-permute-start(bf16[512,512]{1,0:T(8,128)(2,1)S(1)} %pad_maximum_fusion.6), channel_id=1, source_target_pairs={{0,2},{2,0},{4,6},{6,4},{8,10},{10,8},{12,14},{14,12},{16,18},{18,... | collective-permute-start | bytes 1572872 | tf_op jit(solution)/shard_map/ppermute | solution.py:395
  116.5 21.1 %collective-permute-start.22 = (bf16[512,256]{1,0:T(8,128)(2,1)}, bf16[512,256]{1,0:T(8,128)(2,1)}, u32[]{:S(2)}, u32[]{:S(2)}) collective-permute-start(bf16[512,256]{1,0:T(8,128)(2,1)} %get-tuple-element.91), channel_id=1, source_target_pairs={{4,0},{6,2},{8,4},{10,6},{12,8},{14,10},{16,12},{18,14},{20,16},{2... | collective-permute-start | bytes 786440 | tf_op jit(solution)/shard_map/ppermute | solution.py:391
  126.6 11.0 %collective-permute-start.23 = (bf16[512,256]{1,0:T(8,128)(2,1)}, bf16[512,256]{1,0:T(8,128)(2,1)}, u32[]{:S(2)}, u32[]{:S(2)}) collective-permute-start(bf16[512,256]{1,0:T(8,128)(2,1)} %get-tuple-element.104), channel_id=1, source_target_pairs={{8,0},{10,2},{12,4},{14,6},{16,8},{18,10},{20,12},{22,14},{24,16},... | collective-permute-start | bytes 786440 | tf_op jit(solution)/shard_map/ppermute | solution.py:391
  145.8 41.6 %collective-permute-start.26 = (bf16[256,2688]{1,0:T(8,128)(2,1)}, bf16[256,2688]{1,0:T(8,128)(2,1)S(1)}, u32[]{:S(2)}, u32[]{:S(2)}) collective-permute-start(bf16[256,2688]{1,0:T(8,128)(2,1)} %get-tuple-element.107), channel_id=1, source_target_pairs={{0,1},{1,0},{2,3},{3,2},{4,5},{5,4},{6,7},{7,6},{8,9},{9,8},{10,11... | collective-permute-start | bytes 4128776 | tf_op jit(solution)/shard_map/ppermute | solution.py:400
  157.6 19.1 %collective-permute-start.24 = (bf16[2,256,1024]{2,1,0:T(8,128)(2,1)S(1)}, bf16[2,256,1024]{2,1,0:T(8,128)(2,1)S(1)}, u32[]{:S(2)}, u32[]{:S(2)}) collective-permute-start(bf16[2,256,1024]{2,1,0:T(8,128)(2,1)S(1)} %pad_maximum_fusion.1), channel_id=1, source_target_pairs={{0,2},{2,0},{4,6},{6,4},{8,10},{10,8},{12,14},{14,12},{16,18},{18,... | collective-permute-start | bytes 3145736 | tf_op jit(solution)/shard_map/ppermute | solution.py:395
  160.1 16.5 %copy-start.30 = (bf16[336,512]{1,0:T(8,128)(2,1)S(1)}, bf16[336,512]{1,0:T(8,128)(2,1)}, u32[]{:S(2)}) copy-start(bf16[336,512]{1,0:T(8,128)(2,1)} %get-tuple-element.127) | copy-start | bytes 1032196
  160.1 16.5 %copy-start.24 = (bf16[256,512]{1,0:T(8,128)(2,1)S(1)}, bf16[256,512]{1,0:T(8,128)(2,1)}, u32[]{:S(2)}) copy-start(bf16[256,512]{1,0:T(8,128)(2,1)} %get-tuple-element.112) | copy-start | bytes 786436
  160.1 16.5 %copy-start.26 = (bf16[256,512]{1,0:T(8,128)(2,1)S(1)}, bf16[256,512]{1,0:T(8,128)(2,1)}, u32[]{:S(2)}) copy-start(bf16[256,512]{1,0:T(8,128)(2,1)} %get-tuple-element.113) | copy-start | bytes 786436
  160.1 45.2 %collective-permute-start.29 = (bf16[336,512]{1,0:T(8,128)(2,1)}, bf16[336,512]{1,0:T(8,128)(2,1)S(1)}, u32[]{:S(2)}, u32[]{:S(2)}) collective-permute-start(bf16[336,512]{1,0:T(8,128)(2,1)} %get-tuple-element.123), channel_id=1, source_target_pairs={{0,8},{2,10},{4,12},{6,14},{8,16},{10,18},{12,20},{14,22},{16,24},... | collective-permute-start | bytes 1032200 | tf_op jit(solution)/shard_map/ppermute | solution.py:589
  161.4 43.9 %collective-permute-start.30 = (bf16[336,512]{1,0:T(8,128)(2,1)}, bf16[336,512]{1,0:T(8,128)(2,1)S(1)}, u32[]{:S(2)}, u32[]{:S(2)}) collective-permute-start(bf16[336,512]{1,0:T(8,128)(2,1)} %get-tuple-element.125), channel_id=1, source_target_pairs={{0,16},{2,18},{4,20},{6,22},{8,24},{10,26},{12,28},{14,30},{16,0},... | collective-permute-start | bytes 1032200 | tf_op jit(solution)/shard_map/ppermute | solution.py:589
  163.2 13.4 %collective-permute-start.25 = (bf16[512,256]{1,0:T(8,128)(2,1)}, bf16[512,256]{1,0:T(8,128)(2,1)S(1)}, u32[]{:S(2)}, u32[]{:S(2)}) collective-permute-start(bf16[512,256]{1,0:T(8,128)(2,1)} %get-tuple-element.118), channel_id=1, source_target_pairs={{4,0},{6,2},{8,4},{10,6},{12,8},{14,10},{16,12},{18,14},{20,16},{2... | collective-permute-start | bytes 786440 | tf_op jit(solution)/shard_map/ppermute | solution.py:391
  171.2 34.1 %copy-start.17 = (f32[336,512]{1,0:T(8,128)S(1)}, f32[336,512]{1,0:T(8,128)}, u32[]{:S(2)}) copy-start(f32[336,512]{1,0:T(8,128)} %get-tuple-element.105) | copy-start | bytes 2064388
  176.6 28.7 %collective-permute-start.31 = (bf16[336,512]{1,0:T(8,128)(2,1)S(1)}, bf16[336,512]{1,0:T(8,128)(2,1)S(1)}, u32[]{:S(2)}, u32[]{:S(2)}) collective-permute-start(bf16[336,512]{1,0:T(8,128)(2,1)S(1)} %copy-done.30), channel_id=1, source_target_pairs={{0,24},{2,26},{4,28},{6,30},{8,0},{10,2},{12,4},{14,6},{16,8},{18,... | collective-permute-start | bytes 1032200 | tf_op jit(solution)/shard_map/ppermute | solution.py:589
  176.8 28.5 %collective-permute-start.27 = (bf16[512,256]{1,0:T(8,128)(2,1)S(1)}, bf16[512,256]{1,0:T(8,128)(2,1)S(1)}, u32[]{:S(2)}, u32[]{:S(2)}) collective-permute-start(bf16[512,256]{1,0:T(8,128)(2,1)S(1)} %copy-done.31), channel_id=1, source_target_pairs={{8,0},{10,2},{12,4},{14,6},{16,8},{18,10},{20,12},{22,14},{24,16},... | collective-permute-start | bytes 786440 | tf_op jit(solution)/shard_map/ppermute | solution.py:391
  187.4 19.3 %copy-start.14 = (bf16[1,256,2048]{2,1,0:T(8,128)(2,1)}, bf16[1,256,2048]{2,1,0:T(8,128)(2,1)S(1)}, u32[]{:S(2)}) copy-start(bf16[1,256,2048]{2,1,0:T(8,128)(2,1)S(1)} %get-tuple-element.130) | copy-start | bytes 3145732
  187.4 19.3 %copy-start.15 = (bf16[1,256,2048]{2,1,0:T(8,128)(2,1)}, bf16[1,256,2048]{2,1,0:T(8,128)(2,1)S(1)}, u32[]{:S(2)}) copy-start(bf16[1,256,2048]{2,1,0:T(8,128)(2,1)S(1)} %get-tuple-element.129) | copy-start | bytes 3145732
  187.4 19.2 %copy-start.25 = (bf16[512,256]{1,0:T(8,128)(2,1)S(1)}, bf16[512,256]{1,0:T(8,128)(2,1)}, u32[]{:S(2)}) copy-start(bf16[512,256]{1,0:T(8,128)(2,1)} %get-tuple-element.117) | copy-start | bytes 786436
  205.6 2.9 %collective-permute-start.32 = (f32[168,512]{1,0:T(8,128)S(1)}, f32[168,512]{1,0:T(8,128)S(1)}, u32[]{:S(2)}, u32[]{:S(2)}) collective-permute-start(f32[168,512]{1,0:T(8,128)S(1)} %get-tuple-element.131), channel_id=1, source_target_pairs={{0,2},{2,0},{4,6},{6,4},{8,10},{10,8},{12,14},{14,12},{16,18},{18,... | collective-permute-start | bytes 1032200 | tf_op jit(solution)/shard_map/ppermute | solution.py:395
  206.8 1.6 collective-permute-start.28
  (17 other events, 66.4 us)

commit v11 on v6

--- a/solution.py
+++ b/solution.py
@@ -520,7 +520,7 @@
         partial = [run_product(zero_arg, parts, w_value, BF16) for parts in sent]
     else:
         partial = [dot(parts[0], w_value).astype(BF16) for parts in sent]
-    low = after(low, *partial, *over_y.values())
+    low = after(low, *partial)
     e, inv, do_t, dv_far, dv_near, dv_mine = run_probs(
         core_arg, low, queries[0], q_other, d_out[0], keys, chip_rows, half_kv
     )
@@ -528,8 +528,7 @@
 
     value_back = [rotated(x, -s - 1) for s, x in enumerate(partial)]
     over_fsdp = {s: rotated(after(by_place[0, s], sent), s) for s in range(1, n_fsdp)}
-    value_back = [after(x, dv_near) for x in value_back]
-    value_back[0] = after(value_back[0], over_fsdp)
+    value_back = [after(x, dv_near, over_y) for x in value_back]
     value_sum = value_own
     for x in value_back:
         value_sum = value_sum + x.astype(F32)
@@ -537,7 +536,7 @@
     v_own = placed(core, cols(own_values, core, half_kv), swapped(cols(own_values, 1 - core, half_kv)), 0)
 
     over_y[0] = flipped(after(by_place[1, 0], k_near))
-    v_own, over_y[0] = lax.optimization_barrier((v_own, over_y[0]))
+    v_own, over_y[0], over_fsdp = lax.optimization_barrier((v_own, over_y[0], over_fsdp))
     v_far = shifted(v_own, 4)
     own_pairs = [jnp.concatenate([by_place[0, 0], over_y[0]], 1)]
     other_pairs = [swapped(after(own_pairs[0], v_own))]

time: 187 us -> 178 us (0.952)
  waiting for transfers between devices: 46.7 us -> 34.1 us
  other arithmetic: 6.6 us -> 9.07 us
    ppermute x3, waiting for transfers between devices: 20.5 us -> 12.7 us  [shards(): lax.ppermute(by_z[d], 'ctx', [(i, (i + 4 * d) % n_ctx) for i in range(n_c...]
    ppermute x9, starting transfers between devices: 21.8 us -> 27.2 us  [swapped(): lax.ppermute(x, 'ctx', [(i, i ^ 1) for i in range(lax.axis_size('ctx'))])]
    ppermute x7, waiting for transfers between devices: 10.9 us -> 5.68 us  [rotated(): lax.ppermute(x, 'fsdp', [(i, (i + by) % length) for i in range(length)])]
    ppermute x3, starting transfers between devices: 6.81 us -> 2.98 us  [shards(): lax.ppermute(by_z[d], 'ctx', [(i, (i + 4 * d) % n_ctx) for i in range(n_c...]
    ppermute x2, waiting for transfers between devices: 0.01 us -> 3.71 us  [moved(): return lax.ppermute(x, ('ctx', 'fsdp'), pairs)]
    ppermute x4, waiting for transfers between devices: 6.11 us -> 3.42 us  [flipped(): lax.ppermute(x, 'ctx', [(i, i ^ 2) for i in range(lax.axis_size('ctx'))])]
    unnamed x64 -> x58, local copies, waits for them, and re-layouts: 4.99 us -> 4.98 us
  transfers between devices with their start and end apart: 31 -> 31, of which waited for: 10 -> 10; matrix products, arithmetic and copies ran while one was open for 7% -> 9% of each run, Pallas kernels for 32% -> 34%
where the time goes in v11:
time: 178 us; the launch traced here: 176 us
  starting transfers between devices  60.1 us (34%)
  Pallas kernels  59.2 us (33%)
  waiting for transfers between devices  34.1 us (19%)
  local copies, waits for them, and re-layouts  12.3 us (7%)
  other arithmetic  9.07 us (5%)
    ppermute x9, starting transfers between devices, swapped(): lax.ppermute(x, 'ctx', [(i, i ^ 1) for i in range(lax.axis_size('ctx'))])  27.2 us
    ppermute x6, starting transfers between devices, shifted(): lax.ppermute(x, 'ctx', [(i, i + by) for i in range(length) if 0 <= i + by...  17.2 us
    pallas_call x1, Pallas kernels, run_grads(): pl.pallas_call(functools.partial(grads_kernel, blk, n_arr - 1), grid_spec...  16 us
    pallas_call x1, Pallas kernels, run_probs(): pl.pallas_call(functools.partial(probs_kernel, blk, n_arr - 1), grid_spec...  14.3 us
    ppermute x3, waiting for transfers between devices, shards(): lax.ppermute(by_z[d], 'ctx', [(i, (i + 4 * d) % n_ctx) for i in range(n_c...  12.7 us
    pallas_call x2, Pallas kernels, run_product(): pl.pallas_call(product_kernel, grid_spec=pltpu.PrefetchScalarGridSpec(num...  9.55 us
    pallas_call x1, Pallas kernels, run_weight(): pl.pallas_call(functools.partial(weight_kernel, n_z, n), grid_spec=pltpu....  8.12 us
    ppermute x6, waiting for transfers between devices, shifted(): lax.ppermute(x, 'ctx', [(i, i + by) for i in range(length) if 0 <= i + by...  7.5 us
  transfers between devices with their start and end apart: 31, of which 10 were waited for; matrix products, arithmetic and copies ran while one was open for 9% of the time, Pallas kernels for 34%

profile of v11, /device:TPU:9, one launch (start us, length us, event | category | flops | bytes accessed | tf_op | source)
XLA Modules:
  0.0 176.1 jit_solution(16225191024736523207)
XLA Ops:
  0.7 1.2 dynamic-slice_bitcast_fusion.1
  1.9 1.3 collective-permute-start.3
  4.0 1.1 dynamic-slice_bitcast_fusion.5
  5.8 1.0 collective-permute-start
  6.8 2.0 %dynamic-slice_bitcast_fusion = bf16[256,1408]{1,0:T(8,128)(2,1)} fusion(bf16[1,256,5376]{2,1,0:T(8,128)(2,1)} %param.6, s32[]{:T(128)S(6)} %select_n.97), kind=kLoop, calls=%fused_computation.12 | loop fusion | bytes 1441796 | tf_op jit(solution)/shard_map/dynamic_slice | solution.py:469
  9.3 1.0 slice_dynamic-update-slice_fusion.2
  11.0 3.1 %collective-permute-start.2 = (bf16[528,512]{1,0:T(8,128)(2,1)S(1)}, bf16[528,512]{1,0:T(8,128)(2,1)S(1)}, u32[]{:S(2)}, u32[]{:S(2)}) collective-permute-start(bf16[528,512]{1,0:T(8,128)(2,1)S(1)} %pad_maximum_fusion.2.refs_2_), channel_id=1, source_target_pairs={{0,4},{2,6},{4,8},{6,10},{8,12},{10,14},{12,16},{14,18},{16,20},{1... | collective-permute-start | bytes 1622024 | tf_op jit(solution)/shard_map/ppermute | solution.py:386
  14.2 3.2 %collective-permute-start.1 = (bf16[528,512]{1,0:T(8,128)(2,1)S(1)}, bf16[528,512]{1,0:T(8,128)(2,1)S(1)}, u32[]{:S(2)}, u32[]{:S(2)}) collective-permute-start(bf16[528,512]{1,0:T(8,128)(2,1)S(1)} %pad_maximum_fusion.2.refs_2_), channel_id=1, source_target_pairs={{0,8},{2,10},{4,12},{6,14},{8,16},{10,18},{12,20},{14,22},{16,24},... | collective-permute-start | bytes 1622024 | tf_op jit(solution)/shard_map/ppermute | solution.py:386
  17.4 1.1 pad_maximum_fusion
  19.9 4.2 %pieces.1 = (bf16[1344,256]{1,0:T(8,128)(2,1)}, bf16[1344,256]{1,0:T(8,128)(2,1)}, bf16[1344,256]{1,0:T(8,128)(2,1)}, bf16[1344,256]{1,0:T(8,128)(2,1)}) custom-call(s32[2]{0:T(128)} %pad_add_fusion.at_ref, bf16[256,5376]{1,0:T(8,128)(2,1)} %bitcast.29), custom_call_target="tpu_custom_call" | custom-call | flops 1048576 | bytes 4096 | tf_op jit(solution)/shard_map/pieces/pallas_call | solution.py:260
  24.1 4.9 %product.3 = f32[256,1024]{1,0:T(8,128)} custom-call(s32[1]{0:T(128)} %bitcast.10.at_ref, bf16[256,5376]{1,0:T(8,128)(2,1)} %bitcast.30, bf16[2688,1024]{1,0:T(8,128)(2,1)} %w_ref.1), custom_call_target="tpu_custom_call" | custom-call | flops 1048576 | bytes 4096 | tf_op jit(solution)/shard_map/product/pallas_call | solution.py:290
  29.0 1.3 collective-permute-start.7
  30.3 2.8 %collective-permute-done.4.refs_1_ = bf16[256,1408]{1,0:T(8,128)(2,1)} collective-permute-done((bf16[256,1408]{1,0:T(8,128)(2,1)}, bf16[256,1408]{1,0:T(8,128)(2,1)}, u32[]{:S(2)}, u32[]{:S(2)}) %collective-permute-start.4) | collective-permute-done | bytes 720928 | tf_op jit(solution)/shard_map/ppermute | solution.py:395
  33.1 4.7 %product.2 = bf16[256,1024]{1,0:T(8,128)(2,1)} custom-call(s32[1]{0:T(128)} %constant.86.clone.1.at_ref, bf16[256,1280]{1,0:T(8,128)(2,1)} %collective-permute-done.3.refs_0_, bf16[256,1408]{1,0:T(8,128)(2,1)} %collective-permute-done.4.refs_1_, bf16[2688,1024]{1,0:T(8,128)(2,1)} %w_ref.1), custom_call_target="tpu_custom_call" | custom-call | flops 1048576 | bytes 4096 | tf_op jit(solution)/shard_map/product/pallas_call | solution.py:290
  37.8 1.2 collective-permute-start.6
  40.6 1.2 collective-permute-start.9
  41.8 1.0 copy-done
  42.8 14.3 %probs.1 = (bf16[4,2,1280,512]{3,2,1,0:T(8,128)(2,1)}, f32[4,2,1,512]{3,2,1,0:T(1,128)}, bf16[4,2,128,512]{3,2,1,0:T(8,128)(2,1)}, bf16[512,512]{1,0:T(8,128)(2,...) custom-call(s32[1]{0:T(128)} %bitcast.core_ref, s32[1,512]{1,0:T(1,128)} %add_maximum_fusion.low_ref, ...), custom_call_target="tpu_custom_call" | custom-call | flops 1048576 | bytes 4096 | tf_op jit(solution)/shard_map/probs/pallas_call | solution.py:158
  57.6 2.7 %collective-permute-start.8 = (bf16[256,512]{1,0:T(8,128)(2,1)S(1)}, bf16[256,512]{1,0:T(8,128)(2,1)S(1)}, u32[]{:S(2)}, u32[]{:S(2)}) collective-permute-start(bf16[256,512]{1,0:T(8,128)(2,1)S(1)} %get-tuple-element.123), channel_id=1, source_target_pairs={{0,2},{2,0},{4,6},{6,4},{8,10},{10,8},{12,14},{14,12},{16,18},{18,... | collective-permute-start | bytes 786440 | tf_op jit(solution)/shard_map/ppermute | solution.py:390
  60.4 1.3 collective-permute-start.20
  61.8 2.8 %collective-permute-done.10 = bf16[1344,256]{1,0:T(8,128)(2,1)S(1)} collective-permute-done((bf16[1344,256]{1,0:T(8,128)(2,1)}, bf16[1344,256]{1,0:T(8,128)(2,1)S(1)}, u32[]{:S(2)}, u32[]{:S(2)}) %collective-permute-start.10) | collective-permute-done | bytes 688160 | tf_op jit(solution)/shard_map/ppermute | solution.py:395
  64.6 3.2 %collective-permute-start.11 = (bf16[512,512]{1,0:T(8,128)(2,1)S(1)}, bf16[512,512]{1,0:T(8,128)(2,1)S(1)}, u32[]{:S(2)}, u32[]{:S(2)}) collective-permute-start(bf16[512,512]{1,0:T(8,128)(2,1)S(1)} %constant_dynamic-update-slice_fusion.6.refs_5_), channel_id=1, source_target_pairs={{0,8},{2,10},{4,12},{6,14},{8,16},{10,18},{12,20},{14,22},{16,24},... | collective-permute-start | bytes 1572872 | tf_op jit(solution)/shard_map/ppermute | solution.py:386
  67.8 3.4 %collective-permute-done.12 = bf16[512,512]{1,0:T(8,128)(2,1)S(1)} collective-permute-done((bf16[512,512]{1,0:T(8,128)(2,1)}, bf16[512,512]{1,0:T(8,128)(2,1)S(1)}, u32[]{:S(2)}, u32[]{:S(2)}) %collective-permute-start.12) | collective-permute-done | bytes 524320 | tf_op jit(solution)/shard_map/ppermute | solution.py:430
  71.4 2.6 %collective-permute-start.14 = (bf16[512,512]{1,0:T(8,128)(2,1)S(1)}, bf16[512,512]{1,0:T(8,128)(2,1)S(1)}, u32[]{:S(2)}, u32[]{:S(2)}) collective-permute-start(bf16[512,512]{1,0:T(8,128)(2,1)S(1)} %fusion.1), channel_id=1, source_target_pairs={{8,0},{10,2},{12,4},{14,6},{16,8},{18,10},{20,12},{22,14},{24,16},... | collective-permute-start | bytes 1572872 | tf_op jit(solution)/shard_map/ppermute | solution.py:386
  74.1 2.0 %collective-permute-start.21 = (bf16[1344,512]{1,0:T(8,128)(2,1)S(1)}, bf16[1344,512]{1,0:T(8,128)(2,1)}, u32[]{:S(2)}, u32[]{:S(2)}) collective-permute-start(bf16[1344,512]{1,0:T(8,128)(2,1)S(1)} %constant_dynamic-update-slice_fusion.refs_0_), channel_id=1, source_target_pairs={{0,2},{2,0},{4,6},{6,4},{8,10},{10,8},{12,14},{14,12},{16,18},{18,... | collective-permute-start | bytes 4128776 | tf_op jit(solution)/shard_map/ppermute | solution.py:390
  76.2 1.3 collective-permute-start.13
  77.6 7.5 %collective-permute-done.14 = bf16[512,512]{1,0:T(8,128)(2,1)S(1)} collective-permute-done((bf16[512,512]{1,0:T(8,128)(2,1)S(1)}, bf16[512,512]{1,0:T(8,128)(2,1)S(1)}, u32[]{:S(2)}, u32[]{:S(2)}) %collective-permute-start.14) | collective-permute-done | bytes 524320 | tf_op jit(solution)/shard_map/ppermute | solution.py:386
  85.3 1.1 collective-permute-start.15
  86.5 3.1 %collective-permute-start.22 = (bf16[1344,512]{1,0:T(8,128)(2,1)S(1)}, bf16[1344,512]{1,0:T(8,128)(2,1)}, u32[]{:S(2)}, u32[]{:S(2)}) collective-permute-start(bf16[1344,512]{1,0:T(8,128)(2,1)S(1)} %constant_dynamic-update-slice_fusion.2.refs_1_), channel_id=1, source_target_pairs={{0,2},{2,0},{4,6},{6,4},{8,10},{10,8},{12,14},{14,12},{16,18},{18,... | collective-permute-start | bytes 4128776 | tf_op jit(solution)/shard_map/ppermute | solution.py:390
  89.6 2.2 %collective-permute-start.18 = (bf16[512,512]{1,0:T(8,128)(2,1)S(1)}, bf16[512,512]{1,0:T(8,128)(2,1)}, u32[]{:S(2)}, u32[]{:S(2)}) collective-permute-start(bf16[512,512]{1,0:T(8,128)(2,1)S(1)} %fusion.3.refs_4_), channel_id=1, source_target_pairs={{0,5},{1,4},{2,7},{3,6},{4,1},{5,0},{6,3},{7,2},{8,13},{9,12},{10,... | collective-permute-start | bytes 1572872 | tf_op jit(solution)/shard_map/ppermute | solution.py:405
  92.6 16.0 %grads.1 = (bf16[256,2048]{1,0:T(8,128)(2,1)}, bf16[256,2048]{1,0:T(8,128)(2,1)}, bf16[2,256,1024]{2,1,0:T(8,128)(2,1)}, bf16[512,512]{1,0:T(8,128)(2,1)}, bf16[...) custom-call(s32[1]{0:T(128)} %bitcast.core_ref, bf16[4,2,1280,512]{3,2,1,0:T(8,128)(2,1)} %get-tuple-element.62.e_ref, ...), custom_call_target="tpu_custom_call" | custom-call | flops 1048576 | bytes 4096 | tf_op jit(solution)/shard_map/grads/pallas_call | solution.py:201
  109.9 1.0 collective-permute-done.18.refs_7_
  110.9 2.7 %collective-permute-start.24 = (bf16[512,512]{1,0:T(8,128)(2,1)}, bf16[512,512]{1,0:T(8,128)(2,1)}, u32[]{:S(2)}, u32[]{:S(2)}) collective-permute-start(bf16[512,512]{1,0:T(8,128)(2,1)} %get-tuple-element.105), channel_id=1, source_target_pairs={{8,0},{10,2},{12,4},{14,6},{16,8},{18,10},{20,12},{22,14},{24,16},... | collective-permute-start | bytes 1572872 | tf_op jit(solution)/shard_map/ppermute | solution.py:386
  113.7 2.7 %collective-permute-done.17.refs_5_ = bf16[512,512]{1,0:T(8,128)(2,1)} collective-permute-done((bf16[512,512]{1,0:T(8,128)(2,1)S(1)}, bf16[512,512]{1,0:T(8,128)(2,1)}, u32[]{:S(2)}, u32[]{:S(2)}) %collective-permute-start.17) | collective-permute-done | bytes 524320 | tf_op jit(solution)/shard_map/ppermute | solution.py:405
  116.3 2.3 %collective-permute-start.23 = (bf16[512,512]{1,0:T(8,128)(2,1)}, bf16[512,512]{1,0:T(8,128)(2,1)}, u32[]{:S(2)}, u32[]{:S(2)}) collective-permute-start(bf16[512,512]{1,0:T(8,128)(2,1)} %get-tuple-element.85), channel_id=1, source_target_pairs={{4,0},{6,2},{8,4},{10,6},{12,8},{14,10},{16,12},{18,14},{20,16},{2... | collective-permute-start | bytes 1572872 | tf_op jit(solution)/shard_map/ppermute | solution.py:386
  119.5 1.1 constant_dynamic-update-slice_fusion.5.dv_ref
  120.6 1.0 copy-done.6
  121.6 7.0 %tokens.1 = (bf16[256,5376]{1,0:T(8,128)(2,1)}, bf16[256,2688]{1,0:T(8,128)(2,1)}) custom-call(s32[1]{0:T(128)} %bitcast.10.at_ref, bf16[512,1024]{1,0:T(8,128)(2,1)} %copy-done.6, bf16[2688,1024]{1,0:T(8,128)(2,1)} %w_ref.1), custom_call_target="tpu_custom_call" | custom-call | flops 1048576 | bytes 4096 | tf_op jit(solution)/shard_map/tokens/pallas_call | solution.py:364
  129.5 1.4 collective-permute-start.19
  131.0 8.1 %weight.1 = (f32[336,512]{1,0:T(8,128)}, bf16[336,512]{1,0:T(8,128)(2,1)}, bf16[336,512]{1,0:T(8,128)(2,1)}, bf16[336,512]{1,0:T(8,128)(2,1)}) custom-call(s32[2]{0:T(128)} %pad_add_fusion.1.at_ref, bf16[1344,512]{1,0:T(8,128)(2,1)} %copy-done.7, bf16[1344,512]{1,0:T(8,128)(2,1)} %copy-done.8, bf16[1344,512]{1,0:T(8,128)(2,1)} %collective-permute-done.21.refs_2_, ...), custom_call_target="tpu_custom_call" | custom-call | flops 1048576 | bytes 4096 | tf_op jit(solution)/shard_map/weight/pallas_call | solution.py:336
  139.1 1.3 collective-permute-start.27
  140.7 1.4 collective-permute-start.29
  142.1 1.4 add_convert_fusion
  143.6 5.3 %collective-permute-done.27 = bf16[336,512]{1,0:T(8,128)(2,1)S(1)} collective-permute-done((bf16[336,512]{1,0:T(8,128)(2,1)}, bf16[336,512]{1,0:T(8,128)(2,1)S(1)}, u32[]{:S(2)}, u32[]{:S(2)}) %collective-permute-start.27) | collective-permute-done | bytes 344096 | tf_op jit(solution)/shard_map/ppermute | solution.py:600
  148.9 15.3 %collective-permute-start.25 = (bf16[256,512]{1,0:T(8,128)(2,1)S(1)}, bf16[256,512]{1,0:T(8,128)(2,1)S(1)}, u32[]{:S(2)}, u32[]{:S(2)}) collective-permute-start(bf16[256,512]{1,0:T(8,128)(2,1)S(1)} %get-tuple-element.117), channel_id=1, source_target_pairs={{0,2},{2,0},{4,6},{6,4},{8,10},{10,8},{12,14},{14,12},{16,18},{18,... | collective-permute-start | bytes 786440 | tf_op jit(solution)/shard_map/ppermute | solution.py:390
  164.2 6.0 %collective-permute-done.28 = bf16[336,512]{1,0:T(8,128)(2,1)S(1)} collective-permute-done((bf16[336,512]{1,0:T(8,128)(2,1)}, bf16[336,512]{1,0:T(8,128)(2,1)S(1)}, u32[]{:S(2)}, u32[]{:S(2)}) %collective-permute-start.28) | collective-permute-done | bytes 344096 | tf_op jit(solution)/shard_map/ppermute | solution.py:600
  170.1 1.4 collective-permute-done.29
  172.5 1.2 collective-permute-done.30
  (126 shorter events, 14.4 us)
Async XLA Ops:
  0.7 8.4 %copy-start.1 = (bf16[1,256,2048]{2,1,0:T(8,128)(2,1)S(1)}, bf16[1,256,2048]{2,1,0:T(8,128)(2,1)}, u32[]{:S(2)}) copy-start(bf16[1,256,2048]{2,1,0:T(8,128)(2,1)} %param.7) | copy-start | bytes 3145732
  1.9 7.2 %copy-start.9 = (bf16[1,256,2048]{2,1,0:T(8,128)(2,1)S(1)}, bf16[1,256,2048]{2,1,0:T(8,128)(2,1)}, u32[]{:S(2)}) copy-start(bf16[1,256,2048]{2,1,0:T(8,128)(2,1)} %param.10) | copy-start | bytes 3145732
  1.9 27.1 %collective-permute-start.3 = (bf16[256,1280]{1,0:T(8,128)(2,1)S(1)}, bf16[256,1280]{1,0:T(8,128)(2,1)}, u32[]{:S(2)}, u32[]{:S(2)}) collective-permute-start(bf16[256,1280]{1,0:T(8,128)(2,1)S(1)} %dynamic-slice_bitcast_fusion.1), channel_id=1, source_target_pairs={{0,1},{1,0},{2,3},{3,2},{4,5},{5,4},{6,7},{7,6},{8,9},{9,8},{10,11... | collective-permute-start | bytes 1966088 | tf_op jit(solution)/shard_map/ppermute | solution.py:395
  5.8 3.4 %collective-permute-start = (bf16[272,512]{1,0:T(8,128)(2,1)}, bf16[272,512]{1,0:T(8,128)(2,1)}, u32[]{:S(2)}, u32[]{:S(2)}) collective-permute-start(bf16[272,512]{1,0:T(8,128)(2,1)} %maximum_maximum_fusion.1), channel_id=1, source_target_pairs={{0,2},{2,0},{4,6},{6,4},{8,10},{10,8},{12,14},{14,12},{16,18},{18,... | collective-permute-start | bytes 835592 | tf_op jit(solution)/shard_map/ppermute | solution.py:390
  8.8 24.3 %collective-permute-start.4 = (bf16[256,1408]{1,0:T(8,128)(2,1)}, bf16[256,1408]{1,0:T(8,128)(2,1)}, u32[]{:S(2)}, u32[]{:S(2)}) collective-permute-start(bf16[256,1408]{1,0:T(8,128)(2,1)} %dynamic-slice_bitcast_fusion), channel_id=1, source_target_pairs={{0,1},{1,0},{2,3},{3,2},{4,5},{5,4},{6,7},{7,6},{8,9},{9,8},{10,11... | collective-permute-start | bytes 2162696 | tf_op jit(solution)/shard_map/ppermute | solution.py:395
  11.0 13.1 %copy-start.2 = (bf16[528,512]{1,0:T(8,128)(2,1)}, bf16[528,512]{1,0:T(8,128)(2,1)S(1)}, u32[]{:S(2)}) copy-start(bf16[528,512]{1,0:T(8,128)(2,1)S(1)} %pad_maximum_fusion.2.refs_2_) | copy-start | bytes 1622020
  11.0 28.0 %collective-permute-start.2 = (bf16[528,512]{1,0:T(8,128)(2,1)S(1)}, bf16[528,512]{1,0:T(8,128)(2,1)S(1)}, u32[]{:S(2)}, u32[]{:S(2)}) collective-permute-start(bf16[528,512]{1,0:T(8,128)(2,1)S(1)} %pad_maximum_fusion.2.refs_2_), channel_id=1, source_target_pairs={{0,4},{2,6},{4,8},{6,10},{8,12},{10,14},{12,16},{14,18},{16,20},{1... | collective-permute-start | bytes 1622024 | tf_op jit(solution)/shard_map/ppermute | solution.py:386
  14.2 25.1 %collective-permute-start.1 = (bf16[528,512]{1,0:T(8,128)(2,1)S(1)}, bf16[528,512]{1,0:T(8,128)(2,1)S(1)}, u32[]{:S(2)}, u32[]{:S(2)}) collective-permute-start(bf16[528,512]{1,0:T(8,128)(2,1)S(1)} %pad_maximum_fusion.2.refs_2_), channel_id=1, source_target_pairs={{0,8},{2,10},{4,12},{6,14},{8,16},{10,18},{12,20},{14,22},{16,24},... | collective-permute-start | bytes 1622024 | tf_op jit(solution)/shard_map/ppermute | solution.py:386
  18.4 23.4 %collective-permute-start.5 = (bf16[256,2048]{1,0:T(8,128)(2,1)}, bf16[256,2048]{1,0:T(8,128)(2,1)S(1)}, u32[]{:S(2)}, u32[]{:S(2)}) collective-permute-start(bf16[256,2048]{1,0:T(8,128)(2,1)} %pad_maximum_fusion), channel_id=1, source_target_pairs={{0,2},{2,0},{4,6},{6,4},{8,10},{10,8},{12,14},{14,12},{16,18},{18,... | collective-permute-start | bytes 3145736 | tf_op jit(solution)/shard_map/ppermute | solution.py:390
  29.0 28.5 %collective-permute-start.7 = (bf16[1344,256]{1,0:T(8,128)(2,1)}, bf16[1344,256]{1,0:T(8,128)(2,1)S(1)}, u32[]{:S(2)}, u32[]{:S(2)}) collective-permute-start(bf16[1344,256]{1,0:T(8,128)(2,1)} %get-tuple-element.72), channel_id=1, source_target_pairs={{0,4},{2,6},{4,0},{6,2},{8,12},{10,14},{12,8},{14,10},{16,20},{18,... | collective-permute-start | bytes 2064392 | tf_op jit(solution)/shard_map/ppermute | solution.py:430
  37.8 19.6 %collective-permute-start.6 = (bf16[256,1024]{1,0:T(8,128)(2,1)}, bf16[256,1024]{1,0:T(8,128)(2,1)S(1)}, u32[]{:S(2)}, u32[]{:S(2)}) collective-permute-start(bf16[256,1024]{1,0:T(8,128)(2,1)} %product.2), channel_id=1, source_target_pairs={{0,1},{1,0},{2,3},{3,2},{4,5},{5,4},{6,7},{7,6},{8,9},{9,8},{10,11... | collective-permute-start | bytes 1572872 | tf_op jit(solution)/shard_map/ppermute | solution.py:395
  39.0 2.8 %copy-start.10 = (bf16[528,512]{1,0:T(8,128)(2,1)}, bf16[528,512]{1,0:T(8,128)(2,1)S(1)}, u32[]{:S(2)}) copy-start(bf16[528,512]{1,0:T(8,128)(2,1)S(1)} %collective-permute-done.2.refs_1_) | copy-start | bytes 1622020
  39.0 25.6 %collective-permute-start.10 = (bf16[1344,256]{1,0:T(8,128)(2,1)}, bf16[1344,256]{1,0:T(8,128)(2,1)S(1)}, u32[]{:S(2)}, u32[]{:S(2)}) collective-permute-start(bf16[1344,256]{1,0:T(8,128)(2,1)} %get-tuple-element.75), channel_id=1, source_target_pairs={{0,1},{1,0},{2,3},{3,2},{4,5},{5,4},{6,7},{7,6},{8,9},{9,8},{10,11... | collective-permute-start | bytes 2064392 | tf_op jit(solution)/shard_map/ppermute | solution.py:395
  40.6 24.1 %collective-permute-start.9 = (bf16[1344,256]{1,0:T(8,128)(2,1)}, bf16[1344,256]{1,0:T(8,128)(2,1)S(1)}, u32[]{:S(2)}, u32[]{:S(2)}) collective-permute-start(bf16[1344,256]{1,0:T(8,128)(2,1)} %get-tuple-element.74), channel_id=1, source_target_pairs={{0,4},{2,6},{4,0},{6,2},{8,12},{10,14},{12,8},{14,10},{16,20},{18,... | collective-permute-start | bytes 2064392 | tf_op jit(solution)/shard_map/ppermute | solution.py:430
  42.8 14.6 %copy-start.5 = (f32[256,1024]{1,0:T(8,128)S(1)}, f32[256,1024]{1,0:T(8,128)}, u32[]{:S(2)}) copy-start(f32[256,1024]{1,0:T(8,128)} %product.3) | copy-start | bytes 3145732
  57.1 3.3 %copy-start.14 = (bf16[1344,256]{1,0:T(8,128)(2,1)S(1)}, bf16[1344,256]{1,0:T(8,128)(2,1)}, u32[]{:S(2)}) copy-start(bf16[1344,256]{1,0:T(8,128)(2,1)} %get-tuple-element.66) | copy-start | bytes 2064388
  57.1 14.1 %collective-permute-start.12 = (bf16[512,512]{1,0:T(8,128)(2,1)}, bf16[512,512]{1,0:T(8,128)(2,1)S(1)}, u32[]{:S(2)}, u32[]{:S(2)}) collective-permute-start(bf16[512,512]{1,0:T(8,128)(2,1)} %get-tuple-element.71), channel_id=1, source_target_pairs={{0,4},{2,6},{4,0},{6,2},{8,12},{10,14},{12,8},{14,10},{16,20},{18,... | collective-permute-start | bytes 1572872 | tf_op jit(solution)/shard_map/ppermute | solution.py:430
  57.6 13.7 %copy-start.20 = (bf16[512,512]{1,0:T(8,128)(2,1)S(1)}, bf16[512,512]{1,0:T(8,128)(2,1)}, u32[]{:S(2)}) copy-start(bf16[512,512]{1,0:T(8,128)(2,1)} %get-tuple-element.77) | copy-start | bytes 1572868
  57.6 4.1 %collective-permute-start.8 = (bf16[256,512]{1,0:T(8,128)(2,1)S(1)}, bf16[256,512]{1,0:T(8,128)(2,1)S(1)}, u32[]{:S(2)}, u32[]{:S(2)}) collective-permute-start(bf16[256,512]{1,0:T(8,128)(2,1)S(1)} %get-tuple-element.123), channel_id=1, source_target_pairs={{0,2},{2,0},{4,6},{6,4},{8,10},{10,8},{12,14},{14,12},{16,18},{18,... | collective-permute-start | bytes 786440 | tf_op jit(solution)/shard_map/ppermute | solution.py:390
  60.4 26.0 %collective-permute-start.20 = (bf16[1344,256]{1,0:T(8,128)(2,1)S(1)}, bf16[1344,256]{1,0:T(8,128)(2,1)S(1)}, u32[]{:S(2)}, u32[]{:S(2)}) collective-permute-start(bf16[1344,256]{1,0:T(8,128)(2,1)S(1)} %collective-permute-done.7), channel_id=1, source_target_pairs={{0,1},{1,0},{2,3},{3,2},{4,5},{5,4},{6,7},{7,6},{8,9},{9,8},{10,11... | collective-permute-start | bytes 2064392 | tf_op jit(solution)/shard_map/ppermute | solution.py:395
  61.8 14.4 %copy-start.3 = (bf16[512,512]{1,0:T(8,128)(2,1)}, bf16[512,512]{1,0:T(8,128)(2,1)S(1)}, u32[]{:S(2)}) copy-start(bf16[512,512]{1,0:T(8,128)(2,1)S(1)} %constant_dynamic-update-slice_fusion.6.refs_5_) | copy-start | bytes 1572868
  64.6 11.5 %collective-permute-start.11 = (bf16[512,512]{1,0:T(8,128)(2,1)S(1)}, bf16[512,512]{1,0:T(8,128)(2,1)S(1)}, u32[]{:S(2)}, u32[]{:S(2)}) collective-permute-start(bf16[512,512]{1,0:T(8,128)(2,1)S(1)} %constant_dynamic-update-slice_fusion.6.refs_5_), channel_id=1, source_target_pairs={{0,8},{2,10},{4,12},{6,14},{8,16},{10,18},{12,20},{14,22},{16,24},... | collective-permute-start | bytes 1572872 | tf_op jit(solution)/shard_map/ppermute | solution.py:386
  71.4 13.6 %copy-start.17 = (bf16[512,512]{1,0:T(8,128)(2,1)S(1)}, bf16[512,512]{1,0:T(8,128)(2,1)}, u32[]{:S(2)}) copy-start(bf16[512,512]{1,0:T(8,128)(2,1)} %get-tuple-element.80) | copy-start | bytes 1572868
  71.4 13.6 %collective-permute-start.14 = (bf16[512,512]{1,0:T(8,128)(2,1)S(1)}, bf16[512,512]{1,0:T(8,128)(2,1)S(1)}, u32[]{:S(2)}, u32[]{:S(2)}) collective-permute-start(bf16[512,512]{1,0:T(8,128)(2,1)S(1)} %fusion.1), channel_id=1, source_target_pairs={{8,0},{10,2},{12,4},{14,6},{16,8},{18,10},{20,12},{22,14},{24,16},... | collective-permute-start | bytes 1572872 | tf_op jit(solution)/shard_map/ppermute | solution.py:386
  74.1 11.2 %copy-start.7 = (bf16[1344,512]{1,0:T(8,128)(2,1)}, bf16[1344,512]{1,0:T(8,128)(2,1)S(1)}, u32[]{:S(2)}) copy-start(bf16[1344,512]{1,0:T(8,128)(2,1)S(1)} %constant_dynamic-update-slice_fusion.refs_0_) | copy-start | bytes 4128772
  74.1 55.4 %collective-permute-start.21 = (bf16[1344,512]{1,0:T(8,128)(2,1)S(1)}, bf16[1344,512]{1,0:T(8,128)(2,1)}, u32[]{:S(2)}, u32[]{:S(2)}) collective-permute-start(bf16[1344,512]{1,0:T(8,128)(2,1)S(1)} %constant_dynamic-update-slice_fusion.refs_0_), channel_id=1, source_target_pairs={{0,2},{2,0},{4,6},{6,4},{8,10},{10,8},{12,14},{14,12},{16,18},{18,... | collective-permute-start | bytes 4128776 | tf_op jit(solution)/shard_map/ppermute | solution.py:390
  76.2 10.3 %copy-start.12 = (bf16[512,512]{1,0:T(8,128)(2,1)}, bf16[512,512]{1,0:T(8,128)(2,1)S(1)}, u32[]{:S(2)}) copy-start(bf16[512,512]{1,0:T(8,128)(2,1)S(1)} %collective-permute-done.11.refs_3_) | copy-start | bytes 1572868
  76.2 15.6 %collective-permute-start.13 = (bf16[512,512]{1,0:T(8,128)(2,1)S(1)}, bf16[512,512]{1,0:T(8,128)(2,1)S(1)}, u32[]{:S(2)}, u32[]{:S(2)}) collective-permute-start(bf16[512,512]{1,0:T(8,128)(2,1)S(1)} %broadcast_select_fusion), channel_id=1, source_target_pairs={{0,4},{2,6},{4,0},{6,2},{8,12},{10,14},{12,8},{14,10},{16,20},{18,... | collective-permute-start | bytes 1572872 | tf_op jit(solution)/shard_map/ppermute | solution.py:430
  85.3 23.3 %copy-start.4 = (bf16[512,512]{1,0:T(8,128)(2,1)}, bf16[512,512]{1,0:T(8,128)(2,1)S(1)}, u32[]{:S(2)}) copy-start(bf16[512,512]{1,0:T(8,128)(2,1)S(1)} %fusion.3.refs_4_) | copy-start | bytes 1572868
  85.3 23.3 %collective-permute-start.15 = (bf16[512,512]{1,0:T(8,128)(2,1)S(1)}, bf16[512,512]{1,0:T(8,128)(2,1)S(1)}, u32[]{:S(2)}, u32[]{:S(2)}) collective-permute-start(bf16[512,512]{1,0:T(8,128)(2,1)S(1)} %fusion.3.refs_4_), channel_id=1, source_target_pairs={{0,1},{1,0},{2,3},{3,2},{4,5},{5,4},{6,7},{7,6},{8,9},{9,8},{10,11... | collective-permute-start | bytes 1572872 | tf_op jit(solution)/shard_map/ppermute | solution.py:395
  86.5 22.1 %copy-start.8 = (bf16[1344,512]{1,0:T(8,128)(2,1)}, bf16[1344,512]{1,0:T(8,128)(2,1)S(1)}, u32[]{:S(2)}) copy-start(bf16[1344,512]{1,0:T(8,128)(2,1)S(1)} %constant_dynamic-update-slice_fusion.2.refs_1_) | copy-start | bytes 4128772
  86.5 44.5 %collective-permute-start.22 = (bf16[1344,512]{1,0:T(8,128)(2,1)S(1)}, bf16[1344,512]{1,0:T(8,128)(2,1)}, u32[]{:S(2)}, u32[]{:S(2)}) collective-permute-start(bf16[1344,512]{1,0:T(8,128)(2,1)S(1)} %constant_dynamic-update-slice_fusion.2.refs_1_), channel_id=1, source_target_pairs={{0,2},{2,0},{4,6},{6,4},{8,10},{10,8},{12,14},{14,12},{16,18},{18,... | collective-permute-start | bytes 4128776 | tf_op jit(solution)/shard_map/ppermute | solution.py:390
  89.6 21.3 %collective-permute-start.18 = (bf16[512,512]{1,0:T(8,128)(2,1)S(1)}, bf16[512,512]{1,0:T(8,128)(2,1)}, u32[]{:S(2)}, u32[]{:S(2)}) collective-permute-start(bf16[512,512]{1,0:T(8,128)(2,1)S(1)} %fusion.3.refs_4_), channel_id=1, source_target_pairs={{0,5},{1,4},{2,7},{3,6},{4,1},{5,0},{6,3},{7,2},{8,13},{9,12},{10,... | collective-permute-start | bytes 1572872 | tf_op jit(solution)/shard_map/ppermute | solution.py:405
  91.8 24.5 %collective-permute-start.17 = (bf16[512,512]{1,0:T(8,128)(2,1)S(1)}, bf16[512,512]{1,0:T(8,128)(2,1)}, u32[]{:S(2)}, u32[]{:S(2)}) collective-permute-start(bf16[512,512]{1,0:T(8,128)(2,1)S(1)} %fusion.3.refs_4_), channel_id=1, source_target_pairs={{0,4},{1,5},{2,6},{3,7},{4,0},{5,1},{6,2},{7,3},{8,12},{9,13},{10,... | collective-permute-start | bytes 1572872 | tf_op jit(solution)/shard_map/ppermute | solution.py:405
  108.6 7.7 %copy-start.13 = (bf16[512,512]{1,0:T(8,128)(2,1)}, bf16[512,512]{1,0:T(8,128)(2,1)S(1)}, u32[]{:S(2)}) copy-start(bf16[512,512]{1,0:T(8,128)(2,1)S(1)} %collective-permute-done.15.refs_6_) | copy-start | bytes 1572868
  109.6 9.9 %collective-permute-start.16 = (bf16[512,512]{1,0:T(8,128)(2,1)}, bf16[512,512]{1,0:T(8,128)(2,1)}, u32[]{:S(2)}, u32[]{:S(2)}) collective-permute-start(bf16[512,512]{1,0:T(8,128)(2,1)} %pad_maximum_fusion.5), channel_id=1, source_target_pairs={{0,2},{2,0},{4,6},{6,4},{8,10},{10,8},{12,14},{14,12},{16,18},{18,... | collective-permute-start | bytes 1572872 | tf_op jit(solution)/shard_map/ppermute | solution.py:390
  110.9 28.1 %collective-permute-start.24 = (bf16[512,512]{1,0:T(8,128)(2,1)}, bf16[512,512]{1,0:T(8,128)(2,1)}, u32[]{:S(2)}, u32[]{:S(2)}) collective-permute-start(bf16[512,512]{1,0:T(8,128)(2,1)} %get-tuple-element.105), channel_id=1, source_target_pairs={{8,0},{10,2},{12,4},{14,6},{16,8},{18,10},{20,12},{22,14},{24,16},... | collective-permute-start | bytes 1572872 | tf_op jit(solution)/shard_map/ppermute | solution.py:386
  116.3 22.8 %collective-permute-start.23 = (bf16[512,512]{1,0:T(8,128)(2,1)}, bf16[512,512]{1,0:T(8,128)(2,1)}, u32[]{:S(2)}, u32[]{:S(2)}) collective-permute-start(bf16[512,512]{1,0:T(8,128)(2,1)} %get-tuple-element.85), channel_id=1, source_target_pairs={{4,0},{6,2},{8,4},{10,6},{12,8},{14,10},{16,12},{18,14},{20,16},{2... | collective-permute-start | bytes 1572872 | tf_op jit(solution)/shard_map/ppermute | solution.py:386
  128.6 45.3 %collective-permute-start.26 = (bf16[256,2688]{1,0:T(8,128)(2,1)}, bf16[256,2688]{1,0:T(8,128)(2,1)S(1)}, u32[]{:S(2)}, u32[]{:S(2)}) collective-permute-start(bf16[256,2688]{1,0:T(8,128)(2,1)} %get-tuple-element.91), channel_id=1, source_target_pairs={{0,1},{1,0},{2,3},{3,2},{4,5},{5,4},{6,7},{7,6},{8,9},{9,8},{10,11... | collective-permute-start | bytes 4128776 | tf_op jit(solution)/shard_map/ppermute | solution.py:395
  129.5 12.5 %copy-start.21 = (bf16[512,512]{1,0:T(8,128)(2,1)S(1)}, bf16[512,512]{1,0:T(8,128)(2,1)}, u32[]{:S(2)}) copy-start(bf16[512,512]{1,0:T(8,128)(2,1)} %get-tuple-element.94) | copy-start | bytes 1572868
  129.5 44.1 %collective-permute-start.19 = (bf16[2,256,1024]{2,1,0:T(8,128)(2,1)}, bf16[2,256,1024]{2,1,0:T(8,128)(2,1)S(1)}, u32[]{:S(2)}, u32[]{:S(2)}) collective-permute-start(bf16[2,256,1024]{2,1,0:T(8,128)(2,1)} %get-tuple-element.92), channel_id=1, source_target_pairs={{0,2},{2,0},{4,6},{6,4},{8,10},{10,8},{12,14},{14,12},{16,18},{18,... | collective-permute-start | bytes 3145736 | tf_op jit(solution)/shard_map/ppermute | solution.py:390
  139.1 32.4 %copy-start.15 = (f32[336,512]{1,0:T(8,128)S(1)}, f32[336,512]{1,0:T(8,128)}, u32[]{:S(2)}) copy-start(f32[336,512]{1,0:T(8,128)} %get-tuple-element.109) | copy-start | bytes 2064388
  139.1 9.8 %collective-permute-start.27 = (bf16[336,512]{1,0:T(8,128)(2,1)}, bf16[336,512]{1,0:T(8,128)(2,1)S(1)}, u32[]{:S(2)}, u32[]{:S(2)}) collective-permute-start(bf16[336,512]{1,0:T(8,128)(2,1)} %get-tuple-element.110), channel_id=1, source_target_pairs={{0,8},{2,10},{4,12},{6,14},{8,16},{10,18},{12,20},{14,22},{16,24},... | collective-permute-start | bytes 1032200 | tf_op jit(solution)/shard_map/ppermute | solution.py:600
  140.4 29.7 %collective-permute-start.28 = (bf16[336,512]{1,0:T(8,128)(2,1)}, bf16[336,512]{1,0:T(8,128)(2,1)S(1)}, u32[]{:S(2)}, u32[]{:S(2)}) collective-permute-start(bf16[336,512]{1,0:T(8,128)(2,1)} %get-tuple-element.111), channel_id=1, source_target_pairs={{0,16},{2,18},{4,20},{6,22},{8,24},{10,26},{12,28},{14,30},{16,0},... | collective-permute-start | bytes 1032200 | tf_op jit(solution)/shard_map/ppermute | solution.py:600
  140.7 30.8 %collective-permute-start.29 = (bf16[336,512]{1,0:T(8,128)(2,1)}, bf16[336,512]{1,0:T(8,128)(2,1)S(1)}, u32[]{:S(2)}, u32[]{:S(2)}) collective-permute-start(bf16[336,512]{1,0:T(8,128)(2,1)} %get-tuple-element.112), channel_id=1, source_target_pairs={{0,24},{2,26},{4,28},{6,30},{8,0},{10,2},{12,4},{14,6},{16,8},{18,... | collective-permute-start | bytes 1032200 | tf_op jit(solution)/shard_map/ppermute | solution.py:600
  148.9 23.5 %collective-permute-start.25 = (bf16[256,512]{1,0:T(8,128)(2,1)S(1)}, bf16[256,512]{1,0:T(8,128)(2,1)S(1)}, u32[]{:S(2)}, u32[]{:S(2)}) collective-permute-start(bf16[256,512]{1,0:T(8,128)(2,1)S(1)} %get-tuple-element.117), channel_id=1, source_target_pairs={{0,2},{2,0},{4,6},{6,4},{8,10},{10,8},{12,14},{14,12},{16,18},{18,... | collective-permute-start | bytes 786440 | tf_op jit(solution)/shard_map/ppermute | solution.py:390
  171.8 2.5 %copy-start.22 = (bf16[256,5376]{1,0:T(8,128)(2,1)S(1)}, bf16[256,5376]{1,0:T(8,128)(2,1)}, u32[]{:S(2)}) copy-start(bf16[256,5376]{1,0:T(8,128)(2,1)} %get-tuple-element.108) | copy-start | bytes 8257540
  171.8 1.8 %collective-permute-start.30 = (f32[168,512]{1,0:T(8,128)S(1)}, f32[168,512]{1,0:T(8,128)S(1)}, u32[]{:S(2)}, u32[]{:S(2)}) collective-permute-start(f32[168,512]{1,0:T(8,128)S(1)} %get-tuple-element.115), channel_id=1, source_target_pairs={{0,2},{2,0},{4,6},{6,4},{8,10},{10,8},{12,14},{14,12},{16,18},{18,... | collective-permute-start | bytes 1032200 | tf_op jit(solution)/shard_map/ppermute | solution.py:390
  (11 other events, 16.2 us)

commit v12 on v11

--- a/solution.py
+++ b/solution.py
@@ -282,7 +282,7 @@
 def run_product(at, parts, w, kind):
     rows = parts[0].shape[0]
     depth, width = w.shape
-    tile = 512
+    tile = width
     if len(parts) == 1:
         x_specs = [pl.BlockSpec((rows, depth), lambda j, at: (0, at[0]))]
     else:
@@ -562,12 +562,10 @@
     dk_back = [shifted(dk_near, -2), shifted(dk_far, -4)]
 
     dv_fsdp = [after(x, dk_near) for x in dv_fsdp]
-    dv_over_y = [after(x, dk_near) for x in dv_over_y]
     dv_other = swapped(jnp.concatenate([rows_of(x, 1 - core, shard_rows) for x in dv_fsdp], 0))
     dv_rows = placed(
         core, jnp.concatenate([rows_of(x, core, shard_rows) for x in dv_fsdp], 0), dv_other, 1
     )
-    dv_rows = after(dv_rows, *dv_over_y)
     if aligned:
         d_tokens, *made = run_tokens(fsdp_arg, dv_rows, w_value, n_fsdp)
     else:
@@ -579,6 +577,7 @@
         back = rotated(made[s - 1], -s)
         d_tokens = lax.dynamic_update_slice_in_dim(d_tokens, back, ((my_fsdp + s) % n_fsdp) * slab, 1)
 
+    dv_over_y = [after(x, *made) for x in dv_over_y]
     dv_pairs = list(zip(dv_fsdp, dv_over_y))
     if out_rows % 8 == 0:
         at = after(jnp.stack([core, my_z]).astype(jnp.int32), *made)

time: 178 us -> 183 us (1.028)
  starting transfers between devices: 60.1 us -> 64.6 us
  waiting for transfers between devices: 34.1 us -> 30.5 us
  local copies, waits for them, and re-layouts: 12.3 us -> 14.2 us
    ppermute x9, starting transfers between devices: 27.2 us -> 31.4 us  [swapped(): lax.ppermute(x, 'ctx', [(i, i ^ 1) for i in range(lax.axis_size('ctx'))])]
    ppermute x2, waiting for transfers between devices: 3.71 us -> 0.01 us  [moved(): return lax.ppermute(x, ('ctx', 'fsdp'), pairs)]
    ppermute x6, waiting for transfers between devices: 7.5 us -> 4.88 us  [shifted(): lax.ppermute(x, 'ctx', [(i, i + by) for i in range(length) if 0 <= i + by...]
    ppermute x7, waiting for transfers between devices: 5.68 us -> 7.87 us  [rotated(): lax.ppermute(x, 'fsdp', [(i, (i + by) % length) for i in range(length)])]
    ppermute x3, starting transfers between devices: 2.98 us -> 4.99 us  [shards(): lax.ppermute(by_z[d], 'ctx', [(i, (i + 4 * d) % n_ctx) for i in range(n_c...]
    unnamed x58 -> x64, local copies, waits for them, and re-layouts: 4.98 us -> 5 us
  transfers between devices with their start and end apart: 31 -> 31, of which waited for: 10 -> 10; matrix products, arithmetic and copies ran while one was open for 9% -> 10% of each run, Pallas kernels for 34% -> 34%
where the time goes in v12:
time: 183 us; the launch traced here: 181 us
  starting transfers between devices  64.6 us (35%)
  Pallas kernels  60.8 us (33%)
  waiting for transfers between devices  30.5 us (17%)
  local copies, waits for them, and re-layouts  14.2 us (8%)
  other arithmetic  9.28 us (5%)
    ppermute x9, starting transfers between devices, swapped(): lax.ppermute(x, 'ctx', [(i, i ^ 1) for i in range(lax.axis_size('ctx'))])  31.4 us
    pallas_call x1, Pallas kernels, run_grads(): pl.pallas_call(functools.partial(grads_kernel, blk, n_arr - 1), grid_spec...  16 us
    ppermute x6, starting transfers between devices, shifted(): lax.ppermute(x, 'ctx', [(i, i + by) for i in range(length) if 0 <= i + by...  16 us
    pallas_call x1, Pallas kernels, run_probs(): pl.pallas_call(functools.partial(probs_kernel, blk, n_arr - 1), grid_spec...  14.3 us
    ppermute x3, waiting for transfers between devices, shards(): lax.ppermute(by_z[d], 'ctx', [(i, (i + 4 * d) % n_ctx) for i in range(n_c...  12 us
    pallas_call x2, Pallas kernels, run_product(): pl.pallas_call(product_kernel, grid_spec=pltpu.PrefetchScalarGridSpec(num...  11.1 us
    pallas_call x1, Pallas kernels, run_weight(): pl.pallas_call(functools.partial(weight_kernel, n_z, n), grid_spec=pltpu....  8.14 us
    ppermute x7, waiting for transfers between devices, rotated(): lax.ppermute(x, 'fsdp', [(i, (i + by) % length) for i in range(length)])  7.87 us
  transfers between devices with their start and end apart: 31, of which 10 were waited for; matrix products, arithmetic and copies ran while one was open for 10% of the time, Pallas kernels for 34%

profile of v12, /device:TPU:9, one launch (start us, length us, event | category | flops | bytes accessed | tf_op | source)
XLA Modules:
  0.0 180.6 jit_solution(12408241263905723588)
XLA Ops:
  0.7 1.2 dynamic-slice_bitcast_fusion.1
  1.9 1.3 collective-permute-start.3
  4.0 1.1 dynamic-slice_bitcast_fusion.5
  6.8 2.0 %dynamic-slice_bitcast_fusion = bf16[256,1408]{1,0:T(8,128)(2,1)} fusion(bf16[1,256,5376]{2,1,0:T(8,128)(2,1)} %param.6, s32[]{:T(128)S(6)} %select_n.97), kind=kLoop, calls=%fused_computation.12 | loop fusion | bytes 1441796 | tf_op jit(solution)/shard_map/dynamic_slice | solution.py:469
  9.3 1.0 slice_dynamic-update-slice_fusion.2
  11.0 3.1 %collective-permute-start.2 = (bf16[528,512]{1,0:T(8,128)(2,1)S(1)}, bf16[528,512]{1,0:T(8,128)(2,1)S(1)}, u32[]{:S(2)}, u32[]{:S(2)}) collective-permute-start(bf16[528,512]{1,0:T(8,128)(2,1)S(1)} %pad_maximum_fusion.2.refs_2_), channel_id=1, source_target_pairs={{0,4},{2,6},{4,8},{6,10},{8,12},{10,14},{12,16},{14,18},{16,20},{1... | collective-permute-start | bytes 1622024 | tf_op jit(solution)/shard_map/ppermute | solution.py:386
  14.2 3.2 %collective-permute-start.1 = (bf16[528,512]{1,0:T(8,128)(2,1)S(1)}, bf16[528,512]{1,0:T(8,128)(2,1)S(1)}, u32[]{:S(2)}, u32[]{:S(2)}) collective-permute-start(bf16[528,512]{1,0:T(8,128)(2,1)S(1)} %pad_maximum_fusion.2.refs_2_), channel_id=1, source_target_pairs={{0,8},{2,10},{4,12},{6,14},{8,16},{10,18},{12,20},{14,22},{16,24},... | collective-permute-start | bytes 1622024 | tf_op jit(solution)/shard_map/ppermute | solution.py:386
  17.4 1.1 pad_maximum_fusion
  19.9 4.2 %pieces.1 = (bf16[1344,256]{1,0:T(8,128)(2,1)}, bf16[1344,256]{1,0:T(8,128)(2,1)}, bf16[1344,256]{1,0:T(8,128)(2,1)}, bf16[1344,256]{1,0:T(8,128)(2,1)}) custom-call(s32[2]{0:T(128)} %pad_add_fusion.at_ref, bf16[256,5376]{1,0:T(8,128)(2,1)} %bitcast.29), custom_call_target="tpu_custom_call" | custom-call | flops 1048576 | bytes 4096 | tf_op jit(solution)/shard_map/pieces/pallas_call | solution.py:260
  24.1 5.6 %product.3 = f32[256,1024]{1,0:T(8,128)} custom-call(s32[1]{0:T(128)} %bitcast.10.at_ref, bf16[256,5376]{1,0:T(8,128)(2,1)} %bitcast.30, bf16[2688,1024]{1,0:T(8,128)(2,1)} %w_ref.1), custom_call_target="tpu_custom_call" | custom-call | flops 1048576 | bytes 4096 | tf_op jit(solution)/shard_map/product/pallas_call | solution.py:290
  29.7 1.3 collective-permute-start.7
  31.0 2.1 %collective-permute-done.4.refs_1_ = bf16[256,1408]{1,0:T(8,128)(2,1)} collective-permute-done((bf16[256,1408]{1,0:T(8,128)(2,1)}, bf16[256,1408]{1,0:T(8,128)(2,1)}, u32[]{:S(2)}, u32[]{:S(2)}) %collective-permute-start.4) | collective-permute-done | bytes 720928 | tf_op jit(solution)/shard_map/ppermute | solution.py:395
  33.1 5.4 %product.2 = bf16[256,1024]{1,0:T(8,128)(2,1)} custom-call(s32[1]{0:T(128)} %constant.86.clone.1.at_ref, bf16[256,1280]{1,0:T(8,128)(2,1)} %collective-permute-done.3.refs_0_, bf16[256,1408]{1,0:T(8,128)(2,1)} %collective-permute-done.4.refs_1_, bf16[2688,1024]{1,0:T(8,128)(2,1)} %w_ref.1), custom_call_target="tpu_custom_call" | custom-call | flops 1048576 | bytes 4096 | tf_op jit(solution)/shard_map/product/pallas_call | solution.py:290
  38.6 1.2 collective-permute-start.6
  41.3 1.2 collective-permute-start.9
  43.5 14.3 %probs.1 = (bf16[4,2,1280,512]{3,2,1,0:T(8,128)(2,1)}, f32[4,2,1,512]{3,2,1,0:T(1,128)}, bf16[4,2,128,512]{3,2,1,0:T(8,128)(2,1)}, bf16[512,512]{1,0:T(8,128)(2,...) custom-call(s32[1]{0:T(128)} %bitcast.core_ref, s32[1,512]{1,0:T(1,128)} %add_maximum_fusion.low_ref, ...), custom_call_target="tpu_custom_call" | custom-call | flops 1048576 | bytes 4096 | tf_op jit(solution)/shard_map/probs/pallas_call | solution.py:158
  58.4 2.7 %collective-permute-start.8 = (bf16[256,512]{1,0:T(8,128)(2,1)S(1)}, bf16[256,512]{1,0:T(8,128)(2,1)S(1)}, u32[]{:S(2)}, u32[]{:S(2)}) collective-permute-start(bf16[256,512]{1,0:T(8,128)(2,1)S(1)} %get-tuple-element.121), channel_id=1, source_target_pairs={{0,2},{2,0},{4,6},{6,4},{8,10},{10,8},{12,14},{14,12},{16,18},{18,... | collective-permute-start | bytes 786440 | tf_op jit(solution)/shard_map/ppermute | solution.py:390
  61.2 1.1 collective-permute-done.8
  62.3 3.1 %collective-permute-done.10 = bf16[1344,256]{1,0:T(8,128)(2,1)S(1)} collective-permute-done((bf16[1344,256]{1,0:T(8,128)(2,1)}, bf16[1344,256]{1,0:T(8,128)(2,1)S(1)}, u32[]{:S(2)}, u32[]{:S(2)}) %collective-permute-start.10) | collective-permute-done | bytes 688160 | tf_op jit(solution)/shard_map/ppermute | solution.py:395
  65.4 3.2 %collective-permute-start.11 = (bf16[512,512]{1,0:T(8,128)(2,1)S(1)}, bf16[512,512]{1,0:T(8,128)(2,1)S(1)}, u32[]{:S(2)}, u32[]{:S(2)}) collective-permute-start(bf16[512,512]{1,0:T(8,128)(2,1)S(1)} %constant_dynamic-update-slice_fusion.6.refs_5_), channel_id=1, source_target_pairs={{0,8},{2,10},{4,12},{6,14},{8,16},{10,18},{12,20},{14,22},{16,24},... | collective-permute-start | bytes 1572872 | tf_op jit(solution)/shard_map/ppermute | solution.py:386
  68.6 3.4 %collective-permute-done.12 = bf16[512,512]{1,0:T(8,128)(2,1)S(1)} collective-permute-done((bf16[512,512]{1,0:T(8,128)(2,1)}, bf16[512,512]{1,0:T(8,128)(2,1)S(1)}, u32[]{:S(2)}, u32[]{:S(2)}) %collective-permute-start.12) | collective-permute-done | bytes 524320 | tf_op jit(solution)/shard_map/ppermute | solution.py:430
  72.2 2.6 %collective-permute-start.14 = (bf16[512,512]{1,0:T(8,128)(2,1)S(1)}, bf16[512,512]{1,0:T(8,128)(2,1)S(1)}, u32[]{:S(2)}, u32[]{:S(2)}) collective-permute-start(bf16[512,512]{1,0:T(8,128)(2,1)S(1)} %fusion.1), channel_id=1, source_target_pairs={{8,0},{10,2},{12,4},{14,6},{16,8},{18,10},{20,12},{22,14},{24,16},... | collective-permute-start | bytes 1572872 | tf_op jit(solution)/shard_map/ppermute | solution.py:386
  74.9 1.1 collective-permute-start.18
  76.0 1.1 constant_dynamic-update-slice_fusion.refs_0_
  77.2 2.4 %collective-permute-start.19 = (bf16[1344,512]{1,0:T(8,128)(2,1)S(1)}, bf16[1344,512]{1,0:T(8,128)(2,1)}, u32[]{:S(2)}, u32[]{:S(2)}) collective-permute-start(bf16[1344,512]{1,0:T(8,128)(2,1)S(1)} %constant_dynamic-update-slice_fusion.refs_0_), channel_id=1, source_target_pairs={{0,2},{2,0},{4,6},{6,4},{8,10},{10,8},{12,14},{14,12},{16,18},{18,... | collective-permute-start | bytes 4128776 | tf_op jit(solution)/shard_map/ppermute | solution.py:390
  79.7 1.3 collective-permute-start.13
  81.0 4.9 %collective-permute-done.14 = bf16[512,512]{1,0:T(8,128)(2,1)S(1)} collective-permute-done((bf16[512,512]{1,0:T(8,128)(2,1)S(1)}, bf16[512,512]{1,0:T(8,128)(2,1)S(1)}, u32[]{:S(2)}, u32[]{:S(2)}) %collective-permute-start.14) | collective-permute-done | bytes 524320 | tf_op jit(solution)/shard_map/ppermute | solution.py:386
  86.1 1.3 collective-permute-start.15
  87.4 2.7 %collective-permute-done.18 = bf16[1344,256]{1,0:T(8,128)(2,1)S(1)} collective-permute-done((bf16[1344,256]{1,0:T(8,128)(2,1)}, bf16[1344,256]{1,0:T(8,128)(2,1)S(1)}, u32[]{:S(2)}, u32[]{:S(2)}) %collective-permute-start.18) | collective-permute-done | bytes 688160 | tf_op jit(solution)/shard_map/ppermute | solution.py:395
  90.2 5.3 %collective-permute-start.20 = (bf16[1344,512]{1,0:T(8,128)(2,1)S(1)}, bf16[1344,512]{1,0:T(8,128)(2,1)}, u32[]{:S(2)}, u32[]{:S(2)}) collective-permute-start(bf16[1344,512]{1,0:T(8,128)(2,1)S(1)} %constant_dynamic-update-slice_fusion.2.refs_1_), channel_id=1, source_target_pairs={{0,2},{2,0},{4,6},{6,4},{8,10},{10,8},{12,14},{14,12},{16,18},{18,... | collective-permute-start | bytes 4128776 | tf_op jit(solution)/shard_map/ppermute | solution.py:390
  95.6 2.2 %collective-permute-start.22 = (bf16[512,512]{1,0:T(8,128)(2,1)S(1)}, bf16[512,512]{1,0:T(8,128)(2,1)S(1)}, u32[]{:S(2)}, u32[]{:S(2)}) collective-permute-start(bf16[512,512]{1,0:T(8,128)(2,1)S(1)} %fusion.3.refs_4_), channel_id=1, source_target_pairs={{0,5},{1,4},{2,7},{3,6},{4,1},{5,0},{6,3},{7,2},{8,13},{9,12},{10,... | collective-permute-start | bytes 1572872 | tf_op jit(solution)/shard_map/ppermute | solution.py:405
  98.5 16.0 %grads.1 = (bf16[256,2048]{1,0:T(8,128)(2,1)}, bf16[256,2048]{1,0:T(8,128)(2,1)}, bf16[2,256,1024]{2,1,0:T(8,128)(2,1)}, bf16[512,512]{1,0:T(8,128)(2,1)}, bf16[...) custom-call(s32[1]{0:T(128)} %bitcast.core_ref, bf16[4,2,1280,512]{3,2,1,0:T(8,128)(2,1)} %get-tuple-element.61.e_ref, ...), custom_call_target="tpu_custom_call" | custom-call | flops 1048576 | bytes 4096 | tf_op jit(solution)/shard_map/grads/pallas_call | solution.py:201
  116.1 1.9 %collective-permute-start.24 = (bf16[512,512]{1,0:T(8,128)(2,1)}, bf16[512,512]{1,0:T(8,128)(2,1)}, u32[]{:S(2)}, u32[]{:S(2)}) collective-permute-start(bf16[512,512]{1,0:T(8,128)(2,1)} %get-tuple-element.103), channel_id=1, source_target_pairs={{8,0},{10,2},{12,4},{14,6},{16,8},{18,10},{20,12},{22,14},{24,16},... | collective-permute-start | bytes 1572872 | tf_op jit(solution)/shard_map/ppermute | solution.py:386
  118.0 1.9 %collective-permute-start.23 = (bf16[512,512]{1,0:T(8,128)(2,1)}, bf16[512,512]{1,0:T(8,128)(2,1)}, u32[]{:S(2)}, u32[]{:S(2)}) collective-permute-start(bf16[512,512]{1,0:T(8,128)(2,1)} %get-tuple-element.84), channel_id=1, source_target_pairs={{4,0},{6,2},{8,4},{10,6},{12,8},{14,10},{16,12},{18,14},{20,16},{2... | collective-permute-start | bytes 1572872 | tf_op jit(solution)/shard_map/ppermute | solution.py:386
  120.7 1.1 maximum_maximum_fusion
  121.8 1.1 constant_dynamic-update-slice_fusion.5.dv_ref
  123.9 7.0 %tokens.1 = (bf16[256,5376]{1,0:T(8,128)(2,1)}, bf16[256,2688]{1,0:T(8,128)(2,1)}) custom-call(s32[1]{0:T(128)} %bitcast.10.at_ref, bf16[512,1024]{1,0:T(8,128)(2,1)} %copy-done.6, bf16[2688,1024]{1,0:T(8,128)(2,1)} %w_ref.1), custom_call_target="tpu_custom_call" | custom-call | flops 1048576 | bytes 4096 | tf_op jit(solution)/shard_map/tokens/pallas_call | solution.py:364
  131.2 2.3 %collective-permute-start.17 = (bf16[2,256,1024]{2,1,0:T(8,128)(2,1)}, bf16[2,256,1024]{2,1,0:T(8,128)(2,1)S(1)}, u32[]{:S(2)}, u32[]{:S(2)}) collective-permute-start(bf16[2,256,1024]{2,1,0:T(8,128)(2,1)} %get-tuple-element.88), channel_id=1, source_target_pairs={{0,2},{2,0},{4,6},{6,4},{8,10},{10,8},{12,14},{14,12},{16,18},{18,... | collective-permute-start | bytes 3145736 | tf_op jit(solution)/shard_map/ppermute | solution.py:390
  133.5 8.1 %weight.1 = (f32[336,512]{1,0:T(8,128)}, bf16[336,512]{1,0:T(8,128)(2,1)}, bf16[336,512]{1,0:T(8,128)(2,1)}, bf16[336,512]{1,0:T(8,128)(2,1)}) custom-call(s32[2]{0:T(128)} %pad_add_fusion.1.at_ref, bf16[1344,512]{1,0:T(8,128)(2,1)} %copy-done.7, bf16[1344,512]{1,0:T(8,128)(2,1)} %copy-done.8, bf16[1344,512]{1,0:T(8,128)(2,1)} %collective-permute-done.19.refs_2_, ...), custom_call_target="tpu_custom_call" | custom-call | flops 1048576 | bytes 4096 | tf_op jit(solution)/shard_map/weight/pallas_call | solution.py:336
  141.6 1.8 collective-permute-start.27
  143.4 1.8 %collective-permute-start.28 = (bf16[336,512]{1,0:T(8,128)(2,1)}, bf16[336,512]{1,0:T(8,128)(2,1)S(1)}, u32[]{:S(2)}, u32[]{:S(2)}) collective-permute-start(bf16[336,512]{1,0:T(8,128)(2,1)} %get-tuple-element.109), channel_id=1, source_target_pairs={{0,16},{2,18},{4,20},{6,22},{8,24},{10,26},{12,28},{14,30},{16,0},... | collective-permute-start | bytes 1032200 | tf_op jit(solution)/shard_map/ppermute | solution.py:599
  145.2 1.4 collective-permute-start.29
  146.6 1.4 add_convert_fusion
  148.1 3.3 %collective-permute-done.27 = bf16[336,512]{1,0:T(8,128)(2,1)S(1)} collective-permute-done((bf16[336,512]{1,0:T(8,128)(2,1)}, bf16[336,512]{1,0:T(8,128)(2,1)S(1)}, u32[]{:S(2)}, u32[]{:S(2)}) %collective-permute-start.27) | collective-permute-done | bytes 344096 | tf_op jit(solution)/shard_map/ppermute | solution.py:599
  151.4 15.9 %collective-permute-start.25 = (bf16[256,512]{1,0:T(8,128)(2,1)S(1)}, bf16[256,512]{1,0:T(8,128)(2,1)S(1)}, u32[]{:S(2)}, u32[]{:S(2)}) collective-permute-start(bf16[256,512]{1,0:T(8,128)(2,1)S(1)} %get-tuple-element.115), channel_id=1, source_target_pairs={{0,2},{2,0},{4,6},{6,4},{8,10},{10,8},{12,14},{14,12},{16,18},{18,... | collective-permute-start | bytes 786440 | tf_op jit(solution)/shard_map/ppermute | solution.py:390
  167.3 5.8 %collective-permute-done.28 = bf16[336,512]{1,0:T(8,128)(2,1)S(1)} collective-permute-done((bf16[336,512]{1,0:T(8,128)(2,1)}, bf16[336,512]{1,0:T(8,128)(2,1)S(1)}, u32[]{:S(2)}, u32[]{:S(2)}) %collective-permute-start.28) | collective-permute-done | bytes 344096 | tf_op jit(solution)/shard_map/ppermute | solution.py:599
  173.1 2.9 %collective-permute-done.29 = bf16[336,512]{1,0:T(8,128)(2,1)S(1)} collective-permute-done((bf16[336,512]{1,0:T(8,128)(2,1)}, bf16[336,512]{1,0:T(8,128)(2,1)S(1)}, u32[]{:S(2)}, u32[]{:S(2)}) %collective-permute-start.29) | collective-permute-done | bytes 344096 | tf_op jit(solution)/shard_map/ppermute | solution.py:599
  177.0 1.2 collective-permute-done.30
  (132 shorter events, 16.4 us)
Async XLA Ops:
  0.7 8.4 %copy-start.1 = (bf16[1,256,2048]{2,1,0:T(8,128)(2,1)S(1)}, bf16[1,256,2048]{2,1,0:T(8,128)(2,1)}, u32[]{:S(2)}) copy-start(bf16[1,256,2048]{2,1,0:T(8,128)(2,1)} %param.7) | copy-start | bytes 3145732
  1.9 7.2 %copy-start.9 = (bf16[1,256,2048]{2,1,0:T(8,128)(2,1)S(1)}, bf16[1,256,2048]{2,1,0:T(8,128)(2,1)}, u32[]{:S(2)}) copy-start(bf16[1,256,2048]{2,1,0:T(8,128)(2,1)} %param.10) | copy-start | bytes 3145732
  1.9 27.8 %collective-permute-start.3 = (bf16[256,1280]{1,0:T(8,128)(2,1)S(1)}, bf16[256,1280]{1,0:T(8,128)(2,1)}, u32[]{:S(2)}, u32[]{:S(2)}) collective-permute-start(bf16[256,1280]{1,0:T(8,128)(2,1)S(1)} %dynamic-slice_bitcast_fusion.1), channel_id=1, source_target_pairs={{0,1},{1,0},{2,3},{3,2},{4,5},{5,4},{6,7},{7,6},{8,9},{9,8},{10,11... | collective-permute-start | bytes 1966088 | tf_op jit(solution)/shard_map/ppermute | solution.py:395
  5.8 3.4 %collective-permute-start = (bf16[272,512]{1,0:T(8,128)(2,1)}, bf16[272,512]{1,0:T(8,128)(2,1)}, u32[]{:S(2)}, u32[]{:S(2)}) collective-permute-start(bf16[272,512]{1,0:T(8,128)(2,1)} %maximum_maximum_fusion.1), channel_id=1, source_target_pairs={{0,2},{2,0},{4,6},{6,4},{8,10},{10,8},{12,14},{14,12},{16,18},{18,... | collective-permute-start | bytes 835592 | tf_op jit(solution)/shard_map/ppermute | solution.py:390
  8.8 24.3 %collective-permute-start.4 = (bf16[256,1408]{1,0:T(8,128)(2,1)}, bf16[256,1408]{1,0:T(8,128)(2,1)}, u32[]{:S(2)}, u32[]{:S(2)}) collective-permute-start(bf16[256,1408]{1,0:T(8,128)(2,1)} %dynamic-slice_bitcast_fusion), channel_id=1, source_target_pairs={{0,1},{1,0},{2,3},{3,2},{4,5},{5,4},{6,7},{7,6},{8,9},{9,8},{10,11... | collective-permute-start | bytes 2162696 | tf_op jit(solution)/shard_map/ppermute | solution.py:395
  11.0 13.1 %copy-start.2 = (bf16[528,512]{1,0:T(8,128)(2,1)}, bf16[528,512]{1,0:T(8,128)(2,1)S(1)}, u32[]{:S(2)}) copy-start(bf16[528,512]{1,0:T(8,128)(2,1)S(1)} %pad_maximum_fusion.2.refs_2_) | copy-start | bytes 1622020
  11.0 28.8 %collective-permute-start.2 = (bf16[528,512]{1,0:T(8,128)(2,1)S(1)}, bf16[528,512]{1,0:T(8,128)(2,1)S(1)}, u32[]{:S(2)}, u32[]{:S(2)}) collective-permute-start(bf16[528,512]{1,0:T(8,128)(2,1)S(1)} %pad_maximum_fusion.2.refs_2_), channel_id=1, source_target_pairs={{0,4},{2,6},{4,8},{6,10},{8,12},{10,14},{12,16},{14,18},{16,20},{1... | collective-permute-start | bytes 1622024 | tf_op jit(solution)/shard_map/ppermute | solution.py:386
  14.2 25.9 %collective-permute-start.1 = (bf16[528,512]{1,0:T(8,128)(2,1)S(1)}, bf16[528,512]{1,0:T(8,128)(2,1)S(1)}, u32[]{:S(2)}, u32[]{:S(2)}) collective-permute-start(bf16[528,512]{1,0:T(8,128)(2,1)S(1)} %pad_maximum_fusion.2.refs_2_), channel_id=1, source_target_pairs={{0,8},{2,10},{4,12},{6,14},{8,16},{10,18},{12,20},{14,22},{16,24},... | collective-permute-start | bytes 1622024 | tf_op jit(solution)/shard_map/ppermute | solution.py:386
  18.4 24.1 %collective-permute-start.5 = (bf16[256,2048]{1,0:T(8,128)(2,1)}, bf16[256,2048]{1,0:T(8,128)(2,1)S(1)}, u32[]{:S(2)}, u32[]{:S(2)}) collective-permute-start(bf16[256,2048]{1,0:T(8,128)(2,1)} %pad_maximum_fusion), channel_id=1, source_target_pairs={{0,2},{2,0},{4,6},{6,4},{8,10},{10,8},{12,14},{14,12},{16,18},{18,... | collective-permute-start | bytes 3145736 | tf_op jit(solution)/shard_map/ppermute | solution.py:390
  29.7 28.4 %collective-permute-start.7 = (bf16[1344,256]{1,0:T(8,128)(2,1)}, bf16[1344,256]{1,0:T(8,128)(2,1)}, u32[]{:S(2)}, u32[]{:S(2)}) collective-permute-start(bf16[1344,256]{1,0:T(8,128)(2,1)} %get-tuple-element.71), channel_id=1, source_target_pairs={{0,4},{2,6},{4,0},{6,2},{8,12},{10,14},{12,8},{14,10},{16,20},{18,... | collective-permute-start | bytes 2064392 | tf_op jit(solution)/shard_map/ppermute | solution.py:430
  38.6 19.6 %collective-permute-start.6 = (bf16[256,1024]{1,0:T(8,128)(2,1)}, bf16[256,1024]{1,0:T(8,128)(2,1)S(1)}, u32[]{:S(2)}, u32[]{:S(2)}) collective-permute-start(bf16[256,1024]{1,0:T(8,128)(2,1)} %product.2), channel_id=1, source_target_pairs={{0,1},{1,0},{2,3},{3,2},{4,5},{5,4},{6,7},{7,6},{8,9},{9,8},{10,11... | collective-permute-start | bytes 1572872 | tf_op jit(solution)/shard_map/ppermute | solution.py:395
  39.8 2.8 %copy-start.10 = (bf16[528,512]{1,0:T(8,128)(2,1)}, bf16[528,512]{1,0:T(8,128)(2,1)S(1)}, u32[]{:S(2)}) copy-start(bf16[528,512]{1,0:T(8,128)(2,1)S(1)} %collective-permute-done.2.refs_1_) | copy-start | bytes 1622020
  39.8 25.6 %collective-permute-start.10 = (bf16[1344,256]{1,0:T(8,128)(2,1)}, bf16[1344,256]{1,0:T(8,128)(2,1)S(1)}, u32[]{:S(2)}, u32[]{:S(2)}) collective-permute-start(bf16[1344,256]{1,0:T(8,128)(2,1)} %get-tuple-element.74), channel_id=1, source_target_pairs={{0,1},{1,0},{2,3},{3,2},{4,5},{5,4},{6,7},{7,6},{8,9},{9,8},{10,11... | collective-permute-start | bytes 2064392 | tf_op jit(solution)/shard_map/ppermute | solution.py:395
  41.3 24.1 %collective-permute-start.9 = (bf16[1344,256]{1,0:T(8,128)(2,1)}, bf16[1344,256]{1,0:T(8,128)(2,1)}, u32[]{:S(2)}, u32[]{:S(2)}) collective-permute-start(bf16[1344,256]{1,0:T(8,128)(2,1)} %get-tuple-element.73), channel_id=1, source_target_pairs={{0,4},{2,6},{4,0},{6,2},{8,12},{10,14},{12,8},{14,10},{16,20},{18,... | collective-permute-start | bytes 2064392 | tf_op jit(solution)/shard_map/ppermute | solution.py:430
  43.5 14.7 %copy-start.5 = (f32[256,1024]{1,0:T(8,128)S(1)}, f32[256,1024]{1,0:T(8,128)}, u32[]{:S(2)}) copy-start(f32[256,1024]{1,0:T(8,128)} %product.3) | copy-start | bytes 3145732
  57.9 14.2 %copy-start.22 = (bf16[512,512]{1,0:T(8,128)(2,1)S(1)}, bf16[512,512]{1,0:T(8,128)(2,1)}, u32[]{:S(2)}) copy-start(bf16[512,512]{1,0:T(8,128)(2,1)} %get-tuple-element.76) | copy-start | bytes 1572868
  57.9 14.2 %collective-permute-start.12 = (bf16[512,512]{1,0:T(8,128)(2,1)}, bf16[512,512]{1,0:T(8,128)(2,1)S(1)}, u32[]{:S(2)}, u32[]{:S(2)}) collective-permute-start(bf16[512,512]{1,0:T(8,128)(2,1)} %get-tuple-element.70), channel_id=1, source_target_pairs={{0,4},{2,6},{4,0},{6,2},{8,12},{10,14},{12,8},{14,10},{16,20},{18,... | collective-permute-start | bytes 1572872 | tf_op jit(solution)/shard_map/ppermute | solution.py:430
  58.3 16.5 %copy-start.16 = (bf16[1344,256]{1,0:T(8,128)(2,1)S(1)}, bf16[1344,256]{1,0:T(8,128)(2,1)}, u32[]{:S(2)}) copy-start(bf16[1344,256]{1,0:T(8,128)(2,1)} %get-tuple-element.65) | copy-start | bytes 2064388
  58.4 3.9 %collective-permute-start.8 = (bf16[256,512]{1,0:T(8,128)(2,1)S(1)}, bf16[256,512]{1,0:T(8,128)(2,1)S(1)}, u32[]{:S(2)}, u32[]{:S(2)}) collective-permute-start(bf16[256,512]{1,0:T(8,128)(2,1)S(1)} %get-tuple-element.121), channel_id=1, source_target_pairs={{0,2},{2,0},{4,6},{6,4},{8,10},{10,8},{12,14},{14,12},{16,18},{18,... | collective-permute-start | bytes 786440 | tf_op jit(solution)/shard_map/ppermute | solution.py:390
  62.3 17.3 %copy-start.3 = (bf16[512,512]{1,0:T(8,128)(2,1)}, bf16[512,512]{1,0:T(8,128)(2,1)S(1)}, u32[]{:S(2)}) copy-start(bf16[512,512]{1,0:T(8,128)(2,1)S(1)} %constant_dynamic-update-slice_fusion.6.refs_5_) | copy-start | bytes 1572868
  65.4 11.8 %copy-start.14 = (bf16[1344,256]{1,0:T(8,128)(2,1)}, bf16[1344,256]{1,0:T(8,128)(2,1)S(1)}, u32[]{:S(2)}) copy-start(bf16[1344,256]{1,0:T(8,128)(2,1)S(1)} %collective-permute-done.10) | copy-start | bytes 2064388
  65.4 14.2 %collective-permute-start.11 = (bf16[512,512]{1,0:T(8,128)(2,1)S(1)}, bf16[512,512]{1,0:T(8,128)(2,1)S(1)}, u32[]{:S(2)}, u32[]{:S(2)}) collective-permute-start(bf16[512,512]{1,0:T(8,128)(2,1)S(1)} %constant_dynamic-update-slice_fusion.6.refs_5_), channel_id=1, source_target_pairs={{0,8},{2,10},{4,12},{6,14},{8,16},{10,18},{12,20},{14,22},{16,24},... | collective-permute-start | bytes 1572872 | tf_op jit(solution)/shard_map/ppermute | solution.py:386
  72.2 13.6 %copy-start.19 = (bf16[512,512]{1,0:T(8,128)(2,1)S(1)}, bf16[512,512]{1,0:T(8,128)(2,1)}, u32[]{:S(2)}) copy-start(bf16[512,512]{1,0:T(8,128)(2,1)} %get-tuple-element.79) | copy-start | bytes 1572868
  72.2 13.6 %collective-permute-start.14 = (bf16[512,512]{1,0:T(8,128)(2,1)S(1)}, bf16[512,512]{1,0:T(8,128)(2,1)S(1)}, u32[]{:S(2)}, u32[]{:S(2)}) collective-permute-start(bf16[512,512]{1,0:T(8,128)(2,1)S(1)} %fusion.1), channel_id=1, source_target_pairs={{8,0},{10,2},{12,4},{14,6},{16,8},{18,10},{20,12},{22,14},{24,16},... | collective-permute-start | bytes 1572872 | tf_op jit(solution)/shard_map/ppermute | solution.py:386
  74.9 15.3 %collective-permute-start.18 = (bf16[1344,256]{1,0:T(8,128)(2,1)}, bf16[1344,256]{1,0:T(8,128)(2,1)S(1)}, u32[]{:S(2)}, u32[]{:S(2)}) collective-permute-start(bf16[1344,256]{1,0:T(8,128)(2,1)} %collective-permute-done.7), channel_id=1, source_target_pairs={{0,1},{1,0},{2,3},{3,2},{4,5},{5,4},{6,7},{7,6},{8,9},{9,8},{10,11... | collective-permute-start | bytes 2064392 | tf_op jit(solution)/shard_map/ppermute | solution.py:395
  77.2 10.3 %copy-start.7 = (bf16[1344,512]{1,0:T(8,128)(2,1)}, bf16[1344,512]{1,0:T(8,128)(2,1)S(1)}, u32[]{:S(2)}) copy-start(bf16[1344,512]{1,0:T(8,128)(2,1)S(1)} %constant_dynamic-update-slice_fusion.refs_0_) | copy-start | bytes 4128772
  77.2 54.0 %collective-permute-start.19 = (bf16[1344,512]{1,0:T(8,128)(2,1)S(1)}, bf16[1344,512]{1,0:T(8,128)(2,1)}, u32[]{:S(2)}, u32[]{:S(2)}) collective-permute-start(bf16[1344,512]{1,0:T(8,128)(2,1)S(1)} %constant_dynamic-update-slice_fusion.refs_0_), channel_id=1, source_target_pairs={{0,2},{2,0},{4,6},{6,4},{8,10},{10,8},{12,14},{14,12},{16,18},{18,... | collective-permute-start | bytes 4128776 | tf_op jit(solution)/shard_map/ppermute | solution.py:390
  79.6 7.8 %copy-start.15 = (bf16[1344,256]{1,0:T(8,128)(2,1)S(1)}, bf16[1344,256]{1,0:T(8,128)(2,1)}, u32[]{:S(2)}) copy-start(bf16[1344,256]{1,0:T(8,128)(2,1)} %copy-done.14) | copy-start | bytes 2064388
  79.6 7.8 %copy-start.12 = (bf16[512,512]{1,0:T(8,128)(2,1)}, bf16[512,512]{1,0:T(8,128)(2,1)S(1)}, u32[]{:S(2)}) copy-start(bf16[512,512]{1,0:T(8,128)(2,1)S(1)} %collective-permute-done.11.refs_3_) | copy-start | bytes 1572868
  79.7 18.1 %collective-permute-start.13 = (bf16[512,512]{1,0:T(8,128)(2,1)S(1)}, bf16[512,512]{1,0:T(8,128)(2,1)S(1)}, u32[]{:S(2)}, u32[]{:S(2)}) collective-permute-start(bf16[512,512]{1,0:T(8,128)(2,1)S(1)} %broadcast_select_fusion), channel_id=1, source_target_pairs={{0,4},{2,6},{4,0},{6,2},{8,12},{10,14},{12,8},{14,10},{16,20},{18,... | collective-permute-start | bytes 1572872 | tf_op jit(solution)/shard_map/ppermute | solution.py:430
  86.1 29.8 %copy-start.4 = (bf16[512,512]{1,0:T(8,128)(2,1)}, bf16[512,512]{1,0:T(8,128)(2,1)S(1)}, u32[]{:S(2)}) copy-start(bf16[512,512]{1,0:T(8,128)(2,1)S(1)} %fusion.3.refs_4_) | copy-start | bytes 1572868
  86.1 28.5 %collective-permute-start.15 = (bf16[512,512]{1,0:T(8,128)(2,1)S(1)}, bf16[512,512]{1,0:T(8,128)(2,1)S(1)}, u32[]{:S(2)}, u32[]{:S(2)}) collective-permute-start(bf16[512,512]{1,0:T(8,128)(2,1)S(1)} %fusion.3.refs_4_), channel_id=1, source_target_pairs={{0,1},{1,0},{2,3},{3,2},{4,5},{5,4},{6,7},{7,6},{8,9},{9,8},{10,11... | collective-permute-start | bytes 1572872 | tf_op jit(solution)/shard_map/ppermute | solution.py:395
  90.2 24.3 %copy-start.8 = (bf16[1344,512]{1,0:T(8,128)(2,1)}, bf16[1344,512]{1,0:T(8,128)(2,1)S(1)}, u32[]{:S(2)}) copy-start(bf16[1344,512]{1,0:T(8,128)(2,1)S(1)} %constant_dynamic-update-slice_fusion.2.refs_1_) | copy-start | bytes 4128772
  90.2 43.2 %collective-permute-start.20 = (bf16[1344,512]{1,0:T(8,128)(2,1)S(1)}, bf16[1344,512]{1,0:T(8,128)(2,1)}, u32[]{:S(2)}, u32[]{:S(2)}) collective-permute-start(bf16[1344,512]{1,0:T(8,128)(2,1)S(1)} %constant_dynamic-update-slice_fusion.2.refs_1_), channel_id=1, source_target_pairs={{0,2},{2,0},{4,6},{6,4},{8,10},{10,8},{12,14},{14,12},{16,18},{18,... | collective-permute-start | bytes 4128776 | tf_op jit(solution)/shard_map/ppermute | solution.py:390
  95.6 20.5 %collective-permute-start.22 = (bf16[512,512]{1,0:T(8,128)(2,1)S(1)}, bf16[512,512]{1,0:T(8,128)(2,1)S(1)}, u32[]{:S(2)}, u32[]{:S(2)}) collective-permute-start(bf16[512,512]{1,0:T(8,128)(2,1)S(1)} %fusion.3.refs_4_), channel_id=1, source_target_pairs={{0,5},{1,4},{2,7},{3,6},{4,1},{5,0},{6,3},{7,2},{8,13},{9,12},{10,... | collective-permute-start | bytes 1572872 | tf_op jit(solution)/shard_map/ppermute | solution.py:405
  115.5 2.5 %collective-permute-start.16 = (bf16[512,512]{1,0:T(8,128)(2,1)S(1)}, bf16[512,512]{1,0:T(8,128)(2,1)}, u32[]{:S(2)}, u32[]{:S(2)}) collective-permute-start(bf16[512,512]{1,0:T(8,128)(2,1)S(1)} %pad_maximum_fusion.5), channel_id=1, source_target_pairs={{0,2},{2,0},{4,6},{6,4},{8,10},{10,8},{12,14},{14,12},{16,18},{18,... | collective-permute-start | bytes 1572872 | tf_op jit(solution)/shard_map/ppermute | solution.py:390
  115.8 15.1 %collective-permute-start.21 = (bf16[512,512]{1,0:T(8,128)(2,1)S(1)}, bf16[512,512]{1,0:T(8,128)(2,1)}, u32[]{:S(2)}, u32[]{:S(2)}) collective-permute-start(bf16[512,512]{1,0:T(8,128)(2,1)S(1)} %fusion.3.refs_4_), channel_id=1, source_target_pairs={{0,4},{1,5},{2,6},{3,7},{4,0},{5,1},{6,2},{7,3},{8,12},{9,13},{10,... | collective-permute-start | bytes 1572872 | tf_op jit(solution)/shard_map/ppermute | solution.py:405
  116.1 25.5 %collective-permute-start.24 = (bf16[512,512]{1,0:T(8,128)(2,1)}, bf16[512,512]{1,0:T(8,128)(2,1)}, u32[]{:S(2)}, u32[]{:S(2)}) collective-permute-start(bf16[512,512]{1,0:T(8,128)(2,1)} %get-tuple-element.103), channel_id=1, source_target_pairs={{8,0},{10,2},{12,4},{14,6},{16,8},{18,10},{20,12},{22,14},{24,16},... | collective-permute-start | bytes 1572872 | tf_op jit(solution)/shard_map/ppermute | solution.py:386
  118.0 23.6 %collective-permute-start.23 = (bf16[512,512]{1,0:T(8,128)(2,1)}, bf16[512,512]{1,0:T(8,128)(2,1)}, u32[]{:S(2)}, u32[]{:S(2)}) collective-permute-start(bf16[512,512]{1,0:T(8,128)(2,1)} %get-tuple-element.84), channel_id=1, source_target_pairs={{4,0},{6,2},{8,4},{10,6},{12,8},{14,10},{16,12},{18,14},{20,16},{2... | collective-permute-start | bytes 1572872 | tf_op jit(solution)/shard_map/ppermute | solution.py:386
  130.9 47.5 %collective-permute-start.26 = (bf16[256,2688]{1,0:T(8,128)(2,1)}, bf16[256,2688]{1,0:T(8,128)(2,1)S(1)}, u32[]{:S(2)}, u32[]{:S(2)}) collective-permute-start(bf16[256,2688]{1,0:T(8,128)(2,1)} %get-tuple-element.87), channel_id=1, source_target_pairs={{0,1},{1,0},{2,3},{3,2},{4,5},{5,4},{6,7},{7,6},{8,9},{9,8},{10,11... | collective-permute-start | bytes 4128776 | tf_op jit(solution)/shard_map/ppermute | solution.py:395
  131.1 15.5 %copy-start.23 = (bf16[512,512]{1,0:T(8,128)(2,1)S(1)}, bf16[512,512]{1,0:T(8,128)(2,1)}, u32[]{:S(2)}) copy-start(bf16[512,512]{1,0:T(8,128)(2,1)} %get-tuple-element.90) | copy-start | bytes 1572868
  131.2 47.0 %collective-permute-start.17 = (bf16[2,256,1024]{2,1,0:T(8,128)(2,1)}, bf16[2,256,1024]{2,1,0:T(8,128)(2,1)S(1)}, u32[]{:S(2)}, u32[]{:S(2)}) collective-permute-start(bf16[2,256,1024]{2,1,0:T(8,128)(2,1)} %get-tuple-element.88), channel_id=1, source_target_pairs={{0,2},{2,0},{4,6},{6,4},{8,10},{10,8},{12,14},{14,12},{16,18},{18,... | collective-permute-start | bytes 3145736 | tf_op jit(solution)/shard_map/ppermute | solution.py:390
  141.6 34.5 %copy-start.17 = (f32[336,512]{1,0:T(8,128)S(1)}, f32[336,512]{1,0:T(8,128)}, u32[]{:S(2)}) copy-start(f32[336,512]{1,0:T(8,128)} %get-tuple-element.107) | copy-start | bytes 2064388
  141.6 9.8 %collective-permute-start.27 = (bf16[336,512]{1,0:T(8,128)(2,1)}, bf16[336,512]{1,0:T(8,128)(2,1)S(1)}, u32[]{:S(2)}, u32[]{:S(2)}) collective-permute-start(bf16[336,512]{1,0:T(8,128)(2,1)} %get-tuple-element.108), channel_id=1, source_target_pairs={{0,8},{2,10},{4,12},{6,14},{8,16},{10,18},{12,20},{14,22},{16,24},... | collective-permute-start | bytes 1032200 | tf_op jit(solution)/shard_map/ppermute | solution.py:599
  143.4 29.7 %collective-permute-start.28 = (bf16[336,512]{1,0:T(8,128)(2,1)}, bf16[336,512]{1,0:T(8,128)(2,1)S(1)}, u32[]{:S(2)}, u32[]{:S(2)}) collective-permute-start(bf16[336,512]{1,0:T(8,128)(2,1)} %get-tuple-element.109), channel_id=1, source_target_pairs={{0,16},{2,18},{4,20},{6,22},{8,24},{10,26},{12,28},{14,30},{16,0},... | collective-permute-start | bytes 1032200 | tf_op jit(solution)/shard_map/ppermute | solution.py:599
  145.2 30.9 %collective-permute-start.29 = (bf16[336,512]{1,0:T(8,128)(2,1)}, bf16[336,512]{1,0:T(8,128)(2,1)S(1)}, u32[]{:S(2)}, u32[]{:S(2)}) collective-permute-start(bf16[336,512]{1,0:T(8,128)(2,1)} %get-tuple-element.110), channel_id=1, source_target_pairs={{0,24},{2,26},{4,28},{6,30},{8,0},{10,2},{12,4},{14,6},{16,8},{18,... | collective-permute-start | bytes 1032200 | tf_op jit(solution)/shard_map/ppermute | solution.py:599
  151.4 25.5 %collective-permute-start.25 = (bf16[256,512]{1,0:T(8,128)(2,1)S(1)}, bf16[256,512]{1,0:T(8,128)(2,1)S(1)}, u32[]{:S(2)}, u32[]{:S(2)}) collective-permute-start(bf16[256,512]{1,0:T(8,128)(2,1)S(1)} %get-tuple-element.115), channel_id=1, source_target_pairs={{0,2},{2,0},{4,6},{6,4},{8,10},{10,8},{12,14},{14,12},{16,18},{18,... | collective-permute-start | bytes 786440 | tf_op jit(solution)/shard_map/ppermute | solution.py:390
  176.4 1.8 collective-permute-start.30
  (14 other events, 22.2 us)

commit v13 on v11

--- a/solution.py
+++ b/solution.py
@@ -282,7 +282,7 @@
 def run_product(at, parts, w, kind):
     rows = parts[0].shape[0]
     depth, width = w.shape
-    tile = 512
+    tile = width
     if len(parts) == 1:
         x_specs = [pl.BlockSpec((rows, depth), lambda j, at: (0, at[0]))]
     else:

time: 178 us -> 179 us (level)
  no operation moved by 1% of the time
where the time goes in v13:
time: 179 us; the launch traced here: 177 us
  Pallas kernels  60.7 us (34%)
  starting transfers between devices  60.1 us (34%)
  waiting for transfers between devices  33.6 us (19%)
  local copies, waits for them, and re-layouts  12.2 us (7%)
  other arithmetic  9.07 us (5%)
    ppermute x9, starting transfers between devices, swapped(): lax.ppermute(x, 'ctx', [(i, i ^ 1) for i in range(lax.axis_size('ctx'))])  27.1 us
    ppermute x6, starting transfers between devices, shifted(): lax.ppermute(x, 'ctx', [(i, i + by) for i in range(length) if 0 <= i + by...  17 us
    pallas_call x1, Pallas kernels, run_grads(): pl.pallas_call(functools.partial(grads_kernel, blk, n_arr - 1), grid_spec...  16 us
    pallas_call x1, Pallas kernels, run_probs(): pl.pallas_call(functools.partial(probs_kernel, blk, n_arr - 1), grid_spec...  14.3 us
    ppermute x3, waiting for transfers between devices, shards(): lax.ppermute(by_z[d], 'ctx', [(i, (i + 4 * d) % n_ctx) for i in range(n_c...  12.7 us
    pallas_call x2, Pallas kernels, run_product(): pl.pallas_call(product_kernel, grid_spec=pltpu.PrefetchScalarGridSpec(num...  11.1 us
    pallas_call x1, Pallas kernels, run_weight(): pl.pallas_call(functools.partial(weight_kernel, n_z, n), grid_spec=pltpu....  8.12 us
    ppermute x6, waiting for transfers between devices, shifted(): lax.ppermute(x, 'ctx', [(i, i + by) for i in range(length) if 0 <= i + by...  7.56 us
  transfers between devices with their start and end apart: 31, of which 10 were waited for; matrix products, arithmetic and copies ran while one was open for 9% of the time, Pallas kernels for 34%

profile of v13, /device:TPU:9, one launch (start us, length us, event | category | flops | bytes accessed | tf_op | source)
XLA Modules:
  0.0 177.0 jit_solution(15027761121998138954)
XLA Ops:
  0.7 1.2 dynamic-slice_bitcast_fusion.1
  1.9 1.3 collective-permute-start.3
  4.0 1.1 dynamic-slice_bitcast_fusion.5
  6.8 2.0 %dynamic-slice_bitcast_fusion = bf16[256,1408]{1,0:T(8,128)(2,1)} fusion(bf16[1,256,5376]{2,1,0:T(8,128)(2,1)} %param.6, s32[]{:T(128)S(6)} %select_n.97), kind=kLoop, calls=%fused_computation.12 | loop fusion | bytes 1441796 | tf_op jit(solution)/shard_map/dynamic_slice | solution.py:469
  9.3 1.0 slice_dynamic-update-slice_fusion.2
  11.0 3.1 %collective-permute-start.2 = (bf16[528,512]{1,0:T(8,128)(2,1)S(1)}, bf16[528,512]{1,0:T(8,128)(2,1)S(1)}, u32[]{:S(2)}, u32[]{:S(2)}) collective-permute-start(bf16[528,512]{1,0:T(8,128)(2,1)S(1)} %pad_maximum_fusion.2.refs_2_), channel_id=1, source_target_pairs={{0,4},{2,6},{4,8},{6,10},{8,12},{10,14},{12,16},{14,18},{16,20},{1... | collective-permute-start | bytes 1622024 | tf_op jit(solution)/shard_map/ppermute | solution.py:386
  14.2 3.2 %collective-permute-start.1 = (bf16[528,512]{1,0:T(8,128)(2,1)S(1)}, bf16[528,512]{1,0:T(8,128)(2,1)S(1)}, u32[]{:S(2)}, u32[]{:S(2)}) collective-permute-start(bf16[528,512]{1,0:T(8,128)(2,1)S(1)} %pad_maximum_fusion.2.refs_2_), channel_id=1, source_target_pairs={{0,8},{2,10},{4,12},{6,14},{8,16},{10,18},{12,20},{14,22},{16,24},... | collective-permute-start | bytes 1622024 | tf_op jit(solution)/shard_map/ppermute | solution.py:386
  17.4 1.1 pad_maximum_fusion
  19.9 4.2 %pieces.1 = (bf16[1344,256]{1,0:T(8,128)(2,1)}, bf16[1344,256]{1,0:T(8,128)(2,1)}, bf16[1344,256]{1,0:T(8,128)(2,1)}, bf16[1344,256]{1,0:T(8,128)(2,1)}) custom-call(s32[2]{0:T(128)} %pad_add_fusion.at_ref, bf16[256,5376]{1,0:T(8,128)(2,1)} %bitcast.29), custom_call_target="tpu_custom_call" | custom-call | flops 1048576 | bytes 4096 | tf_op jit(solution)/shard_map/pieces/pallas_call | solution.py:260
  24.1 5.6 %product.3 = f32[256,1024]{1,0:T(8,128)} custom-call(s32[1]{0:T(128)} %bitcast.10.at_ref, bf16[256,5376]{1,0:T(8,128)(2,1)} %bitcast.30, bf16[2688,1024]{1,0:T(8,128)(2,1)} %w_ref.1), custom_call_target="tpu_custom_call" | custom-call | flops 1048576 | bytes 4096 | tf_op jit(solution)/shard_map/product/pallas_call | solution.py:290
  29.7 1.3 collective-permute-start.7
  31.0 2.1 %collective-permute-done.4.refs_1_ = bf16[256,1408]{1,0:T(8,128)(2,1)} collective-permute-done((bf16[256,1408]{1,0:T(8,128)(2,1)}, bf16[256,1408]{1,0:T(8,128)(2,1)}, u32[]{:S(2)}, u32[]{:S(2)}) %collective-permute-start.4) | collective-permute-done | bytes 720928 | tf_op jit(solution)/shard_map/ppermute | solution.py:395
  33.1 5.4 %product.2 = bf16[256,1024]{1,0:T(8,128)(2,1)} custom-call(s32[1]{0:T(128)} %constant.86.clone.1.at_ref, bf16[256,1280]{1,0:T(8,128)(2,1)} %collective-permute-done.3.refs_0_, bf16[256,1408]{1,0:T(8,128)(2,1)} %collective-permute-done.4.refs_1_, bf16[2688,1024]{1,0:T(8,128)(2,1)} %w_ref.1), custom_call_target="tpu_custom_call" | custom-call | flops 1048576 | bytes 4096 | tf_op jit(solution)/shard_map/product/pallas_call | solution.py:290
  38.6 1.2 collective-permute-start.6
  41.3 1.2 collective-permute-start.9
  42.6 1.0 copy-done
  43.5 14.3 %probs.1 = (bf16[4,2,1280,512]{3,2,1,0:T(8,128)(2,1)}, f32[4,2,1,512]{3,2,1,0:T(1,128)}, bf16[4,2,128,512]{3,2,1,0:T(8,128)(2,1)}, bf16[512,512]{1,0:T(8,128)(2,...) custom-call(s32[1]{0:T(128)} %bitcast.core_ref, s32[1,512]{1,0:T(1,128)} %add_maximum_fusion.low_ref, ...), custom_call_target="tpu_custom_call" | custom-call | flops 1048576 | bytes 4096 | tf_op jit(solution)/shard_map/probs/pallas_call | solution.py:158
  58.4 2.7 %collective-permute-start.8 = (bf16[256,512]{1,0:T(8,128)(2,1)S(1)}, bf16[256,512]{1,0:T(8,128)(2,1)S(1)}, u32[]{:S(2)}, u32[]{:S(2)}) collective-permute-start(bf16[256,512]{1,0:T(8,128)(2,1)S(1)} %get-tuple-element.123), channel_id=1, source_target_pairs={{0,2},{2,0},{4,6},{6,4},{8,10},{10,8},{12,14},{14,12},{16,18},{18,... | collective-permute-start | bytes 786440 | tf_op jit(solution)/shard_map/ppermute | solution.py:390
  61.2 1.3 collective-permute-start.20
  62.6 2.8 %collective-permute-done.10 = bf16[1344,256]{1,0:T(8,128)(2,1)S(1)} collective-permute-done((bf16[1344,256]{1,0:T(8,128)(2,1)}, bf16[1344,256]{1,0:T(8,128)(2,1)S(1)}, u32[]{:S(2)}, u32[]{:S(2)}) %collective-permute-start.10) | collective-permute-done | bytes 688160 | tf_op jit(solution)/shard_map/ppermute | solution.py:395
  65.4 3.2 %collective-permute-start.11 = (bf16[512,512]{1,0:T(8,128)(2,1)S(1)}, bf16[512,512]{1,0:T(8,128)(2,1)S(1)}, u32[]{:S(2)}, u32[]{:S(2)}) collective-permute-start(bf16[512,512]{1,0:T(8,128)(2,1)S(1)} %constant_dynamic-update-slice_fusion.6.refs_5_), channel_id=1, source_target_pairs={{0,8},{2,10},{4,12},{6,14},{8,16},{10,18},{12,20},{14,22},{16,24},... | collective-permute-start | bytes 1572872 | tf_op jit(solution)/shard_map/ppermute | solution.py:386
  68.6 3.4 %collective-permute-done.12 = bf16[512,512]{1,0:T(8,128)(2,1)S(1)} collective-permute-done((bf16[512,512]{1,0:T(8,128)(2,1)}, bf16[512,512]{1,0:T(8,128)(2,1)S(1)}, u32[]{:S(2)}, u32[]{:S(2)}) %collective-permute-start.12) | collective-permute-done | bytes 524320 | tf_op jit(solution)/shard_map/ppermute | solution.py:430
  72.2 2.6 %collective-permute-start.14 = (bf16[512,512]{1,0:T(8,128)(2,1)S(1)}, bf16[512,512]{1,0:T(8,128)(2,1)S(1)}, u32[]{:S(2)}, u32[]{:S(2)}) collective-permute-start(bf16[512,512]{1,0:T(8,128)(2,1)S(1)} %fusion.1), channel_id=1, source_target_pairs={{8,0},{10,2},{12,4},{14,6},{16,8},{18,10},{20,12},{22,14},{24,16},... | collective-permute-start | bytes 1572872 | tf_op jit(solution)/shard_map/ppermute | solution.py:386
  74.9 2.0 %collective-permute-start.21 = (bf16[1344,512]{1,0:T(8,128)(2,1)S(1)}, bf16[1344,512]{1,0:T(8,128)(2,1)}, u32[]{:S(2)}, u32[]{:S(2)}) collective-permute-start(bf16[1344,512]{1,0:T(8,128)(2,1)S(1)} %constant_dynamic-update-slice_fusion.refs_0_), channel_id=1, source_target_pairs={{0,2},{2,0},{4,6},{6,4},{8,10},{10,8},{12,14},{14,12},{16,18},{18,... | collective-permute-start | bytes 4128776 | tf_op jit(solution)/shard_map/ppermute | solution.py:390
  77.0 1.3 collective-permute-start.13
  78.3 7.5 %collective-permute-done.14 = bf16[512,512]{1,0:T(8,128)(2,1)S(1)} collective-permute-done((bf16[512,512]{1,0:T(8,128)(2,1)S(1)}, bf16[512,512]{1,0:T(8,128)(2,1)S(1)}, u32[]{:S(2)}, u32[]{:S(2)}) %collective-permute-start.14) | collective-permute-done | bytes 524320 | tf_op jit(solution)/shard_map/ppermute | solution.py:386
  86.1 1.3 collective-permute-start.15
  87.5 3.1 %collective-permute-start.22 = (bf16[1344,512]{1,0:T(8,128)(2,1)S(1)}, bf16[1344,512]{1,0:T(8,128)(2,1)}, u32[]{:S(2)}, u32[]{:S(2)}) collective-permute-start(bf16[1344,512]{1,0:T(8,128)(2,1)S(1)} %constant_dynamic-update-slice_fusion.2.refs_1_), channel_id=1, source_target_pairs={{0,2},{2,0},{4,6},{6,4},{8,10},{10,8},{12,14},{14,12},{16,18},{18,... | collective-permute-start | bytes 4128776 | tf_op jit(solution)/shard_map/ppermute | solution.py:390
  90.5 2.1 %collective-permute-start.18 = (bf16[512,512]{1,0:T(8,128)(2,1)S(1)}, bf16[512,512]{1,0:T(8,128)(2,1)}, u32[]{:S(2)}, u32[]{:S(2)}) collective-permute-start(bf16[512,512]{1,0:T(8,128)(2,1)S(1)} %fusion.3.refs_4_), channel_id=1, source_target_pairs={{0,5},{1,4},{2,7},{3,6},{4,1},{5,0},{6,3},{7,2},{8,13},{9,12},{10,... | collective-permute-start | bytes 1572872 | tf_op jit(solution)/shard_map/ppermute | solution.py:405
  93.4 16.0 %grads.1 = (bf16[256,2048]{1,0:T(8,128)(2,1)}, bf16[256,2048]{1,0:T(8,128)(2,1)}, bf16[2,256,1024]{2,1,0:T(8,128)(2,1)}, bf16[512,512]{1,0:T(8,128)(2,1)}, bf16[...) custom-call(s32[1]{0:T(128)} %bitcast.core_ref, bf16[4,2,1280,512]{3,2,1,0:T(8,128)(2,1)} %get-tuple-element.62.e_ref, ...), custom_call_target="tpu_custom_call" | custom-call | flops 1048576 | bytes 4096 | tf_op jit(solution)/shard_map/grads/pallas_call | solution.py:201
  110.7 1.1 collective-permute-done.18.refs_7_
  111.8 2.6 %collective-permute-start.24 = (bf16[512,512]{1,0:T(8,128)(2,1)}, bf16[512,512]{1,0:T(8,128)(2,1)}, u32[]{:S(2)}, u32[]{:S(2)}) collective-permute-start(bf16[512,512]{1,0:T(8,128)(2,1)} %get-tuple-element.105), channel_id=1, source_target_pairs={{8,0},{10,2},{12,4},{14,6},{16,8},{18,10},{20,12},{22,14},{24,16},... | collective-permute-start | bytes 1572872 | tf_op jit(solution)/shard_map/ppermute | solution.py:386
  114.4 2.7 %collective-permute-done.17.refs_5_ = bf16[512,512]{1,0:T(8,128)(2,1)} collective-permute-done((bf16[512,512]{1,0:T(8,128)(2,1)S(1)}, bf16[512,512]{1,0:T(8,128)(2,1)}, u32[]{:S(2)}, u32[]{:S(2)}) %collective-permute-start.17) | collective-permute-done | bytes 524320 | tf_op jit(solution)/shard_map/ppermute | solution.py:405
  117.1 2.3 %collective-permute-start.23 = (bf16[512,512]{1,0:T(8,128)(2,1)}, bf16[512,512]{1,0:T(8,128)(2,1)}, u32[]{:S(2)}, u32[]{:S(2)}) collective-permute-start(bf16[512,512]{1,0:T(8,128)(2,1)} %get-tuple-element.85), channel_id=1, source_target_pairs={{4,0},{6,2},{8,4},{10,6},{12,8},{14,10},{16,12},{18,14},{20,16},{2... | collective-permute-start | bytes 1572872 | tf_op jit(solution)/shard_map/ppermute | solution.py:386
  120.2 1.1 constant_dynamic-update-slice_fusion.5.dv_ref
  121.4 1.0 copy-done.6
  122.3 7.0 %tokens.1 = (bf16[256,5376]{1,0:T(8,128)(2,1)}, bf16[256,2688]{1,0:T(8,128)(2,1)}) custom-call(s32[1]{0:T(128)} %bitcast.10.at_ref, bf16[512,1024]{1,0:T(8,128)(2,1)} %copy-done.6, bf16[2688,1024]{1,0:T(8,128)(2,1)} %w_ref.1), custom_call_target="tpu_custom_call" | custom-call | flops 1048576 | bytes 4096 | tf_op jit(solution)/shard_map/tokens/pallas_call | solution.py:364
  129.3 1.1 collective-permute-start.26
  130.4 1.4 collective-permute-start.19
  131.9 8.1 %weight.1 = (f32[336,512]{1,0:T(8,128)}, bf16[336,512]{1,0:T(8,128)(2,1)}, bf16[336,512]{1,0:T(8,128)(2,1)}, bf16[336,512]{1,0:T(8,128)(2,1)}) custom-call(s32[2]{0:T(128)} %pad_add_fusion.1.at_ref, bf16[1344,512]{1,0:T(8,128)(2,1)} %copy-done.7, bf16[1344,512]{1,0:T(8,128)(2,1)} %copy-done.8, bf16[1344,512]{1,0:T(8,128)(2,1)} %collective-permute-done.21.refs_2_, ...), custom_call_target="tpu_custom_call" | custom-call | flops 1048576 | bytes 4096 | tf_op jit(solution)/shard_map/weight/pallas_call | solution.py:336
  140.0 1.3 collective-permute-start.27
  141.6 1.4 collective-permute-start.29
  143.0 1.4 add_convert_fusion
  144.5 5.3 %collective-permute-done.27 = bf16[336,512]{1,0:T(8,128)(2,1)S(1)} collective-permute-done((bf16[336,512]{1,0:T(8,128)(2,1)}, bf16[336,512]{1,0:T(8,128)(2,1)S(1)}, u32[]{:S(2)}, u32[]{:S(2)}) %collective-permute-start.27) | collective-permute-done | bytes 344096 | tf_op jit(solution)/shard_map/ppermute | solution.py:600
  149.8 15.3 %collective-permute-start.25 = (bf16[256,512]{1,0:T(8,128)(2,1)S(1)}, bf16[256,512]{1,0:T(8,128)(2,1)S(1)}, u32[]{:S(2)}, u32[]{:S(2)}) collective-permute-start(bf16[256,512]{1,0:T(8,128)(2,1)S(1)} %get-tuple-element.117), channel_id=1, source_target_pairs={{0,2},{2,0},{4,6},{6,4},{8,10},{10,8},{12,14},{14,12},{16,18},{18,... | collective-permute-start | bytes 786440 | tf_op jit(solution)/shard_map/ppermute | solution.py:390
  165.0 6.0 %collective-permute-done.28 = bf16[336,512]{1,0:T(8,128)(2,1)S(1)} collective-permute-done((bf16[336,512]{1,0:T(8,128)(2,1)}, bf16[336,512]{1,0:T(8,128)(2,1)S(1)}, u32[]{:S(2)}, u32[]{:S(2)}) %collective-permute-start.28) | collective-permute-done | bytes 344096 | tf_op jit(solution)/shard_map/ppermute | solution.py:600
  171.0 1.4 collective-permute-done.29
  173.4 1.2 collective-permute-done.30
  (126 shorter events, 14.4 us)
Async XLA Ops:
  0.7 8.4 %copy-start.1 = (bf16[1,256,2048]{2,1,0:T(8,128)(2,1)S(1)}, bf16[1,256,2048]{2,1,0:T(8,128)(2,1)}, u32[]{:S(2)}) copy-start(bf16[1,256,2048]{2,1,0:T(8,128)(2,1)} %param.7) | copy-start | bytes 3145732
  1.9 7.2 %copy-start.9 = (bf16[1,256,2048]{2,1,0:T(8,128)(2,1)S(1)}, bf16[1,256,2048]{2,1,0:T(8,128)(2,1)}, u32[]{:S(2)}) copy-start(bf16[1,256,2048]{2,1,0:T(8,128)(2,1)} %param.10) | copy-start | bytes 3145732
  1.9 27.8 %collective-permute-start.3 = (bf16[256,1280]{1,0:T(8,128)(2,1)S(1)}, bf16[256,1280]{1,0:T(8,128)(2,1)}, u32[]{:S(2)}, u32[]{:S(2)}) collective-permute-start(bf16[256,1280]{1,0:T(8,128)(2,1)S(1)} %dynamic-slice_bitcast_fusion.1), channel_id=1, source_target_pairs={{0,1},{1,0},{2,3},{3,2},{4,5},{5,4},{6,7},{7,6},{8,9},{9,8},{10,11... | collective-permute-start | bytes 1966088 | tf_op jit(solution)/shard_map/ppermute | solution.py:395
  5.8 3.4 %collective-permute-start = (bf16[272,512]{1,0:T(8,128)(2,1)}, bf16[272,512]{1,0:T(8,128)(2,1)}, u32[]{:S(2)}, u32[]{:S(2)}) collective-permute-start(bf16[272,512]{1,0:T(8,128)(2,1)} %maximum_maximum_fusion.1), channel_id=1, source_target_pairs={{0,2},{2,0},{4,6},{6,4},{8,10},{10,8},{12,14},{14,12},{16,18},{18,... | collective-permute-start | bytes 835592 | tf_op jit(solution)/shard_map/ppermute | solution.py:390
  8.8 24.3 %collective-permute-start.4 = (bf16[256,1408]{1,0:T(8,128)(2,1)}, bf16[256,1408]{1,0:T(8,128)(2,1)}, u32[]{:S(2)}, u32[]{:S(2)}) collective-permute-start(bf16[256,1408]{1,0:T(8,128)(2,1)} %dynamic-slice_bitcast_fusion), channel_id=1, source_target_pairs={{0,1},{1,0},{2,3},{3,2},{4,5},{5,4},{6,7},{7,6},{8,9},{9,8},{10,11... | collective-permute-start | bytes 2162696 | tf_op jit(solution)/shard_map/ppermute | solution.py:395
  11.0 13.1 %copy-start.2 = (bf16[528,512]{1,0:T(8,128)(2,1)}, bf16[528,512]{1,0:T(8,128)(2,1)S(1)}, u32[]{:S(2)}) copy-start(bf16[528,512]{1,0:T(8,128)(2,1)S(1)} %pad_maximum_fusion.2.refs_2_) | copy-start | bytes 1622020
  11.0 28.8 %collective-permute-start.2 = (bf16[528,512]{1,0:T(8,128)(2,1)S(1)}, bf16[528,512]{1,0:T(8,128)(2,1)S(1)}, u32[]{:S(2)}, u32[]{:S(2)}) collective-permute-start(bf16[528,512]{1,0:T(8,128)(2,1)S(1)} %pad_maximum_fusion.2.refs_2_), channel_id=1, source_target_pairs={{0,4},{2,6},{4,8},{6,10},{8,12},{10,14},{12,16},{14,18},{16,20},{1... | collective-permute-start | bytes 1622024 | tf_op jit(solution)/shard_map/ppermute | solution.py:386
  14.2 25.9 %collective-permute-start.1 = (bf16[528,512]{1,0:T(8,128)(2,1)S(1)}, bf16[528,512]{1,0:T(8,128)(2,1)S(1)}, u32[]{:S(2)}, u32[]{:S(2)}) collective-permute-start(bf16[528,512]{1,0:T(8,128)(2,1)S(1)} %pad_maximum_fusion.2.refs_2_), channel_id=1, source_target_pairs={{0,8},{2,10},{4,12},{6,14},{8,16},{10,18},{12,20},{14,22},{16,24},... | collective-permute-start | bytes 1622024 | tf_op jit(solution)/shard_map/ppermute | solution.py:386
  18.4 24.1 %collective-permute-start.5 = (bf16[256,2048]{1,0:T(8,128)(2,1)}, bf16[256,2048]{1,0:T(8,128)(2,1)S(1)}, u32[]{:S(2)}, u32[]{:S(2)}) collective-permute-start(bf16[256,2048]{1,0:T(8,128)(2,1)} %pad_maximum_fusion), channel_id=1, source_target_pairs={{0,2},{2,0},{4,6},{6,4},{8,10},{10,8},{12,14},{14,12},{16,18},{18,... | collective-permute-start | bytes 3145736 | tf_op jit(solution)/shard_map/ppermute | solution.py:390
  29.7 28.4 %collective-permute-start.7 = (bf16[1344,256]{1,0:T(8,128)(2,1)}, bf16[1344,256]{1,0:T(8,128)(2,1)S(1)}, u32[]{:S(2)}, u32[]{:S(2)}) collective-permute-start(bf16[1344,256]{1,0:T(8,128)(2,1)} %get-tuple-element.72), channel_id=1, source_target_pairs={{0,4},{2,6},{4,0},{6,2},{8,12},{10,14},{12,8},{14,10},{16,20},{18,... | collective-permute-start | bytes 2064392 | tf_op jit(solution)/shard_map/ppermute | solution.py:430
  38.6 19.6 %collective-permute-start.6 = (bf16[256,1024]{1,0:T(8,128)(2,1)}, bf16[256,1024]{1,0:T(8,128)(2,1)S(1)}, u32[]{:S(2)}, u32[]{:S(2)}) collective-permute-start(bf16[256,1024]{1,0:T(8,128)(2,1)} %product.2), channel_id=1, source_target_pairs={{0,1},{1,0},{2,3},{3,2},{4,5},{5,4},{6,7},{7,6},{8,9},{9,8},{10,11... | collective-permute-start | bytes 1572872 | tf_op jit(solution)/shard_map/ppermute | solution.py:395
  39.8 2.8 %copy-start.10 = (bf16[528,512]{1,0:T(8,128)(2,1)}, bf16[528,512]{1,0:T(8,128)(2,1)S(1)}, u32[]{:S(2)}) copy-start(bf16[528,512]{1,0:T(8,128)(2,1)S(1)} %collective-permute-done.2.refs_1_) | copy-start | bytes 1622020
  39.8 25.6 %collective-permute-start.10 = (bf16[1344,256]{1,0:T(8,128)(2,1)}, bf16[1344,256]{1,0:T(8,128)(2,1)S(1)}, u32[]{:S(2)}, u32[]{:S(2)}) collective-permute-start(bf16[1344,256]{1,0:T(8,128)(2,1)} %get-tuple-element.75), channel_id=1, source_target_pairs={{0,1},{1,0},{2,3},{3,2},{4,5},{5,4},{6,7},{7,6},{8,9},{9,8},{10,11... | collective-permute-start | bytes 2064392 | tf_op jit(solution)/shard_map/ppermute | solution.py:395
  41.3 24.1 %collective-permute-start.9 = (bf16[1344,256]{1,0:T(8,128)(2,1)}, bf16[1344,256]{1,0:T(8,128)(2,1)S(1)}, u32[]{:S(2)}, u32[]{:S(2)}) collective-permute-start(bf16[1344,256]{1,0:T(8,128)(2,1)} %get-tuple-element.74), channel_id=1, source_target_pairs={{0,4},{2,6},{4,0},{6,2},{8,12},{10,14},{12,8},{14,10},{16,20},{18,... | collective-permute-start | bytes 2064392 | tf_op jit(solution)/shard_map/ppermute | solution.py:430
  43.5 14.6 %copy-start.5 = (f32[256,1024]{1,0:T(8,128)S(1)}, f32[256,1024]{1,0:T(8,128)}, u32[]{:S(2)}) copy-start(f32[256,1024]{1,0:T(8,128)} %product.3) | copy-start | bytes 3145732
  57.9 3.3 %copy-start.14 = (bf16[1344,256]{1,0:T(8,128)(2,1)S(1)}, bf16[1344,256]{1,0:T(8,128)(2,1)}, u32[]{:S(2)}) copy-start(bf16[1344,256]{1,0:T(8,128)(2,1)} %get-tuple-element.66) | copy-start | bytes 2064388
  57.9 14.2 %collective-permute-start.12 = (bf16[512,512]{1,0:T(8,128)(2,1)}, bf16[512,512]{1,0:T(8,128)(2,1)S(1)}, u32[]{:S(2)}, u32[]{:S(2)}) collective-permute-start(bf16[512,512]{1,0:T(8,128)(2,1)} %get-tuple-element.71), channel_id=1, source_target_pairs={{0,4},{2,6},{4,0},{6,2},{8,12},{10,14},{12,8},{14,10},{16,20},{18,... | collective-permute-start | bytes 1572872 | tf_op jit(solution)/shard_map/ppermute | solution.py:430
  58.3 13.7 %copy-start.20 = (bf16[512,512]{1,0:T(8,128)(2,1)S(1)}, bf16[512,512]{1,0:T(8,128)(2,1)}, u32[]{:S(2)}) copy-start(bf16[512,512]{1,0:T(8,128)(2,1)} %get-tuple-element.77) | copy-start | bytes 1572868
  58.4 4.1 %collective-permute-start.8 = (bf16[256,512]{1,0:T(8,128)(2,1)S(1)}, bf16[256,512]{1,0:T(8,128)(2,1)S(1)}, u32[]{:S(2)}, u32[]{:S(2)}) collective-permute-start(bf16[256,512]{1,0:T(8,128)(2,1)S(1)} %get-tuple-element.123), channel_id=1, source_target_pairs={{0,2},{2,0},{4,6},{6,4},{8,10},{10,8},{12,14},{14,12},{16,18},{18,... | collective-permute-start | bytes 786440 | tf_op jit(solution)/shard_map/ppermute | solution.py:390
  61.2 26.2 %collective-permute-start.20 = (bf16[1344,256]{1,0:T(8,128)(2,1)S(1)}, bf16[1344,256]{1,0:T(8,128)(2,1)S(1)}, u32[]{:S(2)}, u32[]{:S(2)}) collective-permute-start(bf16[1344,256]{1,0:T(8,128)(2,1)S(1)} %collective-permute-done.7), channel_id=1, source_target_pairs={{0,1},{1,0},{2,3},{3,2},{4,5},{5,4},{6,7},{7,6},{8,9},{9,8},{10,11... | collective-permute-start | bytes 2064392 | tf_op jit(solution)/shard_map/ppermute | solution.py:395
  62.5 14.4 %copy-start.3 = (bf16[512,512]{1,0:T(8,128)(2,1)}, bf16[512,512]{1,0:T(8,128)(2,1)S(1)}, u32[]{:S(2)}) copy-start(bf16[512,512]{1,0:T(8,128)(2,1)S(1)} %constant_dynamic-update-slice_fusion.6.refs_5_) | copy-start | bytes 1572868
  65.4 11.5 %collective-permute-start.11 = (bf16[512,512]{1,0:T(8,128)(2,1)S(1)}, bf16[512,512]{1,0:T(8,128)(2,1)S(1)}, u32[]{:S(2)}, u32[]{:S(2)}) collective-permute-start(bf16[512,512]{1,0:T(8,128)(2,1)S(1)} %constant_dynamic-update-slice_fusion.6.refs_5_), channel_id=1, source_target_pairs={{0,8},{2,10},{4,12},{6,14},{8,16},{10,18},{12,20},{14,22},{16,24},... | collective-permute-start | bytes 1572872 | tf_op jit(solution)/shard_map/ppermute | solution.py:386
  72.2 13.7 %copy-start.17 = (bf16[512,512]{1,0:T(8,128)(2,1)S(1)}, bf16[512,512]{1,0:T(8,128)(2,1)}, u32[]{:S(2)}) copy-start(bf16[512,512]{1,0:T(8,128)(2,1)} %get-tuple-element.80) | copy-start | bytes 1572868
  72.2 13.6 %collective-permute-start.14 = (bf16[512,512]{1,0:T(8,128)(2,1)S(1)}, bf16[512,512]{1,0:T(8,128)(2,1)S(1)}, u32[]{:S(2)}, u32[]{:S(2)}) collective-permute-start(bf16[512,512]{1,0:T(8,128)(2,1)S(1)} %fusion.1), channel_id=1, source_target_pairs={{8,0},{10,2},{12,4},{14,6},{16,8},{18,10},{20,12},{22,14},{24,16},... | collective-permute-start | bytes 1572872 | tf_op jit(solution)/shard_map/ppermute | solution.py:386
  74.9 11.2 %copy-start.7 = (bf16[1344,512]{1,0:T(8,128)(2,1)}, bf16[1344,512]{1,0:T(8,128)(2,1)S(1)}, u32[]{:S(2)}) copy-start(bf16[1344,512]{1,0:T(8,128)(2,1)S(1)} %constant_dynamic-update-slice_fusion.refs_0_) | copy-start | bytes 4128772
  74.9 55.6 %collective-permute-start.21 = (bf16[1344,512]{1,0:T(8,128)(2,1)S(1)}, bf16[1344,512]{1,0:T(8,128)(2,1)}, u32[]{:S(2)}, u32[]{:S(2)}) collective-permute-start(bf16[1344,512]{1,0:T(8,128)(2,1)S(1)} %constant_dynamic-update-slice_fusion.refs_0_), channel_id=1, source_target_pairs={{0,2},{2,0},{4,6},{6,4},{8,10},{10,8},{12,14},{14,12},{16,18},{18,... | collective-permute-start | bytes 4128776 | tf_op jit(solution)/shard_map/ppermute | solution.py:390
  76.9 10.5 %copy-start.12 = (bf16[512,512]{1,0:T(8,128)(2,1)}, bf16[512,512]{1,0:T(8,128)(2,1)S(1)}, u32[]{:S(2)}) copy-start(bf16[512,512]{1,0:T(8,128)(2,1)S(1)} %collective-permute-done.11.refs_3_) | copy-start | bytes 1572868
  77.0 15.6 %collective-permute-start.13 = (bf16[512,512]{1,0:T(8,128)(2,1)S(1)}, bf16[512,512]{1,0:T(8,128)(2,1)S(1)}, u32[]{:S(2)}, u32[]{:S(2)}) collective-permute-start(bf16[512,512]{1,0:T(8,128)(2,1)S(1)} %broadcast_select_fusion), channel_id=1, source_target_pairs={{0,4},{2,6},{4,0},{6,2},{8,12},{10,14},{12,8},{14,10},{16,20},{18,... | collective-permute-start | bytes 1572872 | tf_op jit(solution)/shard_map/ppermute | solution.py:430
  86.1 23.3 %copy-start.4 = (bf16[512,512]{1,0:T(8,128)(2,1)}, bf16[512,512]{1,0:T(8,128)(2,1)S(1)}, u32[]{:S(2)}) copy-start(bf16[512,512]{1,0:T(8,128)(2,1)S(1)} %fusion.3.refs_4_) | copy-start | bytes 1572868
  86.1 23.3 %collective-permute-start.15 = (bf16[512,512]{1,0:T(8,128)(2,1)S(1)}, bf16[512,512]{1,0:T(8,128)(2,1)S(1)}, u32[]{:S(2)}, u32[]{:S(2)}) collective-permute-start(bf16[512,512]{1,0:T(8,128)(2,1)S(1)} %fusion.3.refs_4_), channel_id=1, source_target_pairs={{0,1},{1,0},{2,3},{3,2},{4,5},{5,4},{6,7},{7,6},{8,9},{9,8},{10,11... | collective-permute-start | bytes 1572872 | tf_op jit(solution)/shard_map/ppermute | solution.py:395
  87.4 22.0 %copy-start.8 = (bf16[1344,512]{1,0:T(8,128)(2,1)}, bf16[1344,512]{1,0:T(8,128)(2,1)S(1)}, u32[]{:S(2)}) copy-start(bf16[1344,512]{1,0:T(8,128)(2,1)S(1)} %constant_dynamic-update-slice_fusion.2.refs_1_) | copy-start | bytes 4128772
  87.5 44.4 %collective-permute-start.22 = (bf16[1344,512]{1,0:T(8,128)(2,1)S(1)}, bf16[1344,512]{1,0:T(8,128)(2,1)}, u32[]{:S(2)}, u32[]{:S(2)}) collective-permute-start(bf16[1344,512]{1,0:T(8,128)(2,1)S(1)} %constant_dynamic-update-slice_fusion.2.refs_1_), channel_id=1, source_target_pairs={{0,2},{2,0},{4,6},{6,4},{8,10},{10,8},{12,14},{14,12},{16,18},{18,... | collective-permute-start | bytes 4128776 | tf_op jit(solution)/shard_map/ppermute | solution.py:390
  90.5 21.3 %collective-permute-start.18 = (bf16[512,512]{1,0:T(8,128)(2,1)S(1)}, bf16[512,512]{1,0:T(8,128)(2,1)}, u32[]{:S(2)}, u32[]{:S(2)}) collective-permute-start(bf16[512,512]{1,0:T(8,128)(2,1)S(1)} %fusion.3.refs_4_), channel_id=1, source_target_pairs={{0,5},{1,4},{2,7},{3,6},{4,1},{5,0},{6,3},{7,2},{8,13},{9,12},{10,... | collective-permute-start | bytes 1572872 | tf_op jit(solution)/shard_map/ppermute | solution.py:405
  92.6 24.5 %collective-permute-start.17 = (bf16[512,512]{1,0:T(8,128)(2,1)S(1)}, bf16[512,512]{1,0:T(8,128)(2,1)}, u32[]{:S(2)}, u32[]{:S(2)}) collective-permute-start(bf16[512,512]{1,0:T(8,128)(2,1)S(1)} %fusion.3.refs_4_), channel_id=1, source_target_pairs={{0,4},{1,5},{2,6},{3,7},{4,0},{5,1},{6,2},{7,3},{8,12},{9,13},{10,... | collective-permute-start | bytes 1572872 | tf_op jit(solution)/shard_map/ppermute | solution.py:405
  109.4 7.7 %copy-start.13 = (bf16[512,512]{1,0:T(8,128)(2,1)}, bf16[512,512]{1,0:T(8,128)(2,1)S(1)}, u32[]{:S(2)}) copy-start(bf16[512,512]{1,0:T(8,128)(2,1)S(1)} %collective-permute-done.15.refs_6_) | copy-start | bytes 1572868
  110.4 9.8 %collective-permute-start.16 = (bf16[512,512]{1,0:T(8,128)(2,1)}, bf16[512,512]{1,0:T(8,128)(2,1)}, u32[]{:S(2)}, u32[]{:S(2)}) collective-permute-start(bf16[512,512]{1,0:T(8,128)(2,1)} %pad_maximum_fusion.5), channel_id=1, source_target_pairs={{0,2},{2,0},{4,6},{6,4},{8,10},{10,8},{12,14},{14,12},{16,18},{18,... | collective-permute-start | bytes 1572872 | tf_op jit(solution)/shard_map/ppermute | solution.py:390
  111.8 28.2 %collective-permute-start.24 = (bf16[512,512]{1,0:T(8,128)(2,1)}, bf16[512,512]{1,0:T(8,128)(2,1)}, u32[]{:S(2)}, u32[]{:S(2)}) collective-permute-start(bf16[512,512]{1,0:T(8,128)(2,1)} %get-tuple-element.105), channel_id=1, source_target_pairs={{8,0},{10,2},{12,4},{14,6},{16,8},{18,10},{20,12},{22,14},{24,16},... | collective-permute-start | bytes 1572872 | tf_op jit(solution)/shard_map/ppermute | solution.py:386
  117.1 22.9 %collective-permute-start.23 = (bf16[512,512]{1,0:T(8,128)(2,1)}, bf16[512,512]{1,0:T(8,128)(2,1)}, u32[]{:S(2)}, u32[]{:S(2)}) collective-permute-start(bf16[512,512]{1,0:T(8,128)(2,1)} %get-tuple-element.85), channel_id=1, source_target_pairs={{4,0},{6,2},{8,4},{10,6},{12,8},{14,10},{16,12},{18,14},{20,16},{2... | collective-permute-start | bytes 1572872 | tf_op jit(solution)/shard_map/ppermute | solution.py:386
  129.3 45.4 %collective-permute-start.26 = (bf16[256,2688]{1,0:T(8,128)(2,1)}, bf16[256,2688]{1,0:T(8,128)(2,1)S(1)}, u32[]{:S(2)}, u32[]{:S(2)}) collective-permute-start(bf16[256,2688]{1,0:T(8,128)(2,1)} %get-tuple-element.91), channel_id=1, source_target_pairs={{0,1},{1,0},{2,3},{3,2},{4,5},{5,4},{6,7},{7,6},{8,9},{9,8},{10,11... | collective-permute-start | bytes 4128776 | tf_op jit(solution)/shard_map/ppermute | solution.py:395
  130.4 12.5 %copy-start.21 = (bf16[512,512]{1,0:T(8,128)(2,1)S(1)}, bf16[512,512]{1,0:T(8,128)(2,1)}, u32[]{:S(2)}) copy-start(bf16[512,512]{1,0:T(8,128)(2,1)} %get-tuple-element.94) | copy-start | bytes 1572868
  130.4 44.1 %collective-permute-start.19 = (bf16[2,256,1024]{2,1,0:T(8,128)(2,1)}, bf16[2,256,1024]{2,1,0:T(8,128)(2,1)S(1)}, u32[]{:S(2)}, u32[]{:S(2)}) collective-permute-start(bf16[2,256,1024]{2,1,0:T(8,128)(2,1)} %get-tuple-element.92), channel_id=1, source_target_pairs={{0,2},{2,0},{4,6},{6,4},{8,10},{10,8},{12,14},{14,12},{16,18},{18,... | collective-permute-start | bytes 3145736 | tf_op jit(solution)/shard_map/ppermute | solution.py:390
  140.0 32.4 %copy-start.15 = (f32[336,512]{1,0:T(8,128)S(1)}, f32[336,512]{1,0:T(8,128)}, u32[]{:S(2)}) copy-start(f32[336,512]{1,0:T(8,128)} %get-tuple-element.109) | copy-start | bytes 2064388
  140.0 9.8 %collective-permute-start.27 = (bf16[336,512]{1,0:T(8,128)(2,1)}, bf16[336,512]{1,0:T(8,128)(2,1)S(1)}, u32[]{:S(2)}, u32[]{:S(2)}) collective-permute-start(bf16[336,512]{1,0:T(8,128)(2,1)} %get-tuple-element.110), channel_id=1, source_target_pairs={{0,8},{2,10},{4,12},{6,14},{8,16},{10,18},{12,20},{14,22},{16,24},... | collective-permute-start | bytes 1032200 | tf_op jit(solution)/shard_map/ppermute | solution.py:600
  141.3 29.7 %collective-permute-start.28 = (bf16[336,512]{1,0:T(8,128)(2,1)}, bf16[336,512]{1,0:T(8,128)(2,1)S(1)}, u32[]{:S(2)}, u32[]{:S(2)}) collective-permute-start(bf16[336,512]{1,0:T(8,128)(2,1)} %get-tuple-element.111), channel_id=1, source_target_pairs={{0,16},{2,18},{4,20},{6,22},{8,24},{10,26},{12,28},{14,30},{16,0},... | collective-permute-start | bytes 1032200 | tf_op jit(solution)/shard_map/ppermute | solution.py:600
  141.6 30.8 %collective-permute-start.29 = (bf16[336,512]{1,0:T(8,128)(2,1)}, bf16[336,512]{1,0:T(8,128)(2,1)S(1)}, u32[]{:S(2)}, u32[]{:S(2)}) collective-permute-start(bf16[336,512]{1,0:T(8,128)(2,1)} %get-tuple-element.112), channel_id=1, source_target_pairs={{0,24},{2,26},{4,28},{6,30},{8,0},{10,2},{12,4},{14,6},{16,8},{18,... | collective-permute-start | bytes 1032200 | tf_op jit(solution)/shard_map/ppermute | solution.py:600
  149.8 23.5 %collective-permute-start.25 = (bf16[256,512]{1,0:T(8,128)(2,1)S(1)}, bf16[256,512]{1,0:T(8,128)(2,1)S(1)}, u32[]{:S(2)}, u32[]{:S(2)}) collective-permute-start(bf16[256,512]{1,0:T(8,128)(2,1)S(1)} %get-tuple-element.117), channel_id=1, source_target_pairs={{0,2},{2,0},{4,6},{6,4},{8,10},{10,8},{12,14},{14,12},{16,18},{18,... | collective-permute-start | bytes 786440 | tf_op jit(solution)/shard_map/ppermute | solution.py:390
  172.7 2.5 %copy-start.22 = (bf16[256,5376]{1,0:T(8,128)(2,1)S(1)}, bf16[256,5376]{1,0:T(8,128)(2,1)}, u32[]{:S(2)}) copy-start(bf16[256,5376]{1,0:T(8,128)(2,1)} %get-tuple-element.108) | copy-start | bytes 8257540
  172.7 1.8 %collective-permute-start.30 = (f32[168,512]{1,0:T(8,128)S(1)}, f32[168,512]{1,0:T(8,128)S(1)}, u32[]{:S(2)}, u32[]{:S(2)}) collective-permute-start(f32[168,512]{1,0:T(8,128)S(1)} %get-tuple-element.115), channel_id=1, source_target_pairs={{0,2},{2,0},{4,6},{6,4},{8,10},{10,8},{12,14},{14,12},{16,18},{18,... | collective-permute-start | bytes 1032200 | tf_op jit(solution)/shard_map/ppermute | solution.py:390
  (11 other events, 16.2 us)
